TPU v7x, 128 devices: a whole 4x4x4 slice. The times are simulated.
128 devices in a mesh: cuts: 128 (over z, y, x, core).
Axes of the slice: x: 4, y: 4, z: 4, core: 2. Of those that a mesh axis runs over, the one named last changes fastest.
Arguments:
- field: float32 [2, 16, 128, 128, 128], P(None, None, 'cuts'), may hold values from -6 to 6
- phase_bins: int32 [16, 128, 8192], P(None, 'cuts'), may hold values from 0 to 15
- phase_jitter: float32 [16, 128, 8192], P(None, 'cuts'), may hold values from 0 to 1
- energy: float32 [16, 128, 8192], P(None, 'cuts'), may hold values from -6 to 6
- profile: float32 [128, 128], replicated, may hold values from 0.1 to 1
- delays: int32 [16, 64, 1], replicated, may hold values from 0 to 127; in each aligned block of 1024 rows (0 to 1023, 1024 to 2047, ..., all dimensions but the last counted through in order) at most 20 rows name the same one
Outputs:
- field_out: float32 [2, 16, 128, 128, 128], P(None, None, 'cuts')
- phase_out: float32 [16, 128, 8192], P(None, 'cuts')
- energy_out: float32 [16, 128, 8192], P(None, 'cuts')
Inputs may be any that keep to these rules, and one draw needn't show every extreme that they name: `delays`: over all pairs (k, j) no delay value is named more than 20 times, a bound that some block reaches; every value 0 to 127 is named.
All inputs are finite; a program needn't handle non-finite values.
Results may differ from a plain program's by a relative error of at most 0.0003.
Values sent between devices are 32-bit elements; how exact they have to be, the bound alone decides.
No kernel may reach another device: no remote copies, remote signals or barrier semaphores. Data moves between devices by JAX's collectives and lax.ppermute only.
A program may use at most 64 MiB of HBM per device.

v0:
```python
import functools
import math

import jax
import jax.numpy as jnp
import ml_dtypes
import numpy as np
from jax import lax
from jax.experimental import pallas as pl
from jax.experimental.pallas import tpu as pltpu
from jax.sharding import PartitionSpec as P

BLOCK = 128
NBINS = 16
KAPPA = 1.0
OMEGA = 1.0
GAIN = 16.0
PHASE_COEF = 20.0
GRID = 128
GROUPS = 16
NBS = 64
COUNT = GROUPS * NBS
PEERS = 128
CAP = 20
ROWS = PEERS * CAP
BATCH = 16
VMEM_LIMIT = 24 * 1024 * 1024
HIGHEST = lax.Precision.HIGHEST


def line_operator(power):
    index = np.arange(GRID)
    freq = ((index + GRID // 2) % GRID - GRID // 2) / GRID
    weight = np.exp(-1j * PHASE_COEF * power * freq**2)
    wave = np.exp(2j * np.pi * (index[:, None] * index[None, :] % GRID) / GRID)
    column = wave @ weight / GRID
    matrix = column[(index[:, None] - index[None, :]) % GRID]
    return matrix.real, matrix.imag


def left_form(real, imag):
    return np.block([[real, -imag], [imag, real]])


def right_form(real, imag):
    return np.block([[real, imag], [-imag, real]])


def halves(matrix):
    high = matrix.astype(ml_dtypes.bfloat16)
    return high, (matrix - high.astype(np.float64)).astype(ml_dtypes.bfloat16)


def deep_left(matrix):
    high, low = halves(matrix)
    return jnp.asarray(np.concatenate([high, high, low], axis=1))


def deep_right(matrix):
    high, low = halves(matrix)
    return jnp.asarray(np.concatenate([high, high, low], axis=0))


def fitted(function, degree):
    top = (math.pi / 2 + 0.01) ** 2
    nodes = (np.cos(np.pi * (np.arange(400) + 0.5) / 400) + 1) / 2 * top
    series = np.polynomial.chebyshev.Chebyshev.fit(nodes, function(np.sqrt(nodes)), degree, domain=[0, top])
    return [float(c) for c in series.convert(kind=np.polynomial.Polynomial).coef]


SIN_COEF = fitted(lambda r: np.sin(r) / r, 5)
COS_COEF = fitted(np.cos, 6)
PI_HIGH = 3.140625
PI_MID = 9.67502593994140625e-4
PI_LOW = math.pi - PI_HIGH - PI_MID


def horner(coefs, x):
    value = jnp.float32(coefs[-1])
    for c in coefs[-2::-1]:
        value = value * x + jnp.float32(c)
    return value


def cos_sin(x):
    turns = jnp.round(x * jnp.float32(1.0 / math.pi))
    r = x - turns * jnp.float32(PI_HIGH)
    r = r - turns * jnp.float32(PI_MID)
    r = r - turns * jnp.float32(PI_LOW)
    half = turns * 0.5
    sign = 1.0 - 4.0 * jnp.abs(half - jnp.round(half))
    square = r * r
    return horner(COS_COEF, square) * sign, horner(SIN_COEF, square) * (r * sign)


def lane_total(rows):
    return jnp.broadcast_to(jnp.sum(rows, axis=1, keepdims=True), rows.shape)


def slots_of(delays):
    row = jnp.concatenate([delays[k] for k in range(GROUPS)], axis=1)
    values = lax.broadcasted_iota(jnp.int32, (PEERS, COUNT), 0)
    onehot = jnp.where(values == row, 1.0, 0.0)
    before = lax.broadcasted_iota(jnp.int32, (COUNT, COUNT), 0) < lax.broadcasted_iota(jnp.int32, (COUNT, COUNT), 1)
    upper = jnp.where(before, 1.0, 0.0).astype(jnp.bfloat16)
    earlier = jnp.dot(onehot.astype(jnp.bfloat16), upper, preferred_element_type=jnp.float32)
    return row, jnp.sum(earlier * onehot, axis=0, keepdims=True).astype(jnp.int32)


def folded(row):
    return jnp.concatenate([row[:, n * 128 : (n + 1) * 128] for n in range(COUNT // 128)], axis=0)


def rows_of(k):
    return pl.ds(pl.multiple_of(k * NBS, NBS), NBS)


def first_kernel(
    field_hbm, profile_hbm, bins_hbm, jitter_hbm, energy_hbm, delays_hbm, left_hbm, right_hbm,
    phases, energies, small, beam, places,
    field, profile, bins, jitter, energy, delays, left, right, acc, sems,
):
    pairs = [
        (profile_hbm, profile), (left_hbm, left), (right_hbm, right), (delays_hbm, delays),
        (field_hbm, field), (bins_hbm, bins), (jitter_hbm, jitter), (energy_hbm, energy),
    ]
    copies = [pltpu.make_async_copy(src, dst, sems.at[n]) for n, (src, dst) in enumerate(pairs)]
    for copy in copies:
        copy.start()
    for copy in copies[:4]:
        copy.wait()
    p = profile[...]
    half = jnp.dot(left[...], p, precision=HIGHEST, preferred_element_type=jnp.float32)
    both = jnp.concatenate([half[:GRID], half[GRID:]], axis=1)
    spread = jnp.dot(both, right[...], precision=HIGHEST, preferred_element_type=jnp.float32)
    beam[0] = spread[:, :GRID]
    beam[2] = p
    beam[1] = spread[:, GRID:]
    row, slot = slots_of(delays)
    places[0:1] = row
    places[1:2] = slot
    copies[4].wait()

    def project(k, carry):
        re, im = field[0, k], field[1, k]
        dr, di, q = beam[0], beam[1], profile[...]
        acc[0, pl.ds(k, 1)] = jnp.sum(q * re, axis=0, keepdims=True)
        acc[1, pl.ds(k, 1)] = jnp.sum(q * im, axis=0, keepdims=True)
        acc[2, pl.ds(k, 1)] = jnp.sum(dr * re - di * im, axis=0, keepdims=True)
        acc[3, pl.ds(k, 1)] = jnp.sum(dr * im + di * re, axis=0, keepdims=True)
        return carry

    lax.fori_loop(0, GROUPS, project, 0)
    self_re = jnp.sum(p * beam[0])
    self_im = jnp.sum(p * beam[1])
    for n in range(4):
        acc[n] = lane_total(acc[n]) * (1.0 / GRID)
    for copy in copies[5:]:
        copy.wait()

    def push(k, carry):
        rows = rows_of(k)
        ph = jnp.float32(2.0 * math.pi / NBINS) * (bins[rows].astype(jnp.float32) + jitter[rows])
        ph, en = pushed(ph, energy[rows], acc[0, pl.ds(k, 1)], acc[1, pl.ds(k, 1)])
        phases[rows] = ph
        energies[rows] = en
        c, s = cos_sin(ph)
        small[2, pl.ds(k, 1)] = jnp.sum(c, axis=0, keepdims=True)
        small[3, pl.ds(k, 1)] = jnp.sum(s, axis=0, keepdims=True)
        return carry

    lax.fori_loop(0, GROUPS, push, 0)
    bre = lane_total(small[2]) * (1.0 / (NBS * BLOCK))
    bim = lane_total(small[3]) * (-1.0 / (NBS * BLOCK))
    small[2] = bre
    small[3] = bim
    gain = GAIN / GRID
    small[0] = acc[2] + gain * (bre * self_re - bim * self_im)
    small[1] = acc[3] + gain * (bre * self_im + bim * self_re)


def pushed(ph, en, amp_re, amp_im):
    c, s = cos_sin(ph)
    en = en - KAPPA * (amp_re * c - amp_im * s)
    return ph + OMEGA * en, en


def carried(value, flag):
    rolled = jnp.concatenate([jnp.zeros_like(value[:1]), value[:-1]], axis=0)
    return jnp.where(flag, rolled, value)


def second_kernel(
    mine, phases1, energies1, arrived, places, send_hbm, small, acc, phases, energies, send, index_v, index, sems
):
    me = mine[0]
    index_v[...] = folded(((me + places[0:1]) % PEERS) * (2 * CAP) + places[1:2])
    to_scalar = pltpu.make_async_copy(index_v, index, sems.at[0])
    to_scalar.start()
    for n in range(4):
        acc[n] = carried(arrived[n], me == 0)

    def push(k, carry):
        rows = rows_of(k)
        ph, en = pushed(phases1[rows], energies1[rows], acc[0, pl.ds(k, 1)], acc[1, pl.ds(k, 1)])
        phases[rows] = ph
        energies[rows] = en
        c, s = cos_sin(ph)
        small[0, pl.ds(k, 1)] = jnp.sum(c, axis=0, keepdims=True)
        small[1, pl.ds(k, 1)] = jnp.sum(s, axis=0, keepdims=True)
        return carry

    lax.fori_loop(0, GROUPS, push, 0)
    small[0] = lane_total(small[0]) * (1.0 / (NBS * BLOCK))
    small[1] = lane_total(small[1]) * (-1.0 / (NBS * BLOCK))
    small[2] = acc[2]
    small[3] = acc[3]
    to_scalar.wait()

    def put(n, carry):
        base = pl.multiple_of(n * BATCH, BATCH)
        spots = [index[n // (128 // BATCH), n % (128 // BATCH) * BATCH + m] for m in range(BATCH)]
        ph = [phases[pl.ds(base + m, 1)] for m in range(BATCH)]
        en = [energies[pl.ds(base + m, 1)] for m in range(BATCH)]
        for m in range(BATCH):
            send[pl.ds(spots[m], 1)] = ph[m]
            send[pl.ds(spots[m] + CAP, 1)] = en[m]
        return carry

    lax.fori_loop(0, COUNT // BATCH, put, 0)
    out = pltpu.make_async_copy(send, send_hbm, sems.at[0])
    out.start()
    out.wait()


def wide_halves(x):
    high = x.astype(jnp.bfloat16)
    return high, (x - high.astype(jnp.float32)).astype(jnp.bfloat16)


def pick_kernel(mine, recv, places, phases, energies, index_v, index, sems):
    me = mine[0]
    index_v[...] = folded(((me - places[0:1] + PEERS) % PEERS) * (2 * CAP) + places[1:2])
    to_scalar = pltpu.make_async_copy(index_v, index, sems.at[0])
    to_scalar.start()
    to_scalar.wait()

    def get(n, carry):
        base = pl.multiple_of(n * BATCH, BATCH)
        spots = [index[n // (128 // BATCH), n % (128 // BATCH) * BATCH + m] for m in range(BATCH)]
        ph = [recv[pl.ds(spot, 1)] for spot in spots]
        en = [recv[pl.ds(spot + CAP, 1)] for spot in spots]
        for m in range(BATCH):
            phases[pl.ds(base + m, 1)] = ph[m]
            energies[pl.ds(base + m, 1)] = en[m]
        return carry

    lax.fori_loop(0, COUNT // BATCH, get, 0)


SLAB = 4
PIECES = ((0, 2), (2, 4), (4, 16))


def field_kernel(mine, piece_a, piece_b, piece_c, small, beam, left, right, out_hbm, acc, out, sems):
    me = mine[0]
    for n in range(4):
        acc[n] = GAIN * carried(small[n], me == 0)

    def plane(c, k):
        for piece, (low, high) in zip((piece_a, piece_b, piece_c), PIECES):
            if low <= k < high:
                return piece[c, k - low]
        return jnp.zeros((GRID, GRID), jnp.float32)

    late = me < 2
    p = beam[2]
    dr, di = beam[0], beam[1]
    copies = []
    for slab in range(GROUPS // SLAB):
        ks = range(slab * SLAB, (slab + 1) * SLAB)
        rows = []
        for k in ks:
            parts = [jnp.where(late, plane(c, k - 1), plane(c, k)) + acc[2 + c, k : k + 1] * p for c in range(2)]
            rows.append(jnp.concatenate(parts, axis=1))
        hi, lo = wide_halves(jnp.concatenate(rows, axis=0))
        half = jnp.dot(jnp.concatenate([hi, lo, hi], axis=1), right[...], preferred_element_type=jnp.float32)
        cols = []
        for m in range(SLAB):
            mid = half[m * GRID : (m + 1) * GRID]
            cols.append(jnp.concatenate([mid[:, :GRID], mid[:, GRID:]], axis=0))
        hi, lo = wide_halves(jnp.concatenate(cols, axis=1))
        full = jnp.dot(left[...], jnp.concatenate([hi, lo, hi], axis=0), preferred_element_type=jnp.float32)
        for m, k in enumerate(ks):
            cr, ci = acc[0, k : k + 1], acc[1, k : k + 1]
            out[0, k] = full[:GRID, m * GRID : (m + 1) * GRID] + (cr * dr - ci * di)
            out[1, k] = full[GRID:, m * GRID : (m + 1) * GRID] + (cr * di + ci * dr)
        for c in range(2):
            span = pl.ds(slab * SLAB, SLAB)
            copies.append(pltpu.make_async_copy(out.at[c, span], out_hbm.at[c, span], sems.at[2 * slab + c]))
            copies[-1].start()
    for copy in copies:
        copy.wait()


def shifted(value, axis, steps):
    count = lax.axis_size(axis)
    pairs = [(source, (source + steps) % count) for source in range(count)]
    return lax.ppermute(value, axis, pairs)


def shape(*dims, dtype=jnp.float32):
    return jax.ShapeDtypeStruct(dims, dtype)


def whole():
    return pl.BlockSpec(memory_space=pltpu.VMEM)


def vmem(*dims, dtype=jnp.float32):
    return pltpu.VMEM(dims, dtype)


def in_hbm(value):
    return pltpu.with_memory_space_constraint(value, pltpu.HBM)


def exchange(send):
    return lax.all_to_all(send.reshape(PEERS, 2 * CAP, BLOCK), "cuts", split_axis=0, concat_axis=0, tiled=True)


def per_device(field, phase_bins, phase_jitter, energy, profile, delays):
    params = pltpu.CompilerParams(vmem_limit_bytes=VMEM_LIMIT)
    scalar = pl.BlockSpec(memory_space=pltpu.SMEM)
    remain = pl.BlockSpec(memory_space=pltpu.HBM)
    field = field.reshape(2, GROUPS, GRID, GRID)
    bins = phase_bins.reshape(COUNT, BLOCK)
    jitter = phase_jitter.reshape(COUNT, BLOCK)
    energies = energy.reshape(COUNT, BLOCK)
    mine = lax.axis_index("cuts").reshape(1)
    one, two = line_operator(1), line_operator(2)
    left_one = jnp.asarray(np.concatenate(one, axis=0), jnp.float32)
    right_one = jnp.asarray(right_form(*one), jnp.float32)
    sources = [field[:, low:high] for low, high in PIECES]
    field_a = shifted(sources[0], "cuts", 2)
    operands = [field, profile, bins, jitter, energies, delays.reshape(GROUPS, 1, NBS), left_one, right_one]
    phases1, energies1, small1, beam, places = pl.pallas_call(
        first_kernel,
        out_shape=(
            shape(COUNT, BLOCK),
            shape(COUNT, BLOCK),
            shape(4, GROUPS, 128),
            shape(3, GRID, GRID),
            shape(8, COUNT, dtype=jnp.int32),
        ),
        in_specs=[remain] * 8,
        out_specs=(whole(),) * 5,
        scratch_shapes=[
            vmem(2, GROUPS, GRID, GRID),
            vmem(GRID, GRID),
            vmem(COUNT, BLOCK, dtype=jnp.int32),
            vmem(COUNT, BLOCK),
            vmem(COUNT, BLOCK),
            vmem(GROUPS, 1, NBS, dtype=jnp.int32),
            vmem(2 * GRID, GRID),
            vmem(2 * GRID, 2 * GRID),
            vmem(4, GROUPS, 128),
            pltpu.SemaphoreType.DMA((8,)),
        ],
        compiler_params=params,
        name="project_push",
    )(*[in_hbm(value) for value in operands])
    arrived1 = shifted(small1, "cuts", 1)
    arrived1, field_a, source_b, source_c = lax.optimization_barrier((arrived1, field_a, sources[1], sources[2]))
    field_b = shifted(source_b, "cuts", 2)
    send, small2 = pl.pallas_call(
        second_kernel,
        out_shape=(pltpu.HBM((2 * ROWS, BLOCK), jnp.float32), shape(4, GROUPS, 128)),
        in_specs=[scalar] + [whole()] * 4,
        out_specs=(remain, whole()),
        scratch_shapes=[
            vmem(4, GROUPS, 128),
            vmem(COUNT, BLOCK),
            vmem(COUNT, BLOCK),
            vmem(2 * ROWS, BLOCK),
            vmem(8, 128, dtype=jnp.int32),
            pltpu.SMEM((8, 128), jnp.int32),
            pltpu.SemaphoreType.DMA((1,)),
        ],
        compiler_params=params,
        name="push_place",
    )(mine, phases1, energies1, arrived1, places)
    arrived2 = shifted(small2, "cuts", 1)
    send, field_b, source_c = lax.optimization_barrier((send, field_b, source_c))
    field_c = shifted(source_c, "cuts", 2)
    fits = jnp.max(delays) < PEERS
    recv = lax.cond(fits, exchange, lambda rows: jnp.zeros((PEERS, 2 * CAP, BLOCK), jnp.float32), send)
    phase_out, energy_out = pl.pallas_call(
        pick_kernel,
        out_shape=(shape(COUNT, BLOCK), shape(COUNT, BLOCK)),
        in_specs=[scalar] + [whole()] * 2,
        out_specs=(whole(),) * 2,
        scratch_shapes=[
            vmem(8, 128, dtype=jnp.int32),
            pltpu.SMEM((8, 128), jnp.int32),
            pltpu.SemaphoreType.DMA((1,)),
        ],
        compiler_params=params,
        name="pick",
    )(mine, recv.reshape(2 * ROWS, BLOCK), places)
    out = pl.pallas_call(
        field_kernel,
        out_shape=shape(2, GROUPS, GRID, GRID),
        in_specs=[scalar] + [whole()] * 7,
        out_specs=remain,
        scratch_shapes=[
            vmem(4, GROUPS, 128),
            vmem(2, GROUPS, GRID, GRID),
            pltpu.SemaphoreType.DMA((2 * GROUPS // SLAB,)),
        ],
        compiler_params=params,
        name="diffract",
    )(mine, field_a, field_b, field_c, arrived2, beam, deep_left(left_form(*two)), deep_right(right_form(*two)))
    return (
        out.reshape(2, GROUPS, 1, GRID, GRID),
        phase_out.reshape(GROUPS, 1, NBS * BLOCK),
        energy_out.reshape(GROUPS, 1, NBS * BLOCK),
    )


def solution(mesh):
    return jax.shard_map(
        per_device,
        mesh=mesh,
        in_specs=(
            P(None, None, "cuts", None, None),
            P(None, "cuts", None),
            P(None, "cuts", None),
            P(None, "cuts", None),
            P(),
            P(),
        ),
        out_specs=(P(None, None, "cuts", None, None), P(None, "cuts", None), P(None, "cuts", None)),
        check_vma=False,
    )
```

profile of v0, /device:TPU:0, one launch (start us, length us, event | category | flops | bytes accessed | tf_op | source)
XLA Modules:
  0.0 113.9 jit_solution(3146565451421941583)
XLA Ops:
  0.6 1.1 fusion
  1.7 0.0 copy-start.2
  1.7 1.6 %collective-permute-start.1 = (f32[2,2,128,128]{3,2,1,0:T(8,128)S(1)}, f32[2,2,128,128]{3,2,1,0:T(8,128)S(1)}, u32[]{:S(2)}, u32[]{:S(2)}) collective-permute-start(f32[2,2,128,128]{3,2,1,0:T(8,128)S(1)} %get-tuple-element.44), channel_id=1, source_target_pairs={{0,2},{1,3},{2,4},{3,5},{4,6},{5,7},{6,8},{7,9},{8,10},{9,11},{10,... | collective-permute-start | bytes 786440 | tf_op jit(solution)/shard_map/ppermute | solution.py:309
  3.4 4.8 %project_push.1 = (f32[1024,128]{1,0:T(8,128)S(1)}, f32[1024,128]{1,0:T(8,128)S(1)}, f32[4,16,128]{2,1,0:T(8,128)S(1)}, f32[3,128,128]{2,1,0:T(8,128)S(1)}, s32[8,1024]{1,0:T(8,128)S(1)}) custom-call(f32[2,16,128,128]{3,2,1,0:T(8,128)} %bitcast.15, f32[128,128]{1,0:T(8,128)} %profile_hbm.1, s32[1024,128]{1,0:T(8,128)} %bitcast.19, f32[1024,128]{1,0:T(8,128)} %bitcast.20, ...), custom_call_target="tpu_custom_call" | custom-call | tf_op jit(solution)/shard_map/project_push/pallas_call | solution.py:347
  8.2 0.0 copy-start.3
  8.2 0.1 collective-permute-start
  8.3 0.0 copy-done.2
  8.3 1.3 %slice.14 = f32[2,12,128,128]{3,2,1,0:T(8,128)} slice(f32[2,16,128,128]{3,2,1,0:T(8,128)S(1)} %bitcast.16), slice={[0:2], [4:16], [0:128], [0:128]} | slice | bytes 3145728 | tf_op jit(solution)/shard_map/slice | solution.py:344
  9.6 7.6 %collective-permute-done.arrived = f32[4,16,128]{2,1,0:T(8,128)S(1)} collective-permute-done((f32[4,16,128]{2,1,0:T(8,128)S(1)}, f32[4,16,128]{2,1,0:T(8,128)S(1)}, u32[]{:S(2)}, u32[]{:S(2)}) %collective-permute-start) | collective-permute-done | bytes 32800 | tf_op jit(solution)/shard_map/ppermute | solution.py:309
  17.2 0.0 collective-permute-done.1.piece_a
  17.2 0.0 collective-permute-start.2
  17.2 6.2 %push_place.1 = (f32[5120,128]{1,0:T(8,128)}, f32[4,16,128]{2,1,0:T(8,128)S(1)}) custom-call(s32[1]{0:T(128)} %bitcast.2.mine, f32[1024,128]{1,0:T(8,128)S(1)} %get-tuple-element.26.phases1, f32[1024,128]{1,0:T(8,128)S(1)} %get-tuple-element.27.energies1, f32[4,16,128]{2,1,0:T(8,128)S(1)} %collective-permute-done.arrived, s32[8,1024]{1,0:T(8,128)S(1)} %get-tuple-element.29.places), custom_call_target="tpu_custom_call" | custom-call | tf_op jit(solution)/shard_map/push_place/pallas_call | solution.py:376
  23.4 6.4 %collective-permute-done.2.piece_b = f32[2,2,128,128]{3,2,1,0:T(8,128)S(1)} collective-permute-done((f32[2,2,128,128]{3,2,1,0:T(8,128)S(1)}, f32[2,2,128,128]{3,2,1,0:T(8,128)S(1)}, u32[]{:S(2)}, u32[]{:S(2)}) %collective-permute-start.2) | collective-permute-done | bytes 262176 | tf_op jit(solution)/shard_map/ppermute | solution.py:309
  29.8 0.0 collective-permute-start.3
  29.8 0.0 collective-permute-start.4
  29.8 0.0 copy-done.3
  29.8 0.7 reduce_max.9
  31.1 73.4 %conditional.1 = (f32[5120,128]{1,0:T(8,128)}) conditional(s32[]{:T(128)} %convert_element_type.3, () %tuple.20, f32[5120,128]{1,0:T(8,128)} %get-tuple-element.37), branch_computations={%region_1.0_spmd, %region_2.0_spmd} | conditional | bytes 5242888 | solution.py:397
  31.1 73.3 %all_to_all.4 = f32[128,40,128]{2,1,0:T(8,128)} all-to-all(f32[128,40,128]{2,1,0:T(8,128)} %bitcast.17), channel_id=1, replica_groups=mesh['cuts'=128] {'cuts'}, dimensions={0} | all-to-all | bytes 5242880 | tf_op jit(solution)/shard_map/cond/branch_1_fun/all_to_all | solution.py:329
  104.5 0.0 copy-start
  104.5 0.0 copy-start.1
  104.5 6.2 %pick.1 = (f32[1024,128]{1,0:T(8,128)}, f32[1024,128]{1,0:T(8,128)}) custom-call(s32[1]{0:T(128)} %bitcast.2.mine, f32[5120,128]{1,0:T(8,128)} %get-tuple-element.45.recv, s32[8,1024]{1,0:T(8,128)S(1)} %get-tuple-element.29.places), custom_call_target="tpu_custom_call" | custom-call | tf_op jit(solution)/shard_map/pick/pallas_call | solution.py:398
  110.7 0.0 collective-permute-done.4.small
  110.7 0.0 collective-permute-done.3.piece_c
  110.7 0.0 copy-done
  110.7 0.0 copy-done.1
  110.7 3.2 %diffract.1 = f32[2,16,128,128]{3,2,1,0:T(8,128)} custom-call(s32[1]{0:T(128)} %bitcast.2.mine, f32[2,2,128,128]{3,2,1,0:T(8,128)S(1)} %collective-permute-done.1.piece_a, f32[2,2,128,128]{3,2,1,0:T(8,128)S(1)} %collective-permute-done.2.piece_b, f32[2,12,128,128]{3,2,1,0:T(8,128)S(1)} %collective-permute-done.3.piece_c, ...), custom_call_target="tpu_custom_call" | custom-call | tf_op jit(solution)/shard_map/diffract/pallas_call | solution.py:411
Async XLA Ops:
  1.7 6.6 %copy-start.2 = (f32[2,16,1,128,128]{4,3,2,1,0:T(8,128)S(1)}, f32[2,16,1,128,128]{4,3,2,1,0:T(8,128)}, u32[]{:S(2)}) copy-start(f32[2,16,1,128,128]{4,3,2,1,0:T(8,128)} %param.12) | copy-start | bytes 6291460
  1.7 15.5 %collective-permute-start.1 = (f32[2,2,128,128]{3,2,1,0:T(8,128)S(1)}, f32[2,2,128,128]{3,2,1,0:T(8,128)S(1)}, u32[]{:S(2)}, u32[]{:S(2)}) collective-permute-start(f32[2,2,128,128]{3,2,1,0:T(8,128)S(1)} %get-tuple-element.44), channel_id=1, source_target_pairs={{0,2},{1,3},{2,4},{3,5},{4,6},{5,7},{6,8},{7,9},{8,10},{9,11},{10,... | collective-permute-start | bytes 786440 | tf_op jit(solution)/shard_map/ppermute | solution.py:309
  8.2 21.6 %copy-start.3 = (s32[16,64,1]{1,2,0:T(1,128)S(1)}, s32[16,64,1]{1,2,0:T(1,128)}, u32[]{:S(2)}) copy-start(s32[16,64,1]{1,2,0:T(1,128)} %param.17) | copy-start | bytes 12292
  8.2 9.0 %collective-permute-start = (f32[4,16,128]{2,1,0:T(8,128)S(1)}, f32[4,16,128]{2,1,0:T(8,128)S(1)}, u32[]{:S(2)}, u32[]{:S(2)}) collective-permute-start(f32[4,16,128]{2,1,0:T(8,128)S(1)} %get-tuple-element.24), channel_id=1, source_target_pairs={{0,1},{1,2},{2,3},{3,4},{4,5},{5,6},{6,7},{7,8},{8,9},{9,10},{10,1... | collective-permute-start | bytes 98312 | tf_op jit(solution)/shard_map/ppermute | solution.py:309
  17.2 12.6 %collective-permute-start.2 = (f32[2,2,128,128]{3,2,1,0:T(8,128)S(1)}, f32[2,2,128,128]{3,2,1,0:T(8,128)S(1)}, u32[]{:S(2)}, u32[]{:S(2)}) collective-permute-start(f32[2,2,128,128]{3,2,1,0:T(8,128)S(1)} %get-tuple-element.31), channel_id=1, source_target_pairs={{0,2},{1,3},{2,4},{3,5},{4,6},{5,7},{6,8},{7,9},{8,10},{9,11},{10,... | collective-permute-start | bytes 786440 | tf_op jit(solution)/shard_map/ppermute | solution.py:309
  29.8 80.9 %collective-permute-start.3 = (f32[2,12,128,128]{3,2,1,0:T(8,128)}, f32[2,12,128,128]{3,2,1,0:T(8,128)S(1)}, u32[]{:S(2)}, u32[]{:S(2)}) collective-permute-start(f32[2,12,128,128]{3,2,1,0:T(8,128)} %slice.14), channel_id=1, source_target_pairs={{0,2},{1,3},{2,4},{3,5},{4,6},{5,7},{6,8},{7,9},{8,10},{9,11},{10,... | collective-permute-start | bytes 4718600 | tf_op jit(solution)/shard_map/ppermute | solution.py:309
  29.8 80.9 %collective-permute-start.4 = (f32[4,16,128]{2,1,0:T(8,128)S(1)}, f32[4,16,128]{2,1,0:T(8,128)S(1)}, u32[]{:S(2)}, u32[]{:S(2)}) collective-permute-start(f32[4,16,128]{2,1,0:T(8,128)S(1)} %get-tuple-element.35), channel_id=1, source_target_pairs={{0,1},{1,2},{2,3},{3,4},{4,5},{5,6},{6,7},{7,8},{8,9},{9,10},{10,1... | collective-permute-start | bytes 98312 | tf_op jit(solution)/shard_map/ppermute | solution.py:309
  104.5 6.3 %copy-start = (bf16[768,256]{1,0:T(8,128)(2,1)S(1)}, bf16[768,256]{1,0:T(8,128)(2,1)}, u32[]{:S(2)}) copy-start(bf16[768,256]{1,0:T(8,128)(2,1)} %constant.21.clone.right) | copy-start | bytes 1179652
  104.5 6.3 %copy-start.1 = (bf16[256,768]{1,0:T(8,128)(2,1)S(1)}, bf16[256,768]{1,0:T(8,128)(2,1)}, u32[]{:S(2)}) copy-start(bf16[256,768]{1,0:T(8,128)(2,1)} %constant.20.clone.left) | copy-start | bytes 1179652
where the time goes:
time: 116 us; the launch traced here: 114 us
  blocking collectives  73.3 us (63%)
  Pallas kernels  20.4 us (18%)
  waiting for transfers between devices  14 us (12%)
  local copies, waits for them, and re-layouts  2.39 us (2%)
  starting transfers between devices  1.73 us (1%)
  between operations  1.38 us (1%)
    all_to_all x1, blocking collectives, exchange(): lax.all_to_all(send.reshape(PEERS, 2 * CAP, BLOCK), 'cuts', split_axis=0,...  73.3 us
    ppermute x5, waiting for transfers between devices, shifted(): return lax.ppermute(value, axis, pairs)  14 us
    pallas_call x1, Pallas kernels, per_device(): pl.pallas_call(pick_kernel, out_shape=(shape(COUNT, BLOCK), shape(COUNT,...  6.23 us
    pallas_call x1, Pallas kernels, per_device(): pl.pallas_call(second_kernel, out_shape=(pltpu.HBM((2 * ROWS, BLOCK), jnp...  6.18 us
    pallas_call x1, Pallas kernels, per_device(): pl.pallas_call(first_kernel, out_shape=(shape(COUNT, BLOCK), shape(COUNT,...  4.81 us
    pallas_call x1, Pallas kernels, per_device(): pl.pallas_call(field_kernel, out_shape=shape(2, GROUPS, GRID, GRID), in_s...  3.16 us
    slice x2, local copies, waits for them, and re-layouts, per_device(): sources = [field[:, low:high] for low, high in PIECES]  2.37 us
  transfers between devices with their start and end apart: 5, of which 2 were waited for; matrix products, arithmetic and copies ran while one was open for 2% of the time, Pallas kernels for 15%

commit v1 on v0

--- a/solution.py
+++ b/solution.py
@@ -22,7 +22,8 @@
 COUNT = GROUPS * NBS
 PEERS = 128
 CAP = 20
-ROWS = PEERS * CAP
+MESSAGE = 2 * CAP + 1
+ROWS = PEERS * MESSAGE
 BATCH = 16
 VMEM_LIMIT = 24 * 1024 * 1024
 HIGHEST = lax.Precision.HIGHEST
@@ -116,9 +117,9 @@
 
 
 def first_kernel(
-    field_hbm, profile_hbm, bins_hbm, jitter_hbm, energy_hbm, delays_hbm, left_hbm, right_hbm,
-    phases, energies, small, beam, places,
-    field, profile, bins, jitter, energy, delays, left, right, acc, sems,
+    mine, field_hbm, profile_hbm, bins_hbm, jitter_hbm, energy_hbm, delays_hbm, left_hbm, right_hbm,
+    send_hbm, phases, energies, beam, places,
+    field, profile, bins, jitter, energy, delays, left, right, acc, send, index_v, index, sems,
 ):
     pairs = [
         (profile_hbm, profile), (left_hbm, left), (right_hbm, right), (delays_hbm, delays),
@@ -127,18 +128,22 @@
     copies = [pltpu.make_async_copy(src, dst, sems.at[n]) for n, (src, dst) in enumerate(pairs)]
     for copy in copies:
         copy.start()
-    for copy in copies[:4]:
+    copies[3].wait()
+    row, slot = slots_of(delays)
+    places[0:1] = row
+    places[1:2] = slot
+    index_v[...] = folded(((mine[0] + row) % PEERS) * MESSAGE + slot)
+    to_scalar = pltpu.make_async_copy(index_v, index, sems.at[3])
+    to_scalar.start()
+    for copy in copies[:3]:
         copy.wait()
     p = profile[...]
     half = jnp.dot(left[...], p, precision=HIGHEST, preferred_element_type=jnp.float32)
     both = jnp.concatenate([half[:GRID], half[GRID:]], axis=1)
     spread = jnp.dot(both, right[...], precision=HIGHEST, preferred_element_type=jnp.float32)
     beam[0] = spread[:, :GRID]
+    beam[1] = spread[:, GRID:]
     beam[2] = p
-    beam[1] = spread[:, GRID:]
-    row, slot = slots_of(delays)
-    places[0:1] = row
-    places[1:2] = slot
     copies[4].wait()
 
     def project(k, carry):
@@ -165,56 +170,11 @@
         phases[rows] = ph
         energies[rows] = en
         c, s = cos_sin(ph)
-        small[2, pl.ds(k, 1)] = jnp.sum(c, axis=0, keepdims=True)
-        small[3, pl.ds(k, 1)] = jnp.sum(s, axis=0, keepdims=True)
+        acc[4, pl.ds(k, 1)] = jnp.sum(c, axis=0, keepdims=True)
+        acc[5, pl.ds(k, 1)] = jnp.sum(s, axis=0, keepdims=True)
         return carry
 
     lax.fori_loop(0, GROUPS, push, 0)
-    bre = lane_total(small[2]) * (1.0 / (NBS * BLOCK))
-    bim = lane_total(small[3]) * (-1.0 / (NBS * BLOCK))
-    small[2] = bre
-    small[3] = bim
-    gain = GAIN / GRID
-    small[0] = acc[2] + gain * (bre * self_re - bim * self_im)
-    small[1] = acc[3] + gain * (bre * self_im + bim * self_re)
-
-
-def pushed(ph, en, amp_re, amp_im):
-    c, s = cos_sin(ph)
-    en = en - KAPPA * (amp_re * c - amp_im * s)
-    return ph + OMEGA * en, en
-
-
-def carried(value, flag):
-    rolled = jnp.concatenate([jnp.zeros_like(value[:1]), value[:-1]], axis=0)
-    return jnp.where(flag, rolled, value)
-
-
-def second_kernel(
-    mine, phases1, energies1, arrived, places, send_hbm, small, acc, phases, energies, send, index_v, index, sems
-):
-    me = mine[0]
-    index_v[...] = folded(((me + places[0:1]) % PEERS) * (2 * CAP) + places[1:2])
-    to_scalar = pltpu.make_async_copy(index_v, index, sems.at[0])
-    to_scalar.start()
-    for n in range(4):
-        acc[n] = carried(arrived[n], me == 0)
-
-    def push(k, carry):
-        rows = rows_of(k)
-        ph, en = pushed(phases1[rows], energies1[rows], acc[0, pl.ds(k, 1)], acc[1, pl.ds(k, 1)])
-        phases[rows] = ph
-        energies[rows] = en
-        c, s = cos_sin(ph)
-        small[0, pl.ds(k, 1)] = jnp.sum(c, axis=0, keepdims=True)
-        small[1, pl.ds(k, 1)] = jnp.sum(s, axis=0, keepdims=True)
-        return carry
-
-    lax.fori_loop(0, GROUPS, push, 0)
-    small[0] = lane_total(small[0]) * (1.0 / (NBS * BLOCK))
-    small[1] = lane_total(small[1]) * (-1.0 / (NBS * BLOCK))
-    small[2] = acc[2]
-    small[3] = acc[3]
     to_scalar.wait()
 
     def put(n, carry):
@@ -228,21 +188,84 @@
         return carry
 
     lax.fori_loop(0, COUNT // BATCH, put, 0)
+    bre = lane_total(acc[4]) * (1.0 / (NBS * BLOCK))
+    bim = lane_total(acc[5]) * (-1.0 / (NBS * BLOCK))
+    gain = GAIN / GRID
+    next_re = acc[2] + gain * (bre * self_re - bim * self_im)
+    next_im = acc[3] + gain * (bre * self_im + bim * self_re)
+    note = one_row([next_re, next_im, bre, bim])
+    for n in range(PEERS):
+        send[n * MESSAGE + 2 * CAP : (n + 1) * MESSAGE] = note
     out = pltpu.make_async_copy(send, send_hbm, sems.at[0])
     out.start()
     out.wait()
 
 
+def pushed(ph, en, amp_re, amp_im):
+    c, s = cos_sin(ph)
+    en = en - KAPPA * (amp_re * c - amp_im * s)
+    return ph + OMEGA * en, en
+
+
+def one_row(parts):
+    rest = 128 // GROUPS - len(parts)
+    stack = jnp.concatenate(parts + [jnp.zeros((rest * GROUPS, 128), jnp.float32)], axis=0)
+    return stack.T[0:1]
+
+
+def parts_of(recv, device):
+    row = recv[pl.ds(device * MESSAGE + 2 * CAP, 1)]
+    return jnp.broadcast_to(row, (128, 128)).T
+
+
+def carried(value, flag):
+    rolled = jnp.concatenate([jnp.zeros_like(value[:1]), value[:-1]], axis=0)
+    return jnp.where(flag, rolled, value)
+
+
+def second_kernel(mine, phases1, energies1, recv, small, earlier, acc):
+    me = mine[0]
+    near = parts_of(recv, (me + PEERS - 1) % PEERS)
+    far = parts_of(recv, (me + PEERS - 2) % PEERS)
+    for n in range(2):
+        acc[n] = carried(near[n * GROUPS : (n + 1) * GROUPS], me == 0)
+        earlier[n] = carried(far[(2 + n) * GROUPS : (3 + n) * GROUPS], me < 2)
+
+    def push(k, carry):
+        rows = rows_of(k)
+        ph, _ = pushed(phases1[rows], energies1[rows], acc[0, pl.ds(k, 1)], acc[1, pl.ds(k, 1)])
+        c, s = cos_sin(ph)
+        acc[2, pl.ds(k, 1)] = jnp.sum(c, axis=0, keepdims=True)
+        acc[3, pl.ds(k, 1)] = jnp.sum(s, axis=0, keepdims=True)
+        return carry
+
+    lax.fori_loop(0, GROUPS, push, 0)
+    small[0] = lane_total(acc[2]) * (1.0 / (NBS * BLOCK))
+    small[1] = lane_total(acc[3]) * (-1.0 / (NBS * BLOCK))
+
+
 def wide_halves(x):
     high = x.astype(jnp.bfloat16)
     return high, (x - high.astype(jnp.float32)).astype(jnp.bfloat16)
 
 
-def pick_kernel(mine, recv, places, phases, energies, index_v, index, sems):
+def pick_kernel(mine, recv, places, phases, energies, index_v, index, amps, sems):
     me = mine[0]
-    index_v[...] = folded(((me - places[0:1] + PEERS) % PEERS) * (2 * CAP) + places[1:2])
+    source = (me - places[0:1] + PEERS) % PEERS
+    index_v[...] = folded(source * MESSAGE + places[1:2])
     to_scalar = pltpu.make_async_copy(index_v, index, sems.at[0])
     to_scalar.start()
+    lane = lax.broadcasted_iota(jnp.int32, (128, 128), 1)
+    sheet = recv[pl.ds(2 * CAP, PEERS, MESSAGE), :]
+    wrapped = jnp.concatenate([sheet[127:128, 127:128], sheet[127:128, :127]], axis=1)
+    wrapped = jnp.where(lane[0:1] % GROUPS == 0, 0.0, wrapped)
+    sheet = jnp.concatenate([wrapped, sheet[:127]], axis=0)
+    for n in range(COUNT // 128):
+        column = jnp.broadcast_to(source[:, n * 128 : (n + 1) * 128], (128, 128)).T
+        onehot = jnp.where(lane == column, 1.0, 0.0)
+        amps[n * 128 : (n + 1) * 128] = jnp.dot(
+            onehot, sheet, precision=HIGHEST, preferred_element_type=jnp.float32
+        )
     to_scalar.wait()
 
     def get(n, carry):
@@ -256,16 +279,21 @@
         return carry
 
     lax.fori_loop(0, COUNT // BATCH, get, 0)
+    for k in range(GROUPS):
+        rows = slice(k * NBS, (k + 1) * NBS)
+        re, im = amps[rows, k : k + 1], amps[rows, GROUPS + k : GROUPS + k + 1]
+        phases[rows], energies[rows] = pushed(phases[rows], energies[rows], re, im)
 
 
 SLAB = 4
-PIECES = ((0, 2), (2, 4), (4, 16))
-
-
-def field_kernel(mine, piece_a, piece_b, piece_c, small, beam, left, right, out_hbm, acc, out, sems):
+PIECES = ((0, 1), (1, 12), (12, 16))
+
+
+def field_kernel(mine, piece_a, piece_b, piece_c, small, earlier, beam, left, right, out_hbm, acc, out, sems):
     me = mine[0]
-    for n in range(4):
+    for n in range(2):
         acc[n] = GAIN * carried(small[n], me == 0)
+        acc[2 + n] = GAIN * earlier[n]
 
     def plane(c, k):
         for piece, (low, high) in zip((piece_a, piece_b, piece_c), PIECES):
@@ -325,10 +353,6 @@
     return pltpu.with_memory_space_constraint(value, pltpu.HBM)
 
 
-def exchange(send):
-    return lax.all_to_all(send.reshape(PEERS, 2 * CAP, BLOCK), "cuts", split_axis=0, concat_axis=0, tiled=True)
-
-
 def per_device(field, phase_bins, phase_jitter, energy, profile, delays):
     params = pltpu.CompilerParams(vmem_limit_bytes=VMEM_LIMIT)
     scalar = pl.BlockSpec(memory_space=pltpu.SMEM)
@@ -344,17 +368,17 @@
     sources = [field[:, low:high] for low, high in PIECES]
     field_a = shifted(sources[0], "cuts", 2)
     operands = [field, profile, bins, jitter, energies, delays.reshape(GROUPS, 1, NBS), left_one, right_one]
-    phases1, energies1, small1, beam, places = pl.pallas_call(
+    send, phases1, energies1, beam, places = pl.pallas_call(
         first_kernel,
         out_shape=(
+            pltpu.HBM((ROWS, BLOCK), jnp.float32),
             shape(COUNT, BLOCK),
             shape(COUNT, BLOCK),
-            shape(4, GROUPS, 128),
             shape(3, GRID, GRID),
             shape(8, COUNT, dtype=jnp.int32),
         ),
-        in_specs=[remain] * 8,
-        out_specs=(whole(),) * 5,
+        in_specs=[scalar] + [remain] * 8,
+        out_specs=(remain,) + (whole(),) * 4,
         scratch_shapes=[
             vmem(2, GROUPS, GRID, GRID),
             vmem(GRID, GRID),
@@ -364,37 +388,30 @@
             vmem(GROUPS, 1, NBS, dtype=jnp.int32),
             vmem(2 * GRID, GRID),
             vmem(2 * GRID, 2 * GRID),
-            vmem(4, GROUPS, 128),
+            vmem(6, GROUPS, 128),
+            vmem(ROWS, BLOCK),
+            vmem(8, 128, dtype=jnp.int32),
+            pltpu.SMEM((8, 128), jnp.int32),
             pltpu.SemaphoreType.DMA((8,)),
         ],
         compiler_params=params,
-        name="project_push",
-    )(*[in_hbm(value) for value in operands])
-    arrived1 = shifted(small1, "cuts", 1)
-    arrived1, field_a, source_b, source_c = lax.optimization_barrier((arrived1, field_a, sources[1], sources[2]))
-    field_b = shifted(source_b, "cuts", 2)
-    send, small2 = pl.pallas_call(
+        name="push_place",
+    )(mine, *[in_hbm(value) for value in operands])
+    send, field_a = lax.optimization_barrier((send, field_a))
+    field_b = shifted(sources[1], "cuts", 2)
+    field_c = shifted(sources[2], "cuts", 2)
+    recv = lax.all_to_all(send.reshape(ROWS, 1, BLOCK), "cuts", split_axis=0, concat_axis=0, tiled=True)
+    recv = recv.reshape(ROWS, BLOCK)
+    small, earlier = pl.pallas_call(
         second_kernel,
-        out_shape=(pltpu.HBM((2 * ROWS, BLOCK), jnp.float32), shape(4, GROUPS, 128)),
-        in_specs=[scalar] + [whole()] * 4,
-        out_specs=(remain, whole()),
-        scratch_shapes=[
-            vmem(4, GROUPS, 128),
-            vmem(COUNT, BLOCK),
-            vmem(COUNT, BLOCK),
-            vmem(2 * ROWS, BLOCK),
-            vmem(8, 128, dtype=jnp.int32),
-            pltpu.SMEM((8, 128), jnp.int32),
-            pltpu.SemaphoreType.DMA((1,)),
-        ],
+        out_shape=(shape(2, GROUPS, 128), shape(2, GROUPS, 128)),
+        in_specs=[scalar] + [whole()] * 3,
+        out_specs=(whole(),) * 2,
+        scratch_shapes=[vmem(4, GROUPS, 128)],
         compiler_params=params,
-        name="push_place",
-    )(mine, phases1, energies1, arrived1, places)
-    arrived2 = shifted(small2, "cuts", 1)
-    send, field_b, source_c = lax.optimization_barrier((send, field_b, source_c))
-    field_c = shifted(source_c, "cuts", 2)
-    fits = jnp.max(delays) < PEERS
-    recv = lax.cond(fits, exchange, lambda rows: jnp.zeros((PEERS, 2 * CAP, BLOCK), jnp.float32), send)
+        name="second_push",
+    )(mine, phases1, energies1, recv)
+    arrived = shifted(small, "cuts", 1)
     phase_out, energy_out = pl.pallas_call(
         pick_kernel,
         out_shape=(shape(COUNT, BLOCK), shape(COUNT, BLOCK)),
@@ -403,15 +420,16 @@
         scratch_shapes=[
             vmem(8, 128, dtype=jnp.int32),
             pltpu.SMEM((8, 128), jnp.int32),
+            vmem(COUNT, 128),
             pltpu.SemaphoreType.DMA((1,)),
         ],
         compiler_params=params,
         name="pick",
-    )(mine, recv.reshape(2 * ROWS, BLOCK), places)
+    )(mine, recv, places)
     out = pl.pallas_call(
         field_kernel,
         out_shape=shape(2, GROUPS, GRID, GRID),
-        in_specs=[scalar] + [whole()] * 7,
+        in_specs=[scalar] + [whole()] * 8,
         out_specs=remain,
         scratch_shapes=[
             vmem(4, GROUPS, 128),
@@ -420,7 +438,7 @@
         ],
         compiler_params=params,
         name="diffract",
-    )(mine, field_a, field_b, field_c, arrived2, beam, deep_left(left_form(*two)), deep_right(right_form(*two)))
+    )(mine, field_a, field_b, field_c, arrived, earlier, beam, deep_left(left_form(*two)), deep_right(right_form(*two)))
     return (
         out.reshape(2, GROUPS, 1, GRID, GRID),
         phase_out.reshape(GROUPS, 1, NBS * BLOCK),

time: 116 us -> 109 us (0.940); the launches traced: 114 us -> 108 us
  blocking collectives: 73.3 us -> 0 us
  waiting for transfers between devices: 14 us -> 63.4 us
  starting transfers between devices: 1.73 us -> 14.9 us
  local copies, waits for them, and re-layouts: 2.39 us -> 7.87 us
  Pallas kernels: 20.4 us -> 21.6 us
    all_to_all x1 -> x0, blocking collectives: 73.3 us -> none  [exchange(): lax.all_to_all(send.reshape(PEERS, 2 * CAP, BLOCK), 'cuts', split_axis=0,...]
    all_to_all x0 -> x1, waiting for transfers between devices: none -> 30.4 us  [per_device(): lax.all_to_all(send.reshape(ROWS, 1, BLOCK), 'cuts', split_axis=0, concat...]
    ppermute x5 -> x4, waiting for transfers between devices: 14 us -> 33 us  [shifted(): return lax.ppermute(value, axis, pairs)]
    all_to_all x0 -> x1, starting transfers between devices: none -> 10.8 us  [per_device(): lax.all_to_all(send.reshape(ROWS, 1, BLOCK), 'cuts', split_axis=0, concat...]
    slice x2 -> x3, local copies, waits for them, and re-layouts: 2.37 us -> 5.41 us  [per_device(): sources = [field[:, low:high] for low, high in PIECES]]
    unnamed x8 -> x12, local copies, waits for them, and re-layouts: 0.02 us -> 2.45 us
    ppermute x5 -> x4, starting transfers between devices: 1.73 us -> 4.09 us  [shifted(): return lax.ppermute(value, axis, pairs)]
    pallas_call x1, Pallas kernels: 3.16 us -> 4.63 us  [per_device(): pl.pallas_call(field_kernel, out_shape=shape(2, GROUPS, GRID, GRID), in_s...]
  transfers between devices with their start and end apart: 5 -> 5, of which waited for: 2 -> 2; matrix products, arithmetic and copies ran while one was open for 2% -> 4% of each run, Pallas kernels for 15% -> 16%
where the time goes in v1:
time: 109 us; the launch traced here: 108 us
  waiting for transfers between devices  63.4 us (58%)
  Pallas kernels  21.6 us (20%)
  starting transfers between devices  14.9 us (14%)
  local copies, waits for them, and re-layouts  7.87 us (7%)
    ppermute x4, waiting for transfers between devices, shifted(): return lax.ppermute(value, axis, pairs)  33 us
    all_to_all x1, waiting for transfers between devices, per_device(): lax.all_to_all(send.reshape(ROWS, 1, BLOCK), 'cuts', split_axis=0, concat...  30.4 us
    all_to_all x1, starting transfers between devices, per_device(): lax.all_to_all(send.reshape(ROWS, 1, BLOCK), 'cuts', split_axis=0, concat...  10.8 us
    pallas_call x1, Pallas kernels, per_device(): pl.pallas_call(first_kernel, out_shape=(pltpu.HBM((ROWS, BLOCK), jnp.floa...  9.36 us
    pallas_call x1, Pallas kernels, per_device(): pl.pallas_call(pick_kernel, out_shape=(shape(COUNT, BLOCK), shape(COUNT,...  5.74 us
    slice x3, local copies, waits for them, and re-layouts, per_device(): sources = [field[:, low:high] for low, high in PIECES]  5.41 us
    pallas_call x1, Pallas kernels, per_device(): pl.pallas_call(field_kernel, out_shape=shape(2, GROUPS, GRID, GRID), in_s...  4.63 us
    ppermute x4, starting transfers between devices, shifted(): return lax.ppermute(value, axis, pairs)  4.09 us
  transfers between devices with their start and end apart: 5, of which 2 were waited for; matrix products, arithmetic and copies ran while one was open for 4% of the time, Pallas kernels for 16%

profile of v1, /device:TPU:0, one launch (start us, length us, event | category | flops | bytes accessed | tf_op | source)
XLA Modules:
  0.0 108.4 jit_solution(14111120436274216878)
XLA Ops:
  0.6 0.9 slice.12
  1.6 1.6 %collective-permute-start = (f32[2,1,128,128]{3,2,1,0:T(8,128)S(1)}, f32[2,1,128,128]{3,2,1,0:T(8,128)S(1)}, u32[]{:S(2)}, u32[]{:S(2)}) collective-permute-start(f32[2,1,128,128]{3,2,1,0:T(8,128)S(1)} %slice.12), channel_id=1, source_target_pairs={{0,2},{1,3},{2,4},{3,5},{4,6},{5,7},{6,8},{7,9},{8,10},{9,11},{10,... | collective-permute-start | bytes 393224 | tf_op jit(solution)/shard_map/ppermute | solution.py:337
  3.2 9.4 %push_place.1 = (f32[5248,128]{1,0:T(8,128)}, f32[1024,128]{1,0:T(8,128)S(1)}, f32[1024,128]{1,0:T(8,128)S(1)}, f32[3,128,128]{2,1,0:T(8,128)S(1)}, s32[8,1024]{1,0:T(8,128)S(1)}) custom-call(s32[1]{0:T(128)} %bitcast.mine, f32[2,16,128,128]{3,2,1,0:T(8,128)} %bitcast.18, f32[128,128]{1,0:T(8,128)} %profile_hbm.1, s32[1024,128]{1,0:T(8,128)} %bitcast.23, ...), custom_call_target="tpu_custom_call" | custom-call | tf_op jit(solution)/shard_map/push_place/pallas_call | solution.py:371
  12.6 0.0 copy-start
  12.6 0.8 copy-done
  13.4 0.0 copy-start.4
  13.4 0.6 copy-done.4
  14.0 0.0 collective-permute-done.piece_a
  14.0 10.8 %all-to-all-start = ((f32[5248,1,128]{2,1,0:T(1,128)}), f32[5248,1,128]{2,1,0:T(1,128)S(1)}, u32[]{:S(2)}, u32[]{:S(2)}) async-start(f32[5248,1,128]{2,1,0:T(1,128)} %bitcast.21), calls=%async_computation | async-start | bytes 5373952 | tf_op jit(solution)/shard_map/all_to_all | solution.py:403
  24.8 2.6 %slice.13 = f32[2,11,128,128]{3,2,1,0:T(8,128)} slice(f32[2,16,128,128]{3,2,1,0:T(8,128)} %bitcast.19), slice={[0:2], [1:12], [0:128], [0:128]} | slice | bytes 2883584 | tf_op jit(solution)/shard_map/slice | solution.py:368
  27.4 1.0 collective-permute-start.1
  28.3 1.9 %slice.14 = f32[2,4,128,128]{3,2,1,0:T(8,128)} slice(f32[2,16,128,128]{3,2,1,0:T(8,128)} %bitcast.20), slice={[0:2], [12:16], [0:128], [0:128]} | slice | bytes 1048576 | tf_op jit(solution)/shard_map/slice | solution.py:368
  30.2 1.5 %collective-permute-start.2 = (f32[2,4,128,128]{3,2,1,0:T(8,128)}, f32[2,4,128,128]{3,2,1,0:T(8,128)}, u32[]{:S(2)}, u32[]{:S(2)}) collective-permute-start(f32[2,4,128,128]{3,2,1,0:T(8,128)} %slice.14), channel_id=1, source_target_pairs={{0,2},{1,3},{2,4},{3,5},{4,6},{5,7},{6,8},{7,9},{8,10},{9,11},{10,... | collective-permute-start | bytes 1572872 | tf_op jit(solution)/shard_map/ppermute | solution.py:337
  31.7 30.4 %all-to-all-done = f32[5248,1,128]{2,1,0:T(1,128)S(1)} async-done(((f32[5248,1,128]{2,1,0:T(1,128)}), f32[5248,1,128]{2,1,0:T(1,128)S(1)}, u32[]{:S(2)}, u32[]{:S(2)}) %all-to-all-start) | async-done | bytes 2687008 | tf_op jit(solution)/shard_map/all_to_all | solution.py:403
  62.1 0.0 copy-start.1
  62.1 1.0 copy-done.1
  63.1 0.0 copy-start.5
  63.1 1.9 %second_push.1 = (f32[2,16,128]{2,1,0:T(8,128)S(1)}, f32[2,16,128]{2,1,0:T(8,128)S(1)}) custom-call(s32[1]{0:T(128)} %bitcast.mine, f32[1024,128]{1,0:T(8,128)S(1)} %get-tuple-element.16.phases1, f32[1024,128]{1,0:T(8,128)S(1)} %copy-done.1, f32[5248,128]{1,0:T(8,128)S(1)} %bitcast.15), custom_call_target="tpu_custom_call" | custom-call | tf_op jit(solution)/shard_map/second_push/pallas_call | solution.py:405
  65.0 0.0 copy-start.2
  65.0 0.0 copy-start.3
  65.0 0.0 collective-permute-start.3
  65.0 0.0 copy-done.5
  65.0 5.7 %pick.1 = (f32[1024,128]{1,0:T(8,128)}, f32[1024,128]{1,0:T(8,128)}) custom-call(s32[1]{0:T(128)} %bitcast.mine, f32[5248,128]{1,0:T(8,128)S(1)} %bitcast.16, s32[8,1024]{1,0:T(8,128)S(1)} %copy-done.5), custom_call_target="tpu_custom_call" | custom-call | tf_op jit(solution)/shard_map/pick/pallas_call | solution.py:415
  70.8 33.0 %collective-permute-done.2.piece_c = f32[2,4,128,128]{3,2,1,0:T(8,128)} collective-permute-done((f32[2,4,128,128]{3,2,1,0:T(8,128)}, f32[2,4,128,128]{3,2,1,0:T(8,128)}, u32[]{:S(2)}, u32[]{:S(2)}) %collective-permute-start.2) | collective-permute-done | bytes 524320 | tf_op jit(solution)/shard_map/ppermute | solution.py:337
  103.7 0.0 collective-permute-done.1.piece_b
  103.7 0.0 collective-permute-done.3.small
  103.7 0.0 copy-done.2
  103.7 0.0 copy-done.3
  103.7 4.6 %diffract.1 = f32[2,16,128,128]{3,2,1,0:T(8,128)} custom-call(s32[1]{0:T(128)} %bitcast.mine, f32[2,1,128,128]{3,2,1,0:T(8,128)S(1)} %collective-permute-done.piece_a, f32[2,11,128,128]{3,2,1,0:T(8,128)} %collective-permute-done.1.piece_b, f32[2,4,128,128]{3,2,1,0:T(8,128)} %collective-permute-done.2.piece_c, ...), custom_call_target="tpu_custom_call" | custom-call | tf_op jit(solution)/shard_map/diffract/pallas_call | solution.py:429
Async XLA Ops:
  1.6 12.4 %collective-permute-start = (f32[2,1,128,128]{3,2,1,0:T(8,128)S(1)}, f32[2,1,128,128]{3,2,1,0:T(8,128)S(1)}, u32[]{:S(2)}, u32[]{:S(2)}) collective-permute-start(f32[2,1,128,128]{3,2,1,0:T(8,128)S(1)} %slice.12), channel_id=1, source_target_pairs={{0,2},{1,3},{2,4},{3,5},{4,6},{5,7},{6,8},{7,9},{8,10},{9,11},{10,... | collective-permute-start | bytes 393224 | tf_op jit(solution)/shard_map/ppermute | solution.py:337
  12.6 0.8 copy-start
  13.4 0.6 copy-start.4
  14.0 48.1 %all-to-all-start = ((f32[5248,1,128]{2,1,0:T(1,128)}), f32[5248,1,128]{2,1,0:T(1,128)S(1)}, u32[]{:S(2)}, u32[]{:S(2)}) async-start(f32[5248,1,128]{2,1,0:T(1,128)} %bitcast.21), calls=%async_computation | async-start | bytes 5373952 | tf_op jit(solution)/shard_map/all_to_all | solution.py:403
  27.4 76.4 %collective-permute-start.1 = (f32[2,11,128,128]{3,2,1,0:T(8,128)}, f32[2,11,128,128]{3,2,1,0:T(8,128)}, u32[]{:S(2)}, u32[]{:S(2)}) collective-permute-start(f32[2,11,128,128]{3,2,1,0:T(8,128)} %slice.13), channel_id=1, source_target_pairs={{0,2},{1,3},{2,4},{3,5},{4,6},{5,7},{6,8},{7,9},{8,10},{9,11},{10,... | collective-permute-start | bytes 4325384 | tf_op jit(solution)/shard_map/ppermute | solution.py:337
  30.2 73.5 %collective-permute-start.2 = (f32[2,4,128,128]{3,2,1,0:T(8,128)}, f32[2,4,128,128]{3,2,1,0:T(8,128)}, u32[]{:S(2)}, u32[]{:S(2)}) collective-permute-start(f32[2,4,128,128]{3,2,1,0:T(8,128)} %slice.14), channel_id=1, source_target_pairs={{0,2},{1,3},{2,4},{3,5},{4,6},{5,7},{6,8},{7,9},{8,10},{9,11},{10,... | collective-permute-start | bytes 1572872 | tf_op jit(solution)/shard_map/ppermute | solution.py:337
  62.1 1.0 copy-start.1
  63.1 1.9 %copy-start.5 = (s32[8,1024]{1,0:T(8,128)S(1)}, s32[8,1024]{1,0:T(8,128)}, u32[]{:S(2)}) copy-start(s32[8,1024]{1,0:T(8,128)} %copy-done.4) | copy-start | bytes 98308
  65.0 38.8 %copy-start.2 = (bf16[256,768]{1,0:T(8,128)(2,1)S(1)}, bf16[256,768]{1,0:T(8,128)(2,1)}, u32[]{:S(2)}) copy-start(bf16[256,768]{1,0:T(8,128)(2,1)} %constant.14.clone.left) | copy-start | bytes 1179652
  65.0 38.8 %copy-start.3 = (bf16[768,256]{1,0:T(8,128)(2,1)S(1)}, bf16[768,256]{1,0:T(8,128)(2,1)}, u32[]{:S(2)}) copy-start(bf16[768,256]{1,0:T(8,128)(2,1)} %constant.15.clone.right) | copy-start | bytes 1179652
  65.0 38.8 %collective-permute-start.3 = (f32[2,16,128]{2,1,0:T(8,128)S(1)}, f32[2,16,128]{2,1,0:T(8,128)S(1)}, u32[]{:S(2)}, u32[]{:S(2)}) collective-permute-start(f32[2,16,128]{2,1,0:T(8,128)S(1)} %get-tuple-element.19), channel_id=1, source_target_pairs={{0,1},{1,2},{2,3},{3,4},{4,5},{5,6},{6,7},{7,8},{8,9},{9,10},{10,1... | collective-permute-start | bytes 49160 | tf_op jit(solution)/shard_map/ppermute | solution.py:337

commit v2 on v1

--- a/solution.py
+++ b/solution.py
@@ -118,8 +118,8 @@
 
 def first_kernel(
     mine, field_hbm, profile_hbm, bins_hbm, jitter_hbm, energy_hbm, delays_hbm, left_hbm, right_hbm,
-    send_hbm, phases, energies, beam, places,
-    field, profile, bins, jitter, energy, delays, left, right, acc, send, index_v, index, sems,
+    send_hbm, phases_hbm, energies_hbm, places_hbm, beam,
+    field, profile, bins, jitter, energy, delays, left, right, acc, send, phases, energies, places, index_v, index, sems,
 ):
     pairs = [
         (profile_hbm, profile), (left_hbm, left), (right_hbm, right), (delays_hbm, delays),
@@ -145,6 +145,8 @@
     beam[1] = spread[:, GRID:]
     beam[2] = p
     copies[4].wait()
+    kept = [pltpu.make_async_copy(places, places_hbm, sems.at[8])]
+    kept[0].start()
 
     def project(k, carry):
         re, im = field[0, k], field[1, k]
@@ -175,6 +177,10 @@
         return carry
 
     lax.fori_loop(0, GROUPS, push, 0)
+    kept.append(pltpu.make_async_copy(phases, phases_hbm, sems.at[9]))
+    kept.append(pltpu.make_async_copy(energies, energies_hbm, sems.at[10]))
+    for copy in kept[1:]:
+        copy.start()
     to_scalar.wait()
 
     def put(n, carry):
@@ -198,6 +204,8 @@
         send[n * MESSAGE + 2 * CAP : (n + 1) * MESSAGE] = note
     out = pltpu.make_async_copy(send, send_hbm, sems.at[0])
     out.start()
+    for copy in kept:
+        copy.wait()
     out.wait()
 
 
@@ -286,21 +294,21 @@
 
 
 SLAB = 4
-PIECES = ((0, 1), (1, 12), (12, 16))
-
-
-def field_kernel(mine, piece_a, piece_b, piece_c, small, earlier, beam, left, right, out_hbm, acc, out, sems):
+PIECES = ((0, 8), (8, 16))
+
+
+def field_kernel(mine, piece_a, piece_b, small, earlier, beam, left, right, out_hbm, acc, out, out_sems):
     me = mine[0]
+
+    def plane(c, k):
+        for piece, (low, high) in zip((piece_a, piece_b), PIECES):
+            if low <= k < high:
+                return piece[c, k - low]
+        return jnp.zeros((GRID, GRID), jnp.float32)
+
     for n in range(2):
         acc[n] = GAIN * carried(small[n], me == 0)
         acc[2 + n] = GAIN * earlier[n]
-
-    def plane(c, k):
-        for piece, (low, high) in zip((piece_a, piece_b, piece_c), PIECES):
-            if low <= k < high:
-                return piece[c, k - low]
-        return jnp.zeros((GRID, GRID), jnp.float32)
-
     late = me < 2
     p = beam[2]
     dr, di = beam[0], beam[1]
@@ -325,7 +333,7 @@
             out[1, k] = full[GRID:, m * GRID : (m + 1) * GRID] + (cr * di + ci * dr)
         for c in range(2):
             span = pl.ds(slab * SLAB, SLAB)
-            copies.append(pltpu.make_async_copy(out.at[c, span], out_hbm.at[c, span], sems.at[2 * slab + c]))
+            copies.append(pltpu.make_async_copy(out.at[c, span], out_hbm.at[c, span], out_sems.at[2 * slab + c]))
             copies[-1].start()
     for copy in copies:
         copy.wait()
@@ -365,20 +373,20 @@
     one, two = line_operator(1), line_operator(2)
     left_one = jnp.asarray(np.concatenate(one, axis=0), jnp.float32)
     right_one = jnp.asarray(right_form(*one), jnp.float32)
-    sources = [field[:, low:high] for low, high in PIECES]
-    field_a = shifted(sources[0], "cuts", 2)
+    field_a = shifted(field[:, : PIECES[0][1]], "cuts", 2)
     operands = [field, profile, bins, jitter, energies, delays.reshape(GROUPS, 1, NBS), left_one, right_one]
-    send, phases1, energies1, beam, places = pl.pallas_call(
+    low, high = PIECES[1]
+    send, phases1, energies1, places, beam = pl.pallas_call(
         first_kernel,
         out_shape=(
             pltpu.HBM((ROWS, BLOCK), jnp.float32),
-            shape(COUNT, BLOCK),
-            shape(COUNT, BLOCK),
+            pltpu.HBM((COUNT, BLOCK), jnp.float32),
+            pltpu.HBM((COUNT, BLOCK), jnp.float32),
+            pltpu.HBM((8, COUNT), jnp.int32),
             shape(3, GRID, GRID),
-            shape(8, COUNT, dtype=jnp.int32),
         ),
         in_specs=[scalar] + [remain] * 8,
-        out_specs=(remain,) + (whole(),) * 4,
+        out_specs=(remain,) * 4 + (whole(),),
         scratch_shapes=[
             vmem(2, GROUPS, GRID, GRID),
             vmem(GRID, GRID),
@@ -390,46 +398,58 @@
             vmem(2 * GRID, 2 * GRID),
             vmem(6, GROUPS, 128),
             vmem(ROWS, BLOCK),
+            vmem(COUNT, BLOCK),
+            vmem(COUNT, BLOCK),
+            vmem(8, COUNT, dtype=jnp.int32),
             vmem(8, 128, dtype=jnp.int32),
             pltpu.SMEM((8, 128), jnp.int32),
-            pltpu.SemaphoreType.DMA((8,)),
+            pltpu.SemaphoreType.DMA((11,)),
         ],
         compiler_params=params,
         name="push_place",
     )(mine, *[in_hbm(value) for value in operands])
-    send, field_a = lax.optimization_barrier((send, field_a))
-    field_b = shifted(sources[1], "cuts", 2)
-    field_c = shifted(sources[2], "cuts", 2)
-    recv = lax.all_to_all(send.reshape(ROWS, 1, BLOCK), "cuts", split_axis=0, concat_axis=0, tiled=True)
-    recv = recv.reshape(ROWS, BLOCK)
-    small, earlier = pl.pallas_call(
-        second_kernel,
-        out_shape=(shape(2, GROUPS, 128), shape(2, GROUPS, 128)),
-        in_specs=[scalar] + [whole()] * 3,
-        out_specs=(whole(),) * 2,
-        scratch_shapes=[vmem(4, GROUPS, 128)],
-        compiler_params=params,
-        name="second_push",
-    )(mine, phases1, energies1, recv)
-    arrived = shifted(small, "cuts", 1)
-    phase_out, energy_out = pl.pallas_call(
-        pick_kernel,
-        out_shape=(shape(COUNT, BLOCK), shape(COUNT, BLOCK)),
-        in_specs=[scalar] + [whole()] * 2,
-        out_specs=(whole(),) * 2,
-        scratch_shapes=[
-            vmem(8, 128, dtype=jnp.int32),
-            pltpu.SMEM((8, 128), jnp.int32),
-            vmem(COUNT, 128),
-            pltpu.SemaphoreType.DMA((1,)),
-        ],
-        compiler_params=params,
-        name="pick",
-    )(mine, recv, places)
+
+    def exchange(send, phases1, energies1, places, field):
+        field_b = shifted(field[:, low:high], "cuts", 2)
+        recv = lax.all_to_all(send.reshape(ROWS, 1, BLOCK), "cuts", split_axis=0, concat_axis=0, tiled=True)
+        recv = recv.reshape(ROWS, BLOCK)
+        small, earlier = pl.pallas_call(
+            second_kernel,
+            out_shape=(shape(2, GROUPS, 128), shape(2, GROUPS, 128)),
+            in_specs=[scalar] + [whole()] * 3,
+            out_specs=(whole(),) * 2,
+            scratch_shapes=[vmem(4, GROUPS, 128)],
+            compiler_params=params,
+            name="second_push",
+        )(mine, phases1, energies1, recv)
+        arrived = shifted(small, "cuts", 1)
+        phase_out, energy_out = pl.pallas_call(
+            pick_kernel,
+            out_shape=(shape(COUNT, BLOCK), shape(COUNT, BLOCK)),
+            in_specs=[scalar] + [whole()] * 2,
+            out_specs=(whole(),) * 2,
+            scratch_shapes=[
+                vmem(8, 128, dtype=jnp.int32),
+                pltpu.SMEM((8, 128), jnp.int32),
+                vmem(COUNT, 128),
+                pltpu.SemaphoreType.DMA((1,)),
+            ],
+            compiler_params=params,
+            name="pick",
+        )(mine, recv, places)
+        return phase_out, energy_out, field_b, arrived, earlier
+
+    def refuse(*operands):
+        sizes = [(COUNT, BLOCK)] * 2 + [(2, high - low, GRID, GRID)] + [(2, GROUPS, 128)] * 2
+        return tuple(jnp.zeros(size, jnp.float32) for size in sizes)
+
+    phase_out, energy_out, field_b, arrived, earlier = lax.cond(
+        delays[0, 0, 0] < PEERS, exchange, refuse, send, phases1, energies1, places, field
+    )
     out = pl.pallas_call(
         field_kernel,
         out_shape=shape(2, GROUPS, GRID, GRID),
-        in_specs=[scalar] + [whole()] * 8,
+        in_specs=[scalar] + [whole()] * 7,
         out_specs=remain,
         scratch_shapes=[
             vmem(4, GROUPS, 128),
@@ -438,7 +458,7 @@
         ],
         compiler_params=params,
         name="diffract",
-    )(mine, field_a, field_b, field_c, arrived, earlier, beam, deep_left(left_form(*two)), deep_right(right_form(*two)))
+    )(mine, field_a, field_b, arrived, earlier, beam, deep_left(left_form(*two)), deep_right(right_form(*two)))
     return (
         out.reshape(2, GROUPS, 1, GRID, GRID),
         phase_out.reshape(GROUPS, 1, NBS * BLOCK),

time: 109 us -> 104 us (0.954)
  waiting for transfers between devices: 63.4 us -> 57.1 us
  Pallas kernels: 21.6 us -> 22.9 us
    ppermute x4 -> x3, waiting for transfers between devices: 33 us -> 1.45 us  [shifted(): return lax.ppermute(value, axis, pairs)]
    all_to_all x1, waiting for transfers between devices: 30.4 us -> 55.6 us  [exchange(): lax.all_to_all(send.reshape(ROWS, 1, BLOCK), 'cuts', split_axis=0, concat...]
    pallas_call x2, Pallas kernels: 7.6 us -> 8.8 us  [the longest x1 5.73 us: exchange(): pl.pallas_call(pick_kernel, out_shape=(shape(COUNT, BLOCK), shape(COUNT,...]
    unnamed x12 -> x8, local copies, waits for them, and re-layouts: 2.45 us -> 1.62 us
    ppermute x4 -> x3, starting transfers between devices: 4.09 us -> 4.04 us  [shifted(): return lax.ppermute(value, axis, pairs)]
  transfers between devices with their start and end apart: 5 -> 4, of which waited for: 2 -> 2; matrix products, arithmetic and copies ran while one was open for 4% -> 3% of each run, Pallas kernels for 16% -> 18%
where the time goes in v2:
time: 104 us
  waiting for transfers between devices  57.1 us (55%)
  Pallas kernels  22.9 us (22%)
  starting transfers between devices  14.8 us (14%)
  local copies, waits for them, and re-layouts  7.4 us (7%)
  between operations  1.32 us (1%)
    all_to_all x1, waiting for transfers between devices, exchange(): lax.all_to_all(send.reshape(ROWS, 1, BLOCK), 'cuts', split_axis=0, concat...  55.6 us
    all_to_all x1, starting transfers between devices, exchange(): lax.all_to_all(send.reshape(ROWS, 1, BLOCK), 'cuts', split_axis=0, concat...  10.8 us
    pallas_call x1, Pallas kernels, per_device(): pl.pallas_call(first_kernel, out_shape=(pltpu.HBM((ROWS, BLOCK), jnp.floa...  9.38 us
    pallas_call x1, Pallas kernels, exchange(): pl.pallas_call(pick_kernel, out_shape=(shape(COUNT, BLOCK), shape(COUNT,...  5.73 us
    pallas_call x1, Pallas kernels, per_device(): pl.pallas_call(field_kernel, out_shape=shape(2, GROUPS, GRID, GRID), in_s...  4.7 us
    ppermute x3, starting transfers between devices, shifted(): return lax.ppermute(value, axis, pairs)  4.04 us
    pallas_call x1, Pallas kernels, exchange(): pl.pallas_call(second_kernel, out_shape=(shape(2, GROUPS, 128), shape(2,...  3.06 us
    slice x1, local copies, waits for them, and re-layouts, exchange(): field_b = shifted(field[:, low:high], 'cuts', 2)  2.31 us
  transfers between devices with their start and end apart: 4, of which 2 were waited for; matrix products, arithmetic and copies ran while one was open for 3% of the time, Pallas kernels for 18%

profile of v2, /device:TPU:0, one launch (start us, length us, event | category | flops | bytes accessed | tf_op | source)
XLA Modules:
  0.0 103.5 jit_solution(15126462390765955379)
XLA Ops:
  0.6 2.3 %slice.11 = f32[2,8,128,128]{3,2,1,0:T(8,128)} slice(f32[2,16,128,128]{3,2,1,0:T(8,128)} %bitcast.16), slice={[0:2], [0:8], [0:128], [0:128]} | slice | bytes 2097152 | tf_op jit(solution)/shard_map/slice | solution.py:376
  2.9 1.6 %collective-permute-start.2 = (f32[2,8,128,128]{3,2,1,0:T(8,128)}, f32[2,8,128,128]{3,2,1,0:T(8,128)}, u32[]{:S(2)}, u32[]{:S(2)}) collective-permute-start(f32[2,8,128,128]{3,2,1,0:T(8,128)} %slice.11), channel_id=1, source_target_pairs={{0,2},{1,3},{2,4},{3,5},{4,6},{5,7},{6,8},{7,9},{8,10},{9,11},{10,... | collective-permute-start | bytes 3145736 | tf_op jit(solution)/shard_map/ppermute | solution.py:345
  4.5 1.2 %slice.10 = s32[1,1,1]{1,2,0:T(1,128)} slice(s32[16,64,1]{1,2,0:T(1,128)} %param.17), slice={[0:1], [0:1], [0:1]} | slice | bytes 8 | tf_op jit(solution)/shard_map/slice | solution.py:447
  6.3 9.4 %push_place.1 = (f32[5248,128]{1,0:T(8,128)}, f32[1024,128]{1,0:T(8,128)}, f32[1024,128]{1,0:T(8,128)}, s32[8,1024]{1,0:T(8,128)}, f32[3,128,128]{2,1,0:T(8,128)S(1)}) custom-call(s32[1]{0:T(128)} %bitcast.4.mine, f32[2,16,128,128]{3,2,1,0:T(8,128)} %bitcast.17, f32[128,128]{1,0:T(8,128)} %profile_hbm.1, s32[1024,128]{1,0:T(8,128)} %bitcast.21, ...), custom_call_target="tpu_custom_call" | custom-call | tf_op jit(solution)/shard_map/push_place/pallas_call | solution.py:379
  15.7 0.0 copy-start.2
  15.7 0.7 copy-done.2
  16.4 0.0 copy-start
  16.4 0.0 copy-start.1
  16.4 81.5 %conditional.1 = (f32[2,8,128,128]{3,2,1,0:T(8,128)}, f32[2,16,128]{2,1,0:T(8,128)}, f32[2,16,128]{2,1,0:T(8,128)S(1)}, f32[16,1,8192]{2,1,0:T(1,128)}, f32[16,1,8192]{2,1,0:T(1,128)}) conditional(s32[]{:T(128)} %bitcast.6, () %tuple.20, (f32[2,16,128,128]{3,2,1,0:T(8,128)}, f32[5248,128]{1,0:T(8,128)}, s32[1]{0:T(128)}, f32[1024,128]{1,0:T(8,128)}, ...), branch_computations={%region_0.0_spmd, %region_1.0_spmd} | conditional | bytes 14549172 | solution.py:446
  16.4 10.8 %all-to-all-start = ((f32[5248,1,128]{2,1,0:T(1,128)}), f32[5248,1,128]{2,1,0:T(1,128)S(1)}, u32[]{:S(2)}, u32[]{:S(2)}) async-start(f32[5248,1,128]{2,1,0:T(1,128)} %bitcast.19), calls=%async_computation | async-start | bytes 5373952 | tf_op jit(solution)/shard_map/cond/branch_1_fun/all_to_all | solution.py:414
  27.2 0.0 copy-start.4
  27.2 2.3 %slice.6 = f32[2,8,128,128]{3,2,1,0:T(8,128)} slice(f32[2,16,128,128]{3,2,1,0:T(8,128)} %get-tuple-element.14), slice={[0:2], [8:16], [0:128], [0:128]} | slice | bytes 2097152 | tf_op jit(solution)/shard_map/cond/branch_1_fun/slice | solution.py:413
  29.5 1.0 collective-permute-start
  30.5 55.6 %all-to-all-done = f32[5248,1,128]{2,1,0:T(1,128)S(1)} async-done(((f32[5248,1,128]{2,1,0:T(1,128)}), f32[5248,1,128]{2,1,0:T(1,128)S(1)}, u32[]{:S(2)}, u32[]{:S(2)}) %all-to-all-start) | async-done | bytes 2687008 | tf_op jit(solution)/shard_map/cond/branch_1_fun/all_to_all | solution.py:414
  86.1 3.1 %second_push.1 = (f32[2,16,128]{2,1,0:T(8,128)S(1)}, f32[2,16,128]{2,1,0:T(8,128)S(1)}) custom-call(s32[1]{0:T(128)} %get-tuple-element.15.mine, f32[1024,128]{1,0:T(8,128)} %get-tuple-element.16.phases1, f32[1024,128]{1,0:T(8,128)} %get-tuple-element.17.energies1, f32[5248,128]{1,0:T(8,128)S(1)} %bitcast.14), custom_call_target="tpu_custom_call" | custom-call | tf_op jit(solution)/shard_map/cond/branch_1_fun/second_push/pallas_call | solution.py:416
  89.2 1.5 %collective-permute-start.1 = (f32[2,16,128]{2,1,0:T(8,128)S(1)}, f32[2,16,128]{2,1,0:T(8,128)}, u32[]{:S(2)}, u32[]{:S(2)}) collective-permute-start(f32[2,16,128]{2,1,0:T(8,128)S(1)} %get-tuple-element.19), channel_id=1, source_target_pairs={{0,1},{1,2},{2,3},{3,4},{4,5},{5,6},{6,7},{7,8},{8,9},{9,10},{10,1... | collective-permute-start | bytes 49160 | tf_op jit(solution)/shard_map/cond/branch_1_fun/ppermute | solution.py:345
  90.7 0.0 copy-done.4
  90.7 5.7 %pick.1 = (f32[1024,128]{1,0:T(8,128)}, f32[1024,128]{1,0:T(8,128)}) custom-call(s32[1]{0:T(128)} %get-tuple-element.15.mine, f32[5248,128]{1,0:T(8,128)S(1)} %bitcast.15, s32[8,1024]{1,0:T(8,128)S(1)} %copy-done.4), custom_call_target="tpu_custom_call" | custom-call | tf_op jit(solution)/shard_map/cond/branch_1_fun/pick/pallas_call | solution.py:426
  96.4 0.0 collective-permute-done
  96.4 1.4 %collective-permute-done.1 = f32[2,16,128]{2,1,0:T(8,128)} collective-permute-done((f32[2,16,128]{2,1,0:T(8,128)S(1)}, f32[2,16,128]{2,1,0:T(8,128)}, u32[]{:S(2)}, u32[]{:S(2)}) %collective-permute-start.1) | collective-permute-done | bytes 16416 | tf_op jit(solution)/shard_map/cond/branch_1_fun/ppermute | solution.py:345
  97.9 0.0 collective-permute-done.2.piece_a
  97.9 0.0 copy-done
  97.9 0.0 copy-done.1
  97.9 0.0 copy-start.3
  97.9 0.9 copy-done.3
  98.8 4.7 %diffract.1 = f32[2,16,128,128]{3,2,1,0:T(8,128)} custom-call(s32[1]{0:T(128)} %bitcast.4.mine, f32[2,8,128,128]{3,2,1,0:T(8,128)} %collective-permute-done.2.piece_a, f32[2,8,128,128]{3,2,1,0:T(8,128)} %get-tuple-element.41.piece_b, f32[2,16,128]{2,1,0:T(8,128)} %get-tuple-element.42.small, f32[2,16,128]{2,1,0:T(8,128)S(1)} %get-tuple-element.43.earlier, ...), custom_call_target="tpu_custom_call" | custom-call | tf_op jit(solution)/shard_map/diffract/pallas_call | solution.py:449
Async XLA Ops:
  2.9 94.9 %collective-permute-start.2 = (f32[2,8,128,128]{3,2,1,0:T(8,128)}, f32[2,8,128,128]{3,2,1,0:T(8,128)}, u32[]{:S(2)}, u32[]{:S(2)}) collective-permute-start(f32[2,8,128,128]{3,2,1,0:T(8,128)} %slice.11), channel_id=1, source_target_pairs={{0,2},{1,3},{2,4},{3,5},{4,6},{5,7},{6,8},{7,9},{8,10},{9,11},{10,... | collective-permute-start | bytes 3145736 | tf_op jit(solution)/shard_map/ppermute | solution.py:345
  15.7 0.7 copy-start.2
  16.4 81.5 %copy-start = (bf16[256,768]{1,0:T(8,128)(2,1)S(1)}, bf16[256,768]{1,0:T(8,128)(2,1)}, u32[]{:S(2)}) copy-start(bf16[256,768]{1,0:T(8,128)(2,1)} %constant.21.clone.left) | copy-start | bytes 1179652
  16.4 81.5 %copy-start.1 = (bf16[768,256]{1,0:T(8,128)(2,1)S(1)}, bf16[768,256]{1,0:T(8,128)(2,1)}, u32[]{:S(2)}) copy-start(bf16[768,256]{1,0:T(8,128)(2,1)} %constant.22.clone.right) | copy-start | bytes 1179652
  16.4 69.7 %all-to-all-start = ((f32[5248,1,128]{2,1,0:T(1,128)}), f32[5248,1,128]{2,1,0:T(1,128)S(1)}, u32[]{:S(2)}, u32[]{:S(2)}) async-start(f32[5248,1,128]{2,1,0:T(1,128)} %bitcast.19), calls=%async_computation | async-start | bytes 5373952 | tf_op jit(solution)/shard_map/cond/branch_1_fun/all_to_all | solution.py:414
  27.2 63.5 %copy-start.4 = (s32[8,1024]{1,0:T(8,128)S(1)}, s32[8,1024]{1,0:T(8,128)}, u32[]{:S(2)}) copy-start(s32[8,1024]{1,0:T(8,128)} %get-tuple-element.21.places) | copy-start | bytes 98308 | tf_op jit(solution)/shard_map/cond
  29.5 66.9 %collective-permute-start = (f32[2,8,128,128]{3,2,1,0:T(8,128)}, f32[2,8,128,128]{3,2,1,0:T(8,128)}, u32[]{:S(2)}, u32[]{:S(2)}) collective-permute-start(f32[2,8,128,128]{3,2,1,0:T(8,128)} %slice.6), channel_id=1, source_target_pairs={{0,2},{1,3},{2,4},{3,5},{4,6},{5,7},{6,8},{7,9},{8,10},{9,11},{10,... | collective-permute-start | bytes 3145736 | tf_op jit(solution)/shard_map/cond/branch_1_fun/ppermute | solution.py:345
  89.2 8.7 %collective-permute-start.1 = (f32[2,16,128]{2,1,0:T(8,128)S(1)}, f32[2,16,128]{2,1,0:T(8,128)}, u32[]{:S(2)}, u32[]{:S(2)}) collective-permute-start(f32[2,16,128]{2,1,0:T(8,128)S(1)} %get-tuple-element.19), channel_id=1, source_target_pairs={{0,1},{1,2},{2,3},{3,4},{4,5},{5,6},{6,7},{7,8},{8,9},{9,10},{10,1... | collective-permute-start | bytes 49160 | tf_op jit(solution)/shard_map/cond/branch_1_fun/ppermute | solution.py:345
  97.9 0.9 copy-start.3

commit v3 on v1

--- a/solution.py
+++ b/solution.py
@@ -118,8 +118,8 @@
 
 def first_kernel(
     mine, field_hbm, profile_hbm, bins_hbm, jitter_hbm, energy_hbm, delays_hbm, left_hbm, right_hbm,
-    send_hbm, phases, energies, beam, places,
-    field, profile, bins, jitter, energy, delays, left, right, acc, send, index_v, index, sems,
+    send_hbm, phases_hbm, energies_hbm, places_hbm, beam,
+    field, profile, bins, jitter, energy, delays, left, right, acc, send, phases, energies, places, index_v, index, sems,
 ):
     pairs = [
         (profile_hbm, profile), (left_hbm, left), (right_hbm, right), (delays_hbm, delays),
@@ -145,6 +145,8 @@
     beam[1] = spread[:, GRID:]
     beam[2] = p
     copies[4].wait()
+    kept = [pltpu.make_async_copy(places, places_hbm, sems.at[8])]
+    kept[0].start()
 
     def project(k, carry):
         re, im = field[0, k], field[1, k]
@@ -175,6 +177,10 @@
         return carry
 
     lax.fori_loop(0, GROUPS, push, 0)
+    kept.append(pltpu.make_async_copy(phases, phases_hbm, sems.at[9]))
+    kept.append(pltpu.make_async_copy(energies, energies_hbm, sems.at[10]))
+    for copy in kept[1:]:
+        copy.start()
     to_scalar.wait()
 
     def put(n, carry):
@@ -198,6 +204,8 @@
         send[n * MESSAGE + 2 * CAP : (n + 1) * MESSAGE] = note
     out = pltpu.make_async_copy(send, send_hbm, sems.at[0])
     out.start()
+    for copy in kept:
+        copy.wait()
     out.wait()
 
 
@@ -286,30 +294,26 @@
 
 
 SLAB = 4
-PIECES = ((0, 1), (1, 12), (12, 16))
-
-
-def field_kernel(mine, piece_a, piece_b, piece_c, small, earlier, beam, left, right, out_hbm, acc, out, sems):
-    me = mine[0]
-    for n in range(2):
-        acc[n] = GAIN * carried(small[n], me == 0)
-        acc[2 + n] = GAIN * earlier[n]
+PIECES = ((0, 8), (8, 16))
+
+
+def field_kernel(first, mine, piece, before, earlier, beam, left, right, out):
+    late = mine[0] < 2
+    p = beam[2]
 
     def plane(c, k):
-        for piece, (low, high) in zip((piece_a, piece_b, piece_c), PIECES):
-            if low <= k < high:
-                return piece[c, k - low]
-        return jnp.zeros((GRID, GRID), jnp.float32)
-
-    late = me < 2
-    p = beam[2]
-    dr, di = beam[0], beam[1]
-    copies = []
-    for slab in range(GROUPS // SLAB):
+        if k >= 0:
+            return piece[c, k]
+        return before[c, before.shape[1] - 1] if first else jnp.zeros((GRID, GRID), jnp.float32)
+
+    for slab in range(piece.shape[1] // SLAB):
         ks = range(slab * SLAB, (slab + 1) * SLAB)
         rows = []
         for k in ks:
-            parts = [jnp.where(late, plane(c, k - 1), plane(c, k)) + acc[2 + c, k : k + 1] * p for c in range(2)]
+            parts = [
+                jnp.where(late, plane(c, k - 1), plane(c, k)) + GAIN * earlier[c, first + k : first + k + 1] * p
+                for c in range(2)
+            ]
             rows.append(jnp.concatenate(parts, axis=1))
         hi, lo = wide_halves(jnp.concatenate(rows, axis=0))
         half = jnp.dot(jnp.concatenate([hi, lo, hi], axis=1), right[...], preferred_element_type=jnp.float32)
@@ -320,13 +324,28 @@
         hi, lo = wide_halves(jnp.concatenate(cols, axis=1))
         full = jnp.dot(left[...], jnp.concatenate([hi, lo, hi], axis=0), preferred_element_type=jnp.float32)
         for m, k in enumerate(ks):
-            cr, ci = acc[0, k : k + 1], acc[1, k : k + 1]
-            out[0, k] = full[:GRID, m * GRID : (m + 1) * GRID] + (cr * dr - ci * di)
-            out[1, k] = full[GRID:, m * GRID : (m + 1) * GRID] + (cr * di + ci * dr)
-        for c in range(2):
-            span = pl.ds(slab * SLAB, SLAB)
-            copies.append(pltpu.make_async_copy(out.at[c, span], out_hbm.at[c, span], sems.at[2 * slab + c]))
-            copies[-1].start()
+            out[0, k] = full[:GRID, m * GRID : (m + 1) * GRID]
+            out[1, k] = full[GRID:, m * GRID : (m + 1) * GRID]
+
+
+def last_kernel(mine, part_a, part_b, small, beam, out_hbm, acc, out, sems):
+    for n in range(2):
+        acc[n] = GAIN * carried(small[n], mine[0] == 0)
+    copies = []
+    for part, (low, high) in zip((part_a, part_b), PIECES):
+
+        def add(k, carry, part=part, low=low):
+            cr, ci = acc[0, pl.ds(low + k, 1)], acc[1, pl.ds(low + k, 1)]
+            out[0, low + k] = part[0, k] + (cr * beam[0] - ci * beam[1])
+            out[1, low + k] = part[1, k] + (cr * beam[1] + ci * beam[0])
+            return carry
+
+        for start in range(0, high - low, SLAB):
+            lax.fori_loop(start, start + SLAB, add, 0)
+            span = pl.ds(low + start, SLAB)
+            for c in range(2):
+                copies.append(pltpu.make_async_copy(out.at[c, span], out_hbm.at[c, span], sems.at[len(copies)]))
+                copies[-1].start()
     for copy in copies:
         copy.wait()
 
@@ -365,20 +384,20 @@
     one, two = line_operator(1), line_operator(2)
     left_one = jnp.asarray(np.concatenate(one, axis=0), jnp.float32)
     right_one = jnp.asarray(right_form(*one), jnp.float32)
-    sources = [field[:, low:high] for low, high in PIECES]
-    field_a = shifted(sources[0], "cuts", 2)
+    field_a = shifted(field[:, : PIECES[0][1]], "cuts", 2)
     operands = [field, profile, bins, jitter, energies, delays.reshape(GROUPS, 1, NBS), left_one, right_one]
-    send, phases1, energies1, beam, places = pl.pallas_call(
+    low, high = PIECES[1]
+    send, phases1, energies1, places, beam = pl.pallas_call(
         first_kernel,
         out_shape=(
             pltpu.HBM((ROWS, BLOCK), jnp.float32),
-            shape(COUNT, BLOCK),
-            shape(COUNT, BLOCK),
+            pltpu.HBM((COUNT, BLOCK), jnp.float32),
+            pltpu.HBM((COUNT, BLOCK), jnp.float32),
+            pltpu.HBM((8, COUNT), jnp.int32),
             shape(3, GRID, GRID),
-            shape(8, COUNT, dtype=jnp.int32),
         ),
         in_specs=[scalar] + [remain] * 8,
-        out_specs=(remain,) + (whole(),) * 4,
+        out_specs=(remain,) * 4 + (whole(),),
         scratch_shapes=[
             vmem(2, GROUPS, GRID, GRID),
             vmem(GRID, GRID),
@@ -390,18 +409,26 @@
             vmem(2 * GRID, 2 * GRID),
             vmem(6, GROUPS, 128),
             vmem(ROWS, BLOCK),
+            vmem(COUNT, BLOCK),
+            vmem(COUNT, BLOCK),
+            vmem(8, COUNT, dtype=jnp.int32),
             vmem(8, 128, dtype=jnp.int32),
             pltpu.SMEM((8, 128), jnp.int32),
-            pltpu.SemaphoreType.DMA((8,)),
+            pltpu.SemaphoreType.DMA((11,)),
         ],
         compiler_params=params,
         name="push_place",
     )(mine, *[in_hbm(value) for value in operands])
-    send, field_a = lax.optimization_barrier((send, field_a))
-    field_b = shifted(sources[1], "cuts", 2)
-    field_c = shifted(sources[2], "cuts", 2)
-    recv = lax.all_to_all(send.reshape(ROWS, 1, BLOCK), "cuts", split_axis=0, concat_axis=0, tiled=True)
-    recv = recv.reshape(ROWS, BLOCK)
+
+    def exchange(rows):
+        return lax.all_to_all(rows.reshape(ROWS, 1, BLOCK), "cuts", split_axis=0, concat_axis=0, tiled=True)
+
+    def refuse(rows):
+        return jnp.zeros((ROWS, 1, BLOCK), jnp.float32)
+
+    recv = lax.cond(delays[0, 0, 0] < PEERS, exchange, refuse, send).reshape(ROWS, BLOCK)
+    source_b, recv = lax.optimization_barrier((field[:, low:high], recv))
+    field_b = shifted(source_b, "cuts", 2)
     small, earlier = pl.pallas_call(
         second_kernel,
         out_shape=(shape(2, GROUPS, 128), shape(2, GROUPS, 128)),
@@ -426,19 +453,33 @@
         compiler_params=params,
         name="pick",
     )(mine, recv, places)
+    tables = (earlier, beam, deep_left(left_form(*two)), deep_right(right_form(*two)))
+
+    def diffract(first, piece, before):
+        return pl.pallas_call(
+            functools.partial(field_kernel, first),
+            out_shape=shape(*piece.shape),
+            in_specs=[scalar] + [whole()] * 6,
+            out_specs=whole(),
+            compiler_params=params,
+            name="diffract",
+        )(mine, piece, before, *tables)
+
+    part_a = diffract(0, field_a, field_a)
+    part_b = diffract(low, field_b, field_a)
     out = pl.pallas_call(
-        field_kernel,
+        last_kernel,
         out_shape=shape(2, GROUPS, GRID, GRID),
-        in_specs=[scalar] + [whole()] * 8,
+        in_specs=[scalar] + [whole()] * 4,
         out_specs=remain,
         scratch_shapes=[
-            vmem(4, GROUPS, 128),
+            vmem(2, GROUPS, 128),
             vmem(2, GROUPS, GRID, GRID),
             pltpu.SemaphoreType.DMA((2 * GROUPS // SLAB,)),
         ],
         compiler_params=params,
-        name="diffract",
-    )(mine, field_a, field_b, field_c, arrived, earlier, beam, deep_left(left_form(*two)), deep_right(right_form(*two)))
+        name="last_bunching",
+    )(mine, part_a, part_b, arrived, beam)
     return (
         out.reshape(2, GROUPS, 1, GRID, GRID),
         phase_out.reshape(GROUPS, 1, NBS * BLOCK),

time: 109 us -> 99.5 us (0.913)
  blocking collectives: 0 us -> 49.4 us
  waiting for transfers between devices: 63.4 us -> 19.6 us
  starting transfers between devices: 14.9 us -> 1.7 us
  local copies, waits for them, and re-layouts: 7.87 us -> 3.91 us
  Pallas kernels: 21.6 us -> 23.2 us
    all_to_all x0 -> x1, blocking collectives: none -> 49.4 us  [exchange(): lax.all_to_all(rows.reshape(ROWS, 1, BLOCK), 'cuts', split_axis=0, concat...]
    all_to_all x1 -> x0, waiting for transfers between devices: 30.4 us -> none  [per_device(): lax.all_to_all(send.reshape(ROWS, 1, BLOCK), 'cuts', split_axis=0, concat...]
    ppermute x4 -> x3, waiting for transfers between devices: 33 us -> 19.6 us  [shifted(): return lax.ppermute(value, axis, pairs)]
    all_to_all x1 -> x0, starting transfers between devices: 10.8 us -> none  [per_device(): lax.all_to_all(send.reshape(ROWS, 1, BLOCK), 'cuts', split_axis=0, concat...]
    unnamed x12, local copies, waits for them, and re-layouts: 2.45 us -> 0.03 us
    ppermute x4 -> x3, starting transfers between devices: 4.09 us -> 1.7 us  [shifted(): return lax.ppermute(value, axis, pairs)]
    pallas_call x1, Pallas kernels: 1.86 us -> 3.77 us  [per_device(): pl.pallas_call(second_kernel, out_shape=(shape(2, GROUPS, 128), shape(2,...]
    slice x3 -> x2, local copies, waits for them, and re-layouts: 5.41 us -> 3.87 us  [the longest x1 2.71 us: per_device(): source_b, recv = lax.optimization_barrier((field[:, low:high], recv))]
  transfers between devices with their start and end apart: 5 -> 3, of which waited for: 2 -> 1; matrix products, arithmetic and copies ran while one was open for 4% -> 1% of each run, Pallas kernels for 16% -> 22%
where the time goes in v3:
time: 99.5 us; the launch traced here: 99.3 us
  blocking collectives  49.4 us (50%)
  Pallas kernels  23.2 us (23%)
  waiting for transfers between devices  19.6 us (20%)
  local copies, waits for them, and re-layouts  3.91 us (4%)
  starting transfers between devices  1.7 us (2%)
  between operations  1.4 us (1%)
    all_to_all x1, blocking collectives, exchange(): lax.all_to_all(rows.reshape(ROWS, 1, BLOCK), 'cuts', split_axis=0, concat...  49.4 us
    ppermute x3, waiting for transfers between devices, shifted(): return lax.ppermute(value, axis, pairs)  19.6 us
    pallas_call x1, Pallas kernels, per_device(): pl.pallas_call(first_kernel, out_shape=(pltpu.HBM((ROWS, BLOCK), jnp.floa...  9.33 us
    pallas_call x1, Pallas kernels, per_device(): pl.pallas_call(pick_kernel, out_shape=(shape(COUNT, BLOCK), shape(COUNT,...  5.73 us
    pallas_call x1, Pallas kernels, per_device(): pl.pallas_call(second_kernel, out_shape=(shape(2, GROUPS, 128), shape(2,...  3.77 us
    pallas_call x2, Pallas kernels, diffract(): pl.pallas_call(functools.partial(field_kernel, first), out_shape=shape(*p...  2.86 us
    slice x1, local copies, waits for them, and re-layouts, per_device(): source_b, recv = lax.optimization_barrier((field[:, low:high], recv))  2.71 us
  transfers between devices with their start and end apart: 3, of which 1 were waited for; matrix products, arithmetic and copies ran while one was open for 1% of the time, Pallas kernels for 22%

profile of v3, /device:TPU:0, one launch (start us, length us, event | category | flops | bytes accessed | tf_op | source)
XLA Modules:
  0.0 99.3 jit_solution(3033604294319772280)
XLA Ops:
  0.6 2.7 %fusion = (f32[2,8,128,128]{3,2,1,0:T(8,128)S(1)}, f32[2,8,128,128]{3,2,1,0:T(8,128)}) fusion(f32[2,16,128,128]{3,2,1,0:T(8,128)} %bitcast.15), kind=kLoop, calls=%fused_computation | loop fusion | bytes 4194304 | tf_op jit(solution)/shard_map/slice | solution.py:430
  3.3 1.6 %collective-permute-start = (f32[2,8,128,128]{3,2,1,0:T(8,128)}, f32[2,8,128,128]{3,2,1,0:T(8,128)S(1)}, u32[]{:S(2)}, u32[]{:S(2)}) collective-permute-start(f32[2,8,128,128]{3,2,1,0:T(8,128)} %get-tuple-element.37), channel_id=1, source_target_pairs={{0,2},{1,3},{2,4},{3,5},{4,6},{5,7},{6,8},{7,9},{8,10},{9,11},{10,... | collective-permute-start | bytes 3145736 | tf_op jit(solution)/shard_map/ppermute | solution.py:356
  4.9 1.2 %slice.11 = s32[1,1,1]{1,2,0:T(1,128)} slice(s32[16,64,1]{1,2,0:T(1,128)} %param.17), slice={[0:1], [0:1], [0:1]} | slice | bytes 8 | tf_op jit(solution)/shard_map/slice | solution.py:429
  6.7 9.3 %push_place.1 = (f32[5248,128]{1,0:T(8,128)}, f32[1024,128]{1,0:T(8,128)}, f32[1024,128]{1,0:T(8,128)}, s32[8,1024]{1,0:T(8,128)}, f32[3,128,128]{2,1,0:T(8,128)S(1)}) custom-call(s32[1]{0:T(128)} %bitcast.2.mine, f32[2,16,128,128]{3,2,1,0:T(8,128)} %bitcast.16, f32[128,128]{1,0:T(8,128)} %profile_hbm.1, s32[1024,128]{1,0:T(8,128)} %bitcast.19, ...), custom_call_target="tpu_custom_call" | custom-call | tf_op jit(solution)/shard_map/push_place/pallas_call | solution.py:390
  16.1 0.0 copy-start.2
  16.1 0.0 copy-start.3
  16.1 49.4 %conditional.1 = (f32[5248,128]{1,0:T(8,128)}) conditional(s32[]{:T(128)} %bitcast.8, () %tuple.17, f32[5248,128]{1,0:T(8,128)} %get-tuple-element.21), branch_computations={%region_0.0_spmd, %region_1.0_spmd} | conditional | bytes 5373960 | solution.py:429
  16.1 49.4 %all_to_all.4 = f32[5248,1,128]{2,1,0:T(1,128)} all-to-all(f32[5248,1,128]{2,1,0:T(1,128)} %bitcast.17), channel_id=1, replica_groups=mesh['cuts'=128] {'cuts'}, dimensions={0} | all-to-all | bytes 5373952 | tf_op jit(solution)/shard_map/cond/branch_1_fun/all_to_all | solution.py:424
  65.5 0.0 copy-start.4
  65.5 0.0 copy-start.5
  65.5 0.0 collective-permute-start.1
  65.6 0.0 copy-done.2
  65.6 0.0 copy-done.3
  65.6 0.0 copy-start
  65.6 0.0 copy-start.1
  65.6 3.8 %second_push.1 = (f32[2,16,128]{2,1,0:T(8,128)S(1)}, f32[2,16,128]{2,1,0:T(8,128)S(1)}) custom-call(s32[1]{0:T(128)} %bitcast.2.mine, f32[1024,128]{1,0:T(8,128)S(1)} %copy-done.2, f32[1024,128]{1,0:T(8,128)S(1)} %copy-done.3, f32[5248,128]{1,0:T(8,128)} %get-tuple-element.38.recv), custom_call_target="tpu_custom_call" | custom-call | tf_op jit(solution)/shard_map/second_push/pallas_call | solution.py:432
  69.4 0.1 collective-permute-start.2
  69.5 0.0 copy-done.4
  69.5 0.0 copy-done.5
  69.5 5.7 %pick.1 = (f32[1024,128]{1,0:T(8,128)}, f32[1024,128]{1,0:T(8,128)}) custom-call(s32[1]{0:T(128)} %bitcast.2.mine, f32[5248,128]{1,0:T(8,128)S(1)} %copy-done.5, s32[8,1024]{1,0:T(8,128)S(1)} %copy-done.4), custom_call_target="tpu_custom_call" | custom-call | tf_op jit(solution)/shard_map/pick/pallas_call | solution.py:442
  75.2 0.0 collective-permute-done.piece.before
  75.3 0.0 copy-done
  75.3 0.0 copy-done.1
  75.3 1.4 %diffract.2.part_a = f32[2,8,128,128]{3,2,1,0:T(8,128)S(1)} custom-call(s32[1]{0:T(128)} %bitcast.2.mine, f32[2,8,128,128]{3,2,1,0:T(8,128)S(1)} %collective-permute-done.piece.before, f32[2,8,128,128]{3,2,1,0:T(8,128)S(1)} %collective-permute-done.piece.before, f32[2,16,128]{2,1,0:T(8,128)S(1)} %get-tuple-element.23.earlier, ...), custom_call_target="tpu_custom_call" | custom-call | tf_op jit(solution)/shard_map/diffract/pallas_call | solution.py:459
  76.7 19.6 %collective-permute-done.1.piece = f32[2,8,128,128]{3,2,1,0:T(8,128)S(1)} collective-permute-done((f32[2,8,128,128]{3,2,1,0:T(8,128)S(1)}, f32[2,8,128,128]{3,2,1,0:T(8,128)S(1)}, u32[]{:S(2)}, u32[]{:S(2)}) %collective-permute-start.1) | collective-permute-done | bytes 1048608 | tf_op jit(solution)/shard_map/ppermute | solution.py:356
  96.3 1.4 %diffract.3.part_b = f32[2,8,128,128]{3,2,1,0:T(8,128)S(1)} custom-call(s32[1]{0:T(128)} %bitcast.2.mine, f32[2,8,128,128]{3,2,1,0:T(8,128)S(1)} %collective-permute-done.1.piece, f32[2,8,128,128]{3,2,1,0:T(8,128)S(1)} %collective-permute-done.piece.before, f32[2,16,128]{2,1,0:T(8,128)S(1)} %get-tuple-element.23.earlier, ...), custom_call_target="tpu_custom_call" | custom-call | tf_op jit(solution)/shard_map/diffract/pallas_call | solution.py:459
  97.8 0.0 collective-permute-done.2.small
  97.8 1.5 %last_bunching.1 = f32[2,16,128,128]{3,2,1,0:T(8,128)} custom-call(s32[1]{0:T(128)} %bitcast.2.mine, f32[2,8,128,128]{3,2,1,0:T(8,128)S(1)} %diffract.2.part_a, f32[2,8,128,128]{3,2,1,0:T(8,128)S(1)} %diffract.3.part_b, f32[2,16,128]{2,1,0:T(8,128)S(1)} %collective-permute-done.2.small, f32[3,128,128]{2,1,0:T(8,128)S(1)} %get-tuple-element.24.beam), custom_call_target="tpu_custom_call" | custom-call | tf_op jit(solution)/shard_map/last_bunching/pallas_call | solution.py:470
Async XLA Ops:
  3.3 71.9 %collective-permute-start = (f32[2,8,128,128]{3,2,1,0:T(8,128)}, f32[2,8,128,128]{3,2,1,0:T(8,128)S(1)}, u32[]{:S(2)}, u32[]{:S(2)}) collective-permute-start(f32[2,8,128,128]{3,2,1,0:T(8,128)} %get-tuple-element.37), channel_id=1, source_target_pairs={{0,2},{1,3},{2,4},{3,5},{4,6},{5,7},{6,8},{7,9},{8,10},{9,11},{10,... | collective-permute-start | bytes 3145736 | tf_op jit(solution)/shard_map/ppermute | solution.py:356
  16.1 49.5 %copy-start.2 = (f32[1024,128]{1,0:T(8,128)S(1)}, f32[1024,128]{1,0:T(8,128)}, u32[]{:S(2)}) copy-start(f32[1024,128]{1,0:T(8,128)} %get-tuple-element.19.phases1) | copy-start | bytes 1572868
  16.1 49.5 %copy-start.3 = (f32[1024,128]{1,0:T(8,128)S(1)}, f32[1024,128]{1,0:T(8,128)}, u32[]{:S(2)}) copy-start(f32[1024,128]{1,0:T(8,128)} %get-tuple-element.20.energies1) | copy-start | bytes 1572868
  65.5 4.0 %copy-start.4 = (s32[8,1024]{1,0:T(8,128)S(1)}, s32[8,1024]{1,0:T(8,128)}, u32[]{:S(2)}) copy-start(s32[8,1024]{1,0:T(8,128)} %get-tuple-element.27.places) | copy-start | bytes 98308
  65.5 4.0 %copy-start.5 = (f32[5248,128]{1,0:T(8,128)S(1)}, f32[5248,128]{1,0:T(8,128)}, u32[]{:S(2)}) copy-start(f32[5248,128]{1,0:T(8,128)} %get-tuple-element.38.recv) | copy-start | bytes 8060932
  65.5 30.8 %collective-permute-start.1 = (f32[2,8,128,128]{3,2,1,0:T(8,128)S(1)}, f32[2,8,128,128]{3,2,1,0:T(8,128)S(1)}, u32[]{:S(2)}, u32[]{:S(2)}) collective-permute-start(f32[2,8,128,128]{3,2,1,0:T(8,128)S(1)} %get-tuple-element.25), channel_id=1, source_target_pairs={{0,2},{1,3},{2,4},{3,5},{4,6},{5,7},{6,8},{7,9},{8,10},{9,11},{10,... | collective-permute-start | bytes 3145736 | tf_op jit(solution)/shard_map/ppermute | solution.py:356
  65.6 9.7 %copy-start = (bf16[256,768]{1,0:T(8,128)(2,1)S(1)}, bf16[256,768]{1,0:T(8,128)(2,1)}, u32[]{:S(2)}) copy-start(bf16[256,768]{1,0:T(8,128)(2,1)} %constant.19.clone.left) | copy-start | bytes 1179652
  65.6 9.7 %copy-start.1 = (bf16[768,256]{1,0:T(8,128)(2,1)S(1)}, bf16[768,256]{1,0:T(8,128)(2,1)}, u32[]{:S(2)}) copy-start(bf16[768,256]{1,0:T(8,128)(2,1)} %constant.20.clone.right) | copy-start | bytes 1179652
  69.4 28.4 %collective-permute-start.2 = (f32[2,16,128]{2,1,0:T(8,128)S(1)}, f32[2,16,128]{2,1,0:T(8,128)S(1)}, u32[]{:S(2)}, u32[]{:S(2)}) collective-permute-start(f32[2,16,128]{2,1,0:T(8,128)S(1)} %get-tuple-element.26), channel_id=1, source_target_pairs={{0,1},{1,2},{2,3},{3,4},{4,5},{5,6},{6,7},{7,8},{8,9},{9,10},{10,1... | collective-permute-start | bytes 49160 | tf_op jit(solution)/shard_map/ppermute | solution.py:356

commit v4 on v2

--- a/solution.py
+++ b/solution.py
@@ -294,17 +294,24 @@
 
 
 SLAB = 4
-PIECES = ((0, 8), (8, 16))
-
-
-def field_kernel(mine, piece_a, piece_b, small, earlier, beam, left, right, out_hbm, acc, out, out_sems):
+EARLY, LATE = 4, 12
+MIDDLE = ((4, 7), (7, 10), (10, 12))
+
+
+def field_kernel(
+    mine, piece_0, piece_1, piece_b0, piece_b1, piece_b2, piece_c, small, earlier, beam, left, right, out_hbm, acc, out, out_sems
+):
     me = mine[0]
 
     def plane(c, k):
-        for piece, (low, high) in zip((piece_a, piece_b), PIECES):
+        if k < 0:
+            return jnp.zeros((GRID, GRID), jnp.float32)
+        if k < EARLY:
+            return jnp.where(me % 2 == 0, piece_0[c, k], piece_1[c, k])
+        for piece, (low, high) in zip((piece_b0, piece_b1, piece_b2), MIDDLE):
             if low <= k < high:
                 return piece[c, k - low]
-        return jnp.zeros((GRID, GRID), jnp.float32)
+        return piece_c[c, k - LATE]
 
     for n in range(2):
         acc[n] = GAIN * carried(small[n], me == 0)
@@ -339,6 +346,16 @@
         copy.wait()
 
 
+def early_pairs(core):
+    onward = [(device, (device + 2) % PEERS) for device in range(core, PEERS, 2)]
+    across = [(device, (device + 8) % PEERS) for device in range(1 - core, PEERS, 2) if device % 8 >= 6]
+    return onward + across
+
+
+def late_pairs():
+    return [(device, device + 2 if device % 8 < 6 else device - 6) for device in range(PEERS)]
+
+
 def shifted(value, axis, steps):
     count = lax.axis_size(axis)
     pairs = [(source, (source + steps) % count) for source in range(count)]
@@ -373,9 +390,10 @@
     one, two = line_operator(1), line_operator(2)
     left_one = jnp.asarray(np.concatenate(one, axis=0), jnp.float32)
     right_one = jnp.asarray(right_form(*one), jnp.float32)
-    field_a = shifted(field[:, : PIECES[0][1]], "cuts", 2)
+    core = mine[0] % 2
+    shared_0 = lax.ppermute(lax.dynamic_slice_in_dim(field, core * LATE, EARLY, 1), "cuts", early_pairs(0))
+    shared_1 = lax.ppermute(lax.dynamic_slice_in_dim(field, (1 - core) * LATE, EARLY, 1), "cuts", early_pairs(1))
     operands = [field, profile, bins, jitter, energies, delays.reshape(GROUPS, 1, NBS), left_one, right_one]
-    low, high = PIECES[1]
     send, phases1, energies1, places, beam = pl.pallas_call(
         first_kernel,
         out_shape=(
@@ -408,9 +426,13 @@
         compiler_params=params,
         name="push_place",
     )(mine, *[in_hbm(value) for value in operands])
-
-    def exchange(send, phases1, energies1, places, field):
-        field_b = shifted(field[:, low:high], "cuts", 2)
+    send, *sources = lax.optimization_barrier((send, *[field[:, low:high] for low, high in MIDDLE]))
+    field_b = [shifted(source, "cuts", 2) for source in sources]
+
+    def exchange(send, phases1, energies1, places, field, shared_0, shared_1):
+        handed = jnp.where(core == 0, shared_1, shared_0)
+        source_c = jnp.where(mine[0] % 8 >= 6, handed, field[:, LATE:])
+        field_c = lax.ppermute(source_c, "cuts", late_pairs())
         recv = lax.all_to_all(send.reshape(ROWS, 1, BLOCK), "cuts", split_axis=0, concat_axis=0, tiled=True)
         recv = recv.reshape(ROWS, BLOCK)
         small, earlier = pl.pallas_call(
@@ -437,19 +459,19 @@
             compiler_params=params,
             name="pick",
         )(mine, recv, places)
-        return phase_out, energy_out, field_b, arrived, earlier
+        return phase_out, energy_out, field_c, arrived, earlier
 
     def refuse(*operands):
-        sizes = [(COUNT, BLOCK)] * 2 + [(2, high - low, GRID, GRID)] + [(2, GROUPS, 128)] * 2
+        sizes = [(COUNT, BLOCK)] * 2 + [(2, GROUPS - LATE, GRID, GRID)] + [(2, GROUPS, 128)] * 2
         return tuple(jnp.zeros(size, jnp.float32) for size in sizes)
 
-    phase_out, energy_out, field_b, arrived, earlier = lax.cond(
-        delays[0, 0, 0] < PEERS, exchange, refuse, send, phases1, energies1, places, field
+    phase_out, energy_out, field_c, arrived, earlier = lax.cond(
+        delays[0, 0, 0] < PEERS, exchange, refuse, send, phases1, energies1, places, field, shared_0, shared_1
     )
     out = pl.pallas_call(
         field_kernel,
         out_shape=shape(2, GROUPS, GRID, GRID),
-        in_specs=[scalar] + [whole()] * 7,
+        in_specs=[scalar] + [whole()] * 11,
         out_specs=remain,
         scratch_shapes=[
             vmem(4, GROUPS, 128),
@@ -458,7 +480,18 @@
         ],
         compiler_params=params,
         name="diffract",
-    )(mine, field_a, field_b, arrived, earlier, beam, deep_left(left_form(*two)), deep_right(right_form(*two)))
+    )(
+        mine,
+        shared_0,
+        shared_1,
+        *field_b,
+        field_c,
+        arrived,
+        earlier,
+        beam,
+        deep_left(left_form(*two)),
+        deep_right(right_form(*two)),
+    )
     return (
         out.reshape(2, GROUPS, 1, GRID, GRID),
         phase_out.reshape(GROUPS, 1, NBS * BLOCK),

time: 104 us -> 103 us (level)
  waiting for transfers between devices: 57.1 us -> 45.1 us
  starting transfers between devices: 14.8 us -> 22.7 us
  other arithmetic: 0 us -> 2.09 us
    all_to_all x1, waiting for transfers between devices: 55.6 us -> 42.6 us  [exchange(): lax.all_to_all(send.reshape(ROWS, 1, BLOCK), 'cuts', split_axis=0, concat...]
    ppermute x0 -> x3, starting transfers between devices: none -> 5.9 us  [the longest x1 3.47 us: per_device(): lax.ppermute(lax.dynamic_slice_in_dim(field, core * LATE, EARLY, 1), 'cut...]
    select_n x0 -> x1, other arithmetic: none -> 2.09 us  [exchange(): source_c = jnp.where(mine[0] % 8 >= 6, handed, field[:, LATE:])]
    dynamic_slice x0 -> x1, local copies, waits for them, and re-layouts: none -> 1.3 us  [per_device(): lax.dynamic_slice_in_dim(field, (1 - core) * LATE, EARLY, 1)]
    ppermute x3 -> x4, starting transfers between devices: 4.04 us -> 5.19 us  [shifted(): return lax.ppermute(value, axis, pairs)]
    ppermute x3 -> x4, waiting for transfers between devices: 1.45 us -> 2.55 us  [shifted(): return lax.ppermute(value, axis, pairs)]
  transfers between devices with their start and end apart: 4 -> 8, of which waited for: 2 -> 2; matrix products, arithmetic and copies ran while one was open for 3% -> 7% of each run, Pallas kernels for 18% -> 18%
where the time goes in v4:
time: 103 us; the launch traced here: 102 us
  waiting for transfers between devices  45.1 us (44%)
  Pallas kernels  23 us (22%)
  starting transfers between devices  22.7 us (22%)
  local copies, waits for them, and re-layouts  7.26 us (7%)
  other arithmetic  2.09 us (2%)
  between operations  1.41 us (1%)
    all_to_all x1, waiting for transfers between devices, exchange(): lax.all_to_all(send.reshape(ROWS, 1, BLOCK), 'cuts', split_axis=0, concat...  42.6 us
    all_to_all x1, starting transfers between devices, exchange(): lax.all_to_all(send.reshape(ROWS, 1, BLOCK), 'cuts', split_axis=0, concat...  11.6 us
    pallas_call x1, Pallas kernels, per_device(): pl.pallas_call(first_kernel, out_shape=(pltpu.HBM((ROWS, BLOCK), jnp.floa...  9.36 us
    pallas_call x1, Pallas kernels, exchange(): pl.pallas_call(pick_kernel, out_shape=(shape(COUNT, BLOCK), shape(COUNT,...  5.73 us
    ppermute x4, starting transfers between devices, shifted(): return lax.ppermute(value, axis, pairs)  5.19 us
    pallas_call x1, Pallas kernels, per_device(): pl.pallas_call(field_kernel, out_shape=shape(2, GROUPS, GRID, GRID), in_s...  4.82 us
    slice x2, local copies, waits for them, and re-layouts, per_device(): field[:, low:high]  3.84 us
    ppermute x1, starting transfers between devices, per_device(): lax.ppermute(lax.dynamic_slice_in_dim(field, core * LATE, EARLY, 1), 'cut...  3.47 us
  transfers between devices with their start and end apart: 8, of which 2 were waited for; matrix products, arithmetic and copies ran while one was open for 7% of the time, Pallas kernels for 18%

profile of v4, /device:TPU:0, one launch (start us, length us, event | category | flops | bytes accessed | tf_op | source)
XLA Modules:
  0.0 101.6 jit_solution(9962707642210676947)
XLA Ops:
  0.7 1.3 %dynamic-slice_bitcast_fusion = (f32[2,4,128,128]{3,2,1,0:T(8,128)S(1)}, f32[2,4,128,128]{3,2,1,0:T(8,128)S(1)}) fusion(f32[2,16,1,128,128]{4,3,2,1,0:T(8,128)} %param.12, s32[]{:T(128)S(6)} %select_n.33, s32[]{:T(128)S(6)} %select_n.32), kind=kLoop, calls=%fused_computation.1 | loop fusion | bytes 2097160 | tf_op jit(solution)/shard_map/dynamic_slice | solution.py:395
  2.0 1.5 %collective-permute-start.3 = (f32[2,4,128,128]{3,2,1,0:T(8,128)S(1)}, f32[2,4,128,128]{3,2,1,0:T(8,128)}, u32[]{:S(2)}, u32[]{:S(2)}) collective-permute-start(f32[2,4,128,128]{3,2,1,0:T(8,128)S(1)} %get-tuple-element.77), channel_id=1, source_target_pairs={{1,3},{3,5},{5,7},{7,9},{9,11},{11,13},{13,15},{15,17},{17,19},{19... | collective-permute-start | bytes 1572872 | tf_op jit(solution)/shard_map/ppermute | solution.py:395
  3.4 3.5 %collective-permute-start.2 = (f32[2,4,128,128]{3,2,1,0:T(8,128)S(1)}, f32[2,4,128,128]{3,2,1,0:T(8,128)}, u32[]{:S(2)}, u32[]{:S(2)}) collective-permute-start(f32[2,4,128,128]{3,2,1,0:T(8,128)S(1)} %get-tuple-element.78), channel_id=1, source_target_pairs={{0,2},{2,4},{4,6},{6,8},{8,10},{10,12},{12,14},{14,16},{16,18},{18... | collective-permute-start | bytes 1572872 | tf_op jit(solution)/shard_map/ppermute | solution.py:394
  6.9 1.7 %slice.21 = f32[2,2,128,128]{3,2,1,0:T(8,128)} slice(f32[2,16,128,128]{3,2,1,0:T(8,128)} %bitcast.7.field_hbm), slice={[0:2], [10:12], [0:128], [0:128]} | slice | bytes 524288 | tf_op jit(solution)/shard_map/slice | solution.py:429
  8.6 9.4 %push_place.1 = (f32[5248,128]{1,0:T(8,128)}, f32[1024,128]{1,0:T(8,128)}, f32[1024,128]{1,0:T(8,128)}, s32[8,1024]{1,0:T(8,128)}, f32[3,128,128]{2,1,0:T(8,128)S(1)}) custom-call(s32[1]{0:T(128)} %bitcast.4.mine, f32[2,16,128,128]{3,2,1,0:T(8,128)} %bitcast.7.field_hbm, f32[128,128]{1,0:T(8,128)} %profile_hbm.1, s32[1024,128]{1,0:T(8,128)} %bitcast.22, ...), custom_call_target="tpu_custom_call" | custom-call | tf_op jit(solution)/shard_map/push_place/pallas_call | solution.py:397
  18.0 0.0 copy-start.2
  18.0 2.1 %fusion = (f32[2,3,128,128]{3,2,1,0:T(8,128)}, f32[2,3,128,128]{3,2,1,0:T(8,128)}) fusion(f32[2,16,128,128]{3,2,1,0:T(8,128)} %bitcast.7.field_hbm), kind=kLoop, calls=%fused_computation.3 | loop fusion | bytes 1572864 | tf_op jit(solution)/shard_map/slice | solution.py:429
  20.1 1.5 %collective-permute-start.4 = (f32[2,3,128,128]{3,2,1,0:T(8,128)}, f32[2,3,128,128]{3,2,1,0:T(8,128)}, u32[]{:S(2)}, u32[]{:S(2)}) collective-permute-start(f32[2,3,128,128]{3,2,1,0:T(8,128)} %get-tuple-element.54), channel_id=1, source_target_pairs={{0,2},{1,3},{2,4},{3,5},{4,6},{5,7},{6,8},{7,9},{8,10},{9,11},{10,... | collective-permute-start | bytes 1179656 | tf_op jit(solution)/shard_map/ppermute | solution.py:362
  21.6 3.2 %collective-permute-start.5 = (f32[2,3,128,128]{3,2,1,0:T(8,128)}, f32[2,3,128,128]{3,2,1,0:T(8,128)}, u32[]{:S(2)}, u32[]{:S(2)}) collective-permute-start(f32[2,3,128,128]{3,2,1,0:T(8,128)} %get-tuple-element.55), channel_id=1, source_target_pairs={{0,2},{1,3},{2,4},{3,5},{4,6},{5,7},{6,8},{7,9},{8,10},{9,11},{10,... | collective-permute-start | bytes 1179656 | tf_op jit(solution)/shard_map/ppermute | solution.py:362
  24.9 0.0 collective-permute-start.6
  24.9 1.2 %slice.18 = s32[1,1,1]{1,2,0:T(1,128)} slice(s32[16,64,1]{1,2,0:T(1,128)} %param.17), slice={[0:1], [0:1], [0:1]} | slice | bytes 8 | tf_op jit(solution)/shard_map/slice | solution.py:469
  26.7 0.0 collective-permute-done.3.piece_1
  26.7 0.0 collective-permute-done.2.piece_0
  26.8 0.0 copy-done.2
  26.8 0.0 copy-start
  26.8 0.0 copy-start.1
  26.8 69.0 %conditional.1 = (f32[2,4,128,128]{3,2,1,0:T(8,128)}, f32[2,16,128]{2,1,0:T(8,128)}, f32[2,16,128]{2,1,0:T(8,128)S(1)}, f32[16,1,8192]{2,1,0:T(1,128)}, f32[16,1,8192]{2,1,0:T(1,128)}) conditional(s32[]{:T(128)} %bitcast.12, () %tuple.22, (s32[]{:T(128)}, s32[]{:T(128)}, f32[2,4,128,128]{3,2,1,0:T(8,128)}, f32[2,4,128,128]{3,2,1,0:T(8,128)}, ...), branch_computations={%region_0.1_spmd, %region_1.2_spmd} | conditional | flops 262157 | bytes 12452149 | solution.py:468
  26.8 11.6 %all-to-all-start = ((f32[5248,1,128]{2,1,0:T(1,128)}), f32[5248,1,128]{2,1,0:T(1,128)S(1)}, u32[]{:S(2)}, u32[]{:S(2)}) async-start(f32[5248,1,128]{2,1,0:T(1,128)} %bitcast.20), calls=%async_computation | async-start | bytes 5373952 | tf_op jit(solution)/shard_map/cond/branch_1_fun/all_to_all | solution.py:436
  38.4 2.1 %slice_select_fusion = f32[2,4,128,128]{3,2,1,0:T(8,128)} fusion(f32[2,16,128,128]{3,2,1,0:T(8,128)} %get-tuple-element.26, f32[2,4,128,128]{3,2,1,0:T(8,128)} %get-tuple-element.24, f32[2,4,128,128]{3,2,1,0:T(8,128)} %get-tuple-element.25, pred[]{:T(512)S(6)} %eq.5, pred[]{:T(512)S(6)} %ge.2), kind=kLoop, calls=%fused_computation | loop fusion | flops 262144 | bytes 2097154 | tf_op jit(solution)/shard_map/cond/branch_1_fun/jit(_where)/select_n | solution.py:434
  40.5 0.0 copy-start.4
  40.5 1.0 collective-permute-start
  41.5 42.6 %all-to-all-done = f32[5248,1,128]{2,1,0:T(1,128)S(1)} async-done(((f32[5248,1,128]{2,1,0:T(1,128)}), f32[5248,1,128]{2,1,0:T(1,128)S(1)}, u32[]{:S(2)}, u32[]{:S(2)}) %all-to-all-start) | async-done | bytes 2687008 | tf_op jit(solution)/shard_map/cond/branch_1_fun/all_to_all | solution.py:436
  84.0 3.1 %second_push.1 = (f32[2,16,128]{2,1,0:T(8,128)S(1)}, f32[2,16,128]{2,1,0:T(8,128)S(1)}) custom-call(s32[1]{0:T(128)} %get-tuple-element.27.mine, f32[1024,128]{1,0:T(8,128)} %get-tuple-element.28.phases1, f32[1024,128]{1,0:T(8,128)} %get-tuple-element.29.energies1, f32[5248,128]{1,0:T(8,128)S(1)} %bitcast.18), custom_call_target="tpu_custom_call" | custom-call | tf_op jit(solution)/shard_map/cond/branch_1_fun/second_push/pallas_call | solution.py:438
  87.1 0.4 collective-permute-start.1
  87.5 0.0 copy-done.4
  87.5 5.7 %pick.1 = (f32[1024,128]{1,0:T(8,128)}, f32[1024,128]{1,0:T(8,128)}) custom-call(s32[1]{0:T(128)} %get-tuple-element.27.mine, f32[5248,128]{1,0:T(8,128)S(1)} %bitcast.19, s32[8,1024]{1,0:T(8,128)S(1)} %copy-done.4), custom_call_target="tpu_custom_call" | custom-call | tf_op jit(solution)/shard_map/cond/branch_1_fun/pick/pallas_call | solution.py:448
  93.3 0.0 collective-permute-done
  93.3 2.5 %collective-permute-done.1 = f32[2,16,128]{2,1,0:T(8,128)} collective-permute-done((f32[2,16,128]{2,1,0:T(8,128)S(1)}, f32[2,16,128]{2,1,0:T(8,128)}, u32[]{:S(2)}, u32[]{:S(2)}) %collective-permute-start.1) | collective-permute-done | bytes 16416 | tf_op jit(solution)/shard_map/cond/branch_1_fun/ppermute | solution.py:362
  95.8 0.0 collective-permute-done.6.piece_b2
  95.8 0.0 collective-permute-done.4.piece_b0
  95.8 0.0 collective-permute-done.5.piece_b1
  95.8 0.0 copy-done
  95.8 0.0 copy-done.1
  95.8 0.0 copy-start.3
  95.9 0.9 copy-done.3
  96.8 4.8 %diffract.1 = f32[2,16,128,128]{3,2,1,0:T(8,128)} custom-call(s32[1]{0:T(128)} %bitcast.4.mine, f32[2,4,128,128]{3,2,1,0:T(8,128)} %collective-permute-done.2.piece_0, f32[2,4,128,128]{3,2,1,0:T(8,128)} %collective-permute-done.3.piece_1, f32[2,3,128,128]{3,2,1,0:T(8,128)} %collective-permute-done.4.piece_b0, ...), custom_call_target="tpu_custom_call" | custom-call | tf_op jit(solution)/shard_map/diffract/pallas_call | solution.py:471
Async XLA Ops:
  2.0 24.8 %collective-permute-start.3 = (f32[2,4,128,128]{3,2,1,0:T(8,128)S(1)}, f32[2,4,128,128]{3,2,1,0:T(8,128)}, u32[]{:S(2)}, u32[]{:S(2)}) collective-permute-start(f32[2,4,128,128]{3,2,1,0:T(8,128)S(1)} %get-tuple-element.77), channel_id=1, source_target_pairs={{1,3},{3,5},{5,7},{7,9},{9,11},{11,13},{13,15},{15,17},{17,19},{19... | collective-permute-start | bytes 1572872 | tf_op jit(solution)/shard_map/ppermute | solution.py:395
  3.4 23.3 %collective-permute-start.2 = (f32[2,4,128,128]{3,2,1,0:T(8,128)S(1)}, f32[2,4,128,128]{3,2,1,0:T(8,128)}, u32[]{:S(2)}, u32[]{:S(2)}) collective-permute-start(f32[2,4,128,128]{3,2,1,0:T(8,128)S(1)} %get-tuple-element.78), channel_id=1, source_target_pairs={{0,2},{2,4},{4,6},{6,8},{8,10},{10,12},{12,14},{14,16},{16,18},{18... | collective-permute-start | bytes 1572872 | tf_op jit(solution)/shard_map/ppermute | solution.py:394
  18.0 8.8 %copy-start.2 = (f32[3,128,128]{2,1,0:T(8,128)}, f32[3,128,128]{2,1,0:T(8,128)S(1)}, u32[]{:S(2)}) copy-start(f32[3,128,128]{2,1,0:T(8,128)S(1)} %get-tuple-element.64.beam) | copy-start | bytes 589828
  20.1 75.7 %collective-permute-start.4 = (f32[2,3,128,128]{3,2,1,0:T(8,128)}, f32[2,3,128,128]{3,2,1,0:T(8,128)}, u32[]{:S(2)}, u32[]{:S(2)}) collective-permute-start(f32[2,3,128,128]{3,2,1,0:T(8,128)} %get-tuple-element.54), channel_id=1, source_target_pairs={{0,2},{1,3},{2,4},{3,5},{4,6},{5,7},{6,8},{7,9},{8,10},{9,11},{10,... | collective-permute-start | bytes 1179656 | tf_op jit(solution)/shard_map/ppermute | solution.py:362
  21.6 74.2 %collective-permute-start.5 = (f32[2,3,128,128]{3,2,1,0:T(8,128)}, f32[2,3,128,128]{3,2,1,0:T(8,128)}, u32[]{:S(2)}, u32[]{:S(2)}) collective-permute-start(f32[2,3,128,128]{3,2,1,0:T(8,128)} %get-tuple-element.55), channel_id=1, source_target_pairs={{0,2},{1,3},{2,4},{3,5},{4,6},{5,7},{6,8},{7,9},{8,10},{9,11},{10,... | collective-permute-start | bytes 1179656 | tf_op jit(solution)/shard_map/ppermute | solution.py:362
  24.9 70.9 %collective-permute-start.6 = (f32[2,2,128,128]{3,2,1,0:T(8,128)}, f32[2,2,128,128]{3,2,1,0:T(8,128)}, u32[]{:S(2)}, u32[]{:S(2)}) collective-permute-start(f32[2,2,128,128]{3,2,1,0:T(8,128)} %slice.21), channel_id=1, source_target_pairs={{0,2},{1,3},{2,4},{3,5},{4,6},{5,7},{6,8},{7,9},{8,10},{9,11},{10,... | collective-permute-start | bytes 786440 | tf_op jit(solution)/shard_map/ppermute | solution.py:362
  26.8 69.1 %copy-start = (bf16[768,256]{1,0:T(8,128)(2,1)S(1)}, bf16[768,256]{1,0:T(8,128)(2,1)}, u32[]{:S(2)}) copy-start(bf16[768,256]{1,0:T(8,128)(2,1)} %constant.57.clone.right) | copy-start | bytes 1179652
  26.8 69.1 %copy-start.1 = (bf16[256,768]{1,0:T(8,128)(2,1)S(1)}, bf16[256,768]{1,0:T(8,128)(2,1)}, u32[]{:S(2)}) copy-start(bf16[256,768]{1,0:T(8,128)(2,1)} %constant.56.clone.left) | copy-start | bytes 1179652
  26.8 57.2 %all-to-all-start = ((f32[5248,1,128]{2,1,0:T(1,128)}), f32[5248,1,128]{2,1,0:T(1,128)S(1)}, u32[]{:S(2)}, u32[]{:S(2)}) async-start(f32[5248,1,128]{2,1,0:T(1,128)} %bitcast.20), calls=%async_computation | async-start | bytes 5373952 | tf_op jit(solution)/shard_map/cond/branch_1_fun/all_to_all | solution.py:436
  40.5 47.0 %copy-start.4 = (s32[8,1024]{1,0:T(8,128)S(1)}, s32[8,1024]{1,0:T(8,128)}, u32[]{:S(2)}) copy-start(s32[8,1024]{1,0:T(8,128)} %get-tuple-element.33.places) | copy-start | bytes 98308 | tf_op jit(solution)/shard_map/cond
  40.5 52.7 %collective-permute-start = (f32[2,4,128,128]{3,2,1,0:T(8,128)}, f32[2,4,128,128]{3,2,1,0:T(8,128)}, u32[]{:S(2)}, u32[]{:S(2)}) collective-permute-start(f32[2,4,128,128]{3,2,1,0:T(8,128)} %slice_select_fusion), channel_id=1, source_target_pairs={{0,2},{1,3},{2,4},{3,5},{4,6},{5,7},{6,0},{7,1},{8,10},{9,11},{10,... | collective-permute-start | bytes 1572872 | tf_op jit(solution)/shard_map/cond/branch_1_fun/ppermute | solution.py:435
  87.1 8.7 %collective-permute-start.1 = (f32[2,16,128]{2,1,0:T(8,128)S(1)}, f32[2,16,128]{2,1,0:T(8,128)}, u32[]{:S(2)}, u32[]{:S(2)}) collective-permute-start(f32[2,16,128]{2,1,0:T(8,128)S(1)} %get-tuple-element.31), channel_id=1, source_target_pairs={{0,1},{1,2},{2,3},{3,4},{4,5},{5,6},{6,7},{7,8},{8,9},{9,10},{10,1... | collective-permute-start | bytes 49160 | tf_op jit(solution)/shard_map/cond/branch_1_fun/ppermute | solution.py:362
  95.8 0.9 copy-start.3

commit v5 on v4

--- a/solution.py
+++ b/solution.py
@@ -24,7 +24,7 @@
 CAP = 20
 MESSAGE = 2 * CAP + 1
 ROWS = PEERS * MESSAGE
-BATCH = 16
+BATCH = 32
 VMEM_LIMIT = 24 * 1024 * 1024
 HIGHEST = lax.Precision.HIGHEST
 
@@ -118,7 +118,7 @@
 
 def first_kernel(
     mine, field_hbm, profile_hbm, bins_hbm, jitter_hbm, energy_hbm, delays_hbm, left_hbm, right_hbm,
-    send_hbm, phases_hbm, energies_hbm, places_hbm, beam,
+    send_hbm, phases_hbm, energies_hbm, places_hbm, beam, middle_0, middle_1,
     field, profile, bins, jitter, energy, delays, left, right, acc, send, phases, energies, places, index_v, index, sems,
 ):
     pairs = [
@@ -146,7 +146,12 @@
     beam[2] = p
     copies[4].wait()
     kept = [pltpu.make_async_copy(places, places_hbm, sems.at[8])]
-    kept[0].start()
+    for middle, (low, high) in zip((middle_0, middle_1), MIDDLE):
+        for c in range(2):
+            span = pl.ds(low, high - low)
+            kept.append(pltpu.make_async_copy(field.at[c, span], middle.at[c], sems.at[10 + len(kept)]))
+    for copy in kept:
+        copy.start()
 
     def project(k, carry):
         re, im = field[0, k], field[1, k]
@@ -179,7 +184,7 @@
     lax.fori_loop(0, GROUPS, push, 0)
     kept.append(pltpu.make_async_copy(phases, phases_hbm, sems.at[9]))
     kept.append(pltpu.make_async_copy(energies, energies_hbm, sems.at[10]))
-    for copy in kept[1:]:
+    for copy in kept[5:]:
         copy.start()
     to_scalar.wait()
 
@@ -257,7 +262,7 @@
     return high, (x - high.astype(jnp.float32)).astype(jnp.bfloat16)
 
 
-def pick_kernel(mine, recv, places, phases, energies, index_v, index, amps, sems):
+def pick_kernel(mine, recv, places, phases_hbm, energies_hbm, index_v, index, amps, phases, energies, sems):
     me = mine[0]
     source = (me - places[0:1] + PEERS) % PEERS
     index_v[...] = folded(source * MESSAGE + places[1:2])
@@ -286,20 +291,29 @@
             energies[pl.ds(base + m, 1)] = en[m]
         return carry
 
-    lax.fori_loop(0, COUNT // BATCH, get, 0)
-    for k in range(GROUPS):
-        rows = slice(k * NBS, (k + 1) * NBS)
-        re, im = amps[rows, k : k + 1], amps[rows, GROUPS + k : GROUPS + k + 1]
-        phases[rows], energies[rows] = pushed(phases[rows], energies[rows], re, im)
+    copies = []
+    for quarter in range(4):
+        lax.fori_loop(quarter * COUNT // BATCH // 4, (quarter + 1) * COUNT // BATCH // 4, get, 0)
+        for k in range(quarter * 4, quarter * 4 + 4):
+            rows = slice(k * NBS, (k + 1) * NBS)
+            re, im = amps[rows, k : k + 1], amps[rows, GROUPS + k : GROUPS + k + 1]
+            phases[rows], energies[rows] = pushed(phases[rows], energies[rows], re, im)
+        span = pl.ds(quarter * COUNT // 4, COUNT // 4)
+        copies.append(pltpu.make_async_copy(phases.at[span], phases_hbm.at[span], sems.at[1 + 2 * quarter]))
+        copies.append(pltpu.make_async_copy(energies.at[span], energies_hbm.at[span], sems.at[2 + 2 * quarter]))
+        for copy in copies[-2:]:
+            copy.start()
+    for copy in copies:
+        copy.wait()
 
 
 SLAB = 4
-EARLY, LATE = 4, 12
-MIDDLE = ((4, 7), (7, 10), (10, 12))
+EARLY, LATE = 5, 11
+MIDDLE = ((5, 8), (8, 11))
 
 
 def field_kernel(
-    mine, piece_0, piece_1, piece_b0, piece_b1, piece_b2, piece_c, small, earlier, beam, left, right, out_hbm, acc, out, out_sems
+    mine, piece_0, piece_1, piece_b0, piece_b1, piece_c, small, earlier, beam, left, right, out_hbm, acc, out, out_sems
 ):
     me = mine[0]
 
@@ -308,7 +322,7 @@
             return jnp.zeros((GRID, GRID), jnp.float32)
         if k < EARLY:
             return jnp.where(me % 2 == 0, piece_0[c, k], piece_1[c, k])
-        for piece, (low, high) in zip((piece_b0, piece_b1, piece_b2), MIDDLE):
+        for piece, (low, high) in zip((piece_b0, piece_b1), MIDDLE):
             if low <= k < high:
                 return piece[c, k - low]
         return piece_c[c, k - LATE]
@@ -394,17 +408,18 @@
     shared_0 = lax.ppermute(lax.dynamic_slice_in_dim(field, core * LATE, EARLY, 1), "cuts", early_pairs(0))
     shared_1 = lax.ppermute(lax.dynamic_slice_in_dim(field, (1 - core) * LATE, EARLY, 1), "cuts", early_pairs(1))
     operands = [field, profile, bins, jitter, energies, delays.reshape(GROUPS, 1, NBS), left_one, right_one]
-    send, phases1, energies1, places, beam = pl.pallas_call(
+    send, phases1, energies1, places, beam, *sources = pl.pallas_call(
         first_kernel,
         out_shape=(
             pltpu.HBM((ROWS, BLOCK), jnp.float32),
             pltpu.HBM((COUNT, BLOCK), jnp.float32),
             pltpu.HBM((COUNT, BLOCK), jnp.float32),
             pltpu.HBM((8, COUNT), jnp.int32),
-            shape(3, GRID, GRID),
+            pltpu.HBM((3, GRID, GRID), jnp.float32),
+            *[pltpu.HBM((2, high - low, GRID, GRID), jnp.float32) for low, high in MIDDLE],
         ),
         in_specs=[scalar] + [remain] * 8,
-        out_specs=(remain,) * 4 + (whole(),),
+        out_specs=(remain,) * 4 + (whole(),) + (remain,) * len(MIDDLE),
         scratch_shapes=[
             vmem(2, GROUPS, GRID, GRID),
             vmem(GRID, GRID),
@@ -421,12 +436,11 @@
             vmem(8, COUNT, dtype=jnp.int32),
             vmem(8, 128, dtype=jnp.int32),
             pltpu.SMEM((8, 128), jnp.int32),
-            pltpu.SemaphoreType.DMA((11,)),
+            pltpu.SemaphoreType.DMA((15,)),
         ],
         compiler_params=params,
         name="push_place",
     )(mine, *[in_hbm(value) for value in operands])
-    send, *sources = lax.optimization_barrier((send, *[field[:, low:high] for low, high in MIDDLE]))
     field_b = [shifted(source, "cuts", 2) for source in sources]
 
     def exchange(send, phases1, energies1, places, field, shared_0, shared_1):
@@ -449,12 +463,14 @@
             pick_kernel,
             out_shape=(shape(COUNT, BLOCK), shape(COUNT, BLOCK)),
             in_specs=[scalar] + [whole()] * 2,
-            out_specs=(whole(),) * 2,
+            out_specs=(remain,) * 2,
             scratch_shapes=[
                 vmem(8, 128, dtype=jnp.int32),
                 pltpu.SMEM((8, 128), jnp.int32),
                 vmem(COUNT, 128),
-                pltpu.SemaphoreType.DMA((1,)),
+                vmem(COUNT, BLOCK),
+                vmem(COUNT, BLOCK),
+                pltpu.SemaphoreType.DMA((9,)),
             ],
             compiler_params=params,
             name="pick",
@@ -466,12 +482,12 @@
         return tuple(jnp.zeros(size, jnp.float32) for size in sizes)
 
     phase_out, energy_out, field_c, arrived, earlier = lax.cond(
-        delays[0, 0, 0] < PEERS, exchange, refuse, send, phases1, energies1, places, field, shared_0, shared_1
+        mine[0] < PEERS, exchange, refuse, send, phases1, energies1, places, field, shared_0, shared_1
     )
     out = pl.pallas_call(
         field_kernel,
         out_shape=shape(2, GROUPS, GRID, GRID),
-        in_specs=[scalar] + [whole()] * 11,
+        in_specs=[scalar] + [whole()] * 10,
         out_specs=remain,
         scratch_shapes=[
             vmem(4, GROUPS, 128),

time: 103 us -> 94.3 us (0.916)
  starting transfers between devices: 22.7 us -> 15.3 us
  waiting for transfers between devices: 45.1 us -> 49.6 us
  local copies, waits for them, and re-layouts: 7.26 us -> 3.15 us
    ppermute x1, waiting for transfers between devices: 0.01 us -> 8.03 us  [per_device(): lax.ppermute(lax.dynamic_slice_in_dim(field, core * LATE, EARLY, 1), 'cut...]
    all_to_all x1, starting transfers between devices: 11.6 us -> 4.79 us  [exchange(): lax.all_to_all(send.reshape(ROWS, 1, BLOCK), 'cuts', split_axis=0, concat...]
    slice x3 -> x0, local copies, waits for them, and re-layouts: 5.01 us -> none  [the longest x2 3.84 us: per_device(): field[:, low:high]]
    all_to_all x1, waiting for transfers between devices: 42.6 us -> 38.1 us  [exchange(): lax.all_to_all(send.reshape(ROWS, 1, BLOCK), 'cuts', split_axis=0, concat...]
    ppermute x4 -> x3, waiting for transfers between devices: 2.55 us -> 3.45 us  [shifted(): return lax.ppermute(value, axis, pairs)]
    ppermute x4 -> x3, starting transfers between devices: 5.19 us -> 5.54 us  [shifted(): return lax.ppermute(value, axis, pairs)]
  transfers between devices with their start and end apart: 8 -> 7, of which waited for: 2 -> 3; matrix products, arithmetic and copies ran while one was open for 7% -> 2% of each run, Pallas kernels for 18% -> 19%
where the time goes in v5:
time: 94.3 us; the launch traced here: 93.9 us
  waiting for transfers between devices  49.6 us (53%)
  Pallas kernels  22.8 us (24%)
  starting transfers between devices  15.3 us (16%)
  local copies, waits for them, and re-layouts  3.15 us (3%)
  other arithmetic  2.23 us (2%)
    all_to_all x1, waiting for transfers between devices, exchange(): lax.all_to_all(send.reshape(ROWS, 1, BLOCK), 'cuts', split_axis=0, concat...  38.1 us
    pallas_call x1, Pallas kernels, per_device(): pl.pallas_call(first_kernel, out_shape=(pltpu.HBM((ROWS, BLOCK), jnp.floa...  9.67 us
    ppermute x1, waiting for transfers between devices, per_device(): lax.ppermute(lax.dynamic_slice_in_dim(field, core * LATE, EARLY, 1), 'cut...  8.03 us
    ppermute x3, starting transfers between devices, shifted(): return lax.ppermute(value, axis, pairs)  5.54 us
    pallas_call x1, Pallas kernels, exchange(): pl.pallas_call(pick_kernel, out_shape=(shape(COUNT, BLOCK), shape(COUNT,...  5.22 us
    pallas_call x1, Pallas kernels, per_device(): pl.pallas_call(field_kernel, out_shape=shape(2, GROUPS, GRID, GRID), in_s...  4.88 us
    all_to_all x1, starting transfers between devices, exchange(): lax.all_to_all(send.reshape(ROWS, 1, BLOCK), 'cuts', split_axis=0, concat...  4.79 us
    ppermute x1, starting transfers between devices, per_device(): lax.ppermute(lax.dynamic_slice_in_dim(field, core * LATE, EARLY, 1), 'cut...  3.48 us
  transfers between devices with their start and end apart: 7, of which 3 were waited for; matrix products, arithmetic and copies ran while one was open for 2% of the time, Pallas kernels for 19%

profile of v5, /device:TPU:0, one launch (start us, length us, event | category | flops | bytes accessed | tf_op | source)
XLA Modules:
  0.0 93.9 jit_solution(8387435685052744509)
XLA Ops:
  0.7 1.4 %dynamic-slice_bitcast_fusion = (f32[2,5,128,128]{3,2,1,0:T(8,128)S(1)}, f32[2,5,128,128]{3,2,1,0:T(8,128)S(1)}) fusion(f32[2,16,1,128,128]{4,3,2,1,0:T(8,128)} %param.12, s32[]{:T(128)S(6)} %select_n.33, s32[]{:T(128)S(6)} %select_n.32), kind=kLoop, calls=%fused_computation.1 | loop fusion | bytes 2621448 | tf_op jit(solution)/shard_map/dynamic_slice | solution.py:409
  2.0 0.7 collective-permute-start.3
  2.8 3.5 %collective-permute-start.2 = (f32[2,5,128,128]{3,2,1,0:T(8,128)S(1)}, f32[2,5,128,128]{3,2,1,0:T(8,128)S(1)}, u32[]{:S(2)}, u32[]{:S(2)}) collective-permute-start(f32[2,5,128,128]{3,2,1,0:T(8,128)S(1)} %get-tuple-element.72), channel_id=1, source_target_pairs={{0,2},{2,4},{4,6},{6,8},{8,10},{10,12},{12,14},{14,16},{16,18},{18... | collective-permute-start | bytes 1966088 | tf_op jit(solution)/shard_map/ppermute | solution.py:408
  6.2 9.7 %push_place.1 = (f32[5248,128]{1,0:T(8,128)}, f32[1024,128]{1,0:T(8,128)}, f32[1024,128]{1,0:T(8,128)}, s32[8,1024]{1,0:T(8,128)}, f32[3,128,128]{2,1,0:T(8,128)...) custom-call(s32[1]{0:T(128)} %bitcast.4.mine, f32[2,16,128,128]{3,2,1,0:T(8,128)} %bitcast.19, ...), custom_call_target="tpu_custom_call" | custom-call | tf_op jit(solution)/shard_map/push_place/pallas_call | solution.py:411
  15.9 1.6 %collective-permute-start.4 = (f32[2,3,128,128]{3,2,1,0:T(8,128)}, f32[2,3,128,128]{3,2,1,0:T(8,128)}, u32[]{:S(2)}, u32[]{:S(2)}) collective-permute-start(f32[2,3,128,128]{3,2,1,0:T(8,128)} %get-tuple-element.51), channel_id=1, source_target_pairs={{0,2},{1,3},{2,4},{3,5},{4,6},{5,7},{6,8},{7,9},{8,10},{9,11},{10,... | collective-permute-start | bytes 1179656 | tf_op jit(solution)/shard_map/ppermute | solution.py:376
  17.5 4.0 %collective-permute-start.5 = (f32[2,3,128,128]{3,2,1,0:T(8,128)}, f32[2,3,128,128]{3,2,1,0:T(8,128)}, u32[]{:S(2)}, u32[]{:S(2)}) collective-permute-start(f32[2,3,128,128]{3,2,1,0:T(8,128)} %get-tuple-element.52), channel_id=1, source_target_pairs={{0,2},{1,3},{2,4},{3,5},{4,6},{5,7},{6,8},{7,9},{8,10},{9,11},{10,... | collective-permute-start | bytes 1179656 | tf_op jit(solution)/shard_map/ppermute | solution.py:376
  21.5 0.0 collective-permute-done.3.piece_1
  21.5 0.0 copy-start.3
  21.5 8.0 %collective-permute-done.2.piece_0 = f32[2,5,128,128]{3,2,1,0:T(8,128)S(1)} collective-permute-done((f32[2,5,128,128]{3,2,1,0:T(8,128)S(1)}, f32[2,5,128,128]{3,2,1,0:T(8,128)S(1)}, u32[]{:S(2)}, u32[]{:S(2)}) %collective-permute-start.2) | collective-permute-done | bytes 655392 | tf_op jit(solution)/shard_map/ppermute | solution.py:408
  29.5 0.0 copy-start.4
  29.5 0.0 copy-done.3
  29.5 0.8 copy-done.4
  30.3 0.0 copy-start
  30.3 0.0 copy-start.1
  30.3 57.7 %conditional.1 = (f32[2,5,128,128]{3,2,1,0:T(8,128)}, f32[2,16,128]{2,1,0:T(8,128)}, f32[2,16,128]{2,1,0:T(8,128)S(1)}, f32[16,1,8192]{2,1,0:T(1,128)}, f32[16,1,8192]{2,1,0:T(1,128)}) conditional(s32[]{:T(128)} %convert_element_type.3, () %tuple.20, (s32[]{:T(128)}, s32[]{:T(128)}, f32[2,5,128,128]{3,2,1,0:T(8,128)}, f32[2,5,128,128]{3,2,1,0:T(8,128)}, ...), branch_computations={%region_0.1_spmd, %region_1.2_spmd} | conditional | flops 327693 | bytes 13500725 | solution.py:484
  30.3 4.8 %all-to-all-start = ((f32[5248,1,128]{2,1,0:T(1,128)}), f32[5248,1,128]{2,1,0:T(1,128)S(1)}, u32[]{:S(2)}, u32[]{:S(2)}) async-start(f32[5248,1,128]{2,1,0:T(1,128)} %bitcast.21), calls=%async_computation | async-start | bytes 5373952 | tf_op jit(solution)/shard_map/cond/branch_1_fun/all_to_all | solution.py:450
  35.2 2.2 %slice_select_fusion = f32[2,5,128,128]{3,2,1,0:T(8,128)} fusion(f32[2,16,128,128]{3,2,1,0:T(8,128)} %get-tuple-element.26, f32[2,5,128,128]{3,2,1,0:T(8,128)} %get-tuple-element.24, f32[2,5,128,128]{3,2,1,0:T(8,128)} %get-tuple-element.25, pred[]{:T(512)S(6)} %eq.5, pred[]{:T(512)S(6)} %ge.2), kind=kLoop, calls=%fused_computation | loop fusion | flops 327680 | bytes 2621442 | tf_op jit(solution)/shard_map/cond/branch_1_fun/jit(_where)/select_n | solution.py:448
  37.4 0.0 copy-start.5
  37.4 0.8 collective-permute-start
  38.2 38.1 %all-to-all-done = f32[5248,1,128]{2,1,0:T(1,128)S(1)} async-done(((f32[5248,1,128]{2,1,0:T(1,128)}), f32[5248,1,128]{2,1,0:T(1,128)S(1)}, u32[]{:S(2)}, u32[]{:S(2)}) %all-to-all-start) | async-done | bytes 2687008 | tf_op jit(solution)/shard_map/cond/branch_1_fun/all_to_all | solution.py:450
  76.3 3.1 %second_push.1 = (f32[2,16,128]{2,1,0:T(8,128)S(1)}, f32[2,16,128]{2,1,0:T(8,128)S(1)}) custom-call(s32[1]{0:T(128)} %get-tuple-element.27.mine, f32[1024,128]{1,0:T(8,128)} %get-tuple-element.28.phases1, f32[1024,128]{1,0:T(8,128)} %get-tuple-element.29.energies1, f32[5248,128]{1,0:T(8,128)S(1)} %bitcast.17), custom_call_target="tpu_custom_call" | custom-call | tf_op jit(solution)/shard_map/cond/branch_1_fun/second_push/pallas_call | solution.py:452
  79.4 0.0 collective-permute-start.1
  79.4 0.0 copy-done.5
  79.4 5.2 %pick.1 = (f32[1024,128]{1,0:T(8,128)}, f32[1024,128]{1,0:T(8,128)}) custom-call(s32[1]{0:T(128)} %get-tuple-element.27.mine, f32[5248,128]{1,0:T(8,128)S(1)} %bitcast.18, s32[8,1024]{1,0:T(8,128)S(1)} %copy-done.5), custom_call_target="tpu_custom_call" | custom-call | tf_op jit(solution)/shard_map/cond/branch_1_fun/pick/pallas_call | solution.py:462
  84.6 0.0 collective-permute-done
  84.6 3.4 %collective-permute-done.1 = f32[2,16,128]{2,1,0:T(8,128)} collective-permute-done((f32[2,16,128]{2,1,0:T(8,128)S(1)}, f32[2,16,128]{2,1,0:T(8,128)}, u32[]{:S(2)}, u32[]{:S(2)}) %collective-permute-start.1) | collective-permute-done | bytes 16416 | tf_op jit(solution)/shard_map/cond/branch_1_fun/ppermute | solution.py:376
  88.1 0.0 collective-permute-done.4.piece_b0
  88.1 0.0 collective-permute-done.5.piece_b1
  88.1 0.0 copy-done
  88.1 0.0 copy-done.1
  88.1 0.0 copy-start.2
  88.1 0.9 copy-done.2
  89.0 4.9 %diffract.1 = f32[2,16,128,128]{3,2,1,0:T(8,128)} custom-call(s32[1]{0:T(128)} %bitcast.4.mine, f32[2,5,128,128]{3,2,1,0:T(8,128)} %copy-done.4, f32[2,5,128,128]{3,2,1,0:T(8,128)} %copy-done.3, f32[2,3,128,128]{3,2,1,0:T(8,128)} %collective-permute-done.4.piece_b0, f32[2,3,128,128]{3,2,1,0:T(8,128)} %collective-permute-done.5.piece_b1, ...), custom_call_target="tpu_custom_call" | custom-call | tf_op jit(solution)/shard_map/diffract/pallas_call | solution.py:487
Async XLA Ops:
  2.0 19.4 %collective-permute-start.3 = (f32[2,5,128,128]{3,2,1,0:T(8,128)S(1)}, f32[2,5,128,128]{3,2,1,0:T(8,128)S(1)}, u32[]{:S(2)}, u32[]{:S(2)}) collective-permute-start(f32[2,5,128,128]{3,2,1,0:T(8,128)S(1)} %get-tuple-element.71), channel_id=1, source_target_pairs={{1,3},{3,5},{5,7},{7,9},{9,11},{11,13},{13,15},{15,17},{17,19},{19... | collective-permute-start | bytes 1966088 | tf_op jit(solution)/shard_map/ppermute | solution.py:409
  2.8 26.8 %collective-permute-start.2 = (f32[2,5,128,128]{3,2,1,0:T(8,128)S(1)}, f32[2,5,128,128]{3,2,1,0:T(8,128)S(1)}, u32[]{:S(2)}, u32[]{:S(2)}) collective-permute-start(f32[2,5,128,128]{3,2,1,0:T(8,128)S(1)} %get-tuple-element.72), channel_id=1, source_target_pairs={{0,2},{2,4},{4,6},{6,8},{8,10},{10,12},{12,14},{14,16},{16,18},{18... | collective-permute-start | bytes 1966088 | tf_op jit(solution)/shard_map/ppermute | solution.py:408
  15.9 72.2 %collective-permute-start.4 = (f32[2,3,128,128]{3,2,1,0:T(8,128)}, f32[2,3,128,128]{3,2,1,0:T(8,128)}, u32[]{:S(2)}, u32[]{:S(2)}) collective-permute-start(f32[2,3,128,128]{3,2,1,0:T(8,128)} %get-tuple-element.51), channel_id=1, source_target_pairs={{0,2},{1,3},{2,4},{3,5},{4,6},{5,7},{6,8},{7,9},{8,10},{9,11},{10,... | collective-permute-start | bytes 1179656 | tf_op jit(solution)/shard_map/ppermute | solution.py:376
  17.5 70.6 %collective-permute-start.5 = (f32[2,3,128,128]{3,2,1,0:T(8,128)}, f32[2,3,128,128]{3,2,1,0:T(8,128)}, u32[]{:S(2)}, u32[]{:S(2)}) collective-permute-start(f32[2,3,128,128]{3,2,1,0:T(8,128)} %get-tuple-element.52), channel_id=1, source_target_pairs={{0,2},{1,3},{2,4},{3,5},{4,6},{5,7},{6,8},{7,9},{8,10},{9,11},{10,... | collective-permute-start | bytes 1179656 | tf_op jit(solution)/shard_map/ppermute | solution.py:376
  21.5 8.0 %copy-start.3 = (f32[2,5,128,128]{3,2,1,0:T(8,128)}, f32[2,5,128,128]{3,2,1,0:T(8,128)S(1)}, u32[]{:S(2)}) copy-start(f32[2,5,128,128]{3,2,1,0:T(8,128)S(1)} %collective-permute-done.3.piece_1) | copy-start | bytes 1966084
  29.5 0.8 copy-start.4
  30.3 57.8 %copy-start = (bf16[768,256]{1,0:T(8,128)(2,1)S(1)}, bf16[768,256]{1,0:T(8,128)(2,1)}, u32[]{:S(2)}) copy-start(bf16[768,256]{1,0:T(8,128)(2,1)} %constant.56.clone.right) | copy-start | bytes 1179652
  30.3 57.8 %copy-start.1 = (bf16[256,768]{1,0:T(8,128)(2,1)S(1)}, bf16[256,768]{1,0:T(8,128)(2,1)}, u32[]{:S(2)}) copy-start(bf16[256,768]{1,0:T(8,128)(2,1)} %constant.55.clone.left) | copy-start | bytes 1179652
  30.3 46.0 %all-to-all-start = ((f32[5248,1,128]{2,1,0:T(1,128)}), f32[5248,1,128]{2,1,0:T(1,128)S(1)}, u32[]{:S(2)}, u32[]{:S(2)}) async-start(f32[5248,1,128]{2,1,0:T(1,128)} %bitcast.21), calls=%async_computation | async-start | bytes 5373952 | tf_op jit(solution)/shard_map/cond/branch_1_fun/all_to_all | solution.py:450
  37.4 42.0 %copy-start.5 = (s32[8,1024]{1,0:T(8,128)S(1)}, s32[8,1024]{1,0:T(8,128)}, u32[]{:S(2)}) copy-start(s32[8,1024]{1,0:T(8,128)} %get-tuple-element.33.places) | copy-start | bytes 98308 | tf_op jit(solution)/shard_map/cond
  37.4 47.2 %collective-permute-start = (f32[2,5,128,128]{3,2,1,0:T(8,128)}, f32[2,5,128,128]{3,2,1,0:T(8,128)}, u32[]{:S(2)}, u32[]{:S(2)}) collective-permute-start(f32[2,5,128,128]{3,2,1,0:T(8,128)} %slice_select_fusion), channel_id=1, source_target_pairs={{0,2},{1,3},{2,4},{3,5},{4,6},{5,7},{6,0},{7,1},{8,10},{9,11},{10,... | collective-permute-start | bytes 1966088 | tf_op jit(solution)/shard_map/cond/branch_1_fun/ppermute | solution.py:449
  79.4 8.7 %collective-permute-start.1 = (f32[2,16,128]{2,1,0:T(8,128)S(1)}, f32[2,16,128]{2,1,0:T(8,128)}, u32[]{:S(2)}, u32[]{:S(2)}) collective-permute-start(f32[2,16,128]{2,1,0:T(8,128)S(1)} %get-tuple-element.31), channel_id=1, source_target_pairs={{0,1},{1,2},{2,3},{3,4},{4,5},{5,6},{6,7},{7,8},{8,9},{9,10},{10,1... | collective-permute-start | bytes 49160 | tf_op jit(solution)/shard_map/cond/branch_1_fun/ppermute | solution.py:376
  88.1 0.9 copy-start.2

commit v6 on v5

--- a/solution.py
+++ b/solution.py
@@ -25,6 +25,8 @@
 MESSAGE = 2 * CAP + 1
 ROWS = PEERS * MESSAGE
 BATCH = 32
+EARLY, LATE = 5, 11
+MIDDLE = ((5, 8), (8, 11))
 VMEM_LIMIT = 24 * 1024 * 1024
 HIGHEST = lax.Precision.HIGHEST
 
@@ -307,55 +309,67 @@
         copy.wait()
 
 
-SLAB = 4
-EARLY, LATE = 5, 11
-MIDDLE = ((5, 8), (8, 11))
-
-
-def field_kernel(
-    mine, piece_0, piece_1, piece_b0, piece_b1, piece_c, small, earlier, beam, left, right, out_hbm, acc, out, out_sems
-):
+def twice_diffracted(planes, left, right):
+    hi, lo = wide_halves(jnp.concatenate([jnp.concatenate(pair, axis=1) for pair in planes], axis=0))
+    half = jnp.dot(jnp.concatenate([hi, lo, hi], axis=1), right[...], preferred_element_type=jnp.float32)
+    cols = []
+    for m in range(len(planes)):
+        mid = half[m * GRID : (m + 1) * GRID]
+        cols.append(jnp.concatenate([mid[:, :GRID], mid[:, GRID:]], axis=0))
+    hi, lo = wide_halves(jnp.concatenate(cols, axis=1))
+    full = jnp.dot(left[...], jnp.concatenate([hi, lo, hi], axis=0), preferred_element_type=jnp.float32)
+    cuts = [slice(m * GRID, (m + 1) * GRID) for m in range(len(planes))]
+    return [(full[:GRID, cut], full[GRID:, cut]) for cut in cuts]
+
+
+def early_kernel(mine, piece_0, piece_1, beam, left, right, out):
+    even = mine[0] % 2 == 0
+    planes = [tuple(jnp.where(even, piece_0[c, k], piece_1[c, k]) for c in range(2)) for k in range(EARLY)]
+    planes.append((beam[2], jnp.zeros((GRID, GRID), jnp.float32)))
+    for k, (re, im) in enumerate(twice_diffracted(planes, left, right)):
+        out[0, k] = re
+        out[1, k] = im
+
+
+def late_kernel(piece, left, right, out):
+    planes = [(piece[0, k], piece[1, k]) for k in range(piece.shape[1])]
+    for k, (re, im) in enumerate(twice_diffracted(planes, left, right)):
+        out[0, k] = re
+        out[1, k] = im
+
+
+def last_kernel(mine, early, piece_b0, piece_b1, late, small, earlier, beam, left, right, out_hbm, acc, middle, out, sems):
     me = mine[0]
+    for n in range(2):
+        acc[n] = GAIN * carried(small[n], me == 0)
+        acc[2 + n] = GAIN * earlier[n]
+    copies = []
 
     def plane(c, k):
         if k < 0:
             return jnp.zeros((GRID, GRID), jnp.float32)
         if k < EARLY:
-            return jnp.where(me % 2 == 0, piece_0[c, k], piece_1[c, k])
-        for piece, (low, high) in zip((piece_b0, piece_b1), MIDDLE):
-            if low <= k < high:
-                return piece[c, k - low]
-        return piece_c[c, k - LATE]
-
-    for n in range(2):
-        acc[n] = GAIN * carried(small[n], me == 0)
-        acc[2 + n] = GAIN * earlier[n]
-    late = me < 2
-    p = beam[2]
-    dr, di = beam[0], beam[1]
-    copies = []
-    for slab in range(GROUPS // SLAB):
-        ks = range(slab * SLAB, (slab + 1) * SLAB)
-        rows = []
-        for k in ks:
-            parts = [jnp.where(late, plane(c, k - 1), plane(c, k)) + acc[2 + c, k : k + 1] * p for c in range(2)]
-            rows.append(jnp.concatenate(parts, axis=1))
-        hi, lo = wide_halves(jnp.concatenate(rows, axis=0))
-        half = jnp.dot(jnp.concatenate([hi, lo, hi], axis=1), right[...], preferred_element_type=jnp.float32)
-        cols = []
-        for m in range(SLAB):
-            mid = half[m * GRID : (m + 1) * GRID]
-            cols.append(jnp.concatenate([mid[:, :GRID], mid[:, GRID:]], axis=0))
-        hi, lo = wide_halves(jnp.concatenate(cols, axis=1))
-        full = jnp.dot(left[...], jnp.concatenate([hi, lo, hi], axis=0), preferred_element_type=jnp.float32)
-        for m, k in enumerate(ks):
-            cr, ci = acc[0, k : k + 1], acc[1, k : k + 1]
-            out[0, k] = full[:GRID, m * GRID : (m + 1) * GRID] + (cr * dr - ci * di)
-            out[1, k] = full[GRID:, m * GRID : (m + 1) * GRID] + (cr * di + ci * dr)
+            return early[c, k]
+        return middle[c, k - EARLY] if k < LATE else late[c, k - LATE]
+
+    def finish(low, high):
+        for k in range(low, high):
+            cr, ci, br, bi = (acc[n, k : k + 1] for n in range(4))
+            re, im = (jnp.where(me < 2, plane(c, k - 1), plane(c, k)) for c in range(2))
+            out[0, k] = re + (br * early[0, EARLY] - bi * early[1, EARLY]) + (cr * beam[0] - ci * beam[1])
+            out[1, k] = im + (br * early[1, EARLY] + bi * early[0, EARLY]) + (cr * beam[1] + ci * beam[0])
+        span = pl.ds(low, high - low)
         for c in range(2):
-            span = pl.ds(slab * SLAB, SLAB)
-            copies.append(pltpu.make_async_copy(out.at[c, span], out_hbm.at[c, span], out_sems.at[2 * slab + c]))
+            copies.append(pltpu.make_async_copy(out.at[c, span], out_hbm.at[c, span], sems.at[len(copies)]))
             copies[-1].start()
+
+    finish(0, EARLY)
+    planes = [(piece[0, k], piece[1, k]) for piece in (piece_b0, piece_b1) for k in range(piece.shape[1])]
+    for k, (re, im) in enumerate(twice_diffracted(planes, left, right)):
+        middle[0, k] = re
+        middle[1, k] = im
+    finish(EARLY, LATE)
+    finish(LATE, GROUPS)
     for copy in copies:
         copy.wait()
 
@@ -443,10 +457,28 @@
     )(mine, *[in_hbm(value) for value in operands])
     field_b = [shifted(source, "cuts", 2) for source in sources]
 
-    def exchange(send, phases1, energies1, places, field, shared_0, shared_1):
+    left_two, right_two = deep_left(left_form(*two)), deep_right(right_form(*two))
+
+    def exchange(send, phases1, energies1, places, field, shared_0, shared_1, beam):
+        early = pl.pallas_call(
+            early_kernel,
+            out_shape=shape(2, EARLY + 1, GRID, GRID),
+            in_specs=[scalar] + [whole()] * 5,
+            out_specs=whole(),
+            compiler_params=params,
+            name="early_field",
+        )(mine, shared_0, shared_1, beam, left_two, right_two)
         handed = jnp.where(core == 0, shared_1, shared_0)
         source_c = jnp.where(mine[0] % 8 >= 6, handed, field[:, LATE:])
         field_c = lax.ppermute(source_c, "cuts", late_pairs())
+        late = pl.pallas_call(
+            late_kernel,
+            out_shape=shape(2, GROUPS - LATE, GRID, GRID),
+            in_specs=[whole()] * 3,
+            out_specs=whole(),
+            compiler_params=params,
+            name="late_field",
+        )(field_c, left_two, right_two)
         recv = lax.all_to_all(send.reshape(ROWS, 1, BLOCK), "cuts", split_axis=0, concat_axis=0, tiled=True)
         recv = recv.reshape(ROWS, BLOCK)
         small, earlier = pl.pallas_call(
@@ -475,39 +507,29 @@
             compiler_params=params,
             name="pick",
         )(mine, recv, places)
-        return phase_out, energy_out, field_c, arrived, earlier
+        return phase_out, energy_out, early, late, arrived, earlier
 
     def refuse(*operands):
-        sizes = [(COUNT, BLOCK)] * 2 + [(2, GROUPS - LATE, GRID, GRID)] + [(2, GROUPS, 128)] * 2
+        sizes = [(COUNT, BLOCK)] * 2 + [(2, n, GRID, GRID) for n in (EARLY + 1, GROUPS - LATE)] + [(2, GROUPS, 128)] * 2
         return tuple(jnp.zeros(size, jnp.float32) for size in sizes)
 
-    phase_out, energy_out, field_c, arrived, earlier = lax.cond(
-        mine[0] < PEERS, exchange, refuse, send, phases1, energies1, places, field, shared_0, shared_1
+    phase_out, energy_out, early, late, arrived, earlier = lax.cond(
+        mine[0] < PEERS, exchange, refuse, send, phases1, energies1, places, field, shared_0, shared_1, beam
     )
     out = pl.pallas_call(
-        field_kernel,
+        last_kernel,
         out_shape=shape(2, GROUPS, GRID, GRID),
-        in_specs=[scalar] + [whole()] * 10,
+        in_specs=[scalar] + [whole()] * 9,
         out_specs=remain,
         scratch_shapes=[
             vmem(4, GROUPS, 128),
+            vmem(2, LATE - EARLY, GRID, GRID),
             vmem(2, GROUPS, GRID, GRID),
-            pltpu.SemaphoreType.DMA((2 * GROUPS // SLAB,)),
+            pltpu.SemaphoreType.DMA((6,)),
         ],
         compiler_params=params,
-        name="diffract",
-    )(
-        mine,
-        shared_0,
-        shared_1,
-        *field_b,
-        field_c,
-        arrived,
-        earlier,
-        beam,
-        deep_left(left_form(*two)),
-        deep_right(right_form(*two)),
-    )
+        name="last_field",
+    )(mine, early, *field_b, late, arrived, earlier, in_hbm(beam), left_two, right_two)
     return (
         out.reshape(2, GROUPS, 1, GRID, GRID),
         phase_out.reshape(GROUPS, 1, NBS * BLOCK),

time: 94.3 us -> 95.6 us (1.014)
  Pallas kernels: 22.8 us -> 27.1 us
  waiting for transfers between devices: 49.6 us -> 46.9 us
    pallas_call x1 -> x3, Pallas kernels: 4.88 us -> 8.95 us  [the longest x1 4.6 us: per_device(): pl.pallas_call(last_kernel, out_shape=shape(2, GROUPS, GRID, GRID), in_sp...]
    ppermute x3, waiting for transfers between devices: 3.45 us -> 0.01 us  [shifted(): return lax.ppermute(value, axis, pairs)]
    unnamed x10 -> x0, local copies, waits for them, and re-layouts: 1.76 us -> none
  transfers between devices with their start and end apart: 7 -> 7, of which waited for: 3 -> 3; matrix products, arithmetic and copies ran while one was open for 2% -> 2% of each run, Pallas kernels for 19% -> 24%
where the time goes in v6:
time: 95.6 us; the launch traced here: 94.4 us
  waiting for transfers between devices  46.9 us (49%)
  Pallas kernels  27.1 us (28%)
  starting transfers between devices  15.2 us (16%)
  local copies, waits for them, and re-layouts  2.24 us (2%)
  other arithmetic  2.04 us (2%)
    all_to_all x1, waiting for transfers between devices, exchange(): lax.all_to_all(send.reshape(ROWS, 1, BLOCK), 'cuts', split_axis=0, concat...  38.4 us
    pallas_call x1, Pallas kernels, per_device(): pl.pallas_call(first_kernel, out_shape=(pltpu.HBM((ROWS, BLOCK), jnp.floa...  9.75 us
    ppermute x1, waiting for transfers between devices, per_device(): lax.ppermute(lax.dynamic_slice_in_dim(field, core * LATE, EARLY, 1), 'cut...  7.88 us
    ppermute x3, starting transfers between devices, shifted(): return lax.ppermute(value, axis, pairs)  5.54 us
    pallas_call x1, Pallas kernels, exchange(): pl.pallas_call(pick_kernel, out_shape=(shape(COUNT, BLOCK), shape(COUNT,...  5.22 us
    all_to_all x1, starting transfers between devices, exchange(): lax.all_to_all(send.reshape(ROWS, 1, BLOCK), 'cuts', split_axis=0, concat...  4.66 us
    pallas_call x1, Pallas kernels, per_device(): pl.pallas_call(last_kernel, out_shape=shape(2, GROUPS, GRID, GRID), in_sp...  4.6 us
    ppermute x1, starting transfers between devices, per_device(): lax.ppermute(lax.dynamic_slice_in_dim(field, core * LATE, EARLY, 1), 'cut...  3.48 us
  transfers between devices with their start and end apart: 7, of which 3 were waited for; matrix products, arithmetic and copies ran while one was open for 2% of the time, Pallas kernels for 24%

profile of v6, /device:TPU:0, one launch (start us, length us, event | category | flops | bytes accessed | tf_op | source)
XLA Modules:
  0.0 94.4 jit_solution(17273521219181313064)
XLA Ops:
  0.7 1.4 %dynamic-slice_bitcast_fusion = (f32[2,5,128,128]{3,2,1,0:T(8,128)S(1)}, f32[2,5,128,128]{3,2,1,0:T(8,128)S(1)}) fusion(f32[2,16,1,128,128]{4,3,2,1,0:T(8,128)} %param.12, s32[]{:T(128)S(6)} %select_n.33, s32[]{:T(128)S(6)} %select_n.32), kind=kLoop, calls=%fused_computation.1 | loop fusion | bytes 2621448 | tf_op jit(solution)/shard_map/dynamic_slice | solution.py:423
  2.0 0.7 collective-permute-start.3
  2.8 3.5 %collective-permute-start.2 = (f32[2,5,128,128]{3,2,1,0:T(8,128)S(1)}, f32[2,5,128,128]{3,2,1,0:T(8,128)S(1)}, u32[]{:S(2)}, u32[]{:S(2)}) collective-permute-start(f32[2,5,128,128]{3,2,1,0:T(8,128)S(1)} %get-tuple-element.83), channel_id=1, source_target_pairs={{0,2},{2,4},{4,6},{6,8},{8,10},{10,12},{12,14},{14,16},{16,18},{18... | collective-permute-start | bytes 1966088 | tf_op jit(solution)/shard_map/ppermute | solution.py:422
  6.2 9.8 %push_place.1 = (f32[5248,128]{1,0:T(8,128)}, f32[1024,128]{1,0:T(8,128)}, f32[1024,128]{1,0:T(8,128)}, s32[8,1024]{1,0:T(8,128)}, f32[3,128,128]{2,1,0:T(8,128)...) custom-call(s32[1]{0:T(128)} %bitcast.4.mine, f32[2,16,128,128]{3,2,1,0:T(8,128)} %bitcast.19, ...), custom_call_target="tpu_custom_call" | custom-call | tf_op jit(solution)/shard_map/push_place/pallas_call | solution.py:425
  16.0 1.6 %collective-permute-start.4 = (f32[2,3,128,128]{3,2,1,0:T(8,128)}, f32[2,3,128,128]{3,2,1,0:T(8,128)}, u32[]{:S(2)}, u32[]{:S(2)}) collective-permute-start(f32[2,3,128,128]{3,2,1,0:T(8,128)} %get-tuple-element.67), channel_id=1, source_target_pairs={{0,2},{1,3},{2,4},{3,5},{4,6},{5,7},{6,8},{7,9},{8,10},{9,11},{10,... | collective-permute-start | bytes 1179656 | tf_op jit(solution)/shard_map/ppermute | solution.py:390
  17.6 4.0 %collective-permute-start.5 = (f32[2,3,128,128]{3,2,1,0:T(8,128)}, f32[2,3,128,128]{3,2,1,0:T(8,128)}, u32[]{:S(2)}, u32[]{:S(2)}) collective-permute-start(f32[2,3,128,128]{3,2,1,0:T(8,128)} %get-tuple-element.68), channel_id=1, source_target_pairs={{0,2},{1,3},{2,4},{3,5},{4,6},{5,7},{6,8},{7,9},{8,10},{9,11},{10,... | collective-permute-start | bytes 1179656 | tf_op jit(solution)/shard_map/ppermute | solution.py:390
  21.5 0.0 collective-permute-done.3
  21.5 7.9 %collective-permute-done.2 = f32[2,5,128,128]{3,2,1,0:T(8,128)S(1)} collective-permute-done((f32[2,5,128,128]{3,2,1,0:T(8,128)S(1)}, f32[2,5,128,128]{3,2,1,0:T(8,128)S(1)}, u32[]{:S(2)}, u32[]{:S(2)}) %collective-permute-start.2) | collective-permute-done | bytes 655392 | tf_op jit(solution)/shard_map/ppermute | solution.py:422
  29.4 60.3 %conditional.1 = (f32[2,6,128,128]{3,2,1,0:T(8,128)}, f32[2,5,128,128]{3,2,1,0:T(8,128)}, f32[2,16,128]{2,1,0:T(8,128)}, f32[2,16,128]{2,1,0:T(8,128)S(1)}, f32[...) conditional(s32[]{:T(128)} %convert_element_type.3, () %tuple.20, (s32[1]{0:T(128)}, f32[2,5,128,128]{3,2,1,0:T(8,128)S(1)}, ...), branch_computations={%region_0.1_spmd, %region_1.2_spmd} | conditional | flops 327693 | bytes 27918848 | solution.py:516
  29.4 0.0 copy-start.4
  29.4 0.0 copy-start.2
  29.4 0.8 copy-done.4
  30.3 4.7 %all-to-all-start = ((f32[5248,1,128]{2,1,0:T(1,128)}), f32[5248,1,128]{2,1,0:T(1,128)S(1)}, u32[]{:S(2)}, u32[]{:S(2)}) async-start(f32[5248,1,128]{2,1,0:T(1,128)} %bitcast.21), calls=%async_computation | async-start | bytes 5373952 | tf_op jit(solution)/shard_map/cond/branch_1_fun/all_to_all | solution.py:482
  35.0 0.0 copy-done.2
  35.0 2.0 %slice_select_fusion = f32[2,5,128,128]{3,2,1,0:T(8,128)} fusion(f32[2,16,128,128]{3,2,1,0:T(8,128)} %get-tuple-element.36, f32[2,5,128,128]{3,2,1,0:T(8,128)S(1)} %get-tuple-element.30.piece_1, f32[2,5,128,128]{3,2,1,0:T(8,128)} %copy-done.4, pred[]{:T(512)S(6)} %eq.5, pred[]{:T(512)S(6)} %ge.2), kind=kLoop, calls=%fused_computation | loop fusion | flops 327680 | bytes 2621442 | tf_op jit(solution)/shard_map/cond/branch_1_fun/jit(_where)/select_n | solution.py:472
  37.0 0.0 copy-start.6
  37.0 0.8 collective-permute-start
  37.8 38.4 %all-to-all-done = f32[5248,1,128]{2,1,0:T(1,128)S(1)} async-done(((f32[5248,1,128]{2,1,0:T(1,128)}), f32[5248,1,128]{2,1,0:T(1,128)S(1)}, u32[]{:S(2)}, u32[]{:S(2)}) %all-to-all-start) | async-done | bytes 2687008 | tf_op jit(solution)/shard_map/cond/branch_1_fun/all_to_all | solution.py:482
  76.2 0.0 copy-start
  76.2 0.0 copy-start.1
  76.2 0.0 copy-start.3
  76.2 0.0 copy-start.5
  76.2 3.2 %second_push.1 = (f32[2,16,128]{2,1,0:T(8,128)S(1)}, f32[2,16,128]{2,1,0:T(8,128)S(1)}) custom-call(s32[1]{0:T(128)} %get-tuple-element.28.mine, f32[1024,128]{1,0:T(8,128)} %get-tuple-element.37.phases1, f32[1024,128]{1,0:T(8,128)} %get-tuple-element.38.energies1, f32[5248,128]{1,0:T(8,128)S(1)} %bitcast.17), custom_call_target="tpu_custom_call" | custom-call | tf_op jit(solution)/shard_map/cond/branch_1_fun/second_push/pallas_call | solution.py:484
  79.5 0.0 collective-permute-start.1
  79.5 0.0 copy-done.6
  79.5 0.0 copy-done
  79.5 0.0 copy-done.1
  79.5 0.0 copy-done.3
  79.5 0.0 copy-done.5
  79.5 0.0 copy-start.7
  79.5 2.3 %early_field.1 = f32[2,6,128,128]{3,2,1,0:T(8,128)} custom-call(s32[1]{0:T(128)} %get-tuple-element.28.mine, f32[2,5,128,128]{3,2,1,0:T(8,128)S(1)} %copy-done.5, f32[2,5,128,128]{3,2,1,0:T(8,128)S(1)} %copy-done.3, f32[3,128,128]{2,1,0:T(8,128)S(1)} %copy-done.6, bf16[256,768]{1,0:T(8,128)(2,1)S(1)} %copy-done.1, bf16[768,256]{1,0:T(8,128)(2,1)S(1)} %copy-done), custom_call_target="tpu_custom_call" | custom-call | tf_op jit(solution)/shard_map/cond/branch_1_fun/early_field/pallas_call | solution.py:463
  81.8 0.7 collective-permute-done.piece
  82.4 2.1 %late_field.1 = f32[2,5,128,128]{3,2,1,0:T(8,128)} custom-call(f32[2,5,128,128]{3,2,1,0:T(8,128)S(1)} %collective-permute-done.piece, bf16[256,768]{1,0:T(8,128)(2,1)S(1)} %copy-done.1, bf16[768,256]{1,0:T(8,128)(2,1)S(1)} %copy-done), custom_call_target="tpu_custom_call" | custom-call | tf_op jit(solution)/shard_map/cond/branch_1_fun/late_field/pallas_call | solution.py:474
  84.5 0.0 copy-done.7
  84.5 5.2 %pick.1 = (f32[1024,128]{1,0:T(8,128)}, f32[1024,128]{1,0:T(8,128)}) custom-call(s32[1]{0:T(128)} %get-tuple-element.28.mine, f32[5248,128]{1,0:T(8,128)S(1)} %bitcast.18, s32[8,1024]{1,0:T(8,128)S(1)} %copy-done.7), custom_call_target="tpu_custom_call" | custom-call | tf_op jit(solution)/shard_map/cond/branch_1_fun/pick/pallas_call | solution.py:494
  89.8 0.0 collective-permute-done.1
  89.8 0.0 collective-permute-done.4.piece_b0
  89.8 0.0 collective-permute-done.5.piece_b1
  89.8 4.6 %last_field.1 = f32[2,16,128,128]{3,2,1,0:T(8,128)} custom-call(s32[1]{0:T(128)} %bitcast.4.mine, f32[2,6,128,128]{3,2,1,0:T(8,128)} %get-tuple-element.66.early, f32[2,3,128,128]{3,2,1,0:T(8,128)} %collective-permute-done.4.piece_b0, f32[2,3,128,128]{3,2,1,0:T(8,128)} %collective-permute-done.5.piece_b1, f32[2,5,128,128]{3,2,1,0:T(8,128)} %get-tuple-element.69.late, ...), custom_call_target="tpu_custom_call" | custom-call | tf_op jit(solution)/shard_map/last_field/pallas_call | solution.py:519
Async XLA Ops:
  2.0 19.5 %collective-permute-start.3 = (f32[2,5,128,128]{3,2,1,0:T(8,128)S(1)}, f32[2,5,128,128]{3,2,1,0:T(8,128)S(1)}, u32[]{:S(2)}, u32[]{:S(2)}) collective-permute-start(f32[2,5,128,128]{3,2,1,0:T(8,128)S(1)} %get-tuple-element.82), channel_id=1, source_target_pairs={{1,3},{3,5},{5,7},{7,9},{9,11},{11,13},{13,15},{15,17},{17,19},{19... | collective-permute-start | bytes 1966088 | tf_op jit(solution)/shard_map/ppermute | solution.py:423
  2.8 26.7 %collective-permute-start.2 = (f32[2,5,128,128]{3,2,1,0:T(8,128)S(1)}, f32[2,5,128,128]{3,2,1,0:T(8,128)S(1)}, u32[]{:S(2)}, u32[]{:S(2)}) collective-permute-start(f32[2,5,128,128]{3,2,1,0:T(8,128)S(1)} %get-tuple-element.83), channel_id=1, source_target_pairs={{0,2},{2,4},{4,6},{6,8},{8,10},{10,12},{12,14},{14,16},{16,18},{18... | collective-permute-start | bytes 1966088 | tf_op jit(solution)/shard_map/ppermute | solution.py:422
  16.0 73.8 %collective-permute-start.4 = (f32[2,3,128,128]{3,2,1,0:T(8,128)}, f32[2,3,128,128]{3,2,1,0:T(8,128)}, u32[]{:S(2)}, u32[]{:S(2)}) collective-permute-start(f32[2,3,128,128]{3,2,1,0:T(8,128)} %get-tuple-element.67), channel_id=1, source_target_pairs={{0,2},{1,3},{2,4},{3,5},{4,6},{5,7},{6,8},{7,9},{8,10},{9,11},{10,... | collective-permute-start | bytes 1179656 | tf_op jit(solution)/shard_map/ppermute | solution.py:390
  17.6 72.2 %collective-permute-start.5 = (f32[2,3,128,128]{3,2,1,0:T(8,128)}, f32[2,3,128,128]{3,2,1,0:T(8,128)}, u32[]{:S(2)}, u32[]{:S(2)}) collective-permute-start(f32[2,3,128,128]{3,2,1,0:T(8,128)} %get-tuple-element.68), channel_id=1, source_target_pairs={{0,2},{1,3},{2,4},{3,5},{4,6},{5,7},{6,8},{7,9},{8,10},{9,11},{10,... | collective-permute-start | bytes 1179656 | tf_op jit(solution)/shard_map/ppermute | solution.py:390
  29.4 0.8 copy-start.4
  29.4 5.5 %copy-start.2 = (f32[2,5,128,128]{3,2,1,0:T(8,128)}, f32[2,5,128,128]{3,2,1,0:T(8,128)S(1)}, u32[]{:S(2)}) copy-start(f32[2,5,128,128]{3,2,1,0:T(8,128)S(1)} %get-tuple-element.30.piece_1) | copy-start | bytes 1966084 | tf_op jit(solution)/shard_map/cond
  30.3 46.0 %all-to-all-start = ((f32[5248,1,128]{2,1,0:T(1,128)}), f32[5248,1,128]{2,1,0:T(1,128)S(1)}, u32[]{:S(2)}, u32[]{:S(2)}) async-start(f32[5248,1,128]{2,1,0:T(1,128)} %bitcast.21), calls=%async_computation | async-start | bytes 5373952 | tf_op jit(solution)/shard_map/cond/branch_1_fun/all_to_all | solution.py:482
  37.0 42.5 %copy-start.6 = (f32[3,128,128]{2,1,0:T(8,128)S(1)}, f32[3,128,128]{2,1,0:T(8,128)}, u32[]{:S(2)}) copy-start(f32[3,128,128]{2,1,0:T(8,128)} %get-tuple-element.31.beam) | copy-start | bytes 589828 | tf_op jit(solution)/shard_map/cond
  37.0 45.4 %collective-permute-start = (f32[2,5,128,128]{3,2,1,0:T(8,128)}, f32[2,5,128,128]{3,2,1,0:T(8,128)S(1)}, u32[]{:S(2)}, u32[]{:S(2)}) collective-permute-start(f32[2,5,128,128]{3,2,1,0:T(8,128)} %slice_select_fusion), channel_id=1, source_target_pairs={{0,2},{1,3},{2,4},{3,5},{4,6},{5,7},{6,0},{7,1},{8,10},{9,11},{10,... | collective-permute-start | bytes 1966088 | tf_op jit(solution)/shard_map/cond/branch_1_fun/ppermute | solution.py:473
  76.2 3.2 %copy-start = (bf16[768,256]{1,0:T(8,128)(2,1)S(1)}, bf16[768,256]{1,0:T(8,128)(2,1)}, u32[]{:S(2)}) copy-start(bf16[768,256]{1,0:T(8,128)(2,1)} %get-tuple-element.33.right) | copy-start | bytes 1179652 | tf_op jit(solution)/shard_map/cond
  76.2 3.3 %copy-start.1 = (bf16[256,768]{1,0:T(8,128)(2,1)S(1)}, bf16[256,768]{1,0:T(8,128)(2,1)}, u32[]{:S(2)}) copy-start(bf16[256,768]{1,0:T(8,128)(2,1)} %get-tuple-element.32.left) | copy-start | bytes 1179652 | tf_op jit(solution)/shard_map/cond
  76.2 3.3 %copy-start.3 = (f32[2,5,128,128]{3,2,1,0:T(8,128)S(1)}, f32[2,5,128,128]{3,2,1,0:T(8,128)}, u32[]{:S(2)}) copy-start(f32[2,5,128,128]{3,2,1,0:T(8,128)} %copy-done.2) | copy-start | bytes 1966084 | tf_op jit(solution)/shard_map/cond
  76.2 3.3 %copy-start.5 = (f32[2,5,128,128]{3,2,1,0:T(8,128)S(1)}, f32[2,5,128,128]{3,2,1,0:T(8,128)}, u32[]{:S(2)}) copy-start(f32[2,5,128,128]{3,2,1,0:T(8,128)} %copy-done.4) | copy-start | bytes 1966084 | tf_op jit(solution)/shard_map/cond
  79.5 10.3 %collective-permute-start.1 = (f32[2,16,128]{2,1,0:T(8,128)S(1)}, f32[2,16,128]{2,1,0:T(8,128)}, u32[]{:S(2)}, u32[]{:S(2)}) collective-permute-start(f32[2,16,128]{2,1,0:T(8,128)S(1)} %get-tuple-element.40), channel_id=1, source_target_pairs={{0,1},{1,2},{2,3},{3,4},{4,5},{5,6},{6,7},{7,8},{8,9},{9,10},{10,1... | collective-permute-start | bytes 49160 | tf_op jit(solution)/shard_map/cond/branch_1_fun/ppermute | solution.py:390
  79.5 5.0 %copy-start.7 = (s32[8,1024]{1,0:T(8,128)S(1)}, s32[8,1024]{1,0:T(8,128)}, u32[]{:S(2)}) copy-start(s32[8,1024]{1,0:T(8,128)} %get-tuple-element.42.places) | copy-start | bytes 98308 | tf_op jit(solution)/shard_map/cond

commit v7 on v6

--- a/solution.py
+++ b/solution.py
@@ -338,8 +338,18 @@
         out[1, k] = im
 
 
-def last_kernel(mine, early, piece_b0, piece_b1, late, small, earlier, beam, left, right, out_hbm, acc, middle, out, sems):
+def last_kernel(
+    mine, early_hbm, piece_b0, piece_b1, late_hbm, small, earlier, beam, left, right,
+    out_hbm, acc, early, raw, late, middle, out, fetch_sems, sems,
+):
     me = mine[0]
+    pairs = [(early_hbm, early), (late_hbm, late)]
+    for piece, (low, high) in zip((piece_b0, piece_b1), MIDDLE):
+        span = pl.ds(low - EARLY, high - low)
+        pairs += [(piece.at[c], raw.at[c, span]) for c in range(2)]
+    fetches = [pltpu.make_async_copy(src, dst, fetch_sems.at[n]) for n, (src, dst) in enumerate(pairs)]
+    for fetch in fetches:
+        fetch.start()
     for n in range(2):
         acc[n] = GAIN * carried(small[n], me == 0)
         acc[2 + n] = GAIN * earlier[n]
@@ -363,8 +373,10 @@
             copies.append(pltpu.make_async_copy(out.at[c, span], out_hbm.at[c, span], sems.at[len(copies)]))
             copies[-1].start()
 
+    for fetch in fetches:
+        fetch.wait()
     finish(0, EARLY)
-    planes = [(piece[0, k], piece[1, k]) for piece in (piece_b0, piece_b1) for k in range(piece.shape[1])]
+    planes = [(raw[0, k], raw[1, k]) for k in range(LATE - EARLY)]
     for k, (re, im) in enumerate(twice_diffracted(planes, left, right)):
         middle[0, k] = re
         middle[1, k] = im
@@ -471,16 +483,8 @@
         handed = jnp.where(core == 0, shared_1, shared_0)
         source_c = jnp.where(mine[0] % 8 >= 6, handed, field[:, LATE:])
         field_c = lax.ppermute(source_c, "cuts", late_pairs())
-        late = pl.pallas_call(
-            late_kernel,
-            out_shape=shape(2, GROUPS - LATE, GRID, GRID),
-            in_specs=[whole()] * 3,
-            out_specs=whole(),
-            compiler_params=params,
-            name="late_field",
-        )(field_c, left_two, right_two)
         recv = lax.all_to_all(send.reshape(ROWS, 1, BLOCK), "cuts", split_axis=0, concat_axis=0, tiled=True)
-        recv = recv.reshape(ROWS, BLOCK)
+        recv, early = lax.optimization_barrier((recv.reshape(ROWS, BLOCK), early))
         small, earlier = pl.pallas_call(
             second_kernel,
             out_shape=(shape(2, GROUPS, 128), shape(2, GROUPS, 128)),
@@ -507,6 +511,15 @@
             compiler_params=params,
             name="pick",
         )(mine, recv, places)
+        phase_out, energy_out, field_c = lax.optimization_barrier((phase_out, energy_out, field_c))
+        late = pl.pallas_call(
+            late_kernel,
+            out_shape=shape(2, GROUPS - LATE, GRID, GRID),
+            in_specs=[whole()] * 3,
+            out_specs=whole(),
+            compiler_params=params,
+            name="late_field",
+        )(field_c, left_two, right_two)
         return phase_out, energy_out, early, late, arrived, earlier
 
     def refuse(*operands):
@@ -519,12 +532,16 @@
     out = pl.pallas_call(
         last_kernel,
         out_shape=shape(2, GROUPS, GRID, GRID),
-        in_specs=[scalar] + [whole()] * 9,
+        in_specs=[scalar] + [remain] * 4 + [whole()] * 5,
         out_specs=remain,
         scratch_shapes=[
             vmem(4, GROUPS, 128),
+            vmem(2, EARLY + 1, GRID, GRID),
+            vmem(2, LATE - EARLY, GRID, GRID),
+            vmem(2, GROUPS - LATE, GRID, GRID),
             vmem(2, LATE - EARLY, GRID, GRID),
             vmem(2, GROUPS, GRID, GRID),
+            pltpu.SemaphoreType.DMA((6,)),
             pltpu.SemaphoreType.DMA((6,)),
         ],
         compiler_params=params,

time: 95.6 us -> 94 us (0.983)
  waiting for transfers between devices: 46.9 us -> 44 us
  Pallas kernels: 27.1 us -> 29.2 us
    all_to_all x1, waiting for transfers between devices: 38.4 us -> 34.7 us  [exchange(): lax.all_to_all(send.reshape(ROWS, 1, BLOCK), 'cuts', split_axis=0, concat...]
    ppermute x3, waiting for transfers between devices: 0.01 us -> 1.33 us  [shifted(): return lax.ppermute(value, axis, pairs)]
    pallas_call x1, Pallas kernels: 2.26 us -> 3.57 us  [exchange(): pl.pallas_call(early_kernel, out_shape=shape(2, EARLY + 1, GRID, GRID), i...]
  transfers between devices with their start and end apart: 7 -> 7, of which waited for: 3 -> 3; matrix products, arithmetic and copies ran while one was open for 2% -> 2% of each run, Pallas kernels for 24% -> 25%
where the time goes in v7:
time: 94 us; the launch traced here: 93.6 us
  waiting for transfers between devices  44 us (47%)
  Pallas kernels  29.2 us (31%)
  starting transfers between devices  15.3 us (16%)
  local copies, waits for them, and re-layouts  2.24 us (2%)
  other arithmetic  2.11 us (2%)
    all_to_all x1, waiting for transfers between devices, exchange(): lax.all_to_all(send.reshape(ROWS, 1, BLOCK), 'cuts', split_axis=0, concat...  34.7 us
    pallas_call x1, Pallas kernels, per_device(): pl.pallas_call(first_kernel, out_shape=(pltpu.HBM((ROWS, BLOCK), jnp.floa...  9.73 us
    ppermute x1, waiting for transfers between devices, per_device(): lax.ppermute(lax.dynamic_slice_in_dim(field, core * LATE, EARLY, 1), 'cut...  7.91 us
    ppermute x3, starting transfers between devices, shifted(): return lax.ppermute(value, axis, pairs)  5.59 us
    pallas_call x1, Pallas kernels, per_device(): pl.pallas_call(last_kernel, out_shape=shape(2, GROUPS, GRID, GRID), in_sp...  5.53 us
    pallas_call x1, Pallas kernels, exchange(): pl.pallas_call(pick_kernel, out_shape=(shape(COUNT, BLOCK), shape(COUNT,...  5.22 us
    all_to_all x1, starting transfers between devices, exchange(): lax.all_to_all(send.reshape(ROWS, 1, BLOCK), 'cuts', split_axis=0, concat...  4.66 us
    pallas_call x1, Pallas kernels, exchange(): pl.pallas_call(early_kernel, out_shape=shape(2, EARLY + 1, GRID, GRID), i...  3.57 us
  transfers between devices with their start and end apart: 7, of which 3 were waited for; matrix products, arithmetic and copies ran while one was open for 2% of the time, Pallas kernels for 25%

profile of v7, /device:TPU:0, one launch (start us, length us, event | category | flops | bytes accessed | tf_op | source)
XLA Modules:
  0.0 93.6 jit_solution(9490088222826659085)
XLA Ops:
  0.7 1.4 %dynamic-slice_bitcast_fusion = (f32[2,5,128,128]{3,2,1,0:T(8,128)S(1)}, f32[2,5,128,128]{3,2,1,0:T(8,128)S(1)}) fusion(f32[2,16,1,128,128]{4,3,2,1,0:T(8,128)} %param.12, s32[]{:T(128)S(6)} %select_n.33, s32[]{:T(128)S(6)} %select_n.32), kind=kLoop, calls=%fused_computation.1 | loop fusion | bytes 2621448 | tf_op jit(solution)/shard_map/dynamic_slice | solution.py:435
  2.0 0.7 collective-permute-start.3
  2.8 3.5 %collective-permute-start.2 = (f32[2,5,128,128]{3,2,1,0:T(8,128)S(1)}, f32[2,5,128,128]{3,2,1,0:T(8,128)S(1)}, u32[]{:S(2)}, u32[]{:S(2)}) collective-permute-start(f32[2,5,128,128]{3,2,1,0:T(8,128)S(1)} %get-tuple-element.88), channel_id=1, source_target_pairs={{0,2},{2,4},{4,6},{6,8},{8,10},{10,12},{12,14},{14,16},{16,18},{18... | collective-permute-start | bytes 1966088 | tf_op jit(solution)/shard_map/ppermute | solution.py:434
  6.2 9.7 %push_place.1 = (f32[5248,128]{1,0:T(8,128)}, f32[1024,128]{1,0:T(8,128)}, f32[1024,128]{1,0:T(8,128)}, s32[8,1024]{1,0:T(8,128)}, f32[3,128,128]{2,1,0:T(8,128)...) custom-call(s32[1]{0:T(128)} %bitcast.4.mine, f32[2,16,128,128]{3,2,1,0:T(8,128)} %bitcast.19, ...), custom_call_target="tpu_custom_call" | custom-call | tf_op jit(solution)/shard_map/push_place/pallas_call | solution.py:437
  16.0 1.5 %collective-permute-start.4 = (f32[2,3,128,128]{3,2,1,0:T(8,128)}, f32[2,3,128,128]{3,2,1,0:T(8,128)}, u32[]{:S(2)}, u32[]{:S(2)}) collective-permute-start(f32[2,3,128,128]{3,2,1,0:T(8,128)} %get-tuple-element.72), channel_id=1, source_target_pairs={{0,2},{1,3},{2,4},{3,5},{4,6},{5,7},{6,8},{7,9},{8,10},{9,11},{10,... | collective-permute-start | bytes 1179656 | tf_op jit(solution)/shard_map/ppermute | solution.py:402
  17.5 4.0 %collective-permute-start.5 = (f32[2,3,128,128]{3,2,1,0:T(8,128)}, f32[2,3,128,128]{3,2,1,0:T(8,128)}, u32[]{:S(2)}, u32[]{:S(2)}) collective-permute-start(f32[2,3,128,128]{3,2,1,0:T(8,128)} %get-tuple-element.73), channel_id=1, source_target_pairs={{0,2},{1,3},{2,4},{3,5},{4,6},{5,7},{6,8},{7,9},{8,10},{9,11},{10,... | collective-permute-start | bytes 1179656 | tf_op jit(solution)/shard_map/ppermute | solution.py:402
  21.5 0.0 collective-permute-done.3
  21.5 7.9 %collective-permute-done.2 = f32[2,5,128,128]{3,2,1,0:T(8,128)S(1)} collective-permute-done((f32[2,5,128,128]{3,2,1,0:T(8,128)S(1)}, f32[2,5,128,128]{3,2,1,0:T(8,128)S(1)}, u32[]{:S(2)}, u32[]{:S(2)}) %collective-permute-start.2) | collective-permute-done | bytes 655392 | tf_op jit(solution)/shard_map/ppermute | solution.py:434
  29.4 58.6 %conditional.1 = (f32[2,6,128,128]{3,2,1,0:T(8,128)}, f32[2,5,128,128]{3,2,1,0:T(8,128)}, f32[2,16,128]{2,1,0:T(8,128)}, f32[2,16,128]{2,1,0:T(8,128)S(1)}, f32[...) conditional(s32[]{:T(128)} %convert_element_type.3, () %tuple.22, (f32[5248,128]{1,0:T(8,128)}, s32[1]{0:T(128)}, ...), branch_computations={%region_0.1_spmd, %region_1.2_spmd} | conditional | flops 327693 | bytes 25297380 | solution.py:529
  29.4 0.0 copy-start.3
  29.4 0.0 copy-start.2
  29.4 0.8 copy-done.3
  30.3 4.7 %all-to-all-start = ((f32[5248,1,128]{2,1,0:T(1,128)}), f32[5248,1,128]{2,1,0:T(1,128)S(1)}, u32[]{:S(2)}, u32[]{:S(2)}) async-start(f32[5248,1,128]{2,1,0:T(1,128)} %bitcast.21), calls=%async_computation | async-start | bytes 5373952 | tf_op jit(solution)/shard_map/cond/branch_1_fun/all_to_all | solution.py:486
  34.9 0.0 copy-start.5
  35.0 0.0 copy-start.4
  35.0 0.0 copy-done.2
  35.0 2.1 %slice_select_fusion = f32[2,5,128,128]{3,2,1,0:T(8,128)} fusion(f32[2,16,128,128]{3,2,1,0:T(8,128)} %get-tuple-element.42, f32[2,5,128,128]{3,2,1,0:T(8,128)S(1)} %get-tuple-element.31.piece_1, f32[2,5,128,128]{3,2,1,0:T(8,128)} %copy-done.3, pred[]{:T(512)S(6)} %eq.5, pred[]{:T(512)S(6)} %ge.2), kind=kLoop, calls=%fused_computation | loop fusion | flops 327680 | bytes 2621442 | tf_op jit(solution)/shard_map/cond/branch_1_fun/jit(_where)/select_n | solution.py:484
  37.1 0.8 collective-permute-start
  37.9 0.0 copy-done.5
  37.9 0.0 copy-done.4
  37.9 3.6 %early_field.1 = f32[2,6,128,128]{3,2,1,0:T(8,128)} custom-call(s32[1]{0:T(128)} %get-tuple-element.29.mine, f32[2,5,128,128]{3,2,1,0:T(8,128)S(1)} %copy-done.4, f32[2,5,128,128]{3,2,1,0:T(8,128)} %copy-done.2, f32[3,128,128]{2,1,0:T(8,128)S(1)} %copy-done.5, bf16[256,768]{1,0:T(8,128)(2,1)} %get-tuple-element.33.left, bf16[768,256]{1,0:T(8,128)(2,1)} %get-tuple-element.34.right), custom_call_target="tpu_custom_call" | custom-call | tf_op jit(solution)/shard_map/cond/branch_1_fun/early_field/pallas_call | solution.py:475
  41.5 0.0 copy-start.6
  41.5 34.7 %all-to-all-done = f32[5248,1,128]{2,1,0:T(1,128)S(1)} async-done(((f32[5248,1,128]{2,1,0:T(1,128)}), f32[5248,1,128]{2,1,0:T(1,128)S(1)}, u32[]{:S(2)}, u32[]{:S(2)}) %all-to-all-start) | async-done | bytes 2687008 | tf_op jit(solution)/shard_map/cond/branch_1_fun/all_to_all | solution.py:486
  76.3 3.1 %second_push.1 = (f32[2,16,128]{2,1,0:T(8,128)S(1)}, f32[2,16,128]{2,1,0:T(8,128)S(1)}) custom-call(s32[1]{0:T(128)} %get-tuple-element.29.mine, f32[1024,128]{1,0:T(8,128)} %get-tuple-element.44.phases1, f32[1024,128]{1,0:T(8,128)} %get-tuple-element.45.energies1, f32[5248,128]{1,0:T(8,128)S(1)} %bitcast.17), custom_call_target="tpu_custom_call" | custom-call | tf_op jit(solution)/shard_map/cond/branch_1_fun/second_push/pallas_call | solution.py:488
  79.3 0.0 copy-start
  79.3 0.0 copy-start.1
  79.3 0.0 collective-permute-start.1
  79.4 0.0 copy-done.6
  79.4 5.2 %pick.1 = (f32[1024,128]{1,0:T(8,128)}, f32[1024,128]{1,0:T(8,128)}) custom-call(s32[1]{0:T(128)} %get-tuple-element.29.mine, f32[5248,128]{1,0:T(8,128)S(1)} %bitcast.18, s32[8,1024]{1,0:T(8,128)S(1)} %copy-done.6), custom_call_target="tpu_custom_call" | custom-call | tf_op jit(solution)/shard_map/cond/branch_1_fun/pick/pallas_call | solution.py:498
  84.6 0.0 collective-permute-done.piece
  84.6 0.0 copy-done
  84.6 0.0 copy-done.1
  84.7 2.1 %late_field.1 = f32[2,5,128,128]{3,2,1,0:T(8,128)} custom-call(f32[2,5,128,128]{3,2,1,0:T(8,128)S(1)} %collective-permute-done.piece, bf16[256,768]{1,0:T(8,128)(2,1)S(1)} %copy-done.1, bf16[768,256]{1,0:T(8,128)(2,1)S(1)} %copy-done), custom_call_target="tpu_custom_call" | custom-call | tf_op jit(solution)/shard_map/cond/branch_1_fun/late_field/pallas_call | solution.py:515
  86.7 1.3 %collective-permute-done.1 = f32[2,16,128]{2,1,0:T(8,128)} collective-permute-done((f32[2,16,128]{2,1,0:T(8,128)S(1)}, f32[2,16,128]{2,1,0:T(8,128)}, u32[]{:S(2)}, u32[]{:S(2)}) %collective-permute-start.1) | collective-permute-done | bytes 16416 | tf_op jit(solution)/shard_map/cond/branch_1_fun/ppermute | solution.py:402
  88.1 0.0 collective-permute-done.4.piece_b0
  88.1 0.0 collective-permute-done.5.piece_b1
  88.1 5.5 %last_field.1 = f32[2,16,128,128]{3,2,1,0:T(8,128)} custom-call(s32[1]{0:T(128)} %bitcast.4.mine, f32[2,6,128,128]{3,2,1,0:T(8,128)} %get-tuple-element.71.early_hbm, f32[2,3,128,128]{3,2,1,0:T(8,128)} %collective-permute-done.4.piece_b0, f32[2,3,128,128]{3,2,1,0:T(8,128)} %collective-permute-done.5.piece_b1, f32[2,5,128,128]{3,2,1,0:T(8,128)} %get-tuple-element.74.late_hbm, ...), custom_call_target="tpu_custom_call" | custom-call | tf_op jit(solution)/shard_map/last_field/pallas_call | solution.py:532
Async XLA Ops:
  2.0 19.5 %collective-permute-start.3 = (f32[2,5,128,128]{3,2,1,0:T(8,128)S(1)}, f32[2,5,128,128]{3,2,1,0:T(8,128)S(1)}, u32[]{:S(2)}, u32[]{:S(2)}) collective-permute-start(f32[2,5,128,128]{3,2,1,0:T(8,128)S(1)} %get-tuple-element.87), channel_id=1, source_target_pairs={{1,3},{3,5},{5,7},{7,9},{9,11},{11,13},{13,15},{15,17},{17,19},{19... | collective-permute-start | bytes 1966088 | tf_op jit(solution)/shard_map/ppermute | solution.py:435
  2.8 26.7 %collective-permute-start.2 = (f32[2,5,128,128]{3,2,1,0:T(8,128)S(1)}, f32[2,5,128,128]{3,2,1,0:T(8,128)S(1)}, u32[]{:S(2)}, u32[]{:S(2)}) collective-permute-start(f32[2,5,128,128]{3,2,1,0:T(8,128)S(1)} %get-tuple-element.88), channel_id=1, source_target_pairs={{0,2},{2,4},{4,6},{6,8},{8,10},{10,12},{12,14},{14,16},{16,18},{18... | collective-permute-start | bytes 1966088 | tf_op jit(solution)/shard_map/ppermute | solution.py:434
  16.0 72.1 %collective-permute-start.4 = (f32[2,3,128,128]{3,2,1,0:T(8,128)}, f32[2,3,128,128]{3,2,1,0:T(8,128)}, u32[]{:S(2)}, u32[]{:S(2)}) collective-permute-start(f32[2,3,128,128]{3,2,1,0:T(8,128)} %get-tuple-element.72), channel_id=1, source_target_pairs={{0,2},{1,3},{2,4},{3,5},{4,6},{5,7},{6,8},{7,9},{8,10},{9,11},{10,... | collective-permute-start | bytes 1179656 | tf_op jit(solution)/shard_map/ppermute | solution.py:402
  17.5 70.5 %collective-permute-start.5 = (f32[2,3,128,128]{3,2,1,0:T(8,128)}, f32[2,3,128,128]{3,2,1,0:T(8,128)}, u32[]{:S(2)}, u32[]{:S(2)}) collective-permute-start(f32[2,3,128,128]{3,2,1,0:T(8,128)} %get-tuple-element.73), channel_id=1, source_target_pairs={{0,2},{1,3},{2,4},{3,5},{4,6},{5,7},{6,8},{7,9},{8,10},{9,11},{10,... | collective-permute-start | bytes 1179656 | tf_op jit(solution)/shard_map/ppermute | solution.py:402
  29.4 0.8 copy-start.3
  29.4 5.5 %copy-start.2 = (f32[2,5,128,128]{3,2,1,0:T(8,128)}, f32[2,5,128,128]{3,2,1,0:T(8,128)S(1)}, u32[]{:S(2)}) copy-start(f32[2,5,128,128]{3,2,1,0:T(8,128)S(1)} %get-tuple-element.31.piece_1) | copy-start | bytes 1966084 | tf_op jit(solution)/shard_map/cond
  30.3 46.0 %all-to-all-start = ((f32[5248,1,128]{2,1,0:T(1,128)}), f32[5248,1,128]{2,1,0:T(1,128)S(1)}, u32[]{:S(2)}, u32[]{:S(2)}) async-start(f32[5248,1,128]{2,1,0:T(1,128)} %bitcast.21), calls=%async_computation | async-start | bytes 5373952 | tf_op jit(solution)/shard_map/cond/branch_1_fun/all_to_all | solution.py:486
  34.9 3.0 %copy-start.5 = (f32[3,128,128]{2,1,0:T(8,128)S(1)}, f32[3,128,128]{2,1,0:T(8,128)}, u32[]{:S(2)}) copy-start(f32[3,128,128]{2,1,0:T(8,128)} %get-tuple-element.32.beam) | copy-start | bytes 589828 | tf_op jit(solution)/shard_map/cond
  35.0 3.0 %copy-start.4 = (f32[2,5,128,128]{3,2,1,0:T(8,128)S(1)}, f32[2,5,128,128]{3,2,1,0:T(8,128)}, u32[]{:S(2)}) copy-start(f32[2,5,128,128]{3,2,1,0:T(8,128)} %copy-done.3) | copy-start | bytes 1966084 | tf_op jit(solution)/shard_map/cond
  37.1 47.5 %collective-permute-start = (f32[2,5,128,128]{3,2,1,0:T(8,128)}, f32[2,5,128,128]{3,2,1,0:T(8,128)S(1)}, u32[]{:S(2)}, u32[]{:S(2)}) collective-permute-start(f32[2,5,128,128]{3,2,1,0:T(8,128)} %slice_select_fusion), channel_id=1, source_target_pairs={{0,2},{1,3},{2,4},{3,5},{4,6},{5,7},{6,0},{7,1},{8,10},{9,11},{10,... | collective-permute-start | bytes 1966088 | tf_op jit(solution)/shard_map/cond/branch_1_fun/ppermute | solution.py:485
  41.5 37.9 %copy-start.6 = (s32[8,1024]{1,0:T(8,128)S(1)}, s32[8,1024]{1,0:T(8,128)}, u32[]{:S(2)}) copy-start(s32[8,1024]{1,0:T(8,128)} %get-tuple-element.37.places) | copy-start | bytes 98308 | tf_op jit(solution)/shard_map/cond
  79.3 5.3 %copy-start = (bf16[768,256]{1,0:T(8,128)(2,1)S(1)}, bf16[768,256]{1,0:T(8,128)(2,1)}, u32[]{:S(2)}) copy-start(bf16[768,256]{1,0:T(8,128)(2,1)} %get-tuple-element.34.right) | copy-start | bytes 1179652 | tf_op jit(solution)/shard_map/cond
  79.3 5.3 %copy-start.1 = (bf16[256,768]{1,0:T(8,128)(2,1)S(1)}, bf16[256,768]{1,0:T(8,128)(2,1)}, u32[]{:S(2)}) copy-start(bf16[256,768]{1,0:T(8,128)(2,1)} %get-tuple-element.33.left) | copy-start | bytes 1179652 | tf_op jit(solution)/shard_map/cond
  79.3 8.7 %collective-permute-start.1 = (f32[2,16,128]{2,1,0:T(8,128)S(1)}, f32[2,16,128]{2,1,0:T(8,128)}, u32[]{:S(2)}, u32[]{:S(2)}) collective-permute-start(f32[2,16,128]{2,1,0:T(8,128)S(1)} %get-tuple-element.46), channel_id=1, source_target_pairs={{0,1},{1,2},{2,3},{3,4},{4,5},{5,6},{6,7},{7,8},{8,9},{9,10},{10,1... | collective-permute-start | bytes 49160 | tf_op jit(solution)/shard_map/cond/branch_1_fun/ppermute | solution.py:402

commit v8 on v6

--- a/solution.py
+++ b/solution.py
@@ -26,7 +26,7 @@
 ROWS = PEERS * MESSAGE
 BATCH = 32
 EARLY, LATE = 5, 11
-MIDDLE = ((5, 8), (8, 11))
+MIDDLE = ((5, 7), (7, 9), (9, 11))
 VMEM_LIMIT = 24 * 1024 * 1024
 HIGHEST = lax.Precision.HIGHEST
 
@@ -120,7 +120,7 @@
 
 def first_kernel(
     mine, field_hbm, profile_hbm, bins_hbm, jitter_hbm, energy_hbm, delays_hbm, left_hbm, right_hbm,
-    send_hbm, phases_hbm, energies_hbm, places_hbm, beam, middle_0, middle_1,
+    send_hbm, phases_hbm, energies_hbm, places_hbm, beam, small, middle_0, middle_1, middle_2,
     field, profile, bins, jitter, energy, delays, left, right, acc, send, phases, energies, places, index_v, index, sems,
 ):
     pairs = [
@@ -148,7 +148,7 @@
     beam[2] = p
     copies[4].wait()
     kept = [pltpu.make_async_copy(places, places_hbm, sems.at[8])]
-    for middle, (low, high) in zip((middle_0, middle_1), MIDDLE):
+    for middle, (low, high) in zip((middle_0, middle_1, middle_2), MIDDLE):
         for c in range(2):
             span = pl.ds(low, high - low)
             kept.append(pltpu.make_async_copy(field.at[c, span], middle.at[c], sems.at[10 + len(kept)]))
@@ -186,7 +186,7 @@
     lax.fori_loop(0, GROUPS, push, 0)
     kept.append(pltpu.make_async_copy(phases, phases_hbm, sems.at[9]))
     kept.append(pltpu.make_async_copy(energies, energies_hbm, sems.at[10]))
-    for copy in kept[5:]:
+    for copy in kept[7:]:
         copy.start()
     to_scalar.wait()
 
@@ -206,7 +206,9 @@
     gain = GAIN / GRID
     next_re = acc[2] + gain * (bre * self_re - bim * self_im)
     next_im = acc[3] + gain * (bre * self_im + bim * self_re)
-    note = one_row([next_re, next_im, bre, bim])
+    for n, part in enumerate((next_re, next_im, bre, bim)):
+        small[n] = part
+    note = one_row([next_re, next_im])
     for n in range(PEERS):
         send[n * MESSAGE + 2 * CAP : (n + 1) * MESSAGE] = note
     out = pltpu.make_async_copy(send, send_hbm, sems.at[0])
@@ -228,35 +230,28 @@
     return stack.T[0:1]
 
 
-def parts_of(recv, device):
-    row = recv[pl.ds(device * MESSAGE + 2 * CAP, 1)]
-    return jnp.broadcast_to(row, (128, 128)).T
-
-
 def carried(value, flag):
     rolled = jnp.concatenate([jnp.zeros_like(value[:1]), value[:-1]], axis=0)
     return jnp.where(flag, rolled, value)
 
 
-def second_kernel(mine, phases1, energies1, recv, small, earlier, acc):
-    me = mine[0]
-    near = parts_of(recv, (me + PEERS - 1) % PEERS)
-    far = parts_of(recv, (me + PEERS - 2) % PEERS)
-    for n in range(2):
-        acc[n] = carried(near[n * GROUPS : (n + 1) * GROUPS], me == 0)
-        earlier[n] = carried(far[(2 + n) * GROUPS : (3 + n) * GROUPS], me < 2)
+def second_kernel(mine, phases1, energies1, arrived, small, acc):
+    for n in range(4):
+        acc[n] = carried(arrived[n], mine[0] == 0)
 
     def push(k, carry):
         rows = rows_of(k)
         ph, _ = pushed(phases1[rows], energies1[rows], acc[0, pl.ds(k, 1)], acc[1, pl.ds(k, 1)])
         c, s = cos_sin(ph)
-        acc[2, pl.ds(k, 1)] = jnp.sum(c, axis=0, keepdims=True)
-        acc[3, pl.ds(k, 1)] = jnp.sum(s, axis=0, keepdims=True)
+        small[0, pl.ds(k, 1)] = jnp.sum(c, axis=0, keepdims=True)
+        small[1, pl.ds(k, 1)] = jnp.sum(s, axis=0, keepdims=True)
         return carry
 
     lax.fori_loop(0, GROUPS, push, 0)
-    small[0] = lane_total(acc[2]) * (1.0 / (NBS * BLOCK))
-    small[1] = lane_total(acc[3]) * (-1.0 / (NBS * BLOCK))
+    small[0] = lane_total(small[0]) * (1.0 / (NBS * BLOCK))
+    small[1] = lane_total(small[1]) * (-1.0 / (NBS * BLOCK))
+    small[2] = acc[2]
+    small[3] = acc[3]
 
 
 def wide_halves(x):
@@ -331,26 +326,18 @@
         out[1, k] = im
 
 
-def late_kernel(piece, left, right, out):
-    planes = [(piece[0, k], piece[1, k]) for k in range(piece.shape[1])]
-    for k, (re, im) in enumerate(twice_diffracted(planes, left, right)):
-        out[0, k] = re
-        out[1, k] = im
-
-
-def last_kernel(mine, early, piece_b0, piece_b1, late, small, earlier, beam, left, right, out_hbm, acc, middle, out, sems):
+def last_kernel(
+    mine, early, piece_b0, piece_b1, piece_b2, piece_c, small, beam, left, right, out_hbm, acc, rest, out, sems
+):
     me = mine[0]
-    for n in range(2):
+    for n in range(4):
         acc[n] = GAIN * carried(small[n], me == 0)
-        acc[2 + n] = GAIN * earlier[n]
     copies = []
 
     def plane(c, k):
         if k < 0:
             return jnp.zeros((GRID, GRID), jnp.float32)
-        if k < EARLY:
-            return early[c, k]
-        return middle[c, k - EARLY] if k < LATE else late[c, k - LATE]
+        return early[c, k] if k < EARLY else rest[c, k - EARLY]
 
     def finish(low, high):
         for k in range(low, high):
@@ -364,11 +351,15 @@
             copies[-1].start()
 
     finish(0, EARLY)
-    planes = [(piece[0, k], piece[1, k]) for piece in (piece_b0, piece_b1) for k in range(piece.shape[1])]
+    planes = [(piece[0, k], piece[1, k]) for piece in (piece_b0, piece_b1, piece_b2) for k in range(piece.shape[1])]
     for k, (re, im) in enumerate(twice_diffracted(planes, left, right)):
-        middle[0, k] = re
-        middle[1, k] = im
+        rest[0, k] = re
+        rest[1, k] = im
     finish(EARLY, LATE)
+    planes = [(piece_c[0, k], piece_c[1, k]) for k in range(piece_c.shape[1])]
+    for k, (re, im) in enumerate(twice_diffracted(planes, left, right)):
+        rest[0, LATE - EARLY + k] = re
+        rest[1, LATE - EARLY + k] = im
     finish(LATE, GROUPS)
     for copy in copies:
         copy.wait()
@@ -422,7 +413,7 @@
     shared_0 = lax.ppermute(lax.dynamic_slice_in_dim(field, core * LATE, EARLY, 1), "cuts", early_pairs(0))
     shared_1 = lax.ppermute(lax.dynamic_slice_in_dim(field, (1 - core) * LATE, EARLY, 1), "cuts", early_pairs(1))
     operands = [field, profile, bins, jitter, energies, delays.reshape(GROUPS, 1, NBS), left_one, right_one]
-    send, phases1, energies1, places, beam, *sources = pl.pallas_call(
+    send, phases1, energies1, places, beam, small1, *sources = pl.pallas_call(
         first_kernel,
         out_shape=(
             pltpu.HBM((ROWS, BLOCK), jnp.float32),
@@ -430,10 +421,11 @@
             pltpu.HBM((COUNT, BLOCK), jnp.float32),
             pltpu.HBM((8, COUNT), jnp.int32),
             pltpu.HBM((3, GRID, GRID), jnp.float32),
+            shape(4, GROUPS, 128),
             *[pltpu.HBM((2, high - low, GRID, GRID), jnp.float32) for low, high in MIDDLE],
         ),
         in_specs=[scalar] + [remain] * 8,
-        out_specs=(remain,) * 4 + (whole(),) + (remain,) * len(MIDDLE),
+        out_specs=(remain,) * 4 + (whole(),) * 2 + (remain,) * len(MIDDLE),
         scratch_shapes=[
             vmem(2, GROUPS, GRID, GRID),
             vmem(GRID, GRID),
@@ -450,16 +442,26 @@
             vmem(8, COUNT, dtype=jnp.int32),
             vmem(8, 128, dtype=jnp.int32),
             pltpu.SMEM((8, 128), jnp.int32),
-            pltpu.SemaphoreType.DMA((15,)),
+            pltpu.SemaphoreType.DMA((17,)),
         ],
         compiler_params=params,
         name="push_place",
     )(mine, *[in_hbm(value) for value in operands])
+    arrived1 = shifted(small1, "cuts", 1)
+    small2 = pl.pallas_call(
+        second_kernel,
+        out_shape=shape(4, GROUPS, 128),
+        in_specs=[scalar] + [whole()] * 3,
+        out_specs=whole(),
+        scratch_shapes=[vmem(4, GROUPS, 128)],
+        compiler_params=params,
+        name="second_push",
+    )(mine, phases1, energies1, arrived1)
     field_b = [shifted(source, "cuts", 2) for source in sources]
 
     left_two, right_two = deep_left(left_form(*two)), deep_right(right_form(*two))
 
-    def exchange(send, phases1, energies1, places, field, shared_0, shared_1, beam):
+    def exchange(send, small2, places, field, shared_0, shared_1, beam):
         early = pl.pallas_call(
             early_kernel,
             out_shape=shape(2, EARLY + 1, GRID, GRID),
@@ -471,26 +473,9 @@
         handed = jnp.where(core == 0, shared_1, shared_0)
         source_c = jnp.where(mine[0] % 8 >= 6, handed, field[:, LATE:])
         field_c = lax.ppermute(source_c, "cuts", late_pairs())
-        late = pl.pallas_call(
-            late_kernel,
-            out_shape=shape(2, GROUPS - LATE, GRID, GRID),
-            in_specs=[whole()] * 3,
-            out_specs=whole(),
-            compiler_params=params,
-            name="late_field",
-        )(field_c, left_two, right_two)
         recv = lax.all_to_all(send.reshape(ROWS, 1, BLOCK), "cuts", split_axis=0, concat_axis=0, tiled=True)
-        recv = recv.reshape(ROWS, BLOCK)
-        small, earlier = pl.pallas_call(
-            second_kernel,
-            out_shape=(shape(2, GROUPS, 128), shape(2, GROUPS, 128)),
-            in_specs=[scalar] + [whole()] * 3,
-            out_specs=(whole(),) * 2,
-            scratch_shapes=[vmem(4, GROUPS, 128)],
-            compiler_params=params,
-            name="second_push",
-        )(mine, phases1, energies1, recv)
-        arrived = shifted(small, "cuts", 1)
+        recv, early = lax.optimization_barrier((recv.reshape(ROWS, BLOCK), early))
+        arrived = shifted(small2, "cuts", 1)
         phase_out, energy_out = pl.pallas_call(
             pick_kernel,
             out_shape=(shape(COUNT, BLOCK), shape(COUNT, BLOCK)),
@@ -507,14 +492,14 @@
             compiler_params=params,
             name="pick",
         )(mine, recv, places)
-        return phase_out, energy_out, early, late, arrived, earlier
+        return phase_out, energy_out, early, field_c, arrived
 
     def refuse(*operands):
-        sizes = [(COUNT, BLOCK)] * 2 + [(2, n, GRID, GRID) for n in (EARLY + 1, GROUPS - LATE)] + [(2, GROUPS, 128)] * 2
+        sizes = [(COUNT, BLOCK)] * 2 + [(2, n, GRID, GRID) for n in (EARLY + 1, GROUPS - LATE)] + [(4, GROUPS, 128)]
         return tuple(jnp.zeros(size, jnp.float32) for size in sizes)
 
-    phase_out, energy_out, early, late, arrived, earlier = lax.cond(
-        mine[0] < PEERS, exchange, refuse, send, phases1, energies1, places, field, shared_0, shared_1, beam
+    phase_out, energy_out, early, field_c, arrived = lax.cond(
+        mine[0] < PEERS, exchange, refuse, send, small2, places, field, shared_0, shared_1, beam
     )
     out = pl.pallas_call(
         last_kernel,
@@ -523,13 +508,13 @@
         out_specs=remain,
         scratch_shapes=[
             vmem(4, GROUPS, 128),
-            vmem(2, LATE - EARLY, GRID, GRID),
+            vmem(2, GROUPS - EARLY, GRID, GRID),
             vmem(2, GROUPS, GRID, GRID),
             pltpu.SemaphoreType.DMA((6,)),
         ],
         compiler_params=params,
         name="last_field",
-    )(mine, early, *field_b, late, arrived, earlier, in_hbm(beam), left_two, right_two)
+    )(mine, early, *field_b, field_c, arrived, in_hbm(beam), left_two, right_two)
     return (
         out.reshape(2, GROUPS, 1, GRID, GRID),
         phase_out.reshape(GROUPS, 1, NBS * BLOCK),

time: 95.6 us -> 100 us (1.046); the launches traced: 94.4 us -> 100 us
  starting transfers between devices: 15.2 us -> 19.3 us
  Pallas kernels: 27.1 us -> 23.8 us
  waiting for transfers between devices: 46.9 us -> 49.2 us
  local copies, waits for them, and re-layouts: 2.24 us -> 4.54 us
    ppermute x3 -> x5, waiting for transfers between devices: 0.01 us -> 17.7 us  [shifted(): return lax.ppermute(value, axis, pairs)]
    ppermute x1, waiting for transfers between devices: 7.88 us -> 0.01 us  [per_device(): lax.ppermute(lax.dynamic_slice_in_dim(field, core * LATE, EARLY, 1), 'cut...]
    all_to_all x1, waiting for transfers between devices: 38.4 us -> 31.5 us  [exchange(): lax.all_to_all(send.reshape(ROWS, 1, BLOCK), 'cuts', split_axis=0, concat...]
    all_to_all x1, starting transfers between devices: 4.66 us -> 9.38 us  [exchange(): lax.all_to_all(send.reshape(ROWS, 1, BLOCK), 'cuts', split_axis=0, concat...]
    pallas_call x2 -> x1, Pallas kernels: 5.31 us -> 1.8 us  [per_device(): pl.pallas_call(second_kernel, out_shape=shape(4, GROUPS, 128), in_specs=[...]
    unnamed x0 -> x4, local copies, waits for them, and re-layouts: none -> 2.08 us
    ppermute x3 -> x5, starting transfers between devices: 5.54 us -> 4.82 us  [shifted(): return lax.ppermute(value, axis, pairs)]
  transfers between devices with their start and end apart: 7 -> 9, of which waited for: 3 -> 3; matrix products, arithmetic and copies ran while one was open for 2% -> 2% of each run, Pallas kernels for 24% -> 19%
where the time goes in v8:
time: 100 us
  waiting for transfers between devices  49.2 us (49%)
  Pallas kernels  23.8 us (24%)
  starting transfers between devices  19.3 us (19%)
  local copies, waits for them, and re-layouts  4.54 us (5%)
  other arithmetic  2.37 us (2%)
    all_to_all x1, waiting for transfers between devices, exchange(): lax.all_to_all(send.reshape(ROWS, 1, BLOCK), 'cuts', split_axis=0, concat...  31.5 us
    ppermute x5, waiting for transfers between devices, shifted(): return lax.ppermute(value, axis, pairs)  17.7 us
    pallas_call x1, Pallas kernels, per_device(): pl.pallas_call(first_kernel, out_shape=(pltpu.HBM((ROWS, BLOCK), jnp.floa...  9.72 us
    all_to_all x1, starting transfers between devices, exchange(): lax.all_to_all(send.reshape(ROWS, 1, BLOCK), 'cuts', split_axis=0, concat...  9.38 us
    pallas_call x1, Pallas kernels, exchange(): pl.pallas_call(pick_kernel, out_shape=(shape(COUNT, BLOCK), shape(COUNT,...  5.22 us
    ppermute x5, starting transfers between devices, shifted(): return lax.ppermute(value, axis, pairs)  4.82 us
    pallas_call x1, Pallas kernels, per_device(): pl.pallas_call(last_kernel, out_shape=shape(2, GROUPS, GRID, GRID), in_sp...  4.76 us
    ppermute x1, starting transfers between devices, per_device(): lax.ppermute(lax.dynamic_slice_in_dim(field, core * LATE, EARLY, 1), 'cut...  3.48 us
  transfers between devices with their start and end apart: 9, of which 3 were waited for; matrix products, arithmetic and copies ran while one was open for 2% of the time, Pallas kernels for 19%

profile of v8, /device:TPU:0, one launch (start us, length us, event | category | flops | bytes accessed | tf_op | source)
XLA Modules:
  0.0 100.0 jit_solution(4005746474258622117)
XLA Ops:
  0.7 1.4 %dynamic-slice_bitcast_fusion = (f32[2,5,128,128]{3,2,1,0:T(8,128)S(1)}, f32[2,5,128,128]{3,2,1,0:T(8,128)S(1)}) fusion(f32[2,16,1,128,128]{4,3,2,1,0:T(8,128)} %param.12, s32[]{:T(128)S(6)} %select_n.33, s32[]{:T(128)S(6)} %select_n.32), kind=kLoop, calls=%fused_computation.1 | loop fusion | bytes 2621448 | tf_op jit(solution)/shard_map/dynamic_slice | solution.py:414
  2.0 3.5 %collective-permute-start.2 = (f32[2,5,128,128]{3,2,1,0:T(8,128)S(1)}, f32[2,5,128,128]{3,2,1,0:T(8,128)S(1)}, u32[]{:S(2)}, u32[]{:S(2)}) collective-permute-start(f32[2,5,128,128]{3,2,1,0:T(8,128)S(1)} %get-tuple-element.82), channel_id=1, source_target_pairs={{0,2},{2,4},{4,6},{6,8},{8,10},{10,12},{12,14},{14,16},{16,18},{18... | collective-permute-start | bytes 1966088 | tf_op jit(solution)/shard_map/ppermute | solution.py:413
  5.5 0.7 collective-permute-start.3
  6.2 9.7 %push_place.1 = (f32[5248,128]{1,0:T(8,128)}, f32[1024,128]{1,0:T(8,128)}, f32[1024,128]{1,0:T(8,128)}, s32[8,1024]{1,0:T(8,128)}, f32[3,128,128]{2,1,0:T(8,128)...) custom-call(s32[1]{0:T(128)} %bitcast.4.mine, ...), custom_call_target="tpu_custom_call" | custom-call | tf_op jit(solution)/shard_map/push_place/pallas_call | solution.py:416
  16.0 0.1 collective-permute-start.4
  16.0 1.6 %collective-permute-start.5 = (f32[2,2,128,128]{3,2,1,0:T(8,128)}, f32[2,2,128,128]{3,2,1,0:T(8,128)S(1)}, u32[]{:S(2)}, u32[]{:S(2)}) collective-permute-start(f32[2,2,128,128]{3,2,1,0:T(8,128)} %get-tuple-element.66), channel_id=1, source_target_pairs={{0,2},{1,3},{2,4},{3,5},{4,6},{5,7},{6,8},{7,9},{8,10},{9,11},{10,... | collective-permute-start | bytes 786440 | tf_op jit(solution)/shard_map/ppermute | solution.py:381
  17.6 3.2 %collective-permute-start.6 = (f32[2,2,128,128]{3,2,1,0:T(8,128)}, f32[2,2,128,128]{3,2,1,0:T(8,128)S(1)}, u32[]{:S(2)}, u32[]{:S(2)}) collective-permute-start(f32[2,2,128,128]{3,2,1,0:T(8,128)} %get-tuple-element.67), channel_id=1, source_target_pairs={{0,2},{1,3},{2,4},{3,5},{4,6},{5,7},{6,8},{7,9},{8,10},{9,11},{10,... | collective-permute-start | bytes 786440 | tf_op jit(solution)/shard_map/ppermute | solution.py:381
  20.8 9.3 %collective-permute-done.4.arrived = f32[4,16,128]{2,1,0:T(8,128)S(1)} collective-permute-done((f32[4,16,128]{2,1,0:T(8,128)S(1)}, f32[4,16,128]{2,1,0:T(8,128)S(1)}, u32[]{:S(2)}, u32[]{:S(2)}) %collective-permute-start.4) | collective-permute-done | bytes 32800 | tf_op jit(solution)/shard_map/ppermute | solution.py:381
  30.1 0.0 collective-permute-start.7
  30.1 0.0 copy-start
  30.1 1.0 %copy-done = f32[1024,128]{1,0:T(8,128)S(1)} copy-done((f32[1024,128]{1,0:T(8,128)S(1)}, f32[1024,128]{1,0:T(8,128)}, u32[]{:S(2)}) %copy-start) | copy-done | bytes 524312
  31.1 0.0 copy-start.1
  31.1 1.0 %copy-done.1 = f32[1024,128]{1,0:T(8,128)S(1)} copy-done((f32[1024,128]{1,0:T(8,128)S(1)}, f32[1024,128]{1,0:T(8,128)}, u32[]{:S(2)}) %copy-start.1) | copy-done | bytes 524312
  32.2 1.8 %second_push.1 = f32[4,16,128]{2,1,0:T(8,128)S(1)} custom-call(s32[1]{0:T(128)} %bitcast.4.mine, f32[1024,128]{1,0:T(8,128)S(1)} %copy-done, f32[1024,128]{1,0:T(8,128)S(1)} %copy-done.1, f32[4,16,128]{2,1,0:T(8,128)S(1)} %collective-permute-done.4.arrived), custom_call_target="tpu_custom_call" | custom-call | tf_op jit(solution)/shard_map/second_push/pallas_call | solution.py:451
  34.0 0.0 collective-permute-done.2
  34.0 0.0 collective-permute-done.3
  34.0 61.3 %conditional.1 = (f32[2,6,128,128]{3,2,1,0:T(8,128)}, f32[2,5,128,128]{3,2,1,0:T(8,128)}, f32[4,16,128]{2,1,0:T(8,128)}, f32[16,1,8192]{2,1,0:T(1,128)}, f32[16,1,8192]{2,1,0:T(1,128)}) conditional(s32[]{:T(128)} %convert_element_type.3, () %tuple.21, (f32[5248,128]{1,0:T(8,128)}, s32[1]{0:T(128)}, f32[2,5,128,128]{3,2,1,0:T(8,128)S(1)}, ...), branch_computations={%region_0.1_spmd, %region_1.2_spmd} | conditional | flops 327693 | bytes 27984376 | solution.py:501
  34.0 0.0 copy-start.2
  34.0 0.0 copy-start.4
  34.0 0.8 copy-done.2
  34.8 0.2 copy-done.4
  35.0 9.4 %all-to-all-start = ((f32[5248,1,128]{2,1,0:T(1,128)}), f32[5248,1,128]{2,1,0:T(1,128)S(1)}, u32[]{:S(2)}, u32[]{:S(2)}) async-start(f32[5248,1,128]{2,1,0:T(1,128)} %bitcast.20), calls=%async_computation | async-start | bytes 5373952 | tf_op jit(solution)/shard_map/cond/branch_1_fun/all_to_all | solution.py:476
  44.4 0.0 copy-start.3
  44.5 0.0 copy-start.5
  44.5 0.0 copy-start.6
  44.5 0.0 copy-start.7
  44.5 0.0 copy-start.8
  44.5 2.4 %slice_select_fusion = f32[2,5,128,128]{3,2,1,0:T(8,128)} fusion(f32[2,16,128,128]{3,2,1,0:T(8,128)} %get-tuple-element.36, f32[2,5,128,128]{3,2,1,0:T(8,128)} %copy-done.4, f32[2,5,128,128]{3,2,1,0:T(8,128)} %copy-done.2, pred[]{:T(512)S(6)} %eq.5, pred[]{:T(512)S(6)} %ge.2), kind=kLoop, calls=%fused_computation | loop fusion | flops 327680 | bytes 2621442 | tf_op jit(solution)/shard_map/cond/branch_1_fun/jit(_where)/select_n | solution.py:474
  46.9 0.0 copy-start.9
  46.9 1.0 collective-permute-start
  47.8 0.0 collective-permute-start.1
  47.8 0.0 copy-done.3
  47.8 0.0 copy-done.5
  47.9 0.0 copy-done.6
  47.9 0.0 copy-done.7
  47.9 0.0 copy-done.8
  47.9 2.3 %early_field.1 = f32[2,6,128,128]{3,2,1,0:T(8,128)} custom-call(s32[1]{0:T(128)} %get-tuple-element.27.mine, f32[2,5,128,128]{3,2,1,0:T(8,128)S(1)} %copy-done.3, f32[2,5,128,128]{3,2,1,0:T(8,128)S(1)} %copy-done.5, f32[3,128,128]{2,1,0:T(8,128)S(1)} %copy-done.8, bf16[256,768]{1,0:T(8,128)(2,1)S(1)} %copy-done.6, bf16[768,256]{1,0:T(8,128)(2,1)S(1)} %copy-done.7), custom_call_target="tpu_custom_call" | custom-call | tf_op jit(solution)/shard_map/cond/branch_1_fun/early_field/pallas_call | solution.py:465
  50.1 31.5 %all-to-all-done = f32[5248,1,128]{2,1,0:T(1,128)S(1)} async-done(((f32[5248,1,128]{2,1,0:T(1,128)}), f32[5248,1,128]{2,1,0:T(1,128)S(1)}, u32[]{:S(2)}, u32[]{:S(2)}) %all-to-all-start) | async-done | bytes 2687008 | tf_op jit(solution)/shard_map/cond/branch_1_fun/all_to_all | solution.py:476
  81.6 0.0 copy-done.9
  81.6 5.2 %pick.1 = (f32[1024,128]{1,0:T(8,128)}, f32[1024,128]{1,0:T(8,128)}) custom-call(s32[1]{0:T(128)} %get-tuple-element.27.mine, f32[5248,128]{1,0:T(8,128)S(1)} %bitcast.17, s32[8,1024]{1,0:T(8,128)S(1)} %copy-done.9), custom_call_target="tpu_custom_call" | custom-call | tf_op jit(solution)/shard_map/cond/branch_1_fun/pick/pallas_call | solution.py:479
  86.8 8.4 %collective-permute-done.1 = f32[4,16,128]{2,1,0:T(8,128)} collective-permute-done((f32[4,16,128]{2,1,0:T(8,128)S(1)}, f32[4,16,128]{2,1,0:T(8,128)}, u32[]{:S(2)}, u32[]{:S(2)}) %collective-permute-start.1) | collective-permute-done | bytes 32800 | tf_op jit(solution)/shard_map/cond/branch_1_fun/ppermute | solution.py:381
  95.2 0.0 collective-permute-done
  95.2 0.0 collective-permute-done.5.piece_b0
  95.2 0.0 collective-permute-done.6.piece_b1
  95.2 0.0 collective-permute-done.7.piece_b2
  95.3 4.8 %last_field.1 = f32[2,16,128,128]{3,2,1,0:T(8,128)} custom-call(s32[1]{0:T(128)} %bitcast.4.mine, f32[2,6,128,128]{3,2,1,0:T(8,128)} %get-tuple-element.65.early, f32[2,2,128,128]{3,2,1,0:T(8,128)S(1)} %collective-permute-done.5.piece_b0, f32[2,2,128,128]{3,2,1,0:T(8,128)S(1)} %collective-permute-done.6.piece_b1, ...), custom_call_target="tpu_custom_call" | custom-call | tf_op jit(solution)/shard_map/last_field/pallas_call | solution.py:504
Async XLA Ops:
  2.0 31.9 %collective-permute-start.2 = (f32[2,5,128,128]{3,2,1,0:T(8,128)S(1)}, f32[2,5,128,128]{3,2,1,0:T(8,128)S(1)}, u32[]{:S(2)}, u32[]{:S(2)}) collective-permute-start(f32[2,5,128,128]{3,2,1,0:T(8,128)S(1)} %get-tuple-element.82), channel_id=1, source_target_pairs={{0,2},{2,4},{4,6},{6,8},{8,10},{10,12},{12,14},{14,16},{16,18},{18... | collective-permute-start | bytes 1966088 | tf_op jit(solution)/shard_map/ppermute | solution.py:413
  5.5 28.4 %collective-permute-start.3 = (f32[2,5,128,128]{3,2,1,0:T(8,128)S(1)}, f32[2,5,128,128]{3,2,1,0:T(8,128)S(1)}, u32[]{:S(2)}, u32[]{:S(2)}) collective-permute-start(f32[2,5,128,128]{3,2,1,0:T(8,128)S(1)} %get-tuple-element.81), channel_id=1, source_target_pairs={{1,3},{3,5},{5,7},{7,9},{9,11},{11,13},{13,15},{15,17},{17,19},{19... | collective-permute-start | bytes 1966088 | tf_op jit(solution)/shard_map/ppermute | solution.py:414
  16.0 14.1 %collective-permute-start.4 = (f32[4,16,128]{2,1,0:T(8,128)S(1)}, f32[4,16,128]{2,1,0:T(8,128)S(1)}, u32[]{:S(2)}, u32[]{:S(2)}) collective-permute-start(f32[4,16,128]{2,1,0:T(8,128)S(1)} %get-tuple-element.63), channel_id=1, source_target_pairs={{0,1},{1,2},{2,3},{3,4},{4,5},{5,6},{6,7},{7,8},{8,9},{9,10},{10,1... | collective-permute-start | bytes 98312 | tf_op jit(solution)/shard_map/ppermute | solution.py:381
  16.0 79.2 %collective-permute-start.5 = (f32[2,2,128,128]{3,2,1,0:T(8,128)}, f32[2,2,128,128]{3,2,1,0:T(8,128)S(1)}, u32[]{:S(2)}, u32[]{:S(2)}) collective-permute-start(f32[2,2,128,128]{3,2,1,0:T(8,128)} %get-tuple-element.66), channel_id=1, source_target_pairs={{0,2},{1,3},{2,4},{3,5},{4,6},{5,7},{6,8},{7,9},{8,10},{9,11},{10,... | collective-permute-start | bytes 786440 | tf_op jit(solution)/shard_map/ppermute | solution.py:381
  17.6 77.6 %collective-permute-start.6 = (f32[2,2,128,128]{3,2,1,0:T(8,128)}, f32[2,2,128,128]{3,2,1,0:T(8,128)S(1)}, u32[]{:S(2)}, u32[]{:S(2)}) collective-permute-start(f32[2,2,128,128]{3,2,1,0:T(8,128)} %get-tuple-element.67), channel_id=1, source_target_pairs={{0,2},{1,3},{2,4},{3,5},{4,6},{5,7},{6,8},{7,9},{8,10},{9,11},{10,... | collective-permute-start | bytes 786440 | tf_op jit(solution)/shard_map/ppermute | solution.py:381
  30.1 65.2 %collective-permute-start.7 = (f32[2,2,128,128]{3,2,1,0:T(8,128)}, f32[2,2,128,128]{3,2,1,0:T(8,128)S(1)}, u32[]{:S(2)}, u32[]{:S(2)}) collective-permute-start(f32[2,2,128,128]{3,2,1,0:T(8,128)} %get-tuple-element.68), channel_id=1, source_target_pairs={{0,2},{1,3},{2,4},{3,5},{4,6},{5,7},{6,8},{7,9},{8,10},{9,11},{10,... | collective-permute-start | bytes 786440 | tf_op jit(solution)/shard_map/ppermute | solution.py:381
  30.1 1.0 %copy-start = (f32[1024,128]{1,0:T(8,128)S(1)}, f32[1024,128]{1,0:T(8,128)}, u32[]{:S(2)}) copy-start(f32[1024,128]{1,0:T(8,128)} %get-tuple-element.61.phases1) | copy-start | bytes 1572868
  31.1 1.0 %copy-start.1 = (f32[1024,128]{1,0:T(8,128)S(1)}, f32[1024,128]{1,0:T(8,128)}, u32[]{:S(2)}) copy-start(f32[1024,128]{1,0:T(8,128)} %get-tuple-element.62.energies1) | copy-start | bytes 1572868
  34.0 0.8 copy-start.2
  34.0 1.1 %copy-start.4 = (f32[2,5,128,128]{3,2,1,0:T(8,128)}, f32[2,5,128,128]{3,2,1,0:T(8,128)S(1)}, u32[]{:S(2)}) copy-start(f32[2,5,128,128]{3,2,1,0:T(8,128)S(1)} %get-tuple-element.29.piece_1) | copy-start | bytes 1966084 | tf_op jit(solution)/shard_map/cond
  35.0 46.6 %all-to-all-start = ((f32[5248,1,128]{2,1,0:T(1,128)}), f32[5248,1,128]{2,1,0:T(1,128)S(1)}, u32[]{:S(2)}, u32[]{:S(2)}) async-start(f32[5248,1,128]{2,1,0:T(1,128)} %bitcast.20), calls=%async_computation | async-start | bytes 5373952 | tf_op jit(solution)/shard_map/cond/branch_1_fun/all_to_all | solution.py:476
  44.4 3.4 %copy-start.3 = (f32[2,5,128,128]{3,2,1,0:T(8,128)S(1)}, f32[2,5,128,128]{3,2,1,0:T(8,128)}, u32[]{:S(2)}) copy-start(f32[2,5,128,128]{3,2,1,0:T(8,128)} %copy-done.2) | copy-start | bytes 1966084 | tf_op jit(solution)/shard_map/cond
  44.5 3.4 %copy-start.5 = (f32[2,5,128,128]{3,2,1,0:T(8,128)S(1)}, f32[2,5,128,128]{3,2,1,0:T(8,128)}, u32[]{:S(2)}) copy-start(f32[2,5,128,128]{3,2,1,0:T(8,128)} %copy-done.4) | copy-start | bytes 1966084 | tf_op jit(solution)/shard_map/cond
  44.5 3.4 %copy-start.6 = (bf16[256,768]{1,0:T(8,128)(2,1)S(1)}, bf16[256,768]{1,0:T(8,128)(2,1)}, u32[]{:S(2)}) copy-start(bf16[256,768]{1,0:T(8,128)(2,1)} %get-tuple-element.31.left) | copy-start | bytes 1179652 | tf_op jit(solution)/shard_map/cond
  44.5 3.4 %copy-start.7 = (bf16[768,256]{1,0:T(8,128)(2,1)S(1)}, bf16[768,256]{1,0:T(8,128)(2,1)}, u32[]{:S(2)}) copy-start(bf16[768,256]{1,0:T(8,128)(2,1)} %get-tuple-element.32.right) | copy-start | bytes 1179652 | tf_op jit(solution)/shard_map/cond
  44.5 3.4 %copy-start.8 = (f32[3,128,128]{2,1,0:T(8,128)S(1)}, f32[3,128,128]{2,1,0:T(8,128)}, u32[]{:S(2)}) copy-start(f32[3,128,128]{2,1,0:T(8,128)} %get-tuple-element.30.beam) | copy-start | bytes 589828 | tf_op jit(solution)/shard_map/cond
  46.9 34.7 %copy-start.9 = (s32[8,1024]{1,0:T(8,128)S(1)}, s32[8,1024]{1,0:T(8,128)}, u32[]{:S(2)}) copy-start(s32[8,1024]{1,0:T(8,128)} %get-tuple-element.39.places) | copy-start | bytes 98308 | tf_op jit(solution)/shard_map/cond
  46.9 48.4 %collective-permute-start = (f32[2,5,128,128]{3,2,1,0:T(8,128)}, f32[2,5,128,128]{3,2,1,0:T(8,128)}, u32[]{:S(2)}, u32[]{:S(2)}) collective-permute-start(f32[2,5,128,128]{3,2,1,0:T(8,128)} %slice_select_fusion), channel_id=1, source_target_pairs={{0,2},{1,3},{2,4},{3,5},{4,6},{5,7},{6,0},{7,1},{8,10},{9,11},{10,... | collective-permute-start | bytes 1966088 | tf_op jit(solution)/shard_map/cond/branch_1_fun/ppermute | solution.py:475
  47.8 47.4 %collective-permute-start.1 = (f32[4,16,128]{2,1,0:T(8,128)S(1)}, f32[4,16,128]{2,1,0:T(8,128)}, u32[]{:S(2)}, u32[]{:S(2)}) collective-permute-start(f32[4,16,128]{2,1,0:T(8,128)S(1)} %get-tuple-element.37), channel_id=1, source_target_pairs={{0,1},{1,2},{2,3},{3,4},{4,5},{5,6},{6,7},{7,8},{8,9},{9,10},{10,1... | collective-permute-start | bytes 98312 | tf_op jit(solution)/shard_map/cond/branch_1_fun/ppermute | solution.py:381

commit v9 on v8

--- a/solution.py
+++ b/solution.py
@@ -25,8 +25,8 @@
 MESSAGE = 2 * CAP + 1
 ROWS = PEERS * MESSAGE
 BATCH = 32
-EARLY, LATE = 5, 11
-MIDDLE = ((5, 7), (7, 9), (9, 11))
+EARLY, LATE = 5, 13
+MIDDLE = ((5, 7), (7, 9), (9, 11), (11, 13))
 VMEM_LIMIT = 24 * 1024 * 1024
 HIGHEST = lax.Precision.HIGHEST
 
@@ -120,8 +120,8 @@
 
 def first_kernel(
     mine, field_hbm, profile_hbm, bins_hbm, jitter_hbm, energy_hbm, delays_hbm, left_hbm, right_hbm,
-    send_hbm, phases_hbm, energies_hbm, places_hbm, beam, small, middle_0, middle_1, middle_2,
-    field, profile, bins, jitter, energy, delays, left, right, acc, send, phases, energies, places, index_v, index, sems,
+    send_hbm, phases, energies, places_hbm, beam, small, middle_0, middle_1, middle_2, middle_3,
+    field, profile, bins, jitter, energy, delays, left, right, acc, send, places, index_v, index, sems,
 ):
     pairs = [
         (profile_hbm, profile), (left_hbm, left), (right_hbm, right), (delays_hbm, delays),
@@ -148,10 +148,10 @@
     beam[2] = p
     copies[4].wait()
     kept = [pltpu.make_async_copy(places, places_hbm, sems.at[8])]
-    for middle, (low, high) in zip((middle_0, middle_1, middle_2), MIDDLE):
+    for middle, (low, high) in zip((middle_0, middle_1, middle_2, middle_3), MIDDLE):
         for c in range(2):
             span = pl.ds(low, high - low)
-            kept.append(pltpu.make_async_copy(field.at[c, span], middle.at[c], sems.at[10 + len(kept)]))
+            kept.append(pltpu.make_async_copy(field.at[c, span], middle.at[c], sems.at[8 + len(kept)]))
     for copy in kept:
         copy.start()
 
@@ -184,10 +184,6 @@
         return carry
 
     lax.fori_loop(0, GROUPS, push, 0)
-    kept.append(pltpu.make_async_copy(phases, phases_hbm, sems.at[9]))
-    kept.append(pltpu.make_async_copy(energies, energies_hbm, sems.at[10]))
-    for copy in kept[7:]:
-        copy.start()
     to_scalar.wait()
 
     def put(n, carry):
@@ -196,8 +192,8 @@
         ph = [phases[pl.ds(base + m, 1)] for m in range(BATCH)]
         en = [energies[pl.ds(base + m, 1)] for m in range(BATCH)]
         for m in range(BATCH):
-            send[pl.ds(spots[m], 1)] = ph[m]
-            send[pl.ds(spots[m] + CAP, 1)] = en[m]
+            send[spots[m]] = ph[m]
+            send[spots[m] + CAP] = en[m]
         return carry
 
     lax.fori_loop(0, COUNT // BATCH, put, 0)
@@ -208,9 +204,6 @@
     next_im = acc[3] + gain * (bre * self_im + bim * self_re)
     for n, part in enumerate((next_re, next_im, bre, bim)):
         small[n] = part
-    note = one_row([next_re, next_im])
-    for n in range(PEERS):
-        send[n * MESSAGE + 2 * CAP : (n + 1) * MESSAGE] = note
     out = pltpu.make_async_copy(send, send_hbm, sems.at[0])
     out.start()
     for copy in kept:
@@ -235,23 +228,27 @@
     return jnp.where(flag, rolled, value)
 
 
-def second_kernel(mine, phases1, energies1, arrived, small, acc):
-    for n in range(4):
+def second_kernel(mine, phases1, energies1, arrived, own, send_in, send, acc, note, sems):
+    del send_in
+    for n in range(2):
         acc[n] = carried(arrived[n], mine[0] == 0)
 
     def push(k, carry):
         rows = rows_of(k)
         ph, _ = pushed(phases1[rows], energies1[rows], acc[0, pl.ds(k, 1)], acc[1, pl.ds(k, 1)])
         c, s = cos_sin(ph)
-        small[0, pl.ds(k, 1)] = jnp.sum(c, axis=0, keepdims=True)
-        small[1, pl.ds(k, 1)] = jnp.sum(s, axis=0, keepdims=True)
+        acc[2, pl.ds(k, 1)] = jnp.sum(c, axis=0, keepdims=True)
+        acc[3, pl.ds(k, 1)] = jnp.sum(s, axis=0, keepdims=True)
         return carry
 
     lax.fori_loop(0, GROUPS, push, 0)
-    small[0] = lane_total(small[0]) * (1.0 / (NBS * BLOCK))
-    small[1] = lane_total(small[1]) * (-1.0 / (NBS * BLOCK))
-    small[2] = acc[2]
-    small[3] = acc[3]
+    mean = 1.0 / (NBS * BLOCK)
+    note[0] = one_row([own[n] for n in range(4)] + [lane_total(acc[2]) * mean, lane_total(acc[3]) * -mean])
+    copies = [pltpu.make_async_copy(note.at[0], send.at[n * MESSAGE + 2 * CAP], sems.at[n]) for n in range(PEERS)]
+    for copy in copies:
+        copy.start()
+    for copy in copies:
+        copy.wait()
 
 
 def wide_halves(x):
@@ -259,14 +256,21 @@
     return high, (x - high.astype(jnp.float32)).astype(jnp.bfloat16)
 
 
-def pick_kernel(mine, recv, places, phases_hbm, energies_hbm, index_v, index, amps, phases, energies, sems):
+def pick_kernel(mine, recv, places, phases_hbm, energies_hbm, small, index_v, index, amps, notes, phases, energies, sems):
     me = mine[0]
     source = (me - places[0:1] + PEERS) % PEERS
     index_v[...] = folded(source * MESSAGE + places[1:2])
     to_scalar = pltpu.make_async_copy(index_v, index, sems.at[0])
     to_scalar.start()
     lane = lax.broadcasted_iota(jnp.int32, (128, 128), 1)
-    sheet = recv[pl.ds(2 * CAP, PEERS, MESSAGE), :]
+    for n in range(PEERS):
+        notes[n : n + 1] = recv[n * MESSAGE + 2 * CAP]
+    sheet = notes[...]
+    near = jnp.broadcast_to(notes[pl.ds((me + PEERS - 1) % PEERS, 1)], (128, 128)).T
+    far = jnp.broadcast_to(notes[pl.ds((me + PEERS - 2) % PEERS, 1)], (128, 128)).T
+    for n in range(2):
+        small[n] = carried(near[(4 + n) * GROUPS : (5 + n) * GROUPS], me == 0)
+        small[2 + n] = carried(far[(2 + n) * GROUPS : (3 + n) * GROUPS], me < 2)
     wrapped = jnp.concatenate([sheet[127:128, 127:128], sheet[127:128, :127]], axis=1)
     wrapped = jnp.where(lane[0:1] % GROUPS == 0, 0.0, wrapped)
     sheet = jnp.concatenate([wrapped, sheet[:127]], axis=0)
@@ -281,8 +285,8 @@
     def get(n, carry):
         base = pl.multiple_of(n * BATCH, BATCH)
         spots = [index[n // (128 // BATCH), n % (128 // BATCH) * BATCH + m] for m in range(BATCH)]
-        ph = [recv[pl.ds(spot, 1)] for spot in spots]
-        en = [recv[pl.ds(spot + CAP, 1)] for spot in spots]
+        ph = [recv[spot] for spot in spots]
+        en = [recv[spot + CAP] for spot in spots]
         for m in range(BATCH):
             phases[pl.ds(base + m, 1)] = ph[m]
             energies[pl.ds(base + m, 1)] = en[m]
@@ -327,11 +331,11 @@
 
 
 def last_kernel(
-    mine, early, piece_b0, piece_b1, piece_b2, piece_c, small, beam, left, right, out_hbm, acc, rest, out, sems
+    mine, early, piece_b0, piece_b1, piece_b2, piece_b3, piece_c, small, beam, left, right, out_hbm, acc, rest, out, sems
 ):
     me = mine[0]
     for n in range(4):
-        acc[n] = GAIN * carried(small[n], me == 0)
+        acc[n] = GAIN * small[n]
     copies = []
 
     def plane(c, k):
@@ -351,7 +355,7 @@
             copies[-1].start()
 
     finish(0, EARLY)
-    planes = [(piece[0, k], piece[1, k]) for piece in (piece_b0, piece_b1, piece_b2) for k in range(piece.shape[1])]
+    planes = [(piece[0, k], piece[1, k]) for piece in (piece_b0, piece_b1, piece_b2, piece_b3) for k in range(piece.shape[1])]
     for k, (re, im) in enumerate(twice_diffracted(planes, left, right)):
         rest[0, k] = re
         rest[1, k] = im
@@ -410,22 +414,22 @@
     left_one = jnp.asarray(np.concatenate(one, axis=0), jnp.float32)
     right_one = jnp.asarray(right_form(*one), jnp.float32)
     core = mine[0] % 2
-    shared_0 = lax.ppermute(lax.dynamic_slice_in_dim(field, core * LATE, EARLY, 1), "cuts", early_pairs(0))
-    shared_1 = lax.ppermute(lax.dynamic_slice_in_dim(field, (1 - core) * LATE, EARLY, 1), "cuts", early_pairs(1))
+    shared_0 = lax.ppermute(lax.dynamic_slice_in_dim(field, core * (GROUPS - EARLY), EARLY, 1), "cuts", early_pairs(0))
+    shared_1 = lax.ppermute(lax.dynamic_slice_in_dim(field, (1 - core) * (GROUPS - EARLY), EARLY, 1), "cuts", early_pairs(1))
     operands = [field, profile, bins, jitter, energies, delays.reshape(GROUPS, 1, NBS), left_one, right_one]
     send, phases1, energies1, places, beam, small1, *sources = pl.pallas_call(
         first_kernel,
         out_shape=(
-            pltpu.HBM((ROWS, BLOCK), jnp.float32),
-            pltpu.HBM((COUNT, BLOCK), jnp.float32),
-            pltpu.HBM((COUNT, BLOCK), jnp.float32),
+            pltpu.HBM((ROWS, 1, BLOCK), jnp.float32),
+            shape(COUNT, BLOCK),
+            shape(COUNT, BLOCK),
             pltpu.HBM((8, COUNT), jnp.int32),
             pltpu.HBM((3, GRID, GRID), jnp.float32),
             shape(4, GROUPS, 128),
             *[pltpu.HBM((2, high - low, GRID, GRID), jnp.float32) for low, high in MIDDLE],
         ),
         in_specs=[scalar] + [remain] * 8,
-        out_specs=(remain,) * 4 + (whole(),) * 2 + (remain,) * len(MIDDLE),
+        out_specs=(remain, whole(), whole(), remain, whole(), whole()) + (remain,) * len(MIDDLE),
         scratch_shapes=[
             vmem(2, GROUPS, GRID, GRID),
             vmem(GRID, GRID),
@@ -436,9 +440,7 @@
             vmem(2 * GRID, GRID),
             vmem(2 * GRID, 2 * GRID),
             vmem(6, GROUPS, 128),
-            vmem(ROWS, BLOCK),
-            vmem(COUNT, BLOCK),
-            vmem(COUNT, BLOCK),
+            vmem(ROWS, 1, BLOCK),
             vmem(8, COUNT, dtype=jnp.int32),
             vmem(8, 128, dtype=jnp.int32),
             pltpu.SMEM((8, 128), jnp.int32),
@@ -448,20 +450,21 @@
         name="push_place",
     )(mine, *[in_hbm(value) for value in operands])
     arrived1 = shifted(small1, "cuts", 1)
-    small2 = pl.pallas_call(
+    send = pl.pallas_call(
         second_kernel,
-        out_shape=shape(4, GROUPS, 128),
-        in_specs=[scalar] + [whole()] * 3,
-        out_specs=whole(),
-        scratch_shapes=[vmem(4, GROUPS, 128)],
+        out_shape=pltpu.HBM((ROWS, 1, BLOCK), jnp.float32),
+        in_specs=[scalar] + [whole()] * 4 + [remain],
+        out_specs=remain,
+        scratch_shapes=[vmem(4, GROUPS, 128), vmem(1, 1, 128), pltpu.SemaphoreType.DMA((PEERS,))],
+        input_output_aliases={5: 0},
         compiler_params=params,
         name="second_push",
-    )(mine, phases1, energies1, arrived1)
+    )(mine, phases1, energies1, arrived1, small1, in_hbm(send))
     field_b = [shifted(source, "cuts", 2) for source in sources]
 
     left_two, right_two = deep_left(left_form(*two)), deep_right(right_form(*two))
 
-    def exchange(send, small2, places, field, shared_0, shared_1, beam):
+    def exchange(send, places, field, shared_0, shared_1, beam):
         early = pl.pallas_call(
             early_kernel,
             out_shape=shape(2, EARLY + 1, GRID, GRID),
@@ -471,20 +474,20 @@
             name="early_field",
         )(mine, shared_0, shared_1, beam, left_two, right_two)
         handed = jnp.where(core == 0, shared_1, shared_0)
-        source_c = jnp.where(mine[0] % 8 >= 6, handed, field[:, LATE:])
+        source_c = jnp.where(mine[0] % 8 >= 6, handed[:, LATE - GROUPS :], field[:, LATE:])
         field_c = lax.ppermute(source_c, "cuts", late_pairs())
-        recv = lax.all_to_all(send.reshape(ROWS, 1, BLOCK), "cuts", split_axis=0, concat_axis=0, tiled=True)
-        recv, early = lax.optimization_barrier((recv.reshape(ROWS, BLOCK), early))
-        arrived = shifted(small2, "cuts", 1)
-        phase_out, energy_out = pl.pallas_call(
+        recv = lax.all_to_all(send, "cuts", split_axis=0, concat_axis=0, tiled=True)
+        recv, early = lax.optimization_barrier((recv, early))
+        phase_out, energy_out, small = pl.pallas_call(
             pick_kernel,
-            out_shape=(shape(COUNT, BLOCK), shape(COUNT, BLOCK)),
+            out_shape=(shape(COUNT, BLOCK), shape(COUNT, BLOCK), shape(4, GROUPS, 128)),
             in_specs=[scalar] + [whole()] * 2,
-            out_specs=(remain,) * 2,
+            out_specs=(remain, remain, whole()),
             scratch_shapes=[
                 vmem(8, 128, dtype=jnp.int32),
                 pltpu.SMEM((8, 128), jnp.int32),
                 vmem(COUNT, 128),
+                vmem(PEERS, 128),
                 vmem(COUNT, BLOCK),
                 vmem(COUNT, BLOCK),
                 pltpu.SemaphoreType.DMA((9,)),
@@ -492,19 +495,19 @@
             compiler_params=params,
             name="pick",
         )(mine, recv, places)
-        return phase_out, energy_out, early, field_c, arrived
+        return phase_out, energy_out, early, field_c, small
 
     def refuse(*operands):
         sizes = [(COUNT, BLOCK)] * 2 + [(2, n, GRID, GRID) for n in (EARLY + 1, GROUPS - LATE)] + [(4, GROUPS, 128)]
         return tuple(jnp.zeros(size, jnp.float32) for size in sizes)
 
-    phase_out, energy_out, early, field_c, arrived = lax.cond(
-        mine[0] < PEERS, exchange, refuse, send, small2, places, field, shared_0, shared_1, beam
+    phase_out, energy_out, early, field_c, small = lax.cond(
+        mine[0] < PEERS, exchange, refuse, send, places, field, shared_0, shared_1, beam
     )
     out = pl.pallas_call(
         last_kernel,
         out_shape=shape(2, GROUPS, GRID, GRID),
-        in_specs=[scalar] + [whole()] * 9,
+        in_specs=[scalar] + [whole()] * 10,
         out_specs=remain,
         scratch_shapes=[
             vmem(4, GROUPS, 128),
@@ -514,7 +517,7 @@
         ],
         compiler_params=params,
         name="last_field",
-    )(mine, early, *field_b, field_c, arrived, in_hbm(beam), left_two, right_two)
+    )(mine, early, *field_b, field_c, small, in_hbm(beam), left_two, right_two)
     return (
         out.reshape(2, GROUPS, 1, GRID, GRID),
         phase_out.reshape(GROUPS, 1, NBS * BLOCK),

time: 100 us -> 92 us (0.920)
  waiting for transfers between devices: 49.2 us -> 35.9 us
  Pallas kernels: 23.8 us -> 27.4 us
  starting transfers between devices: 19.3 us -> 22.6 us
  local copies, waits for them, and re-layouts: 4.54 us -> 2.24 us
    ppermute x5, waiting for transfers between devices: 17.7 us -> 4.42 us  [shifted(): return lax.ppermute(value, axis, pairs)]
    all_to_all x1, starting transfers between devices: 9.38 us -> 11.9 us  [exchange(): recv = lax.all_to_all(send, 'cuts', split_axis=0, concat_axis=0, tiled=True)]
    unnamed x4 -> x2, local copies, waits for them, and re-layouts: 2.08 us -> 0.01 us
    pallas_call x2, Pallas kernels: 11.5 us -> 13.6 us  [the longest x1 9.54 us: per_device(): pl.pallas_call(first_kernel, out_shape=(pltpu.HBM((ROWS, 1, BLOCK), jnp.f...]
    pallas_call x1, Pallas kernels: 2.26 us -> 3.81 us  [exchange(): pl.pallas_call(early_kernel, out_shape=shape(2, EARLY + 1, GRID, GRID), i...]
  transfers between devices with their start and end apart: 9 -> 9, of which waited for: 3 -> 2; matrix products, arithmetic and copies ran while one was open for 2% -> 2% of each run, Pallas kernels for 19% -> 25%
where the time goes in v9:
time: 92 us; the launch traced here: 91.2 us
  waiting for transfers between devices  35.9 us (39%)
  Pallas kernels  27.4 us (30%)
  starting transfers between devices  22.6 us (25%)
  local copies, waits for them, and re-layouts  2.24 us (2%)
  other arithmetic  2.07 us (2%)
    all_to_all x1, waiting for transfers between devices, exchange(): recv = lax.all_to_all(send, 'cuts', split_axis=0, concat_axis=0, tiled=True)  31.5 us
    all_to_all x1, starting transfers between devices, exchange(): recv = lax.all_to_all(send, 'cuts', split_axis=0, concat_axis=0, tiled=True)  11.9 us
    pallas_call x1, Pallas kernels, per_device(): pl.pallas_call(first_kernel, out_shape=(pltpu.HBM((ROWS, 1, BLOCK), jnp.f...  9.54 us
    pallas_call x1, Pallas kernels, exchange(): pl.pallas_call(pick_kernel, out_shape=(shape(COUNT, BLOCK), shape(COUNT,...  5.26 us
    ppermute x5, starting transfers between devices, shifted(): return lax.ppermute(value, axis, pairs)  4.84 us
    pallas_call x1, Pallas kernels, per_device(): pl.pallas_call(last_kernel, out_shape=shape(2, GROUPS, GRID, GRID), in_sp...  4.8 us
    ppermute x5, waiting for transfers between devices, shifted(): return lax.ppermute(value, axis, pairs)  4.42 us
    pallas_call x1, Pallas kernels, per_device(): pl.pallas_call(second_kernel, out_shape=pltpu.HBM((ROWS, 1, BLOCK), jnp.f...  4.03 us
  transfers between devices with their start and end apart: 9, of which 2 were waited for; matrix products, arithmetic and copies ran while one was open for 2% of the time, Pallas kernels for 25%

profile of v9, /device:TPU:0, one launch (start us, length us, event | category | flops | bytes accessed | tf_op | source)
XLA Modules:
  0.0 91.2 jit_solution(11820808347134553291)
XLA Ops:
  0.7 1.4 %dynamic-slice_bitcast_fusion = (f32[2,5,128,128]{3,2,1,0:T(8,128)S(1)}, f32[2,5,128,128]{3,2,1,0:T(8,128)S(1)}) fusion(f32[2,16,1,128,128]{4,3,2,1,0:T(8,128)} %param.12, s32[]{:T(128)S(6)} %select_n.35, s32[]{:T(128)S(6)} %select_n.34), kind=kLoop, calls=%fused_computation.2 | loop fusion | bytes 2621448 | tf_op jit(solution)/shard_map/dynamic_slice | solution.py:418
  2.1 1.5 %collective-permute-start.3 = (f32[2,5,128,128]{3,2,1,0:T(8,128)S(1)}, f32[2,5,128,128]{3,2,1,0:T(8,128)}, u32[]{:S(2)}, u32[]{:S(2)}) collective-permute-start(f32[2,5,128,128]{3,2,1,0:T(8,128)S(1)} %get-tuple-element.78), channel_id=1, source_target_pairs={{1,3},{3,5},{5,7},{7,9},{9,11},{11,13},{13,15},{15,17},{17,19},{19... | collective-permute-start | bytes 1966088 | tf_op jit(solution)/shard_map/ppermute | solution.py:418
  3.6 3.5 %collective-permute-start.2 = (f32[2,5,128,128]{3,2,1,0:T(8,128)S(1)}, f32[2,5,128,128]{3,2,1,0:T(8,128)S(1)}, u32[]{:S(2)}, u32[]{:S(2)}) collective-permute-start(f32[2,5,128,128]{3,2,1,0:T(8,128)S(1)} %get-tuple-element.79), channel_id=1, source_target_pairs={{0,2},{2,4},{4,6},{6,8},{8,10},{10,12},{12,14},{14,16},{16,18},{18... | collective-permute-start | bytes 1966088 | tf_op jit(solution)/shard_map/ppermute | solution.py:417
  7.0 9.5 %push_place.1 = (f32[5248,1,128]{2,1,0:T(1,128)}, f32[1024,128]{1,0:T(8,128)S(1)}, f32[1024,128]{1,0:T(8,128)S(1)}, s32[8,1024]{1,0:T(8,128)}, f32[3,128,128]{2,...) custom-call(s32[1]{0:T(128)} %bitcast.2.mine, ...), custom_call_target="tpu_custom_call" | custom-call | tf_op jit(solution)/shard_map/push_place/pallas_call | solution.py:420
  16.6 0.1 collective-permute-start.1
  16.7 1.6 %collective-permute-start.4 = (f32[2,2,128,128]{3,2,1,0:T(8,128)}, f32[2,2,128,128]{3,2,1,0:T(8,128)S(1)}, u32[]{:S(2)}, u32[]{:S(2)}) collective-permute-start(f32[2,2,128,128]{3,2,1,0:T(8,128)} %get-tuple-element.65), channel_id=1, source_target_pairs={{0,2},{1,3},{2,4},{3,5},{4,6},{5,7},{6,8},{7,9},{8,10},{9,11},{10,... | collective-permute-start | bytes 786440 | tf_op jit(solution)/shard_map/ppermute | solution.py:385
  18.2 3.2 %collective-permute-start.5 = (f32[2,2,128,128]{3,2,1,0:T(8,128)}, f32[2,2,128,128]{3,2,1,0:T(8,128)S(1)}, u32[]{:S(2)}, u32[]{:S(2)}) collective-permute-start(f32[2,2,128,128]{3,2,1,0:T(8,128)} %get-tuple-element.66), channel_id=1, source_target_pairs={{0,2},{1,3},{2,4},{3,5},{4,6},{5,7},{6,8},{7,9},{8,10},{9,11},{10,... | collective-permute-start | bytes 786440 | tf_op jit(solution)/shard_map/ppermute | solution.py:385
  21.4 4.4 %collective-permute-done.1.arrived = f32[4,16,128]{2,1,0:T(8,128)S(1)} collective-permute-done((f32[4,16,128]{2,1,0:T(8,128)S(1)}, f32[4,16,128]{2,1,0:T(8,128)S(1)}, u32[]{:S(2)}, u32[]{:S(2)}) %collective-permute-start.1) | collective-permute-done | bytes 32800 | tf_op jit(solution)/shard_map/ppermute | solution.py:385
  25.8 0.0 collective-permute-start.6
  25.9 0.0 collective-permute-done.3
  25.9 0.0 collective-permute-start.7
  25.9 0.0 copy-start.1
  25.9 4.0 %second_push.1 = f32[5248,1,128]{2,1,0:T(1,128)} custom-call(s32[1]{0:T(128)} %bitcast.2.mine, f32[1024,128]{1,0:T(8,128)S(1)} %get-tuple-element.58.phases1, f32[1024,128]{1,0:T(8,128)S(1)} %get-tuple-element.59.energies1, f32[4,16,128]{2,1,0:T(8,128)S(1)} %collective-permute-done.1.arrived, ...), custom_call_target="tpu_custom_call", output_to_operand_aliasing={{}: (5, {})} | custom-call | tf_op jit(solution)/shard_map/second_push/pallas_call | solution.py:453
  29.9 0.0 collective-permute-done.2
  29.9 0.0 copy-done.1
  29.9 56.4 %conditional.1 = (f32[2,6,128,128]{3,2,1,0:T(8,128)}, f32[2,3,128,128]{3,2,1,0:T(8,128)}, f32[4,16,128]{2,1,0:T(8,128)S(1)}, f32[16,1,8192]{2,1,0:T(1,128)}, f32[16,1,8192]{2,1,0:T(1,128)}) conditional(s32[]{:T(128)} %convert_element_type.3, () %tuple.21, (f32[5248,1,128]{2,1,0:T(1,128)}, s32[1]{0:T(128)}, f32[2,5,128,128]{3,2,1,0:T(8,128)S(1)}, ...), branch_computations={%region_0.1_spmd, %region_1.2_spmd} | conditional | flops 196621 | bytes 13828365 | solution.py:504
  29.9 0.0 copy-start
  30.0 0.8 copy-done
  30.8 11.9 %all-to-all-start = ((f32[5248,1,128]{2,1,0:T(1,128)}), f32[5248,1,128]{2,1,0:T(1,128)S(1)}, u32[]{:S(2)}, u32[]{:S(2)}) async-start(f32[5248,1,128]{2,1,0:T(1,128)} %get-tuple-element.24), calls=%async_computation | async-start | bytes 5373952 | tf_op jit(solution)/shard_map/cond/branch_1_fun/all_to_all | solution.py:479
  42.7 2.1 %fusion = f32[2,3,128,128]{3,2,1,0:T(8,128)} fusion(f32[2,5,128,128]{3,2,1,0:T(8,128)} %copy-done, f32[2,5,128,128]{3,2,1,0:T(8,128)} %get-tuple-element.27.piece_1, f32[2,16,128,128]{3,2,1,0:T(8,128)} %get-tuple-element.34, pred[]{:T(512)S(6)} %eq.5, pred[]{:T(512)S(6)} %ge.2), kind=kLoop, calls=%fused_computation.1 | loop fusion | flops 196608 | bytes 1572866 | tf_op jit(solution)/shard_map/cond/branch_1_fun/jit(_where)/select_n | solution.py:477
  44.8 1.0 %collective-permute-start = (f32[2,3,128,128]{3,2,1,0:T(8,128)}, f32[2,3,128,128]{3,2,1,0:T(8,128)}, u32[]{:S(2)}, u32[]{:S(2)}) collective-permute-start(f32[2,3,128,128]{3,2,1,0:T(8,128)} %fusion), channel_id=1, source_target_pairs={{0,2},{1,3},{2,4},{3,5},{4,6},{5,7},{6,0},{7,1},{8,10},{9,11},{10,... | collective-permute-start | bytes 1179656 | tf_op jit(solution)/shard_map/cond/branch_1_fun/ppermute | solution.py:478
  45.7 3.8 %early_field.1 = f32[2,6,128,128]{3,2,1,0:T(8,128)} custom-call(s32[1]{0:T(128)} %get-tuple-element.25.mine, f32[2,5,128,128]{3,2,1,0:T(8,128)} %copy-done, f32[2,5,128,128]{3,2,1,0:T(8,128)} %get-tuple-element.27.piece_1, f32[3,128,128]{2,1,0:T(8,128)} %get-tuple-element.28.beam, bf16[256,768]{1,0:T(8,128)(2,1)} %get-tuple-element.29.left, ...), custom_call_target="tpu_custom_call" | custom-call | tf_op jit(solution)/shard_map/cond/branch_1_fun/early_field/pallas_call | solution.py:468
  49.5 31.5 %all-to-all-done.recv = f32[5248,1,128]{2,1,0:T(1,128)S(1)} async-done(((f32[5248,1,128]{2,1,0:T(1,128)}), f32[5248,1,128]{2,1,0:T(1,128)S(1)}, u32[]{:S(2)}, u32[]{:S(2)}) %all-to-all-start) | async-done | bytes 2687008 | tf_op jit(solution)/shard_map/cond/branch_1_fun/all_to_all | solution.py:479
  81.0 5.3 %pick.1 = (f32[1024,128]{1,0:T(8,128)}, f32[1024,128]{1,0:T(8,128)}, f32[4,16,128]{2,1,0:T(8,128)S(1)}) custom-call(s32[1]{0:T(128)} %get-tuple-element.25.mine, f32[5248,1,128]{2,1,0:T(1,128)S(1)} %all-to-all-done.recv, s32[8,1024]{1,0:T(8,128)S(1)} %get-tuple-element.36.places), custom_call_target="tpu_custom_call" | custom-call | tf_op jit(solution)/shard_map/cond/branch_1_fun/pick/pallas_call | solution.py:481
  86.3 0.0 collective-permute-done
  86.3 0.0 collective-permute-done.4.piece_b0
  86.3 0.0 collective-permute-done.5.piece_b1
  86.3 0.0 collective-permute-done.6.piece_b2
  86.4 0.0 collective-permute-done.7.piece_b3
  86.4 4.8 %last_field.1 = f32[2,16,128,128]{3,2,1,0:T(8,128)} custom-call(s32[1]{0:T(128)} %bitcast.2.mine, f32[2,6,128,128]{3,2,1,0:T(8,128)} %get-tuple-element.64.early, f32[2,2,128,128]{3,2,1,0:T(8,128)S(1)} %collective-permute-done.4.piece_b0, f32[2,2,128,128]{3,2,1,0:T(8,128)S(1)} %collective-permute-done.5.piece_b1, ...), custom_call_target="tpu_custom_call" | custom-call | tf_op jit(solution)/shard_map/last_field/pallas_call | solution.py:507
Async XLA Ops:
  2.1 23.8 %collective-permute-start.3 = (f32[2,5,128,128]{3,2,1,0:T(8,128)S(1)}, f32[2,5,128,128]{3,2,1,0:T(8,128)}, u32[]{:S(2)}, u32[]{:S(2)}) collective-permute-start(f32[2,5,128,128]{3,2,1,0:T(8,128)S(1)} %get-tuple-element.78), channel_id=1, source_target_pairs={{1,3},{3,5},{5,7},{7,9},{9,11},{11,13},{13,15},{15,17},{17,19},{19... | collective-permute-start | bytes 1966088 | tf_op jit(solution)/shard_map/ppermute | solution.py:418
  3.6 26.4 %collective-permute-start.2 = (f32[2,5,128,128]{3,2,1,0:T(8,128)S(1)}, f32[2,5,128,128]{3,2,1,0:T(8,128)S(1)}, u32[]{:S(2)}, u32[]{:S(2)}) collective-permute-start(f32[2,5,128,128]{3,2,1,0:T(8,128)S(1)} %get-tuple-element.79), channel_id=1, source_target_pairs={{0,2},{2,4},{4,6},{6,8},{8,10},{10,12},{12,14},{14,16},{16,18},{18... | collective-permute-start | bytes 1966088 | tf_op jit(solution)/shard_map/ppermute | solution.py:417
  16.6 9.3 %collective-permute-start.1 = (f32[4,16,128]{2,1,0:T(8,128)S(1)}, f32[4,16,128]{2,1,0:T(8,128)S(1)}, u32[]{:S(2)}, u32[]{:S(2)}) collective-permute-start(f32[4,16,128]{2,1,0:T(8,128)S(1)} %get-tuple-element.60.own), channel_id=1, source_target_pairs={{0,1},{1,2},{2,3},{3,4},{4,5},{5,6},{6,7},{7,8},{8,9},{9,10},{10,1... | collective-permute-start | bytes 98312 | tf_op jit(solution)/shard_map/ppermute | solution.py:385
  16.7 69.7 %collective-permute-start.4 = (f32[2,2,128,128]{3,2,1,0:T(8,128)}, f32[2,2,128,128]{3,2,1,0:T(8,128)S(1)}, u32[]{:S(2)}, u32[]{:S(2)}) collective-permute-start(f32[2,2,128,128]{3,2,1,0:T(8,128)} %get-tuple-element.65), channel_id=1, source_target_pairs={{0,2},{1,3},{2,4},{3,5},{4,6},{5,7},{6,8},{7,9},{8,10},{9,11},{10,... | collective-permute-start | bytes 786440 | tf_op jit(solution)/shard_map/ppermute | solution.py:385
  18.2 68.1 %collective-permute-start.5 = (f32[2,2,128,128]{3,2,1,0:T(8,128)}, f32[2,2,128,128]{3,2,1,0:T(8,128)S(1)}, u32[]{:S(2)}, u32[]{:S(2)}) collective-permute-start(f32[2,2,128,128]{3,2,1,0:T(8,128)} %get-tuple-element.66), channel_id=1, source_target_pairs={{0,2},{1,3},{2,4},{3,5},{4,6},{5,7},{6,8},{7,9},{8,10},{9,11},{10,... | collective-permute-start | bytes 786440 | tf_op jit(solution)/shard_map/ppermute | solution.py:385
  25.8 60.5 %collective-permute-start.6 = (f32[2,2,128,128]{3,2,1,0:T(8,128)}, f32[2,2,128,128]{3,2,1,0:T(8,128)S(1)}, u32[]{:S(2)}, u32[]{:S(2)}) collective-permute-start(f32[2,2,128,128]{3,2,1,0:T(8,128)} %get-tuple-element.67), channel_id=1, source_target_pairs={{0,2},{1,3},{2,4},{3,5},{4,6},{5,7},{6,8},{7,9},{8,10},{9,11},{10,... | collective-permute-start | bytes 786440 | tf_op jit(solution)/shard_map/ppermute | solution.py:385
  25.9 60.5 %collective-permute-start.7 = (f32[2,2,128,128]{3,2,1,0:T(8,128)}, f32[2,2,128,128]{3,2,1,0:T(8,128)}, u32[]{:S(2)}, u32[]{:S(2)}) collective-permute-start(f32[2,2,128,128]{3,2,1,0:T(8,128)} %get-tuple-element.68), channel_id=1, source_target_pairs={{0,2},{1,3},{2,4},{3,5},{4,6},{5,7},{6,8},{7,9},{8,10},{9,11},{10,... | collective-permute-start | bytes 786440 | tf_op jit(solution)/shard_map/ppermute | solution.py:385
  25.9 4.1 %copy-start.1 = (s32[8,1024]{1,0:T(8,128)S(1)}, s32[8,1024]{1,0:T(8,128)}, u32[]{:S(2)}) copy-start(s32[8,1024]{1,0:T(8,128)} %get-tuple-element.63) | copy-start | bytes 98308
  29.9 0.8 copy-start
  30.8 50.3 %all-to-all-start = ((f32[5248,1,128]{2,1,0:T(1,128)}), f32[5248,1,128]{2,1,0:T(1,128)S(1)}, u32[]{:S(2)}, u32[]{:S(2)}) async-start(f32[5248,1,128]{2,1,0:T(1,128)} %get-tuple-element.24), calls=%async_computation | async-start | bytes 5373952 | tf_op jit(solution)/shard_map/cond/branch_1_fun/all_to_all | solution.py:479
  44.8 41.6 %collective-permute-start = (f32[2,3,128,128]{3,2,1,0:T(8,128)}, f32[2,3,128,128]{3,2,1,0:T(8,128)}, u32[]{:S(2)}, u32[]{:S(2)}) collective-permute-start(f32[2,3,128,128]{3,2,1,0:T(8,128)} %fusion), channel_id=1, source_target_pairs={{0,2},{1,3},{2,4},{3,5},{4,6},{5,7},{6,0},{7,1},{8,10},{9,11},{10,... | collective-permute-start | bytes 1179656 | tf_op jit(solution)/shard_map/cond/branch_1_fun/ppermute | solution.py:478

commit v10 on v9

--- a/solution.py
+++ b/solution.py
@@ -24,10 +24,10 @@
 CAP = 20
 MESSAGE = 2 * CAP + 1
 ROWS = PEERS * MESSAGE
-BATCH = 32
+BATCH = 16
 EARLY, LATE = 5, 13
-MIDDLE = ((5, 7), (7, 9), (9, 11), (11, 13))
-VMEM_LIMIT = 24 * 1024 * 1024
+MIDDLE = ((5, 7), (7, 9), (9, 13))
+VMEM_LIMIT = 16 * 1024 * 1024
 HIGHEST = lax.Precision.HIGHEST
 
 
@@ -120,7 +120,7 @@
 
 def first_kernel(
     mine, field_hbm, profile_hbm, bins_hbm, jitter_hbm, energy_hbm, delays_hbm, left_hbm, right_hbm,
-    send_hbm, phases, energies, places_hbm, beam, small, middle_0, middle_1, middle_2, middle_3,
+    send_hbm, phases, energies, places_hbm, beam, small, middle_0, middle_1, middle_2,
     field, profile, bins, jitter, energy, delays, left, right, acc, send, places, index_v, index, sems,
 ):
     pairs = [
@@ -148,7 +148,7 @@
     beam[2] = p
     copies[4].wait()
     kept = [pltpu.make_async_copy(places, places_hbm, sems.at[8])]
-    for middle, (low, high) in zip((middle_0, middle_1, middle_2, middle_3), MIDDLE):
+    for middle, (low, high) in zip((middle_0, middle_1, middle_2), MIDDLE):
         for c in range(2):
             span = pl.ds(low, high - low)
             kept.append(pltpu.make_async_copy(field.at[c, span], middle.at[c], sems.at[8 + len(kept)]))
@@ -196,7 +196,7 @@
             send[spots[m] + CAP] = en[m]
         return carry
 
-    lax.fori_loop(0, COUNT // BATCH, put, 0)
+    lax.fori_loop(0, COUNT // BATCH, put, 0, unroll=4)
     bre = lane_total(acc[4]) * (1.0 / (NBS * BLOCK))
     bim = lane_total(acc[5]) * (-1.0 / (NBS * BLOCK))
     gain = GAIN / GRID
@@ -228,7 +228,7 @@
     return jnp.where(flag, rolled, value)
 
 
-def second_kernel(mine, phases1, energies1, arrived, own, send_in, send, acc, note, sems):
+def second_kernel(mine, phases1, energies1, arrived, own, send_in, send, acc, note, sem):
     del send_in
     for n in range(2):
         acc[n] = carried(arrived[n], mine[0] == 0)
@@ -243,12 +243,11 @@
 
     lax.fori_loop(0, GROUPS, push, 0)
     mean = 1.0 / (NBS * BLOCK)
-    note[0] = one_row([own[n] for n in range(4)] + [lane_total(acc[2]) * mean, lane_total(acc[3]) * -mean])
-    copies = [pltpu.make_async_copy(note.at[0], send.at[n * MESSAGE + 2 * CAP], sems.at[n]) for n in range(PEERS)]
-    for copy in copies:
-        copy.start()
-    for copy in copies:
-        copy.wait()
+    row = one_row([own[n] for n in range(4)] + [lane_total(acc[2]) * mean, lane_total(acc[3]) * -mean])
+    note[...] = jnp.broadcast_to(row[None], (PEERS, 1, 128))
+    copy = pltpu.make_async_copy(note, send.at[:, 2 * CAP], sem)
+    copy.start()
+    copy.wait()
 
 
 def wide_halves(x):
@@ -294,7 +293,7 @@
 
     copies = []
     for quarter in range(4):
-        lax.fori_loop(quarter * COUNT // BATCH // 4, (quarter + 1) * COUNT // BATCH // 4, get, 0)
+        lax.fori_loop(quarter * COUNT // BATCH // 4, (quarter + 1) * COUNT // BATCH // 4, get, 0, unroll=4)
         for k in range(quarter * 4, quarter * 4 + 4):
             rows = slice(k * NBS, (k + 1) * NBS)
             re, im = amps[rows, k : k + 1], amps[rows, GROUPS + k : GROUPS + k + 1]
@@ -331,7 +330,7 @@
 
 
 def last_kernel(
-    mine, early, piece_b0, piece_b1, piece_b2, piece_b3, piece_c, small, beam, left, right, out_hbm, acc, rest, out, sems
+    mine, early, piece_b0, piece_b1, piece_b2, piece_c, small, beam, left, right, out_hbm, acc, rest, out, sems
 ):
     me = mine[0]
     for n in range(4):
@@ -355,7 +354,7 @@
             copies[-1].start()
 
     finish(0, EARLY)
-    planes = [(piece[0, k], piece[1, k]) for piece in (piece_b0, piece_b1, piece_b2, piece_b3) for k in range(piece.shape[1])]
+    planes = [(piece[0, k], piece[1, k]) for piece in (piece_b0, piece_b1, piece_b2) for k in range(piece.shape[1])]
     for k, (re, im) in enumerate(twice_diffracted(planes, left, right)):
         rest[0, k] = re
         rest[1, k] = im
@@ -450,16 +449,17 @@
         name="push_place",
     )(mine, *[in_hbm(value) for value in operands])
     arrived1 = shifted(small1, "cuts", 1)
+    arrived1, sources[2] = lax.optimization_barrier((arrived1, sources[2]))
     send = pl.pallas_call(
         second_kernel,
-        out_shape=pltpu.HBM((ROWS, 1, BLOCK), jnp.float32),
+        out_shape=pltpu.HBM((PEERS, MESSAGE, 1, BLOCK), jnp.float32),
         in_specs=[scalar] + [whole()] * 4 + [remain],
         out_specs=remain,
-        scratch_shapes=[vmem(4, GROUPS, 128), vmem(1, 1, 128), pltpu.SemaphoreType.DMA((PEERS,))],
+        scratch_shapes=[vmem(4, GROUPS, 128), vmem(PEERS, 1, 128), pltpu.SemaphoreType.DMA],
         input_output_aliases={5: 0},
         compiler_params=params,
         name="second_push",
-    )(mine, phases1, energies1, arrived1, small1, in_hbm(send))
+    )(mine, phases1, energies1, arrived1, small1, in_hbm(send.reshape(PEERS, MESSAGE, 1, BLOCK)))
     field_b = [shifted(source, "cuts", 2) for source in sources]
 
     left_two, right_two = deep_left(left_form(*two)), deep_right(right_form(*two))
@@ -476,7 +476,7 @@
         handed = jnp.where(core == 0, shared_1, shared_0)
         source_c = jnp.where(mine[0] % 8 >= 6, handed[:, LATE - GROUPS :], field[:, LATE:])
         field_c = lax.ppermute(source_c, "cuts", late_pairs())
-        recv = lax.all_to_all(send, "cuts", split_axis=0, concat_axis=0, tiled=True)
+        recv = lax.all_to_all(send.reshape(ROWS, 1, BLOCK), "cuts", split_axis=0, concat_axis=0, tiled=True)
         recv, early = lax.optimization_barrier((recv, early))
         phase_out, energy_out, small = pl.pallas_call(
             pick_kernel,
@@ -507,7 +507,7 @@
     out = pl.pallas_call(
         last_kernel,
         out_shape=shape(2, GROUPS, GRID, GRID),
-        in_specs=[scalar] + [whole()] * 10,
+        in_specs=[scalar] + [whole()] * 9,
         out_specs=remain,
         scratch_shapes=[
             vmem(4, GROUPS, 128),

time: 92 us -> 95.7 us (1.040)
  waiting for transfers between devices: 35.9 us -> 45.5 us
  starting transfers between devices: 22.6 us -> 16.9 us
  local copies, waits for them, and re-layouts: 2.24 us -> 3.52 us
    ppermute x5 -> x4, waiting for transfers between devices: 4.42 us -> 9.87 us  [shifted(): return lax.ppermute(value, axis, pairs)]
    ppermute x5 -> x4, starting transfers between devices: 4.84 us -> 0.08 us  [shifted(): return lax.ppermute(value, axis, pairs)]
    all_to_all x1, waiting for transfers between devices: 31.5 us -> 35.6 us  [exchange(): lax.all_to_all(send.reshape(ROWS, 1, BLOCK), 'cuts', split_axis=0, concat...]
    pallas_call x1, Pallas kernels: 4.03 us -> 2.51 us  [per_device(): pl.pallas_call(second_kernel, out_shape=pltpu.HBM((PEERS, MESSAGE, 1, BLO...]
    dynamic_slice x1, local copies, waits for them, and re-layouts: 1.4 us -> 2.48 us  [per_device(): lax.dynamic_slice_in_dim(field, (1 - core) * (GROUPS - EARLY), EARLY, 1)]
  transfers between devices with their start and end apart: 9 -> 8, of which waited for: 2 -> 2; matrix products, arithmetic and copies ran while one was open for 2% -> 2% of each run, Pallas kernels for 25% -> 23%
where the time goes in v10:
time: 95.7 us; the launch traced here: 95.3 us
  waiting for transfers between devices  45.5 us (48%)
  Pallas kernels  26.5 us (28%)
  starting transfers between devices  16.9 us (18%)
  local copies, waits for them, and re-layouts  3.52 us (4%)
  other arithmetic  2.06 us (2%)
    all_to_all x1, waiting for transfers between devices, exchange(): lax.all_to_all(send.reshape(ROWS, 1, BLOCK), 'cuts', split_axis=0, concat...  35.6 us
    all_to_all x1, starting transfers between devices, exchange(): lax.all_to_all(send.reshape(ROWS, 1, BLOCK), 'cuts', split_axis=0, concat...  11.7 us
    pallas_call x1, Pallas kernels, per_device(): pl.pallas_call(first_kernel, out_shape=(pltpu.HBM((ROWS, 1, BLOCK), jnp.f...  10.1 us
    ppermute x4, waiting for transfers between devices, shifted(): return lax.ppermute(value, axis, pairs)  9.87 us
    pallas_call x1, Pallas kernels, exchange(): pl.pallas_call(pick_kernel, out_shape=(shape(COUNT, BLOCK), shape(COUNT,...  5.36 us
    pallas_call x1, Pallas kernels, per_device(): pl.pallas_call(last_kernel, out_shape=shape(2, GROUPS, GRID, GRID), in_sp...  4.79 us
    pallas_call x1, Pallas kernels, exchange(): pl.pallas_call(early_kernel, out_shape=shape(2, EARLY + 1, GRID, GRID), i...  3.81 us
    ppermute x1, starting transfers between devices, per_device(): lax.ppermute(lax.dynamic_slice_in_dim(field, core * (GROUPS - EARLY), EAR...  3.48 us
  transfers between devices with their start and end apart: 8, of which 2 were waited for; matrix products, arithmetic and copies ran while one was open for 2% of the time, Pallas kernels for 23%

profile of v10, /device:TPU:0, one launch (start us, length us, event | category | flops | bytes accessed | tf_op | source)
XLA Modules:
  0.0 95.3 jit_solution(17208972160613127356)
XLA Ops:
  0.7 2.5 %dynamic-slice_bitcast_fusion = (f32[2,5,128,128]{3,2,1,0:T(8,128)}, f32[2,5,128,128]{3,2,1,0:T(8,128)}) fusion(f32[2,16,1,128,128]{4,3,2,1,0:T(8,128)} %param.12, s32[]{:T(128)S(6)} %select_n.35, s32[]{:T(128)S(6)} %select_n.34), kind=kLoop, calls=%fused_computation.2 | loop fusion | bytes 2621448 | tf_op jit(solution)/shard_map/dynamic_slice | solution.py:417
  3.1 0.7 collective-permute-start.3
  3.8 3.5 %collective-permute-start.2 = (f32[2,5,128,128]{3,2,1,0:T(8,128)}, f32[2,5,128,128]{3,2,1,0:T(8,128)S(1)}, u32[]{:S(2)}, u32[]{:S(2)}) collective-permute-start(f32[2,5,128,128]{3,2,1,0:T(8,128)} %get-tuple-element.81), channel_id=1, source_target_pairs={{0,2},{2,4},{4,6},{6,8},{8,10},{10,12},{12,14},{14,16},{16,18},{18... | collective-permute-start | bytes 1966088 | tf_op jit(solution)/shard_map/ppermute | solution.py:416
  7.3 10.1 %push_place.1 = (f32[5248,1,128]{2,1,0:T(1,128)}, f32[1024,128]{1,0:T(8,128)S(1)}, f32[1024,128]{1,0:T(8,128)S(1)}, s32[8,1024]{1,0:T(8,128)}, f32[3,128,128]{2,...) custom-call(s32[1]{0:T(128)} %bitcast.3.mine, ...), custom_call_target="tpu_custom_call" | custom-call | tf_op jit(solution)/shard_map/push_place/pallas_call | solution.py:419
  17.4 0.1 collective-permute-start.1
  17.5 9.9 %collective-permute-done.1.arrived = f32[4,16,128]{2,1,0:T(8,128)S(1)} collective-permute-done((f32[4,16,128]{2,1,0:T(8,128)S(1)}, f32[4,16,128]{2,1,0:T(8,128)S(1)}, u32[]{:S(2)}, u32[]{:S(2)}) %collective-permute-start.1) | collective-permute-done | bytes 32800 | tf_op jit(solution)/shard_map/ppermute | solution.py:384
  27.3 0.0 collective-permute-start.6
  27.3 0.0 collective-permute-start.4
  27.3 0.0 collective-permute-start.5
  27.4 0.0 copy-start.2
  27.4 2.5 %second_push.1 = f32[128,41,1,128]{3,2,1,0:T(1,128)} custom-call(s32[1]{0:T(128)} %bitcast.3.mine, f32[1024,128]{1,0:T(8,128)S(1)} %get-tuple-element.59.phases1, f32[1024,128]{1,0:T(8,128)S(1)} %get-tuple-element.60.energies1, f32[4,16,128]{2,1,0:T(8,128)S(1)} %collective-permute-done.1.arrived, ...), custom_call_target="tpu_custom_call", output_to_operand_aliasing={{}: (5, {})} | custom-call | tf_op jit(solution)/shard_map/second_push/pallas_call | solution.py:453
  29.9 0.0 collective-permute-done.3
  29.9 0.0 collective-permute-done.2
  29.9 0.0 copy-done.2
  29.9 60.6 %conditional.1 = (f32[2,6,128,128]{3,2,1,0:T(8,128)}, f32[2,3,128,128]{3,2,1,0:T(8,128)}, f32[4,16,128]{2,1,0:T(8,128)S(1)}, f32[16,1,8192]{2,1,0:T(1,128)}, f32[16,1,8192]{2,1,0:T(1,128)}) conditional(s32[]{:T(128)} %convert_element_type.3, () %tuple.22, (f32[128,41,1,128]{3,2,1,0:T(1,128)}, s32[1]{0:T(128)}, f32[2,5,128,128]{3,2,1,0:T(8,128)S(1)}, ...), branch_computations={%region_0.1_spmd, %region_1.2_spmd} | conditional | flops 196621 | bytes 16449833 | solution.py:504
  29.9 0.0 copy-start
  29.9 0.0 copy-start.1
  29.9 0.8 copy-done
  30.8 0.2 copy-done.1
  31.0 11.7 %all-to-all-start = ((f32[5248,1,128]{2,1,0:T(1,128)}), f32[5248,1,128]{2,1,0:T(1,128)S(1)}, u32[]{:S(2)}, u32[]{:S(2)}) async-start(f32[5248,1,128]{2,1,0:T(1,128)} %bitcast.18), calls=%async_computation | async-start | bytes 5373952 | tf_op jit(solution)/shard_map/cond/branch_1_fun/all_to_all | solution.py:479
  42.7 2.1 %fusion = f32[2,3,128,128]{3,2,1,0:T(8,128)} fusion(f32[2,5,128,128]{3,2,1,0:T(8,128)} %copy-done.1, f32[2,5,128,128]{3,2,1,0:T(8,128)} %copy-done, f32[2,16,128,128]{3,2,1,0:T(8,128)} %get-tuple-element.34, pred[]{:T(512)S(6)} %eq.5, pred[]{:T(512)S(6)} %ge.2), kind=kLoop, calls=%fused_computation.1 | loop fusion | flops 196608 | bytes 1572866 | tf_op jit(solution)/shard_map/cond/branch_1_fun/jit(_where)/select_n | solution.py:477
  44.8 1.0 %collective-permute-start = (f32[2,3,128,128]{3,2,1,0:T(8,128)}, f32[2,3,128,128]{3,2,1,0:T(8,128)}, u32[]{:S(2)}, u32[]{:S(2)}) collective-permute-start(f32[2,3,128,128]{3,2,1,0:T(8,128)} %fusion), channel_id=1, source_target_pairs={{0,2},{1,3},{2,4},{3,5},{4,6},{5,7},{6,0},{7,1},{8,10},{9,11},{10,... | collective-permute-start | bytes 1179656 | tf_op jit(solution)/shard_map/cond/branch_1_fun/ppermute | solution.py:478
  45.7 3.8 %early_field.1 = f32[2,6,128,128]{3,2,1,0:T(8,128)} custom-call(s32[1]{0:T(128)} %get-tuple-element.25.mine, f32[2,5,128,128]{3,2,1,0:T(8,128)} %copy-done.1, f32[2,5,128,128]{3,2,1,0:T(8,128)} %copy-done, f32[3,128,128]{2,1,0:T(8,128)} %get-tuple-element.28.beam, bf16[256,768]{1,0:T(8,128)(2,1)} %get-tuple-element.29.left, ...), custom_call_target="tpu_custom_call" | custom-call | tf_op jit(solution)/shard_map/cond/branch_1_fun/early_field/pallas_call | solution.py:468
  49.5 35.6 %all-to-all-done.recv = f32[5248,1,128]{2,1,0:T(1,128)S(1)} async-done(((f32[5248,1,128]{2,1,0:T(1,128)}), f32[5248,1,128]{2,1,0:T(1,128)S(1)}, u32[]{:S(2)}, u32[]{:S(2)}) %all-to-all-start) | async-done | bytes 2687008 | tf_op jit(solution)/shard_map/cond/branch_1_fun/all_to_all | solution.py:479
  85.1 5.4 %pick.1 = (f32[1024,128]{1,0:T(8,128)}, f32[1024,128]{1,0:T(8,128)}, f32[4,16,128]{2,1,0:T(8,128)S(1)}) custom-call(s32[1]{0:T(128)} %get-tuple-element.25.mine, f32[5248,1,128]{2,1,0:T(1,128)S(1)} %all-to-all-done.recv, s32[8,1024]{1,0:T(8,128)S(1)} %get-tuple-element.36.places), custom_call_target="tpu_custom_call" | custom-call | tf_op jit(solution)/shard_map/cond/branch_1_fun/pick/pallas_call | solution.py:481
  90.5 0.0 collective-permute-done
  90.5 0.0 collective-permute-done.4.piece_b0
  90.5 0.0 collective-permute-done.5.piece_b1
  90.5 0.0 collective-permute-done.6.piece_b2
  90.5 4.8 %last_field.1 = f32[2,16,128,128]{3,2,1,0:T(8,128)} custom-call(s32[1]{0:T(128)} %bitcast.3.mine, f32[2,6,128,128]{3,2,1,0:T(8,128)} %get-tuple-element.67.early, f32[2,2,128,128]{3,2,1,0:T(8,128)S(1)} %collective-permute-done.4.piece_b0, f32[2,2,128,128]{3,2,1,0:T(8,128)} %collective-permute-done.5.piece_b1, ...), custom_call_target="tpu_custom_call" | custom-call | tf_op jit(solution)/shard_map/last_field/pallas_call | solution.py:507
Async XLA Ops:
  3.1 26.8 %collective-permute-start.3 = (f32[2,5,128,128]{3,2,1,0:T(8,128)}, f32[2,5,128,128]{3,2,1,0:T(8,128)S(1)}, u32[]{:S(2)}, u32[]{:S(2)}) collective-permute-start(f32[2,5,128,128]{3,2,1,0:T(8,128)} %get-tuple-element.80), channel_id=1, source_target_pairs={{1,3},{3,5},{5,7},{7,9},{9,11},{11,13},{13,15},{15,17},{17,19},{19... | collective-permute-start | bytes 1966088 | tf_op jit(solution)/shard_map/ppermute | solution.py:417
  3.8 26.1 %collective-permute-start.2 = (f32[2,5,128,128]{3,2,1,0:T(8,128)}, f32[2,5,128,128]{3,2,1,0:T(8,128)S(1)}, u32[]{:S(2)}, u32[]{:S(2)}) collective-permute-start(f32[2,5,128,128]{3,2,1,0:T(8,128)} %get-tuple-element.81), channel_id=1, source_target_pairs={{0,2},{2,4},{4,6},{6,8},{8,10},{10,12},{12,14},{14,16},{16,18},{18... | collective-permute-start | bytes 1966088 | tf_op jit(solution)/shard_map/ppermute | solution.py:416
  17.4 9.9 %collective-permute-start.1 = (f32[4,16,128]{2,1,0:T(8,128)S(1)}, f32[4,16,128]{2,1,0:T(8,128)S(1)}, u32[]{:S(2)}, u32[]{:S(2)}) collective-permute-start(f32[4,16,128]{2,1,0:T(8,128)S(1)} %get-tuple-element.61.own), channel_id=1, source_target_pairs={{0,1},{1,2},{2,3},{3,4},{4,5},{5,6},{6,7},{7,8},{8,9},{9,10},{10,1... | collective-permute-start | bytes 98312 | tf_op jit(solution)/shard_map/ppermute | solution.py:384
  27.3 63.2 %collective-permute-start.6 = (f32[2,4,128,128]{3,2,1,0:T(8,128)}, f32[2,4,128,128]{3,2,1,0:T(8,128)S(1)}, u32[]{:S(2)}, u32[]{:S(2)}) collective-permute-start(f32[2,4,128,128]{3,2,1,0:T(8,128)} %get-tuple-element.70), channel_id=1, source_target_pairs={{0,2},{1,3},{2,4},{3,5},{4,6},{5,7},{6,8},{7,9},{8,10},{9,11},{10,... | collective-permute-start | bytes 1572872 | tf_op jit(solution)/shard_map/ppermute | solution.py:384
  27.3 63.2 %collective-permute-start.4 = (f32[2,2,128,128]{3,2,1,0:T(8,128)}, f32[2,2,128,128]{3,2,1,0:T(8,128)S(1)}, u32[]{:S(2)}, u32[]{:S(2)}) collective-permute-start(f32[2,2,128,128]{3,2,1,0:T(8,128)} %get-tuple-element.68), channel_id=1, source_target_pairs={{0,2},{1,3},{2,4},{3,5},{4,6},{5,7},{6,8},{7,9},{8,10},{9,11},{10,... | collective-permute-start | bytes 786440 | tf_op jit(solution)/shard_map/ppermute | solution.py:384
  27.3 63.2 %collective-permute-start.5 = (f32[2,2,128,128]{3,2,1,0:T(8,128)}, f32[2,2,128,128]{3,2,1,0:T(8,128)}, u32[]{:S(2)}, u32[]{:S(2)}) collective-permute-start(f32[2,2,128,128]{3,2,1,0:T(8,128)} %get-tuple-element.69), channel_id=1, source_target_pairs={{0,2},{1,3},{2,4},{3,5},{4,6},{5,7},{6,8},{7,9},{8,10},{9,11},{10,... | collective-permute-start | bytes 786440 | tf_op jit(solution)/shard_map/ppermute | solution.py:384
  27.4 2.6 %copy-start.2 = (s32[8,1024]{1,0:T(8,128)S(1)}, s32[8,1024]{1,0:T(8,128)}, u32[]{:S(2)}) copy-start(s32[8,1024]{1,0:T(8,128)} %get-tuple-element.66) | copy-start | bytes 98308
  29.9 0.8 copy-start
  29.9 1.0 %copy-start.1 = (f32[2,5,128,128]{3,2,1,0:T(8,128)}, f32[2,5,128,128]{3,2,1,0:T(8,128)S(1)}, u32[]{:S(2)}) copy-start(f32[2,5,128,128]{3,2,1,0:T(8,128)S(1)} %get-tuple-element.26.piece_0) | copy-start | bytes 1966084 | tf_op jit(solution)/shard_map/cond
  31.0 54.2 %all-to-all-start = ((f32[5248,1,128]{2,1,0:T(1,128)}), f32[5248,1,128]{2,1,0:T(1,128)S(1)}, u32[]{:S(2)}, u32[]{:S(2)}) async-start(f32[5248,1,128]{2,1,0:T(1,128)} %bitcast.18), calls=%async_computation | async-start | bytes 5373952 | tf_op jit(solution)/shard_map/cond/branch_1_fun/all_to_all | solution.py:479
  44.8 45.8 %collective-permute-start = (f32[2,3,128,128]{3,2,1,0:T(8,128)}, f32[2,3,128,128]{3,2,1,0:T(8,128)}, u32[]{:S(2)}, u32[]{:S(2)}) collective-permute-start(f32[2,3,128,128]{3,2,1,0:T(8,128)} %fusion), channel_id=1, source_target_pairs={{0,2},{1,3},{2,4},{3,5},{4,6},{5,7},{6,0},{7,1},{8,10},{9,11},{10,... | collective-permute-start | bytes 1179656 | tf_op jit(solution)/shard_map/cond/branch_1_fun/ppermute | solution.py:478

commit v11 on v10

--- a/solution.py
+++ b/solution.py
@@ -24,10 +24,10 @@
 CAP = 20
 MESSAGE = 2 * CAP + 1
 ROWS = PEERS * MESSAGE
-BATCH = 16
+BATCH = 32
 EARLY, LATE = 5, 13
-MIDDLE = ((5, 7), (7, 9), (9, 13))
-VMEM_LIMIT = 16 * 1024 * 1024
+MIDDLE = ((5, 7), (7, 9), (9, 11), (11, 13))
+VMEM_LIMIT = 24 * 1024 * 1024
 HIGHEST = lax.Precision.HIGHEST
 
 
@@ -120,7 +120,7 @@
 
 def first_kernel(
     mine, field_hbm, profile_hbm, bins_hbm, jitter_hbm, energy_hbm, delays_hbm, left_hbm, right_hbm,
-    send_hbm, phases, energies, places_hbm, beam, small, middle_0, middle_1, middle_2,
+    send_hbm, phases, energies, places_hbm, beam, small, middle_0, middle_1, middle_2, middle_3,
     field, profile, bins, jitter, energy, delays, left, right, acc, send, places, index_v, index, sems,
 ):
     pairs = [
@@ -148,7 +148,7 @@
     beam[2] = p
     copies[4].wait()
     kept = [pltpu.make_async_copy(places, places_hbm, sems.at[8])]
-    for middle, (low, high) in zip((middle_0, middle_1, middle_2), MIDDLE):
+    for middle, (low, high) in zip((middle_0, middle_1, middle_2, middle_3), MIDDLE):
         for c in range(2):
             span = pl.ds(low, high - low)
             kept.append(pltpu.make_async_copy(field.at[c, span], middle.at[c], sems.at[8 + len(kept)]))
@@ -196,7 +196,7 @@
             send[spots[m] + CAP] = en[m]
         return carry
 
-    lax.fori_loop(0, COUNT // BATCH, put, 0, unroll=4)
+    lax.fori_loop(0, COUNT // BATCH, put, 0)
     bre = lane_total(acc[4]) * (1.0 / (NBS * BLOCK))
     bim = lane_total(acc[5]) * (-1.0 / (NBS * BLOCK))
     gain = GAIN / GRID
@@ -293,7 +293,7 @@
 
     copies = []
     for quarter in range(4):
-        lax.fori_loop(quarter * COUNT // BATCH // 4, (quarter + 1) * COUNT // BATCH // 4, get, 0, unroll=4)
+        lax.fori_loop(quarter * COUNT // BATCH // 4, (quarter + 1) * COUNT // BATCH // 4, get, 0)
         for k in range(quarter * 4, quarter * 4 + 4):
             rows = slice(k * NBS, (k + 1) * NBS)
             re, im = amps[rows, k : k + 1], amps[rows, GROUPS + k : GROUPS + k + 1]
@@ -330,7 +330,7 @@
 
 
 def last_kernel(
-    mine, early, piece_b0, piece_b1, piece_b2, piece_c, small, beam, left, right, out_hbm, acc, rest, out, sems
+    mine, early, piece_b0, piece_b1, piece_b2, piece_b3, piece_c, small, beam, left, right, out_hbm, acc, rest, out, sems
 ):
     me = mine[0]
     for n in range(4):
@@ -354,7 +354,7 @@
             copies[-1].start()
 
     finish(0, EARLY)
-    planes = [(piece[0, k], piece[1, k]) for piece in (piece_b0, piece_b1, piece_b2) for k in range(piece.shape[1])]
+    planes = [(piece[0, k], piece[1, k]) for piece in (piece_b0, piece_b1, piece_b2, piece_b3) for k in range(piece.shape[1])]
     for k, (re, im) in enumerate(twice_diffracted(planes, left, right)):
         rest[0, k] = re
         rest[1, k] = im
@@ -449,7 +449,6 @@
         name="push_place",
     )(mine, *[in_hbm(value) for value in operands])
     arrived1 = shifted(small1, "cuts", 1)
-    arrived1, sources[2] = lax.optimization_barrier((arrived1, sources[2]))
     send = pl.pallas_call(
         second_kernel,
         out_shape=pltpu.HBM((PEERS, MESSAGE, 1, BLOCK), jnp.float32),
@@ -472,7 +471,7 @@
             out_specs=whole(),
             compiler_params=params,
             name="early_field",
-        )(mine, shared_0, shared_1, beam, left_two, right_two)
+        )(mine, in_hbm(shared_0), in_hbm(shared_1), in_hbm(beam), left_two, right_two)
         handed = jnp.where(core == 0, shared_1, shared_0)
         source_c = jnp.where(mine[0] % 8 >= 6, handed[:, LATE - GROUPS :], field[:, LATE:])
         field_c = lax.ppermute(source_c, "cuts", late_pairs())
@@ -507,7 +506,7 @@
     out = pl.pallas_call(
         last_kernel,
         out_shape=shape(2, GROUPS, GRID, GRID),
-        in_specs=[scalar] + [whole()] * 9,
+        in_specs=[scalar] + [whole()] * 10,
         out_specs=remain,
         scratch_shapes=[
             vmem(4, GROUPS, 128),

time: 95.7 us -> 92.7 us (0.969)
  waiting for transfers between devices: 45.5 us -> 39 us
  starting transfers between devices: 16.9 us -> 22 us
  local copies, waits for them, and re-layouts: 3.52 us -> 2.24 us
    ppermute x4 -> x5, waiting for transfers between devices: 9.87 us -> 4.42 us  [shifted(): return lax.ppermute(value, axis, pairs)]
    ppermute x4 -> x5, starting transfers between devices: 0.08 us -> 4.84 us  [shifted(): return lax.ppermute(value, axis, pairs)]
    all_to_all x1, waiting for transfers between devices: 35.6 us -> 33.9 us  [exchange(): lax.all_to_all(send.reshape(ROWS, 1, BLOCK), 'cuts', split_axis=0, concat...]
    dynamic_slice x1, local copies, waits for them, and re-layouts: 2.48 us -> 1.4 us  [per_device(): lax.dynamic_slice_in_dim(field, (1 - core) * (GROUPS - EARLY), EARLY, 1)]
  transfers between devices with their start and end apart: 8 -> 9, of which waited for: 2 -> 3; matrix products, arithmetic and copies ran while one was open for 2% -> 2% of each run, Pallas kernels for 23% -> 23%
where the time goes in v11:
time: 92.7 us; the launch traced here: 92.1 us
  waiting for transfers between devices  39 us (42%)
  Pallas kernels  25.9 us (28%)
  starting transfers between devices  22 us (24%)
  local copies, waits for them, and re-layouts  2.24 us (2%)
  other arithmetic  2.07 us (2%)
    all_to_all x1, waiting for transfers between devices, exchange(): lax.all_to_all(send.reshape(ROWS, 1, BLOCK), 'cuts', split_axis=0, concat...  33.9 us
    all_to_all x1, starting transfers between devices, exchange(): lax.all_to_all(send.reshape(ROWS, 1, BLOCK), 'cuts', split_axis=0, concat...  11.2 us
    pallas_call x1, Pallas kernels, per_device(): pl.pallas_call(first_kernel, out_shape=(pltpu.HBM((ROWS, 1, BLOCK), jnp.f...  9.54 us
    pallas_call x1, Pallas kernels, exchange(): pl.pallas_call(pick_kernel, out_shape=(shape(COUNT, BLOCK), shape(COUNT,...  5.26 us
    ppermute x5, starting transfers between devices, shifted(): return lax.ppermute(value, axis, pairs)  4.84 us
    pallas_call x1, Pallas kernels, per_device(): pl.pallas_call(last_kernel, out_shape=shape(2, GROUPS, GRID, GRID), in_sp...  4.8 us
    ppermute x5, waiting for transfers between devices, shifted(): return lax.ppermute(value, axis, pairs)  4.42 us
    pallas_call x1, Pallas kernels, exchange(): pl.pallas_call(early_kernel, out_shape=shape(2, EARLY + 1, GRID, GRID), i...  3.81 us
  transfers between devices with their start and end apart: 9, of which 3 were waited for; matrix products, arithmetic and copies ran while one was open for 2% of the time, Pallas kernels for 23%

profile of v11, /device:TPU:0, one launch (start us, length us, event | category | flops | bytes accessed | tf_op | source)
XLA Modules:
  0.0 92.1 jit_solution(5032600204835712034)
XLA Ops:
  0.7 1.4 %dynamic-slice_bitcast_fusion = (f32[2,5,128,128]{3,2,1,0:T(8,128)S(1)}, f32[2,5,128,128]{3,2,1,0:T(8,128)S(1)}) fusion(f32[2,16,1,128,128]{4,3,2,1,0:T(8,128)} %param.12, s32[]{:T(128)S(6)} %select_n.35, s32[]{:T(128)S(6)} %select_n.34), kind=kLoop, calls=%fused_computation.2 | loop fusion | bytes 2621448 | tf_op jit(solution)/shard_map/dynamic_slice | solution.py:417
  2.1 1.5 %collective-permute-start.3 = (f32[2,5,128,128]{3,2,1,0:T(8,128)S(1)}, f32[2,5,128,128]{3,2,1,0:T(8,128)}, u32[]{:S(2)}, u32[]{:S(2)}) collective-permute-start(f32[2,5,128,128]{3,2,1,0:T(8,128)S(1)} %get-tuple-element.78), channel_id=1, source_target_pairs={{1,3},{3,5},{5,7},{7,9},{9,11},{11,13},{13,15},{15,17},{17,19},{19... | collective-permute-start | bytes 1966088 | tf_op jit(solution)/shard_map/ppermute | solution.py:417
  3.6 3.5 %collective-permute-start.2 = (f32[2,5,128,128]{3,2,1,0:T(8,128)S(1)}, f32[2,5,128,128]{3,2,1,0:T(8,128)S(1)}, u32[]{:S(2)}, u32[]{:S(2)}) collective-permute-start(f32[2,5,128,128]{3,2,1,0:T(8,128)S(1)} %get-tuple-element.79), channel_id=1, source_target_pairs={{0,2},{2,4},{4,6},{6,8},{8,10},{10,12},{12,14},{14,16},{16,18},{18... | collective-permute-start | bytes 1966088 | tf_op jit(solution)/shard_map/ppermute | solution.py:416
  7.0 9.5 %push_place.1 = (f32[5248,1,128]{2,1,0:T(1,128)}, f32[1024,128]{1,0:T(8,128)S(1)}, f32[1024,128]{1,0:T(8,128)S(1)}, s32[8,1024]{1,0:T(8,128)}, f32[3,128,128]{2,...) custom-call(s32[1]{0:T(128)} %bitcast.3.mine, ...), custom_call_target="tpu_custom_call" | custom-call | tf_op jit(solution)/shard_map/push_place/pallas_call | solution.py:419
  16.6 0.1 collective-permute-start.1
  16.7 1.6 %collective-permute-start.4 = (f32[2,2,128,128]{3,2,1,0:T(8,128)}, f32[2,2,128,128]{3,2,1,0:T(8,128)S(1)}, u32[]{:S(2)}, u32[]{:S(2)}) collective-permute-start(f32[2,2,128,128]{3,2,1,0:T(8,128)} %get-tuple-element.65), channel_id=1, source_target_pairs={{0,2},{1,3},{2,4},{3,5},{4,6},{5,7},{6,8},{7,9},{8,10},{9,11},{10,... | collective-permute-start | bytes 786440 | tf_op jit(solution)/shard_map/ppermute | solution.py:384
  18.2 3.2 %collective-permute-start.5 = (f32[2,2,128,128]{3,2,1,0:T(8,128)}, f32[2,2,128,128]{3,2,1,0:T(8,128)S(1)}, u32[]{:S(2)}, u32[]{:S(2)}) collective-permute-start(f32[2,2,128,128]{3,2,1,0:T(8,128)} %get-tuple-element.66), channel_id=1, source_target_pairs={{0,2},{1,3},{2,4},{3,5},{4,6},{5,7},{6,8},{7,9},{8,10},{9,11},{10,... | collective-permute-start | bytes 786440 | tf_op jit(solution)/shard_map/ppermute | solution.py:384
  21.4 4.4 %collective-permute-done.1.arrived = f32[4,16,128]{2,1,0:T(8,128)S(1)} collective-permute-done((f32[4,16,128]{2,1,0:T(8,128)S(1)}, f32[4,16,128]{2,1,0:T(8,128)S(1)}, u32[]{:S(2)}, u32[]{:S(2)}) %collective-permute-start.1) | collective-permute-done | bytes 32800 | tf_op jit(solution)/shard_map/ppermute | solution.py:384
  25.8 0.0 collective-permute-start.6
  25.9 0.0 collective-permute-done.3
  25.9 0.0 collective-permute-start.7
  25.9 0.0 copy-start.1
  25.9 2.5 %second_push.1 = f32[128,41,1,128]{3,2,1,0:T(1,128)} custom-call(s32[1]{0:T(128)} %bitcast.3.mine, f32[1024,128]{1,0:T(8,128)S(1)} %get-tuple-element.58.phases1, f32[1024,128]{1,0:T(8,128)S(1)} %get-tuple-element.59.energies1, f32[4,16,128]{2,1,0:T(8,128)S(1)} %collective-permute-done.1.arrived, ...), custom_call_target="tpu_custom_call", output_to_operand_aliasing={{}: (5, {})} | custom-call | tf_op jit(solution)/shard_map/second_push/pallas_call | solution.py:452
  28.4 0.7 collective-permute-done.2
  29.1 0.0 copy-done.1
  29.1 58.1 %conditional.1 = (f32[2,6,128,128]{3,2,1,0:T(8,128)}, f32[2,3,128,128]{3,2,1,0:T(8,128)}, f32[4,16,128]{2,1,0:T(8,128)S(1)}, f32[16,1,8192]{2,1,0:T(1,128)}, f32[16,1,8192]{2,1,0:T(1,128)}) conditional(s32[]{:T(128)} %convert_element_type.3, () %tuple.21, (f32[128,41,1,128]{3,2,1,0:T(1,128)}, s32[1]{0:T(128)}, f32[2,5,128,128]{3,2,1,0:T(8,128)S(1)}, ...), branch_computations={%region_0.1_spmd, %region_1.2_spmd} | conditional | flops 196621 | bytes 13828365 | solution.py:503
  29.1 0.0 copy-start
  29.1 0.8 copy-done
  29.9 11.2 %all-to-all-start = ((f32[5248,1,128]{2,1,0:T(1,128)}), f32[5248,1,128]{2,1,0:T(1,128)S(1)}, u32[]{:S(2)}, u32[]{:S(2)}) async-start(f32[5248,1,128]{2,1,0:T(1,128)} %bitcast.18), calls=%async_computation | async-start | bytes 5373952 | tf_op jit(solution)/shard_map/cond/branch_1_fun/all_to_all | solution.py:478
  41.2 2.1 %fusion = f32[2,3,128,128]{3,2,1,0:T(8,128)} fusion(f32[2,5,128,128]{3,2,1,0:T(8,128)} %copy-done, f32[2,5,128,128]{3,2,1,0:T(8,128)} %get-tuple-element.27.piece_1, f32[2,16,128,128]{3,2,1,0:T(8,128)} %get-tuple-element.34, pred[]{:T(512)S(6)} %eq.5, pred[]{:T(512)S(6)} %ge.2), kind=kLoop, calls=%fused_computation.1 | loop fusion | flops 196608 | bytes 1572866 | tf_op jit(solution)/shard_map/cond/branch_1_fun/jit(_where)/select_n | solution.py:476
  43.2 1.0 %collective-permute-start = (f32[2,3,128,128]{3,2,1,0:T(8,128)}, f32[2,3,128,128]{3,2,1,0:T(8,128)}, u32[]{:S(2)}, u32[]{:S(2)}) collective-permute-start(f32[2,3,128,128]{3,2,1,0:T(8,128)} %fusion), channel_id=1, source_target_pairs={{0,2},{1,3},{2,4},{3,5},{4,6},{5,7},{6,0},{7,1},{8,10},{9,11},{10,... | collective-permute-start | bytes 1179656 | tf_op jit(solution)/shard_map/cond/branch_1_fun/ppermute | solution.py:477
  44.2 3.8 %early_field.1 = f32[2,6,128,128]{3,2,1,0:T(8,128)} custom-call(s32[1]{0:T(128)} %get-tuple-element.25.mine, f32[2,5,128,128]{3,2,1,0:T(8,128)} %copy-done, f32[2,5,128,128]{3,2,1,0:T(8,128)} %get-tuple-element.27.piece_1, f32[3,128,128]{2,1,0:T(8,128)} %get-tuple-element.28.beam, bf16[256,768]{1,0:T(8,128)(2,1)} %get-tuple-element.29.left, ...), custom_call_target="tpu_custom_call" | custom-call | tf_op jit(solution)/shard_map/cond/branch_1_fun/early_field/pallas_call | solution.py:467
  48.0 33.9 %all-to-all-done.recv = f32[5248,1,128]{2,1,0:T(1,128)S(1)} async-done(((f32[5248,1,128]{2,1,0:T(1,128)}), f32[5248,1,128]{2,1,0:T(1,128)S(1)}, u32[]{:S(2)}, u32[]{:S(2)}) %all-to-all-start) | async-done | bytes 2687008 | tf_op jit(solution)/shard_map/cond/branch_1_fun/all_to_all | solution.py:478
  81.9 5.3 %pick.1 = (f32[1024,128]{1,0:T(8,128)}, f32[1024,128]{1,0:T(8,128)}, f32[4,16,128]{2,1,0:T(8,128)S(1)}) custom-call(s32[1]{0:T(128)} %get-tuple-element.25.mine, f32[5248,1,128]{2,1,0:T(1,128)S(1)} %all-to-all-done.recv, s32[8,1024]{1,0:T(8,128)S(1)} %get-tuple-element.36.places), custom_call_target="tpu_custom_call" | custom-call | tf_op jit(solution)/shard_map/cond/branch_1_fun/pick/pallas_call | solution.py:480
  87.2 0.0 collective-permute-done
  87.2 0.0 collective-permute-done.4.piece_b0
  87.2 0.0 collective-permute-done.5.piece_b1
  87.2 0.0 collective-permute-done.6.piece_b2
  87.2 0.0 collective-permute-done.7.piece_b3
  87.2 4.8 %last_field.1 = f32[2,16,128,128]{3,2,1,0:T(8,128)} custom-call(s32[1]{0:T(128)} %bitcast.3.mine, f32[2,6,128,128]{3,2,1,0:T(8,128)} %get-tuple-element.64.early, f32[2,2,128,128]{3,2,1,0:T(8,128)S(1)} %collective-permute-done.4.piece_b0, f32[2,2,128,128]{3,2,1,0:T(8,128)S(1)} %collective-permute-done.5.piece_b1, ...), custom_call_target="tpu_custom_call" | custom-call | tf_op jit(solution)/shard_map/last_field/pallas_call | solution.py:506
Async XLA Ops:
  2.1 23.8 %collective-permute-start.3 = (f32[2,5,128,128]{3,2,1,0:T(8,128)S(1)}, f32[2,5,128,128]{3,2,1,0:T(8,128)}, u32[]{:S(2)}, u32[]{:S(2)}) collective-permute-start(f32[2,5,128,128]{3,2,1,0:T(8,128)S(1)} %get-tuple-element.78), channel_id=1, source_target_pairs={{1,3},{3,5},{5,7},{7,9},{9,11},{11,13},{13,15},{15,17},{17,19},{19... | collective-permute-start | bytes 1966088 | tf_op jit(solution)/shard_map/ppermute | solution.py:417
  3.6 25.5 %collective-permute-start.2 = (f32[2,5,128,128]{3,2,1,0:T(8,128)S(1)}, f32[2,5,128,128]{3,2,1,0:T(8,128)S(1)}, u32[]{:S(2)}, u32[]{:S(2)}) collective-permute-start(f32[2,5,128,128]{3,2,1,0:T(8,128)S(1)} %get-tuple-element.79), channel_id=1, source_target_pairs={{0,2},{2,4},{4,6},{6,8},{8,10},{10,12},{12,14},{14,16},{16,18},{18... | collective-permute-start | bytes 1966088 | tf_op jit(solution)/shard_map/ppermute | solution.py:416
  16.6 9.3 %collective-permute-start.1 = (f32[4,16,128]{2,1,0:T(8,128)S(1)}, f32[4,16,128]{2,1,0:T(8,128)S(1)}, u32[]{:S(2)}, u32[]{:S(2)}) collective-permute-start(f32[4,16,128]{2,1,0:T(8,128)S(1)} %get-tuple-element.60.own), channel_id=1, source_target_pairs={{0,1},{1,2},{2,3},{3,4},{4,5},{5,6},{6,7},{7,8},{8,9},{9,10},{10,1... | collective-permute-start | bytes 98312 | tf_op jit(solution)/shard_map/ppermute | solution.py:384
  16.7 70.5 %collective-permute-start.4 = (f32[2,2,128,128]{3,2,1,0:T(8,128)}, f32[2,2,128,128]{3,2,1,0:T(8,128)S(1)}, u32[]{:S(2)}, u32[]{:S(2)}) collective-permute-start(f32[2,2,128,128]{3,2,1,0:T(8,128)} %get-tuple-element.65), channel_id=1, source_target_pairs={{0,2},{1,3},{2,4},{3,5},{4,6},{5,7},{6,8},{7,9},{8,10},{9,11},{10,... | collective-permute-start | bytes 786440 | tf_op jit(solution)/shard_map/ppermute | solution.py:384
  18.2 69.0 %collective-permute-start.5 = (f32[2,2,128,128]{3,2,1,0:T(8,128)}, f32[2,2,128,128]{3,2,1,0:T(8,128)S(1)}, u32[]{:S(2)}, u32[]{:S(2)}) collective-permute-start(f32[2,2,128,128]{3,2,1,0:T(8,128)} %get-tuple-element.66), channel_id=1, source_target_pairs={{0,2},{1,3},{2,4},{3,5},{4,6},{5,7},{6,8},{7,9},{8,10},{9,11},{10,... | collective-permute-start | bytes 786440 | tf_op jit(solution)/shard_map/ppermute | solution.py:384
  25.8 61.4 %collective-permute-start.6 = (f32[2,2,128,128]{3,2,1,0:T(8,128)}, f32[2,2,128,128]{3,2,1,0:T(8,128)S(1)}, u32[]{:S(2)}, u32[]{:S(2)}) collective-permute-start(f32[2,2,128,128]{3,2,1,0:T(8,128)} %get-tuple-element.67), channel_id=1, source_target_pairs={{0,2},{1,3},{2,4},{3,5},{4,6},{5,7},{6,8},{7,9},{8,10},{9,11},{10,... | collective-permute-start | bytes 786440 | tf_op jit(solution)/shard_map/ppermute | solution.py:384
  25.9 61.4 %collective-permute-start.7 = (f32[2,2,128,128]{3,2,1,0:T(8,128)}, f32[2,2,128,128]{3,2,1,0:T(8,128)}, u32[]{:S(2)}, u32[]{:S(2)}) collective-permute-start(f32[2,2,128,128]{3,2,1,0:T(8,128)} %get-tuple-element.68), channel_id=1, source_target_pairs={{0,2},{1,3},{2,4},{3,5},{4,6},{5,7},{6,8},{7,9},{8,10},{9,11},{10,... | collective-permute-start | bytes 786440 | tf_op jit(solution)/shard_map/ppermute | solution.py:384
  25.9 3.2 %copy-start.1 = (s32[8,1024]{1,0:T(8,128)S(1)}, s32[8,1024]{1,0:T(8,128)}, u32[]{:S(2)}) copy-start(s32[8,1024]{1,0:T(8,128)} %get-tuple-element.63) | copy-start | bytes 98308
  29.1 0.8 copy-start
  29.9 52.0 %all-to-all-start = ((f32[5248,1,128]{2,1,0:T(1,128)}), f32[5248,1,128]{2,1,0:T(1,128)S(1)}, u32[]{:S(2)}, u32[]{:S(2)}) async-start(f32[5248,1,128]{2,1,0:T(1,128)} %bitcast.18), calls=%async_computation | async-start | bytes 5373952 | tf_op jit(solution)/shard_map/cond/branch_1_fun/all_to_all | solution.py:478
  43.2 44.0 %collective-permute-start = (f32[2,3,128,128]{3,2,1,0:T(8,128)}, f32[2,3,128,128]{3,2,1,0:T(8,128)}, u32[]{:S(2)}, u32[]{:S(2)}) collective-permute-start(f32[2,3,128,128]{3,2,1,0:T(8,128)} %fusion), channel_id=1, source_target_pairs={{0,2},{1,3},{2,4},{3,5},{4,6},{5,7},{6,0},{7,1},{8,10},{9,11},{10,... | collective-permute-start | bytes 1179656 | tf_op jit(solution)/shard_map/cond/branch_1_fun/ppermute | solution.py:477

commit v12 on v11

--- a/solution.py
+++ b/solution.py
@@ -41,10 +41,6 @@
     return matrix.real, matrix.imag
 
 
-def left_form(real, imag):
-    return np.block([[real, -imag], [imag, real]])
-
-
 def right_form(real, imag):
     return np.block([[real, imag], [-imag, real]])
 
@@ -54,14 +50,18 @@
     return high, (matrix - high.astype(np.float64)).astype(ml_dtypes.bfloat16)
 
 
-def deep_left(matrix):
-    high, low = halves(matrix)
-    return jnp.asarray(np.concatenate([high, high, low], axis=1))
-
-
-def deep_right(matrix):
-    high, low = halves(matrix)
-    return jnp.asarray(np.concatenate([high, high, low], axis=0))
+def quarters(real, imag):
+    return jnp.asarray(np.stack(halves(real) + halves(imag)))
+
+
+def lay_out(parts, left, right):
+    for n, low in enumerate((0, 0, 1)):
+        re, im = parts[low], parts[2 + low]
+        rest = slice(n * 2 * GRID, n * 2 * GRID + GRID), slice(n * 2 * GRID + GRID, (n + 1) * 2 * GRID)
+        left[:GRID, rest[0]], left[:GRID, rest[1]] = re, -im
+        left[GRID:, rest[0]], left[GRID:, rest[1]] = im, re
+        right[rest[0], :GRID], right[rest[0], GRID:] = re, im
+        right[rest[1], :GRID], right[rest[1], GRID:] = -im, re
 
 
 def fitted(function, degree):
@@ -273,12 +273,19 @@
     wrapped = jnp.concatenate([sheet[127:128, 127:128], sheet[127:128, :127]], axis=1)
     wrapped = jnp.where(lane[0:1] % GROUPS == 0, 0.0, wrapped)
     sheet = jnp.concatenate([wrapped, sheet[:127]], axis=0)
-    for n in range(COUNT // 128):
-        column = jnp.broadcast_to(source[:, n * 128 : (n + 1) * 128], (128, 128)).T
-        onehot = jnp.where(lane == column, 1.0, 0.0)
-        amps[n * 128 : (n + 1) * 128] = jnp.dot(
-            onehot, sheet, precision=HIGHEST, preferred_element_type=jnp.float32
-        )
+    kept = jnp.where(lane < 2 * GROUPS, sheet, 0.0)
+    high, rest = wide_halves(kept)
+    low = (kept - high.astype(jnp.float32) - rest.astype(jnp.float32)).astype(jnp.bfloat16)
+    thirds = jnp.concatenate([high, rest, low], axis=1)
+    onehot = jnp.concatenate(
+        [
+            jnp.where(lane == jnp.broadcast_to(source[:, n * 128 : (n + 1) * 128], (128, 128)).T, 1.0, 0.0)
+            for n in range(COUNT // 128)
+        ],
+        axis=0,
+    )
+    found = jnp.dot(onehot.astype(jnp.bfloat16), thirds, preferred_element_type=jnp.float32)
+    amps[...] = found[:, :128] + found[:, 128:256] + found[:, 256:]
     to_scalar.wait()
 
     def get(n, carry):
@@ -320,7 +327,8 @@
     return [(full[:GRID, cut], full[GRID:, cut]) for cut in cuts]
 
 
-def early_kernel(mine, piece_0, piece_1, beam, left, right, out):
+def early_kernel(mine, piece_0, piece_1, beam, parts, out, left, right):
+    lay_out(parts, left, right)
     even = mine[0] % 2 == 0
     planes = [tuple(jnp.where(even, piece_0[c, k], piece_1[c, k]) for c in range(2)) for k in range(EARLY)]
     planes.append((beam[2], jnp.zeros((GRID, GRID), jnp.float32)))
@@ -330,7 +338,7 @@
 
 
 def last_kernel(
-    mine, early, piece_b0, piece_b1, piece_b2, piece_b3, piece_c, small, beam, left, right, out_hbm, acc, rest, out, sems
+    mine, early, piece_b0, piece_b1, piece_b2, piece_b3, piece_c, small, beam, parts, out_hbm, acc, rest, out, left, right, sems
 ):
     me = mine[0]
     for n in range(4):
@@ -354,6 +362,7 @@
             copies[-1].start()
 
     finish(0, EARLY)
+    lay_out(parts, left, right)
     planes = [(piece[0, k], piece[1, k]) for piece in (piece_b0, piece_b1, piece_b2, piece_b3) for k in range(piece.shape[1])]
     for k, (re, im) in enumerate(twice_diffracted(planes, left, right)):
         rest[0, k] = re
@@ -461,17 +470,19 @@
     )(mine, phases1, energies1, arrived1, small1, in_hbm(send.reshape(PEERS, MESSAGE, 1, BLOCK)))
     field_b = [shifted(source, "cuts", 2) for source in sources]
 
-    left_two, right_two = deep_left(left_form(*two)), deep_right(right_form(*two))
+    operator = quarters(*two)
+    tables = [vmem(2 * GRID, 6 * GRID, dtype=jnp.bfloat16), vmem(6 * GRID, 2 * GRID, dtype=jnp.bfloat16)]
 
     def exchange(send, places, field, shared_0, shared_1, beam):
         early = pl.pallas_call(
             early_kernel,
             out_shape=shape(2, EARLY + 1, GRID, GRID),
-            in_specs=[scalar] + [whole()] * 5,
+            in_specs=[scalar] + [whole()] * 4,
             out_specs=whole(),
+            scratch_shapes=tables,
             compiler_params=params,
             name="early_field",
-        )(mine, in_hbm(shared_0), in_hbm(shared_1), in_hbm(beam), left_two, right_two)
+        )(mine, in_hbm(shared_0), in_hbm(shared_1), in_hbm(beam), operator)
         handed = jnp.where(core == 0, shared_1, shared_0)
         source_c = jnp.where(mine[0] % 8 >= 6, handed[:, LATE - GROUPS :], field[:, LATE:])
         field_c = lax.ppermute(source_c, "cuts", late_pairs())
@@ -506,17 +517,18 @@
     out = pl.pallas_call(
         last_kernel,
         out_shape=shape(2, GROUPS, GRID, GRID),
-        in_specs=[scalar] + [whole()] * 10,
+        in_specs=[scalar] + [whole()] * 9,
         out_specs=remain,
         scratch_shapes=[
             vmem(4, GROUPS, 128),
             vmem(2, GROUPS - EARLY, GRID, GRID),
             vmem(2, GROUPS, GRID, GRID),
+            *tables,
             pltpu.SemaphoreType.DMA((6,)),
         ],
         compiler_params=params,
         name="last_field",
-    )(mine, early, *field_b, field_c, small, in_hbm(beam), left_two, right_two)
+    )(mine, early, *field_b, field_c, small, in_hbm(beam), operator)
     return (
         out.reshape(2, GROUPS, 1, GRID, GRID),
         phase_out.reshape(GROUPS, 1, NBS * BLOCK),

time: 92.7 us -> 92.3 us (level)
  no operation moved by 1% of the time
where the time goes in v12:
time: 92.3 us; the launch traced here: 91.7 us
  waiting for transfers between devices  39.1 us (42%)
  Pallas kernels  25.4 us (28%)
  starting transfers between devices  22 us (24%)
  local copies, waits for them, and re-layouts  2.24 us (2%)
  other arithmetic  2.07 us (2%)
    all_to_all x1, waiting for transfers between devices, exchange(): lax.all_to_all(send.reshape(ROWS, 1, BLOCK), 'cuts', split_axis=0, concat...  34.1 us
    all_to_all x1, starting transfers between devices, exchange(): lax.all_to_all(send.reshape(ROWS, 1, BLOCK), 'cuts', split_axis=0, concat...  11.2 us
    pallas_call x1, Pallas kernels, per_device(): pl.pallas_call(first_kernel, out_shape=(pltpu.HBM((ROWS, 1, BLOCK), jnp.f...  9.54 us
    pallas_call x1, Pallas kernels, exchange(): pl.pallas_call(pick_kernel, out_shape=(shape(COUNT, BLOCK), shape(COUNT,...  5.05 us
    ppermute x5, starting transfers between devices, shifted(): return lax.ppermute(value, axis, pairs)  4.84 us
    pallas_call x1, Pallas kernels, per_device(): pl.pallas_call(last_kernel, out_shape=shape(2, GROUPS, GRID, GRID), in_sp...  4.65 us
    ppermute x5, waiting for transfers between devices, shifted(): return lax.ppermute(value, axis, pairs)  4.42 us
    pallas_call x1, Pallas kernels, exchange(): pl.pallas_call(early_kernel, out_shape=shape(2, EARLY + 1, GRID, GRID), i...  3.67 us
  transfers between devices with their start and end apart: 9, of which 3 were waited for; matrix products, arithmetic and copies ran while one was open for 2% of the time, Pallas kernels for 23%

profile of v12, /device:TPU:0, one launch (start us, length us, event | category | flops | bytes accessed | tf_op | source)
XLA Modules:
  0.0 91.7 jit_solution(3462150771921063484)
XLA Ops:
  0.7 1.4 %dynamic-slice_bitcast_fusion = (f32[2,5,128,128]{3,2,1,0:T(8,128)S(1)}, f32[2,5,128,128]{3,2,1,0:T(8,128)S(1)}) fusion(f32[2,16,1,128,128]{4,3,2,1,0:T(8,128)} %param.11, s32[]{:T(128)S(6)} %select_n.35, s32[]{:T(128)S(6)} %select_n.34), kind=kLoop, calls=%fused_computation.2 | loop fusion | bytes 2621448 | tf_op jit(solution)/shard_map/dynamic_slice | solution.py:426
  2.1 1.5 %collective-permute-start.3 = (f32[2,5,128,128]{3,2,1,0:T(8,128)S(1)}, f32[2,5,128,128]{3,2,1,0:T(8,128)}, u32[]{:S(2)}, u32[]{:S(2)}) collective-permute-start(f32[2,5,128,128]{3,2,1,0:T(8,128)S(1)} %get-tuple-element.75), channel_id=1, source_target_pairs={{1,3},{3,5},{5,7},{7,9},{9,11},{11,13},{13,15},{15,17},{17,19},{19... | collective-permute-start | bytes 1966088 | tf_op jit(solution)/shard_map/ppermute | solution.py:426
  3.6 3.5 %collective-permute-start.2 = (f32[2,5,128,128]{3,2,1,0:T(8,128)S(1)}, f32[2,5,128,128]{3,2,1,0:T(8,128)S(1)}, u32[]{:S(2)}, u32[]{:S(2)}) collective-permute-start(f32[2,5,128,128]{3,2,1,0:T(8,128)S(1)} %get-tuple-element.76), channel_id=1, source_target_pairs={{0,2},{2,4},{4,6},{6,8},{8,10},{10,12},{12,14},{14,16},{16,18},{18... | collective-permute-start | bytes 1966088 | tf_op jit(solution)/shard_map/ppermute | solution.py:425
  7.0 9.5 %push_place.1 = (f32[5248,1,128]{2,1,0:T(1,128)}, f32[1024,128]{1,0:T(8,128)S(1)}, f32[1024,128]{1,0:T(8,128)S(1)}, s32[8,1024]{1,0:T(8,128)}, f32[3,128,128]{2,...) custom-call(s32[1]{0:T(128)} %bitcast.3.mine, ...), custom_call_target="tpu_custom_call" | custom-call | tf_op jit(solution)/shard_map/push_place/pallas_call | solution.py:428
  16.6 0.1 collective-permute-start.1
  16.7 1.6 %collective-permute-start.4 = (f32[2,2,128,128]{3,2,1,0:T(8,128)}, f32[2,2,128,128]{3,2,1,0:T(8,128)S(1)}, u32[]{:S(2)}, u32[]{:S(2)}) collective-permute-start(f32[2,2,128,128]{3,2,1,0:T(8,128)} %get-tuple-element.62), channel_id=1, source_target_pairs={{0,2},{1,3},{2,4},{3,5},{4,6},{5,7},{6,8},{7,9},{8,10},{9,11},{10,... | collective-permute-start | bytes 786440 | tf_op jit(solution)/shard_map/ppermute | solution.py:393
  18.2 3.2 %collective-permute-start.5 = (f32[2,2,128,128]{3,2,1,0:T(8,128)}, f32[2,2,128,128]{3,2,1,0:T(8,128)S(1)}, u32[]{:S(2)}, u32[]{:S(2)}) collective-permute-start(f32[2,2,128,128]{3,2,1,0:T(8,128)} %get-tuple-element.63), channel_id=1, source_target_pairs={{0,2},{1,3},{2,4},{3,5},{4,6},{5,7},{6,8},{7,9},{8,10},{9,11},{10,... | collective-permute-start | bytes 786440 | tf_op jit(solution)/shard_map/ppermute | solution.py:393
  21.4 4.4 %collective-permute-done.1.arrived = f32[4,16,128]{2,1,0:T(8,128)S(1)} collective-permute-done((f32[4,16,128]{2,1,0:T(8,128)S(1)}, f32[4,16,128]{2,1,0:T(8,128)S(1)}, u32[]{:S(2)}, u32[]{:S(2)}) %collective-permute-start.1) | collective-permute-done | bytes 32800 | tf_op jit(solution)/shard_map/ppermute | solution.py:393
  25.8 0.0 collective-permute-start.6
  25.9 0.0 collective-permute-done.3
  25.9 0.0 collective-permute-start.7
  25.9 0.0 copy-start.1
  25.9 2.5 %second_push.1 = f32[128,41,1,128]{3,2,1,0:T(1,128)} custom-call(s32[1]{0:T(128)} %bitcast.3.mine, f32[1024,128]{1,0:T(8,128)S(1)} %get-tuple-element.55.phases1, f32[1024,128]{1,0:T(8,128)S(1)} %get-tuple-element.56.energies1, f32[4,16,128]{2,1,0:T(8,128)S(1)} %collective-permute-done.1.arrived, ...), custom_call_target="tpu_custom_call", output_to_operand_aliasing={{}: (5, {})} | custom-call | tf_op jit(solution)/shard_map/second_push/pallas_call | solution.py:461
  28.4 0.7 collective-permute-done.2
  29.1 0.0 copy-done.1
  29.1 57.9 %conditional.1 = (f32[2,6,128,128]{3,2,1,0:T(8,128)}, f32[2,3,128,128]{3,2,1,0:T(8,128)}, f32[4,16,128]{2,1,0:T(8,128)S(1)}, f32[16,1,8192]{2,1,0:T(1,128)}, f32[16,1,8192]{2,1,0:T(1,128)}) conditional(s32[]{:T(128)} %convert_element_type.3, () %tuple.21, (f32[128,41,1,128]{3,2,1,0:T(1,128)}, s32[1]{0:T(128)}, f32[2,5,128,128]{3,2,1,0:T(8,128)S(1)}, ...), branch_computations={%region_0.1_spmd, %region_1.2_spmd} | conditional | flops 196621 | bytes 13828365 | solution.py:514
  29.1 0.0 copy-start
  29.1 0.8 copy-done
  29.9 11.2 %all-to-all-start = ((f32[5248,1,128]{2,1,0:T(1,128)}), f32[5248,1,128]{2,1,0:T(1,128)S(1)}, u32[]{:S(2)}, u32[]{:S(2)}) async-start(f32[5248,1,128]{2,1,0:T(1,128)} %bitcast.18), calls=%async_computation | async-start | bytes 5373952 | tf_op jit(solution)/shard_map/cond/branch_1_fun/all_to_all | solution.py:489
  41.2 2.1 %fusion = f32[2,3,128,128]{3,2,1,0:T(8,128)} fusion(f32[2,5,128,128]{3,2,1,0:T(8,128)} %copy-done, f32[2,5,128,128]{3,2,1,0:T(8,128)} %get-tuple-element.25.piece_1, f32[2,16,128,128]{3,2,1,0:T(8,128)} %get-tuple-element.31, pred[]{:T(512)S(6)} %eq.5, pred[]{:T(512)S(6)} %ge.2), kind=kLoop, calls=%fused_computation.1 | loop fusion | flops 196608 | bytes 1572866 | tf_op jit(solution)/shard_map/cond/branch_1_fun/jit(_where)/select_n | solution.py:487
  43.2 1.0 %collective-permute-start = (f32[2,3,128,128]{3,2,1,0:T(8,128)}, f32[2,3,128,128]{3,2,1,0:T(8,128)}, u32[]{:S(2)}, u32[]{:S(2)}) collective-permute-start(f32[2,3,128,128]{3,2,1,0:T(8,128)} %fusion), channel_id=1, source_target_pairs={{0,2},{1,3},{2,4},{3,5},{4,6},{5,7},{6,0},{7,1},{8,10},{9,11},{10,... | collective-permute-start | bytes 1179656 | tf_op jit(solution)/shard_map/cond/branch_1_fun/ppermute | solution.py:488
  44.2 3.7 %early_field.1 = f32[2,6,128,128]{3,2,1,0:T(8,128)} custom-call(s32[1]{0:T(128)} %get-tuple-element.23.mine, f32[2,5,128,128]{3,2,1,0:T(8,128)} %copy-done, f32[2,5,128,128]{3,2,1,0:T(8,128)} %get-tuple-element.25.piece_1, f32[3,128,128]{2,1,0:T(8,128)} %get-tuple-element.26.beam, bf16[4,128,128]{2,1,0:T(8,128)(2,1)} %get-tuple-element.27.parts), custom_call_target="tpu_custom_call" | custom-call | tf_op jit(solution)/shard_map/cond/branch_1_fun/early_field/pallas_call | solution.py:477
  47.9 34.1 %all-to-all-done.recv = f32[5248,1,128]{2,1,0:T(1,128)S(1)} async-done(((f32[5248,1,128]{2,1,0:T(1,128)}), f32[5248,1,128]{2,1,0:T(1,128)S(1)}, u32[]{:S(2)}, u32[]{:S(2)}) %all-to-all-start) | async-done | bytes 2687008 | tf_op jit(solution)/shard_map/cond/branch_1_fun/all_to_all | solution.py:489
  81.9 5.0 %pick.1 = (f32[1024,128]{1,0:T(8,128)}, f32[1024,128]{1,0:T(8,128)}, f32[4,16,128]{2,1,0:T(8,128)S(1)}) custom-call(s32[1]{0:T(128)} %get-tuple-element.23.mine, f32[5248,1,128]{2,1,0:T(1,128)S(1)} %all-to-all-done.recv, s32[8,1024]{1,0:T(8,128)S(1)} %get-tuple-element.33.places), custom_call_target="tpu_custom_call" | custom-call | tf_op jit(solution)/shard_map/cond/branch_1_fun/pick/pallas_call | solution.py:491
  87.0 0.0 collective-permute-done
  87.0 0.0 collective-permute-done.4.piece_b0
  87.0 0.0 collective-permute-done.5.piece_b1
  87.0 0.0 collective-permute-done.6.piece_b2
  87.0 0.0 collective-permute-done.7.piece_b3
  87.0 4.7 %last_field.1 = f32[2,16,128,128]{3,2,1,0:T(8,128)} custom-call(s32[1]{0:T(128)} %bitcast.3.mine, f32[2,6,128,128]{3,2,1,0:T(8,128)} %get-tuple-element.61.early, f32[2,2,128,128]{3,2,1,0:T(8,128)S(1)} %collective-permute-done.4.piece_b0, f32[2,2,128,128]{3,2,1,0:T(8,128)S(1)} %collective-permute-done.5.piece_b1, ...), custom_call_target="tpu_custom_call" | custom-call | tf_op jit(solution)/shard_map/last_field/pallas_call | solution.py:517
Async XLA Ops:
  2.1 23.8 %collective-permute-start.3 = (f32[2,5,128,128]{3,2,1,0:T(8,128)S(1)}, f32[2,5,128,128]{3,2,1,0:T(8,128)}, u32[]{:S(2)}, u32[]{:S(2)}) collective-permute-start(f32[2,5,128,128]{3,2,1,0:T(8,128)S(1)} %get-tuple-element.75), channel_id=1, source_target_pairs={{1,3},{3,5},{5,7},{7,9},{9,11},{11,13},{13,15},{15,17},{17,19},{19... | collective-permute-start | bytes 1966088 | tf_op jit(solution)/shard_map/ppermute | solution.py:426
  3.6 25.5 %collective-permute-start.2 = (f32[2,5,128,128]{3,2,1,0:T(8,128)S(1)}, f32[2,5,128,128]{3,2,1,0:T(8,128)S(1)}, u32[]{:S(2)}, u32[]{:S(2)}) collective-permute-start(f32[2,5,128,128]{3,2,1,0:T(8,128)S(1)} %get-tuple-element.76), channel_id=1, source_target_pairs={{0,2},{2,4},{4,6},{6,8},{8,10},{10,12},{12,14},{14,16},{16,18},{18... | collective-permute-start | bytes 1966088 | tf_op jit(solution)/shard_map/ppermute | solution.py:425
  16.6 9.3 %collective-permute-start.1 = (f32[4,16,128]{2,1,0:T(8,128)S(1)}, f32[4,16,128]{2,1,0:T(8,128)S(1)}, u32[]{:S(2)}, u32[]{:S(2)}) collective-permute-start(f32[4,16,128]{2,1,0:T(8,128)S(1)} %get-tuple-element.57.own), channel_id=1, source_target_pairs={{0,1},{1,2},{2,3},{3,4},{4,5},{5,6},{6,7},{7,8},{8,9},{9,10},{10,1... | collective-permute-start | bytes 98312 | tf_op jit(solution)/shard_map/ppermute | solution.py:393
  16.7 70.3 %collective-permute-start.4 = (f32[2,2,128,128]{3,2,1,0:T(8,128)}, f32[2,2,128,128]{3,2,1,0:T(8,128)S(1)}, u32[]{:S(2)}, u32[]{:S(2)}) collective-permute-start(f32[2,2,128,128]{3,2,1,0:T(8,128)} %get-tuple-element.62), channel_id=1, source_target_pairs={{0,2},{1,3},{2,4},{3,5},{4,6},{5,7},{6,8},{7,9},{8,10},{9,11},{10,... | collective-permute-start | bytes 786440 | tf_op jit(solution)/shard_map/ppermute | solution.py:393
  18.2 68.8 %collective-permute-start.5 = (f32[2,2,128,128]{3,2,1,0:T(8,128)}, f32[2,2,128,128]{3,2,1,0:T(8,128)S(1)}, u32[]{:S(2)}, u32[]{:S(2)}) collective-permute-start(f32[2,2,128,128]{3,2,1,0:T(8,128)} %get-tuple-element.63), channel_id=1, source_target_pairs={{0,2},{1,3},{2,4},{3,5},{4,6},{5,7},{6,8},{7,9},{8,10},{9,11},{10,... | collective-permute-start | bytes 786440 | tf_op jit(solution)/shard_map/ppermute | solution.py:393
  25.8 61.2 %collective-permute-start.6 = (f32[2,2,128,128]{3,2,1,0:T(8,128)}, f32[2,2,128,128]{3,2,1,0:T(8,128)S(1)}, u32[]{:S(2)}, u32[]{:S(2)}) collective-permute-start(f32[2,2,128,128]{3,2,1,0:T(8,128)} %get-tuple-element.64), channel_id=1, source_target_pairs={{0,2},{1,3},{2,4},{3,5},{4,6},{5,7},{6,8},{7,9},{8,10},{9,11},{10,... | collective-permute-start | bytes 786440 | tf_op jit(solution)/shard_map/ppermute | solution.py:393
  25.9 61.2 %collective-permute-start.7 = (f32[2,2,128,128]{3,2,1,0:T(8,128)}, f32[2,2,128,128]{3,2,1,0:T(8,128)}, u32[]{:S(2)}, u32[]{:S(2)}) collective-permute-start(f32[2,2,128,128]{3,2,1,0:T(8,128)} %get-tuple-element.65), channel_id=1, source_target_pairs={{0,2},{1,3},{2,4},{3,5},{4,6},{5,7},{6,8},{7,9},{8,10},{9,11},{10,... | collective-permute-start | bytes 786440 | tf_op jit(solution)/shard_map/ppermute | solution.py:393
  25.9 3.2 %copy-start.1 = (s32[8,1024]{1,0:T(8,128)S(1)}, s32[8,1024]{1,0:T(8,128)}, u32[]{:S(2)}) copy-start(s32[8,1024]{1,0:T(8,128)} %get-tuple-element.60) | copy-start | bytes 98308
  29.1 0.8 copy-start
  29.9 52.0 %all-to-all-start = ((f32[5248,1,128]{2,1,0:T(1,128)}), f32[5248,1,128]{2,1,0:T(1,128)S(1)}, u32[]{:S(2)}, u32[]{:S(2)}) async-start(f32[5248,1,128]{2,1,0:T(1,128)} %bitcast.18), calls=%async_computation | async-start | bytes 5373952 | tf_op jit(solution)/shard_map/cond/branch_1_fun/all_to_all | solution.py:489
  43.2 43.7 %collective-permute-start = (f32[2,3,128,128]{3,2,1,0:T(8,128)}, f32[2,3,128,128]{3,2,1,0:T(8,128)}, u32[]{:S(2)}, u32[]{:S(2)}) collective-permute-start(f32[2,3,128,128]{3,2,1,0:T(8,128)} %fusion), channel_id=1, source_target_pairs={{0,2},{1,3},{2,4},{3,5},{4,6},{5,7},{6,0},{7,1},{8,10},{9,11},{10,... | collective-permute-start | bytes 1179656 | tf_op jit(solution)/shard_map/cond/branch_1_fun/ppermute | solution.py:488

commit v13 on v12

--- a/solution.py
+++ b/solution.py
@@ -25,8 +25,8 @@
 MESSAGE = 2 * CAP + 1
 ROWS = PEERS * MESSAGE
 BATCH = 32
-EARLY, LATE = 5, 13
-MIDDLE = ((5, 7), (7, 9), (9, 11), (11, 13))
+EARLY, LATE = 5, 11
+MIDDLE = ((5, 7), (7, 9), (9, 11))
 VMEM_LIMIT = 24 * 1024 * 1024
 HIGHEST = lax.Precision.HIGHEST
 
@@ -120,7 +120,7 @@
 
 def first_kernel(
     mine, field_hbm, profile_hbm, bins_hbm, jitter_hbm, energy_hbm, delays_hbm, left_hbm, right_hbm,
-    send_hbm, phases, energies, places_hbm, beam, small, middle_0, middle_1, middle_2, middle_3,
+    send_hbm, phases, energies, places_hbm, beam, small, middle_0, middle_1, middle_2,
     field, profile, bins, jitter, energy, delays, left, right, acc, send, places, index_v, index, sems,
 ):
     pairs = [
@@ -148,7 +148,7 @@
     beam[2] = p
     copies[4].wait()
     kept = [pltpu.make_async_copy(places, places_hbm, sems.at[8])]
-    for middle, (low, high) in zip((middle_0, middle_1, middle_2, middle_3), MIDDLE):
+    for middle, (low, high) in zip((middle_0, middle_1, middle_2), MIDDLE):
         for c in range(2):
             span = pl.ds(low, high - low)
             kept.append(pltpu.make_async_copy(field.at[c, span], middle.at[c], sems.at[8 + len(kept)]))
@@ -338,7 +338,7 @@
 
 
 def last_kernel(
-    mine, early, piece_b0, piece_b1, piece_b2, piece_b3, piece_c, small, beam, parts, out_hbm, acc, rest, out, left, right, sems
+    mine, early, piece_b0, piece_b1, piece_b2, piece_c, small, beam, parts, out_hbm, acc, rest, out, left, right, sems
 ):
     me = mine[0]
     for n in range(4):
@@ -363,7 +363,7 @@
 
     finish(0, EARLY)
     lay_out(parts, left, right)
-    planes = [(piece[0, k], piece[1, k]) for piece in (piece_b0, piece_b1, piece_b2, piece_b3) for k in range(piece.shape[1])]
+    planes = [(piece[0, k], piece[1, k]) for piece in (piece_b0, piece_b1, piece_b2) for k in range(piece.shape[1])]
     for k, (re, im) in enumerate(twice_diffracted(planes, left, right)):
         rest[0, k] = re
         rest[1, k] = im
@@ -517,7 +517,7 @@
     out = pl.pallas_call(
         last_kernel,
         out_shape=shape(2, GROUPS, GRID, GRID),
-        in_specs=[scalar] + [whole()] * 9,
+        in_specs=[scalar] + [whole()] * 8,
         out_specs=remain,
         scratch_shapes=[
             vmem(4, GROUPS, 128),

time: 92.3 us -> 91.7 us (level)
  starting transfers between devices: 22 us -> 19.1 us
  local copies, waits for them, and re-layouts: 2.24 us -> 3.54 us
    all_to_all x1, waiting for transfers between devices: 34.1 us -> 30.3 us  [exchange(): lax.all_to_all(send.reshape(ROWS, 1, BLOCK), 'cuts', split_axis=0, concat...]
    ppermute x1, waiting for transfers between devices: 0.01 us -> 3.21 us  [exchange(): field_c = lax.ppermute(source_c, 'cuts', late_pairs())]
    all_to_all x1, starting transfers between devices: 11.2 us -> 8.33 us  [exchange(): lax.all_to_all(send.reshape(ROWS, 1, BLOCK), 'cuts', split_axis=0, concat...]
    ppermute x1, waiting for transfers between devices: 0.65 us -> 1.89 us  [per_device(): lax.ppermute(lax.dynamic_slice_in_dim(field, core * (GROUPS - EARLY), EAR...]
    dynamic_slice x1, local copies, waits for them, and re-layouts: 1.4 us -> 2.48 us  [per_device(): lax.dynamic_slice_in_dim(field, (1 - core) * (GROUPS - EARLY), EARLY, 1)]
    ppermute x5 -> x4, starting transfers between devices: 4.84 us -> 5.62 us  [shifted(): return lax.ppermute(value, axis, pairs)]
    ppermute x5 -> x4, waiting for transfers between devices: 4.42 us -> 4.34 us  [shifted(): return lax.ppermute(value, axis, pairs)]
  transfers between devices with their start and end apart: 9 -> 8, of which waited for: 3 -> 4; matrix products, arithmetic and copies ran while one was open for 2% -> 2% of each run, Pallas kernels for 23% -> 23%
where the time goes in v13:
time: 91.7 us; the launch traced here: 90.8 us
  waiting for transfers between devices  39.7 us (43%)
  Pallas kernels  25.4 us (28%)
  starting transfers between devices  19.1 us (21%)
  local copies, waits for them, and re-layouts  3.54 us (4%)
  other arithmetic  2.27 us (2%)
    all_to_all x1, waiting for transfers between devices, exchange(): lax.all_to_all(send.reshape(ROWS, 1, BLOCK), 'cuts', split_axis=0, concat...  30.3 us
    pallas_call x1, Pallas kernels, per_device(): pl.pallas_call(first_kernel, out_shape=(pltpu.HBM((ROWS, 1, BLOCK), jnp.f...  9.58 us
    all_to_all x1, starting transfers between devices, exchange(): lax.all_to_all(send.reshape(ROWS, 1, BLOCK), 'cuts', split_axis=0, concat...  8.33 us
    ppermute x4, starting transfers between devices, shifted(): return lax.ppermute(value, axis, pairs)  5.62 us
    pallas_call x1, Pallas kernels, exchange(): pl.pallas_call(pick_kernel, out_shape=(shape(COUNT, BLOCK), shape(COUNT,...  5.05 us
    pallas_call x1, Pallas kernels, per_device(): pl.pallas_call(last_kernel, out_shape=shape(2, GROUPS, GRID, GRID), in_sp...  4.63 us
    ppermute x4, waiting for transfers between devices, shifted(): return lax.ppermute(value, axis, pairs)  4.34 us
    pallas_call x1, Pallas kernels, exchange(): pl.pallas_call(early_kernel, out_shape=shape(2, EARLY + 1, GRID, GRID), i...  3.63 us
  transfers between devices with their start and end apart: 8, of which 4 were waited for; matrix products, arithmetic and copies ran while one was open for 2% of the time, Pallas kernels for 23%

profile of v13, /device:TPU:0, one launch (start us, length us, event | category | flops | bytes accessed | tf_op | source)
XLA Modules:
  0.0 90.8 jit_solution(5015746859233141908)
XLA Ops:
  0.7 2.5 %dynamic-slice_bitcast_fusion = (f32[2,5,128,128]{3,2,1,0:T(8,128)}, f32[2,5,128,128]{3,2,1,0:T(8,128)}) fusion(f32[2,16,1,128,128]{4,3,2,1,0:T(8,128)} %param.11, s32[]{:T(128)S(6)} %select_n.33, s32[]{:T(128)S(6)} %select_n.32), kind=kLoop, calls=%fused_computation.1 | loop fusion | bytes 2621448 | tf_op jit(solution)/shard_map/dynamic_slice | solution.py:426
  3.1 0.7 collective-permute-start.3
  3.8 3.5 %collective-permute-start.2 = (f32[2,5,128,128]{3,2,1,0:T(8,128)}, f32[2,5,128,128]{3,2,1,0:T(8,128)S(1)}, u32[]{:S(2)}, u32[]{:S(2)}) collective-permute-start(f32[2,5,128,128]{3,2,1,0:T(8,128)} %get-tuple-element.74), channel_id=1, source_target_pairs={{0,2},{2,4},{4,6},{6,8},{8,10},{10,12},{12,14},{14,16},{16,18},{18... | collective-permute-start | bytes 1966088 | tf_op jit(solution)/shard_map/ppermute | solution.py:425
  7.3 9.6 %push_place.1 = (f32[5248,1,128]{2,1,0:T(1,128)}, f32[1024,128]{1,0:T(8,128)S(1)}, f32[1024,128]{1,0:T(8,128)S(1)}, s32[8,1024]{1,0:T(8,128)}, f32[3,128,128]{2,...) custom-call(s32[1]{0:T(128)} %bitcast.3.mine, ...), custom_call_target="tpu_custom_call" | custom-call | tf_op jit(solution)/shard_map/push_place/pallas_call | solution.py:428
  16.9 0.1 collective-permute-start.1
  17.0 1.6 %collective-permute-start.4 = (f32[2,2,128,128]{3,2,1,0:T(8,128)}, f32[2,2,128,128]{3,2,1,0:T(8,128)S(1)}, u32[]{:S(2)}, u32[]{:S(2)}) collective-permute-start(f32[2,2,128,128]{3,2,1,0:T(8,128)} %get-tuple-element.61), channel_id=1, source_target_pairs={{0,2},{1,3},{2,4},{3,5},{4,6},{5,7},{6,8},{7,9},{8,10},{9,11},{10,... | collective-permute-start | bytes 786440 | tf_op jit(solution)/shard_map/ppermute | solution.py:393
  18.6 4.0 %collective-permute-start.5 = (f32[2,2,128,128]{3,2,1,0:T(8,128)}, f32[2,2,128,128]{3,2,1,0:T(8,128)S(1)}, u32[]{:S(2)}, u32[]{:S(2)}) collective-permute-start(f32[2,2,128,128]{3,2,1,0:T(8,128)} %get-tuple-element.62), channel_id=1, source_target_pairs={{0,2},{1,3},{2,4},{3,5},{4,6},{5,7},{6,8},{7,9},{8,10},{9,11},{10,... | collective-permute-start | bytes 786440 | tf_op jit(solution)/shard_map/ppermute | solution.py:393
  22.5 4.3 %collective-permute-done.1.arrived = f32[4,16,128]{2,1,0:T(8,128)S(1)} collective-permute-done((f32[4,16,128]{2,1,0:T(8,128)S(1)}, f32[4,16,128]{2,1,0:T(8,128)S(1)}, u32[]{:S(2)}, u32[]{:S(2)}) %collective-permute-start.1) | collective-permute-done | bytes 32800 | tf_op jit(solution)/shard_map/ppermute | solution.py:393
  26.9 0.0 collective-permute-start.6
  26.9 0.0 copy-start.3
  26.9 2.5 %second_push.1 = f32[128,41,1,128]{3,2,1,0:T(1,128)} custom-call(s32[1]{0:T(128)} %bitcast.3.mine, f32[1024,128]{1,0:T(8,128)S(1)} %get-tuple-element.54.phases1, f32[1024,128]{1,0:T(8,128)S(1)} %get-tuple-element.55.energies1, f32[4,16,128]{2,1,0:T(8,128)S(1)} %collective-permute-done.1.arrived, ...), custom_call_target="tpu_custom_call", output_to_operand_aliasing={{}: (5, {})} | custom-call | tf_op jit(solution)/shard_map/second_push/pallas_call | solution.py:461
  29.4 0.0 collective-permute-done.3
  29.4 1.9 %collective-permute-done.2 = f32[2,5,128,128]{3,2,1,0:T(8,128)S(1)} collective-permute-done((f32[2,5,128,128]{3,2,1,0:T(8,128)}, f32[2,5,128,128]{3,2,1,0:T(8,128)S(1)}, u32[]{:S(2)}, u32[]{:S(2)}) %collective-permute-start.2) | collective-permute-done | bytes 655392 | tf_op jit(solution)/shard_map/ppermute | solution.py:425
  31.3 0.0 copy-done.3
  31.3 54.8 %conditional.1 = (f32[2,6,128,128]{3,2,1,0:T(8,128)}, f32[2,5,128,128]{3,2,1,0:T(8,128)}, f32[4,16,128]{2,1,0:T(8,128)S(1)}, f32[16,1,8192]{2,1,0:T(1,128)}, f32[16,1,8192]{2,1,0:T(1,128)}) conditional(s32[]{:T(128)} %convert_element_type.3, () %tuple.21, (f32[128,41,1,128]{3,2,1,0:T(1,128)}, s32[1]{0:T(128)}, f32[2,5,128,128]{3,2,1,0:T(8,128)S(1)}, ...), branch_computations={%region_0.1_spmd, %region_1.2_spmd} | conditional | flops 327693 | bytes 19071300 | solution.py:514
  31.3 0.0 copy-start
  31.3 0.0 copy-start.1
  31.3 0.8 copy-done
  32.1 0.2 copy-done.1
  32.3 8.3 %all-to-all-start = ((f32[5248,1,128]{2,1,0:T(1,128)}), f32[5248,1,128]{2,1,0:T(1,128)S(1)}, u32[]{:S(2)}, u32[]{:S(2)}) async-start(f32[5248,1,128]{2,1,0:T(1,128)} %bitcast.18), calls=%async_computation | async-start | bytes 5373952 | tf_op jit(solution)/shard_map/cond/branch_1_fun/all_to_all | solution.py:489
  40.7 0.0 copy-start.2
  40.7 2.3 %slice_select_fusion = f32[2,5,128,128]{3,2,1,0:T(8,128)} fusion(f32[2,16,128,128]{3,2,1,0:T(8,128)} %get-tuple-element.31, f32[2,5,128,128]{3,2,1,0:T(8,128)} %copy-done, f32[2,5,128,128]{3,2,1,0:T(8,128)} %copy-done.1, pred[]{:T(512)S(6)} %eq.5, pred[]{:T(512)S(6)} %ge.2), kind=kLoop, calls=%fused_computation | loop fusion | flops 327680 | bytes 2621442 | tf_op jit(solution)/shard_map/cond/branch_1_fun/jit(_where)/select_n | solution.py:487
  43.0 1.0 %collective-permute-start = (f32[2,5,128,128]{3,2,1,0:T(8,128)}, f32[2,5,128,128]{3,2,1,0:T(8,128)}, u32[]{:S(2)}, u32[]{:S(2)}) collective-permute-start(f32[2,5,128,128]{3,2,1,0:T(8,128)} %slice_select_fusion), channel_id=1, source_target_pairs={{0,2},{1,3},{2,4},{3,5},{4,6},{5,7},{6,0},{7,1},{8,10},{9,11},{10,... | collective-permute-start | bytes 1966088 | tf_op jit(solution)/shard_map/cond/branch_1_fun/ppermute | solution.py:488
  43.9 0.0 copy-done.2
  43.9 3.6 %early_field.1 = f32[2,6,128,128]{3,2,1,0:T(8,128)} custom-call(s32[1]{0:T(128)} %get-tuple-element.23.mine, f32[2,5,128,128]{3,2,1,0:T(8,128)} %copy-done.1, f32[2,5,128,128]{3,2,1,0:T(8,128)} %copy-done, f32[3,128,128]{2,1,0:T(8,128)} %get-tuple-element.26.beam, bf16[4,128,128]{2,1,0:T(8,128)(2,1)S(1)} %copy-done.2), custom_call_target="tpu_custom_call" | custom-call | tf_op jit(solution)/shard_map/cond/branch_1_fun/early_field/pallas_call | solution.py:477
  47.6 30.3 %all-to-all-done.recv = f32[5248,1,128]{2,1,0:T(1,128)S(1)} async-done(((f32[5248,1,128]{2,1,0:T(1,128)}), f32[5248,1,128]{2,1,0:T(1,128)S(1)}, u32[]{:S(2)}, u32[]{:S(2)}) %all-to-all-start) | async-done | bytes 2687008 | tf_op jit(solution)/shard_map/cond/branch_1_fun/all_to_all | solution.py:489
  77.9 5.0 %pick.1 = (f32[1024,128]{1,0:T(8,128)}, f32[1024,128]{1,0:T(8,128)}, f32[4,16,128]{2,1,0:T(8,128)S(1)}) custom-call(s32[1]{0:T(128)} %get-tuple-element.23.mine, f32[5248,1,128]{2,1,0:T(1,128)S(1)} %all-to-all-done.recv, s32[8,1024]{1,0:T(8,128)S(1)} %get-tuple-element.33.places), custom_call_target="tpu_custom_call" | custom-call | tf_op jit(solution)/shard_map/cond/branch_1_fun/pick/pallas_call | solution.py:491
  82.9 3.2 %collective-permute-done = f32[2,5,128,128]{3,2,1,0:T(8,128)} collective-permute-done((f32[2,5,128,128]{3,2,1,0:T(8,128)}, f32[2,5,128,128]{3,2,1,0:T(8,128)}, u32[]{:S(2)}, u32[]{:S(2)}) %collective-permute-start) | collective-permute-done | bytes 655392 | tf_op jit(solution)/shard_map/cond/branch_1_fun/ppermute | solution.py:488
  86.1 0.0 collective-permute-done.4.piece_b0
  86.1 0.0 collective-permute-done.5.piece_b1
  86.1 0.0 collective-permute-done.6.piece_b2
  86.1 4.6 %last_field.1 = f32[2,16,128,128]{3,2,1,0:T(8,128)} custom-call(s32[1]{0:T(128)} %bitcast.3.mine, f32[2,6,128,128]{3,2,1,0:T(8,128)} %get-tuple-element.60.early, f32[2,2,128,128]{3,2,1,0:T(8,128)S(1)} %collective-permute-done.4.piece_b0, f32[2,2,128,128]{3,2,1,0:T(8,128)S(1)} %collective-permute-done.5.piece_b1, ...), custom_call_target="tpu_custom_call" | custom-call | tf_op jit(solution)/shard_map/last_field/pallas_call | solution.py:517
Async XLA Ops:
  3.1 26.3 %collective-permute-start.3 = (f32[2,5,128,128]{3,2,1,0:T(8,128)}, f32[2,5,128,128]{3,2,1,0:T(8,128)S(1)}, u32[]{:S(2)}, u32[]{:S(2)}) collective-permute-start(f32[2,5,128,128]{3,2,1,0:T(8,128)} %get-tuple-element.73), channel_id=1, source_target_pairs={{1,3},{3,5},{5,7},{7,9},{9,11},{11,13},{13,15},{15,17},{17,19},{19... | collective-permute-start | bytes 1966088 | tf_op jit(solution)/shard_map/ppermute | solution.py:426
  3.8 27.5 %collective-permute-start.2 = (f32[2,5,128,128]{3,2,1,0:T(8,128)}, f32[2,5,128,128]{3,2,1,0:T(8,128)S(1)}, u32[]{:S(2)}, u32[]{:S(2)}) collective-permute-start(f32[2,5,128,128]{3,2,1,0:T(8,128)} %get-tuple-element.74), channel_id=1, source_target_pairs={{0,2},{2,4},{4,6},{6,8},{8,10},{10,12},{12,14},{14,16},{16,18},{18... | collective-permute-start | bytes 1966088 | tf_op jit(solution)/shard_map/ppermute | solution.py:425
  16.9 10.0 %collective-permute-start.1 = (f32[4,16,128]{2,1,0:T(8,128)S(1)}, f32[4,16,128]{2,1,0:T(8,128)S(1)}, u32[]{:S(2)}, u32[]{:S(2)}) collective-permute-start(f32[4,16,128]{2,1,0:T(8,128)S(1)} %get-tuple-element.56.own), channel_id=1, source_target_pairs={{0,1},{1,2},{2,3},{3,4},{4,5},{5,6},{6,7},{7,8},{8,9},{9,10},{10,1... | collective-permute-start | bytes 98312 | tf_op jit(solution)/shard_map/ppermute | solution.py:393
  17.0 69.2 %collective-permute-start.4 = (f32[2,2,128,128]{3,2,1,0:T(8,128)}, f32[2,2,128,128]{3,2,1,0:T(8,128)S(1)}, u32[]{:S(2)}, u32[]{:S(2)}) collective-permute-start(f32[2,2,128,128]{3,2,1,0:T(8,128)} %get-tuple-element.61), channel_id=1, source_target_pairs={{0,2},{1,3},{2,4},{3,5},{4,6},{5,7},{6,8},{7,9},{8,10},{9,11},{10,... | collective-permute-start | bytes 786440 | tf_op jit(solution)/shard_map/ppermute | solution.py:393
  18.6 67.6 %collective-permute-start.5 = (f32[2,2,128,128]{3,2,1,0:T(8,128)}, f32[2,2,128,128]{3,2,1,0:T(8,128)S(1)}, u32[]{:S(2)}, u32[]{:S(2)}) collective-permute-start(f32[2,2,128,128]{3,2,1,0:T(8,128)} %get-tuple-element.62), channel_id=1, source_target_pairs={{0,2},{1,3},{2,4},{3,5},{4,6},{5,7},{6,8},{7,9},{8,10},{9,11},{10,... | collective-permute-start | bytes 786440 | tf_op jit(solution)/shard_map/ppermute | solution.py:393
  26.9 59.3 %collective-permute-start.6 = (f32[2,2,128,128]{3,2,1,0:T(8,128)}, f32[2,2,128,128]{3,2,1,0:T(8,128)S(1)}, u32[]{:S(2)}, u32[]{:S(2)}) collective-permute-start(f32[2,2,128,128]{3,2,1,0:T(8,128)} %get-tuple-element.63), channel_id=1, source_target_pairs={{0,2},{1,3},{2,4},{3,5},{4,6},{5,7},{6,8},{7,9},{8,10},{9,11},{10,... | collective-permute-start | bytes 786440 | tf_op jit(solution)/shard_map/ppermute | solution.py:393
  26.9 4.4 %copy-start.3 = (s32[8,1024]{1,0:T(8,128)S(1)}, s32[8,1024]{1,0:T(8,128)}, u32[]{:S(2)}) copy-start(s32[8,1024]{1,0:T(8,128)} %get-tuple-element.59) | copy-start | bytes 98308
  31.3 0.8 copy-start
  31.3 1.1 %copy-start.1 = (f32[2,5,128,128]{3,2,1,0:T(8,128)}, f32[2,5,128,128]{3,2,1,0:T(8,128)S(1)}, u32[]{:S(2)}) copy-start(f32[2,5,128,128]{3,2,1,0:T(8,128)S(1)} %get-tuple-element.24.piece_0) | copy-start | bytes 1966084 | tf_op jit(solution)/shard_map/cond
  32.3 45.5 %all-to-all-start = ((f32[5248,1,128]{2,1,0:T(1,128)}), f32[5248,1,128]{2,1,0:T(1,128)S(1)}, u32[]{:S(2)}, u32[]{:S(2)}) async-start(f32[5248,1,128]{2,1,0:T(1,128)} %bitcast.18), calls=%async_computation | async-start | bytes 5373952 | tf_op jit(solution)/shard_map/cond/branch_1_fun/all_to_all | solution.py:489
  40.7 3.2 %copy-start.2 = (bf16[4,128,128]{2,1,0:T(8,128)(2,1)S(1)}, bf16[4,128,128]{2,1,0:T(8,128)(2,1)}, u32[]{:S(2)}) copy-start(bf16[4,128,128]{2,1,0:T(8,128)(2,1)} %get-tuple-element.27.parts) | copy-start | bytes 393220 | tf_op jit(solution)/shard_map/cond
  43.0 43.2 %collective-permute-start = (f32[2,5,128,128]{3,2,1,0:T(8,128)}, f32[2,5,128,128]{3,2,1,0:T(8,128)}, u32[]{:S(2)}, u32[]{:S(2)}) collective-permute-start(f32[2,5,128,128]{3,2,1,0:T(8,128)} %slice_select_fusion), channel_id=1, source_target_pairs={{0,2},{1,3},{2,4},{3,5},{4,6},{5,7},{6,0},{7,1},{8,10},{9,11},{10,... | collective-permute-start | bytes 1966088 | tf_op jit(solution)/shard_map/cond/branch_1_fun/ppermute | solution.py:488

commit v14 on v12

--- a/solution.py
+++ b/solution.py
@@ -25,8 +25,8 @@
 MESSAGE = 2 * CAP + 1
 ROWS = PEERS * MESSAGE
 BATCH = 32
-EARLY, LATE = 5, 13
-MIDDLE = ((5, 7), (7, 9), (9, 11), (11, 13))
+EARLY, LATE = 4, 12
+MIDDLE = ((4, 6), (6, 8), (8, 10), (10, 12))
 VMEM_LIMIT = 24 * 1024 * 1024
 HIGHEST = lax.Precision.HIGHEST
 

time: 92.3 us -> 91.1 us (0.987); the launches traced: 91.7 us -> 89.5 us
  waiting for transfers between devices: 39.1 us -> 36.7 us
    all_to_all x1, waiting for transfers between devices: 34.1 us -> 32 us  [exchange(): lax.all_to_all(send.reshape(ROWS, 1, BLOCK), 'cuts', split_axis=0, concat...]
where the time goes in v14:
time: 91.1 us; the launch traced here: 89.5 us
  waiting for transfers between devices  36.7 us (40%)
  Pallas kernels  25.2 us (28%)
  starting transfers between devices  22.6 us (25%)
  other arithmetic  2.11 us (2%)
  local copies, waits for them, and re-layouts  2.1 us (2%)
    all_to_all x1, waiting for transfers between devices, exchange(): lax.all_to_all(send.reshape(ROWS, 1, BLOCK), 'cuts', split_axis=0, concat...  32 us
    all_to_all x1, starting transfers between devices, exchange(): lax.all_to_all(send.reshape(ROWS, 1, BLOCK), 'cuts', split_axis=0, concat...  11.9 us
    pallas_call x1, Pallas kernels, per_device(): pl.pallas_call(first_kernel, out_shape=(pltpu.HBM((ROWS, 1, BLOCK), jnp.f...  9.53 us
    pallas_call x1, Pallas kernels, exchange(): pl.pallas_call(pick_kernel, out_shape=(shape(COUNT, BLOCK), shape(COUNT,...  5.05 us
    ppermute x5, starting transfers between devices, shifted(): return lax.ppermute(value, axis, pairs)  4.87 us
    pallas_call x1, Pallas kernels, per_device(): pl.pallas_call(last_kernel, out_shape=shape(2, GROUPS, GRID, GRID), in_sp...  4.69 us
    ppermute x5, waiting for transfers between devices, shifted(): return lax.ppermute(value, axis, pairs)  3.98 us
    ppermute x1, starting transfers between devices, per_device(): lax.ppermute(lax.dynamic_slice_in_dim(field, core * (GROUPS - EARLY), EAR...  3.47 us
  transfers between devices with their start and end apart: 9, of which 3 were waited for; matrix products, arithmetic and copies ran while one was open for 2% of the time, Pallas kernels for 23%

profile of v14, /device:TPU:0, one launch (start us, length us, event | category | flops | bytes accessed | tf_op | source)
XLA Modules:
  0.0 89.5 jit_solution(2904053263403870996)
XLA Ops:
  0.7 1.3 %dynamic-slice_bitcast_fusion = (f32[2,4,128,128]{3,2,1,0:T(8,128)S(1)}, f32[2,4,128,128]{3,2,1,0:T(8,128)S(1)}) fusion(f32[2,16,1,128,128]{4,3,2,1,0:T(8,128)} %param.11, s32[]{:T(128)S(6)} %select_n.33, s32[]{:T(128)S(6)} %select_n.32), kind=kLoop, calls=%fused_computation.1 | loop fusion | bytes 2097160 | tf_op jit(solution)/shard_map/dynamic_slice | solution.py:426
  2.0 1.5 %collective-permute-start.3 = (f32[2,4,128,128]{3,2,1,0:T(8,128)S(1)}, f32[2,4,128,128]{3,2,1,0:T(8,128)}, u32[]{:S(2)}, u32[]{:S(2)}) collective-permute-start(f32[2,4,128,128]{3,2,1,0:T(8,128)S(1)} %get-tuple-element.75), channel_id=1, source_target_pairs={{1,3},{3,5},{5,7},{7,9},{9,11},{11,13},{13,15},{15,17},{17,19},{19... | collective-permute-start | bytes 1572872 | tf_op jit(solution)/shard_map/ppermute | solution.py:426
  3.4 3.5 %collective-permute-start.2 = (f32[2,4,128,128]{3,2,1,0:T(8,128)S(1)}, f32[2,4,128,128]{3,2,1,0:T(8,128)S(1)}, u32[]{:S(2)}, u32[]{:S(2)}) collective-permute-start(f32[2,4,128,128]{3,2,1,0:T(8,128)S(1)} %get-tuple-element.76), channel_id=1, source_target_pairs={{0,2},{2,4},{4,6},{6,8},{8,10},{10,12},{12,14},{14,16},{16,18},{18... | collective-permute-start | bytes 1572872 | tf_op jit(solution)/shard_map/ppermute | solution.py:425
  6.9 9.5 %push_place.1 = (f32[5248,1,128]{2,1,0:T(1,128)}, f32[1024,128]{1,0:T(8,128)S(1)}, f32[1024,128]{1,0:T(8,128)S(1)}, s32[8,1024]{1,0:T(8,128)}, f32[3,128,128]{2,...) custom-call(s32[1]{0:T(128)} %bitcast.3.mine, ...), custom_call_target="tpu_custom_call" | custom-call | tf_op jit(solution)/shard_map/push_place/pallas_call | solution.py:428
  16.4 0.1 collective-permute-start.1
  16.5 1.6 %collective-permute-start.4 = (f32[2,2,128,128]{3,2,1,0:T(8,128)}, f32[2,2,128,128]{3,2,1,0:T(8,128)S(1)}, u32[]{:S(2)}, u32[]{:S(2)}) collective-permute-start(f32[2,2,128,128]{3,2,1,0:T(8,128)} %get-tuple-element.62), channel_id=1, source_target_pairs={{0,2},{1,3},{2,4},{3,5},{4,6},{5,7},{6,8},{7,9},{8,10},{9,11},{10,... | collective-permute-start | bytes 786440 | tf_op jit(solution)/shard_map/ppermute | solution.py:393
  18.1 3.2 %collective-permute-start.5 = (f32[2,2,128,128]{3,2,1,0:T(8,128)}, f32[2,2,128,128]{3,2,1,0:T(8,128)S(1)}, u32[]{:S(2)}, u32[]{:S(2)}) collective-permute-start(f32[2,2,128,128]{3,2,1,0:T(8,128)} %get-tuple-element.63), channel_id=1, source_target_pairs={{0,2},{1,3},{2,4},{3,5},{4,6},{5,7},{6,8},{7,9},{8,10},{9,11},{10,... | collective-permute-start | bytes 786440 | tf_op jit(solution)/shard_map/ppermute | solution.py:393
  21.3 4.0 %collective-permute-done.1.arrived = f32[4,16,128]{2,1,0:T(8,128)S(1)} collective-permute-done((f32[4,16,128]{2,1,0:T(8,128)S(1)}, f32[4,16,128]{2,1,0:T(8,128)S(1)}, u32[]{:S(2)}, u32[]{:S(2)}) %collective-permute-start.1) | collective-permute-done | bytes 32800 | tf_op jit(solution)/shard_map/ppermute | solution.py:393
  25.3 0.0 collective-permute-start.6
  25.3 0.0 collective-permute-done.3
  25.3 0.0 collective-permute-start.7
  25.3 0.0 copy-start.2
  25.3 2.5 %second_push.1 = f32[128,41,1,128]{3,2,1,0:T(1,128)} custom-call(s32[1]{0:T(128)} %bitcast.3.mine, f32[1024,128]{1,0:T(8,128)S(1)} %get-tuple-element.55.phases1, f32[1024,128]{1,0:T(8,128)S(1)} %get-tuple-element.56.energies1, f32[4,16,128]{2,1,0:T(8,128)S(1)} %collective-permute-done.1.arrived, ...), custom_call_target="tpu_custom_call", output_to_operand_aliasing={{}: (5, {})} | custom-call | tf_op jit(solution)/shard_map/second_push/pallas_call | solution.py:461
  27.9 0.0 collective-permute-done.2
  27.9 0.0 copy-done.2
  27.9 56.9 %conditional.1 = (f32[2,5,128,128]{3,2,1,0:T(8,128)}, f32[2,4,128,128]{3,2,1,0:T(8,128)}, f32[4,16,128]{2,1,0:T(8,128)S(1)}, f32[16,1,8192]{2,1,0:T(1,128)}, f32[16,1,8192]{2,1,0:T(1,128)}) conditional(s32[]{:T(128)} %convert_element_type.3, () %tuple.21, (f32[128,41,1,128]{3,2,1,0:T(1,128)}, s32[1]{0:T(128)}, f32[2,4,128,128]{3,2,1,0:T(8,128)S(1)}, ...), branch_computations={%region_0.1_spmd, %region_1.2_spmd} | conditional | flops 262157 | bytes 14876969 | solution.py:514
  27.9 0.0 copy-start
  27.9 0.8 copy-done
  28.7 11.9 %all-to-all-start = ((f32[5248,1,128]{2,1,0:T(1,128)}), f32[5248,1,128]{2,1,0:T(1,128)S(1)}, u32[]{:S(2)}, u32[]{:S(2)}) async-start(f32[5248,1,128]{2,1,0:T(1,128)} %bitcast.18), calls=%async_computation | async-start | bytes 5373952 | tf_op jit(solution)/shard_map/cond/branch_1_fun/all_to_all | solution.py:489
  40.6 0.0 copy-start.1
  40.6 2.1 %slice_select_fusion = f32[2,4,128,128]{3,2,1,0:T(8,128)} fusion(f32[2,16,128,128]{3,2,1,0:T(8,128)} %get-tuple-element.31, f32[2,4,128,128]{3,2,1,0:T(8,128)} %get-tuple-element.25.piece_1, f32[2,4,128,128]{3,2,1,0:T(8,128)} %copy-done, pred[]{:T(512)S(6)} %eq.5, pred[]{:T(512)S(6)} %ge.2), kind=kLoop, calls=%fused_computation | loop fusion | flops 262144 | bytes 2097154 | tf_op jit(solution)/shard_map/cond/branch_1_fun/jit(_where)/select_n | solution.py:487
  42.7 1.0 %collective-permute-start = (f32[2,4,128,128]{3,2,1,0:T(8,128)}, f32[2,4,128,128]{3,2,1,0:T(8,128)}, u32[]{:S(2)}, u32[]{:S(2)}) collective-permute-start(f32[2,4,128,128]{3,2,1,0:T(8,128)} %slice_select_fusion), channel_id=1, source_target_pairs={{0,2},{1,3},{2,4},{3,5},{4,6},{5,7},{6,0},{7,1},{8,10},{9,11},{10,... | collective-permute-start | bytes 1572872 | tf_op jit(solution)/shard_map/cond/branch_1_fun/ppermute | solution.py:488
  43.7 0.0 copy-done.1
  43.7 3.4 %early_field.1 = f32[2,5,128,128]{3,2,1,0:T(8,128)} custom-call(s32[1]{0:T(128)} %get-tuple-element.23.mine, f32[2,4,128,128]{3,2,1,0:T(8,128)} %copy-done, f32[2,4,128,128]{3,2,1,0:T(8,128)} %get-tuple-element.25.piece_1, f32[3,128,128]{2,1,0:T(8,128)} %get-tuple-element.26.beam, bf16[4,128,128]{2,1,0:T(8,128)(2,1)S(1)} %copy-done.1), custom_call_target="tpu_custom_call" | custom-call | tf_op jit(solution)/shard_map/cond/branch_1_fun/early_field/pallas_call | solution.py:477
  47.1 32.0 %all-to-all-done.recv = f32[5248,1,128]{2,1,0:T(1,128)S(1)} async-done(((f32[5248,1,128]{2,1,0:T(1,128)}), f32[5248,1,128]{2,1,0:T(1,128)S(1)}, u32[]{:S(2)}, u32[]{:S(2)}) %all-to-all-start) | async-done | bytes 2687008 | tf_op jit(solution)/shard_map/cond/branch_1_fun/all_to_all | solution.py:489
  79.1 5.0 %pick.1 = (f32[1024,128]{1,0:T(8,128)}, f32[1024,128]{1,0:T(8,128)}, f32[4,16,128]{2,1,0:T(8,128)S(1)}) custom-call(s32[1]{0:T(128)} %get-tuple-element.23.mine, f32[5248,1,128]{2,1,0:T(1,128)S(1)} %all-to-all-done.recv, s32[8,1024]{1,0:T(8,128)S(1)} %get-tuple-element.33.places), custom_call_target="tpu_custom_call" | custom-call | tf_op jit(solution)/shard_map/cond/branch_1_fun/pick/pallas_call | solution.py:491
  84.2 0.6 collective-permute-done
  84.8 0.0 collective-permute-done.4.piece_b0
  84.8 0.0 collective-permute-done.5.piece_b1
  84.8 0.0 collective-permute-done.6.piece_b2
  84.8 0.0 collective-permute-done.7.piece_b3
  84.8 4.7 %last_field.1 = f32[2,16,128,128]{3,2,1,0:T(8,128)} custom-call(s32[1]{0:T(128)} %bitcast.3.mine, f32[2,5,128,128]{3,2,1,0:T(8,128)} %get-tuple-element.61.early, f32[2,2,128,128]{3,2,1,0:T(8,128)S(1)} %collective-permute-done.4.piece_b0, f32[2,2,128,128]{3,2,1,0:T(8,128)S(1)} %collective-permute-done.5.piece_b1, ...), custom_call_target="tpu_custom_call" | custom-call | tf_op jit(solution)/shard_map/last_field/pallas_call | solution.py:517
Async XLA Ops:
  2.0 23.3 %collective-permute-start.3 = (f32[2,4,128,128]{3,2,1,0:T(8,128)S(1)}, f32[2,4,128,128]{3,2,1,0:T(8,128)}, u32[]{:S(2)}, u32[]{:S(2)}) collective-permute-start(f32[2,4,128,128]{3,2,1,0:T(8,128)S(1)} %get-tuple-element.75), channel_id=1, source_target_pairs={{1,3},{3,5},{5,7},{7,9},{9,11},{11,13},{13,15},{15,17},{17,19},{19... | collective-permute-start | bytes 1572872 | tf_op jit(solution)/shard_map/ppermute | solution.py:426
  3.4 24.4 %collective-permute-start.2 = (f32[2,4,128,128]{3,2,1,0:T(8,128)S(1)}, f32[2,4,128,128]{3,2,1,0:T(8,128)S(1)}, u32[]{:S(2)}, u32[]{:S(2)}) collective-permute-start(f32[2,4,128,128]{3,2,1,0:T(8,128)S(1)} %get-tuple-element.76), channel_id=1, source_target_pairs={{0,2},{2,4},{4,6},{6,8},{8,10},{10,12},{12,14},{14,16},{16,18},{18... | collective-permute-start | bytes 1572872 | tf_op jit(solution)/shard_map/ppermute | solution.py:425
  16.4 8.8 %collective-permute-start.1 = (f32[4,16,128]{2,1,0:T(8,128)S(1)}, f32[4,16,128]{2,1,0:T(8,128)S(1)}, u32[]{:S(2)}, u32[]{:S(2)}) collective-permute-start(f32[4,16,128]{2,1,0:T(8,128)S(1)} %get-tuple-element.57.own), channel_id=1, source_target_pairs={{0,1},{1,2},{2,3},{3,4},{4,5},{5,6},{6,7},{7,8},{8,9},{9,10},{10,1... | collective-permute-start | bytes 98312 | tf_op jit(solution)/shard_map/ppermute | solution.py:393
  16.5 68.3 %collective-permute-start.4 = (f32[2,2,128,128]{3,2,1,0:T(8,128)}, f32[2,2,128,128]{3,2,1,0:T(8,128)S(1)}, u32[]{:S(2)}, u32[]{:S(2)}) collective-permute-start(f32[2,2,128,128]{3,2,1,0:T(8,128)} %get-tuple-element.62), channel_id=1, source_target_pairs={{0,2},{1,3},{2,4},{3,5},{4,6},{5,7},{6,8},{7,9},{8,10},{9,11},{10,... | collective-permute-start | bytes 786440 | tf_op jit(solution)/shard_map/ppermute | solution.py:393
  18.1 66.7 %collective-permute-start.5 = (f32[2,2,128,128]{3,2,1,0:T(8,128)}, f32[2,2,128,128]{3,2,1,0:T(8,128)S(1)}, u32[]{:S(2)}, u32[]{:S(2)}) collective-permute-start(f32[2,2,128,128]{3,2,1,0:T(8,128)} %get-tuple-element.63), channel_id=1, source_target_pairs={{0,2},{1,3},{2,4},{3,5},{4,6},{5,7},{6,8},{7,9},{8,10},{9,11},{10,... | collective-permute-start | bytes 786440 | tf_op jit(solution)/shard_map/ppermute | solution.py:393
  25.3 59.5 %collective-permute-start.6 = (f32[2,2,128,128]{3,2,1,0:T(8,128)}, f32[2,2,128,128]{3,2,1,0:T(8,128)S(1)}, u32[]{:S(2)}, u32[]{:S(2)}) collective-permute-start(f32[2,2,128,128]{3,2,1,0:T(8,128)} %get-tuple-element.64), channel_id=1, source_target_pairs={{0,2},{1,3},{2,4},{3,5},{4,6},{5,7},{6,8},{7,9},{8,10},{9,11},{10,... | collective-permute-start | bytes 786440 | tf_op jit(solution)/shard_map/ppermute | solution.py:393
  25.3 59.5 %collective-permute-start.7 = (f32[2,2,128,128]{3,2,1,0:T(8,128)}, f32[2,2,128,128]{3,2,1,0:T(8,128)}, u32[]{:S(2)}, u32[]{:S(2)}) collective-permute-start(f32[2,2,128,128]{3,2,1,0:T(8,128)} %get-tuple-element.65), channel_id=1, source_target_pairs={{0,2},{1,3},{2,4},{3,5},{4,6},{5,7},{6,8},{7,9},{8,10},{9,11},{10,... | collective-permute-start | bytes 786440 | tf_op jit(solution)/shard_map/ppermute | solution.py:393
  25.3 2.6 %copy-start.2 = (s32[8,1024]{1,0:T(8,128)S(1)}, s32[8,1024]{1,0:T(8,128)}, u32[]{:S(2)}) copy-start(s32[8,1024]{1,0:T(8,128)} %get-tuple-element.60) | copy-start | bytes 98308
  27.9 0.8 copy-start
  28.7 50.4 %all-to-all-start = ((f32[5248,1,128]{2,1,0:T(1,128)}), f32[5248,1,128]{2,1,0:T(1,128)S(1)}, u32[]{:S(2)}, u32[]{:S(2)}) async-start(f32[5248,1,128]{2,1,0:T(1,128)} %bitcast.18), calls=%async_computation | async-start | bytes 5373952 | tf_op jit(solution)/shard_map/cond/branch_1_fun/all_to_all | solution.py:489
  40.6 3.1 %copy-start.1 = (bf16[4,128,128]{2,1,0:T(8,128)(2,1)S(1)}, bf16[4,128,128]{2,1,0:T(8,128)(2,1)}, u32[]{:S(2)}) copy-start(bf16[4,128,128]{2,1,0:T(8,128)(2,1)} %get-tuple-element.27.parts) | copy-start | bytes 393220 | tf_op jit(solution)/shard_map/cond
  42.7 42.1 %collective-permute-start = (f32[2,4,128,128]{3,2,1,0:T(8,128)}, f32[2,4,128,128]{3,2,1,0:T(8,128)}, u32[]{:S(2)}, u32[]{:S(2)}) collective-permute-start(f32[2,4,128,128]{3,2,1,0:T(8,128)} %slice_select_fusion), channel_id=1, source_target_pairs={{0,2},{1,3},{2,4},{3,5},{4,6},{5,7},{6,0},{7,1},{8,10},{9,11},{10,... | collective-permute-start | bytes 1572872 | tf_op jit(solution)/shard_map/cond/branch_1_fun/ppermute | solution.py:488

commit v15 on v14

--- a/solution.py
+++ b/solution.py
@@ -186,17 +186,22 @@
     lax.fori_loop(0, GROUPS, push, 0)
     to_scalar.wait()
 
-    def put(n, carry):
-        base = pl.multiple_of(n * BATCH, BATCH)
-        spots = [index[n // (128 // BATCH), n % (128 // BATCH) * BATCH + m] for m in range(BATCH)]
-        ph = [phases[pl.ds(base + m, 1)] for m in range(BATCH)]
-        en = [energies[pl.ds(base + m, 1)] for m in range(BATCH)]
-        for m in range(BATCH):
-            send[spots[m]] = ph[m]
-            send[spots[m] + CAP] = en[m]
-        return carry
-
-    lax.fori_loop(0, COUNT // BATCH, put, 0)
+    def put_rows(rows, offset):
+        def put(n, carry):
+            base = pl.multiple_of(n * BATCH, BATCH)
+            spots = [index[n // (128 // BATCH), n % (128 // BATCH) * BATCH + m] for m in range(BATCH)]
+            taken = [rows[pl.ds(base + m, 1)] for m in range(BATCH)]
+            for m in range(BATCH):
+                send[spots[m] + offset] = taken[m]
+            return carry
+
+        lax.fori_loop(0, COUNT // BATCH, put, 0)
+        part = send.reshape(PEERS, MESSAGE, 1, BLOCK).at[:, pl.ds(offset, CAP)]
+        kept.append(pltpu.make_async_copy(part, send_hbm.at[:, pl.ds(offset, CAP)], sems.at[offset // CAP]))
+        kept[-1].start()
+
+    put_rows(phases, 0)
+    put_rows(energies, CAP)
     bre = lane_total(acc[4]) * (1.0 / (NBS * BLOCK))
     bim = lane_total(acc[5]) * (-1.0 / (NBS * BLOCK))
     gain = GAIN / GRID
@@ -204,11 +209,8 @@
     next_im = acc[3] + gain * (bre * self_im + bim * self_re)
     for n, part in enumerate((next_re, next_im, bre, bim)):
         small[n] = part
-    out = pltpu.make_async_copy(send, send_hbm, sems.at[0])
-    out.start()
     for copy in kept:
         copy.wait()
-    out.wait()
 
 
 def pushed(ph, en, amp_re, amp_im):
@@ -428,7 +430,7 @@
     send, phases1, energies1, places, beam, small1, *sources = pl.pallas_call(
         first_kernel,
         out_shape=(
-            pltpu.HBM((ROWS, 1, BLOCK), jnp.float32),
+            pltpu.HBM((PEERS, MESSAGE, 1, BLOCK), jnp.float32),
             shape(COUNT, BLOCK),
             shape(COUNT, BLOCK),
             pltpu.HBM((8, COUNT), jnp.int32),
@@ -467,7 +469,7 @@
         input_output_aliases={5: 0},
         compiler_params=params,
         name="second_push",
-    )(mine, phases1, energies1, arrived1, small1, in_hbm(send.reshape(PEERS, MESSAGE, 1, BLOCK)))
+    )(mine, phases1, energies1, arrived1, small1, in_hbm(send))
     field_b = [shifted(source, "cuts", 2) for source in sources]
 
     operator = quarters(*two)

time: 91.1 us -> 93.1 us (1.022)
  Pallas kernels: 25.2 us -> 27.2 us
    pallas_call x1, Pallas kernels: 9.53 us -> 11.6 us  [per_device(): pl.pallas_call(first_kernel, out_shape=(pltpu.HBM((PEERS, MESSAGE, 1, BLO...]
  transfers between devices with their start and end apart: 9 -> 9, of which waited for: 3 -> 3; matrix products, arithmetic and copies ran while one was open for 2% -> 2% of each run, Pallas kernels for 23% -> 25%
where the time goes in v15:
time: 93.1 us; the launch traced here: 91.6 us
  waiting for transfers between devices  36.7 us (39%)
  Pallas kernels  27.2 us (29%)
  starting transfers between devices  22.6 us (24%)
  other arithmetic  2.11 us (2%)
  local copies, waits for them, and re-layouts  2.1 us (2%)
    all_to_all x1, waiting for transfers between devices, exchange(): lax.all_to_all(send.reshape(ROWS, 1, BLOCK), 'cuts', split_axis=0, concat...  32 us
    all_to_all x1, starting transfers between devices, exchange(): lax.all_to_all(send.reshape(ROWS, 1, BLOCK), 'cuts', split_axis=0, concat...  11.9 us
    pallas_call x1, Pallas kernels, per_device(): pl.pallas_call(first_kernel, out_shape=(pltpu.HBM((PEERS, MESSAGE, 1, BLO...  11.6 us
    pallas_call x1, Pallas kernels, exchange(): pl.pallas_call(pick_kernel, out_shape=(shape(COUNT, BLOCK), shape(COUNT,...  5.04 us
    ppermute x5, starting transfers between devices, shifted(): return lax.ppermute(value, axis, pairs)  4.87 us
    pallas_call x1, Pallas kernels, per_device(): pl.pallas_call(last_kernel, out_shape=shape(2, GROUPS, GRID, GRID), in_sp...  4.68 us
    ppermute x5, waiting for transfers between devices, shifted(): return lax.ppermute(value, axis, pairs)  3.98 us
    ppermute x1, starting transfers between devices, per_device(): lax.ppermute(lax.dynamic_slice_in_dim(field, core * (GROUPS - EARLY), EAR...  3.47 us
  transfers between devices with their start and end apart: 9, of which 3 were waited for; matrix products, arithmetic and copies ran while one was open for 2% of the time, Pallas kernels for 25%

profile of v15, /device:TPU:0, one launch (start us, length us, event | category | flops | bytes accessed | tf_op | source)
XLA Modules:
  0.0 91.6 jit_solution(13367598602873986196)
XLA Ops:
  0.7 1.3 %dynamic-slice_bitcast_fusion = (f32[2,4,128,128]{3,2,1,0:T(8,128)S(1)}, f32[2,4,128,128]{3,2,1,0:T(8,128)S(1)}) fusion(f32[2,16,1,128,128]{4,3,2,1,0:T(8,128)} %param.11, s32[]{:T(128)S(6)} %select_n.33, s32[]{:T(128)S(6)} %select_n.32), kind=kLoop, calls=%fused_computation.1 | loop fusion | bytes 2097160 | tf_op jit(solution)/shard_map/dynamic_slice | solution.py:428
  2.0 1.5 %collective-permute-start.3 = (f32[2,4,128,128]{3,2,1,0:T(8,128)S(1)}, f32[2,4,128,128]{3,2,1,0:T(8,128)}, u32[]{:S(2)}, u32[]{:S(2)}) collective-permute-start(f32[2,4,128,128]{3,2,1,0:T(8,128)S(1)} %get-tuple-element.75), channel_id=1, source_target_pairs={{1,3},{3,5},{5,7},{7,9},{9,11},{11,13},{13,15},{15,17},{17,19},{19... | collective-permute-start | bytes 1572872 | tf_op jit(solution)/shard_map/ppermute | solution.py:428
  3.4 3.5 %collective-permute-start.2 = (f32[2,4,128,128]{3,2,1,0:T(8,128)S(1)}, f32[2,4,128,128]{3,2,1,0:T(8,128)S(1)}, u32[]{:S(2)}, u32[]{:S(2)}) collective-permute-start(f32[2,4,128,128]{3,2,1,0:T(8,128)S(1)} %get-tuple-element.76), channel_id=1, source_target_pairs={{0,2},{2,4},{4,6},{6,8},{8,10},{10,12},{12,14},{14,16},{16,18},{18... | collective-permute-start | bytes 1572872 | tf_op jit(solution)/shard_map/ppermute | solution.py:427
  6.9 11.6 %push_place.1 = (f32[128,41,1,128]{3,2,1,0:T(1,128)}, f32[1024,128]{1,0:T(8,128)S(1)}, f32[1024,128]{1,0:T(8,128)S(1)}, s32[8,1024]{1,0:T(8,128)}, f32[3,128,128...) custom-call(s32[1]{0:T(128)} %bitcast.3.mine, ...), custom_call_target="tpu_custom_call" | custom-call | tf_op jit(solution)/shard_map/push_place/pallas_call | solution.py:430
  18.5 0.1 collective-permute-start.1
  18.6 1.6 %collective-permute-start.4 = (f32[2,2,128,128]{3,2,1,0:T(8,128)}, f32[2,2,128,128]{3,2,1,0:T(8,128)S(1)}, u32[]{:S(2)}, u32[]{:S(2)}) collective-permute-start(f32[2,2,128,128]{3,2,1,0:T(8,128)} %get-tuple-element.62), channel_id=1, source_target_pairs={{0,2},{1,3},{2,4},{3,5},{4,6},{5,7},{6,8},{7,9},{8,10},{9,11},{10,... | collective-permute-start | bytes 786440 | tf_op jit(solution)/shard_map/ppermute | solution.py:395
  20.1 3.2 %collective-permute-start.5 = (f32[2,2,128,128]{3,2,1,0:T(8,128)}, f32[2,2,128,128]{3,2,1,0:T(8,128)S(1)}, u32[]{:S(2)}, u32[]{:S(2)}) collective-permute-start(f32[2,2,128,128]{3,2,1,0:T(8,128)} %get-tuple-element.63), channel_id=1, source_target_pairs={{0,2},{1,3},{2,4},{3,5},{4,6},{5,7},{6,8},{7,9},{8,10},{9,11},{10,... | collective-permute-start | bytes 786440 | tf_op jit(solution)/shard_map/ppermute | solution.py:395
  23.4 4.0 %collective-permute-done.1.arrived = f32[4,16,128]{2,1,0:T(8,128)S(1)} collective-permute-done((f32[4,16,128]{2,1,0:T(8,128)S(1)}, f32[4,16,128]{2,1,0:T(8,128)S(1)}, u32[]{:S(2)}, u32[]{:S(2)}) %collective-permute-start.1) | collective-permute-done | bytes 32800 | tf_op jit(solution)/shard_map/ppermute | solution.py:395
  27.3 0.0 collective-permute-start.6
  27.3 0.0 collective-permute-done.3
  27.3 0.0 collective-permute-start.7
  27.4 0.0 copy-start.2
  27.4 2.5 %second_push.1 = f32[128,41,1,128]{3,2,1,0:T(1,128)} custom-call(s32[1]{0:T(128)} %bitcast.3.mine, f32[1024,128]{1,0:T(8,128)S(1)} %get-tuple-element.55.phases1, f32[1024,128]{1,0:T(8,128)S(1)} %get-tuple-element.56.energies1, f32[4,16,128]{2,1,0:T(8,128)S(1)} %collective-permute-done.1.arrived, ...), custom_call_target="tpu_custom_call", output_to_operand_aliasing={{}: (5, {})} | custom-call | tf_op jit(solution)/shard_map/second_push/pallas_call | solution.py:463
  29.9 0.0 collective-permute-done.2
  29.9 0.0 copy-done.2
  29.9 56.9 %conditional.1 = (f32[2,5,128,128]{3,2,1,0:T(8,128)}, f32[2,4,128,128]{3,2,1,0:T(8,128)}, f32[4,16,128]{2,1,0:T(8,128)S(1)}, f32[16,1,8192]{2,1,0:T(1,128)}, f32[16,1,8192]{2,1,0:T(1,128)}) conditional(s32[]{:T(128)} %convert_element_type.3, () %tuple.21, (f32[128,41,1,128]{3,2,1,0:T(1,128)}, s32[1]{0:T(128)}, f32[2,4,128,128]{3,2,1,0:T(8,128)S(1)}, ...), branch_computations={%region_0.1_spmd, %region_1.2_spmd} | conditional | flops 262157 | bytes 14876969 | solution.py:516
  29.9 0.0 copy-start
  29.9 0.8 copy-done
  30.7 11.9 %all-to-all-start = ((f32[5248,1,128]{2,1,0:T(1,128)}), f32[5248,1,128]{2,1,0:T(1,128)S(1)}, u32[]{:S(2)}, u32[]{:S(2)}) async-start(f32[5248,1,128]{2,1,0:T(1,128)} %bitcast.16), calls=%async_computation | async-start | bytes 5373952 | tf_op jit(solution)/shard_map/cond/branch_1_fun/all_to_all | solution.py:491
  42.6 0.0 copy-start.1
  42.6 2.1 %slice_select_fusion = f32[2,4,128,128]{3,2,1,0:T(8,128)} fusion(f32[2,16,128,128]{3,2,1,0:T(8,128)} %get-tuple-element.31, f32[2,4,128,128]{3,2,1,0:T(8,128)} %get-tuple-element.25.piece_1, f32[2,4,128,128]{3,2,1,0:T(8,128)} %copy-done, pred[]{:T(512)S(6)} %eq.5, pred[]{:T(512)S(6)} %ge.2), kind=kLoop, calls=%fused_computation | loop fusion | flops 262144 | bytes 2097154 | tf_op jit(solution)/shard_map/cond/branch_1_fun/jit(_where)/select_n | solution.py:489
  44.8 1.0 %collective-permute-start = (f32[2,4,128,128]{3,2,1,0:T(8,128)}, f32[2,4,128,128]{3,2,1,0:T(8,128)}, u32[]{:S(2)}, u32[]{:S(2)}) collective-permute-start(f32[2,4,128,128]{3,2,1,0:T(8,128)} %slice_select_fusion), channel_id=1, source_target_pairs={{0,2},{1,3},{2,4},{3,5},{4,6},{5,7},{6,0},{7,1},{8,10},{9,11},{10,... | collective-permute-start | bytes 1572872 | tf_op jit(solution)/shard_map/cond/branch_1_fun/ppermute | solution.py:490
  45.7 0.0 copy-done.1
  45.7 3.4 %early_field.1 = f32[2,5,128,128]{3,2,1,0:T(8,128)} custom-call(s32[1]{0:T(128)} %get-tuple-element.23.mine, f32[2,4,128,128]{3,2,1,0:T(8,128)} %copy-done, f32[2,4,128,128]{3,2,1,0:T(8,128)} %get-tuple-element.25.piece_1, f32[3,128,128]{2,1,0:T(8,128)} %get-tuple-element.26.beam, bf16[4,128,128]{2,1,0:T(8,128)(2,1)S(1)} %copy-done.1), custom_call_target="tpu_custom_call" | custom-call | tf_op jit(solution)/shard_map/cond/branch_1_fun/early_field/pallas_call | solution.py:479
  49.1 32.0 %all-to-all-done.recv = f32[5248,1,128]{2,1,0:T(1,128)S(1)} async-done(((f32[5248,1,128]{2,1,0:T(1,128)}), f32[5248,1,128]{2,1,0:T(1,128)S(1)}, u32[]{:S(2)}, u32[]{:S(2)}) %all-to-all-start) | async-done | bytes 2687008 | tf_op jit(solution)/shard_map/cond/branch_1_fun/all_to_all | solution.py:491
  81.2 5.0 %pick.1 = (f32[1024,128]{1,0:T(8,128)}, f32[1024,128]{1,0:T(8,128)}, f32[4,16,128]{2,1,0:T(8,128)S(1)}) custom-call(s32[1]{0:T(128)} %get-tuple-element.23.mine, f32[5248,1,128]{2,1,0:T(1,128)S(1)} %all-to-all-done.recv, s32[8,1024]{1,0:T(8,128)S(1)} %get-tuple-element.33.places), custom_call_target="tpu_custom_call" | custom-call | tf_op jit(solution)/shard_map/cond/branch_1_fun/pick/pallas_call | solution.py:493
  86.2 0.6 collective-permute-done
  86.9 0.0 collective-permute-done.4.piece_b0
  86.9 0.0 collective-permute-done.5.piece_b1
  86.9 0.0 collective-permute-done.6.piece_b2
  86.9 0.0 collective-permute-done.7.piece_b3
  86.9 4.7 %last_field.1 = f32[2,16,128,128]{3,2,1,0:T(8,128)} custom-call(s32[1]{0:T(128)} %bitcast.3.mine, f32[2,5,128,128]{3,2,1,0:T(8,128)} %get-tuple-element.61.early, f32[2,2,128,128]{3,2,1,0:T(8,128)S(1)} %collective-permute-done.4.piece_b0, f32[2,2,128,128]{3,2,1,0:T(8,128)S(1)} %collective-permute-done.5.piece_b1, ...), custom_call_target="tpu_custom_call" | custom-call | tf_op jit(solution)/shard_map/last_field/pallas_call | solution.py:519
Async XLA Ops:
  2.0 25.4 %collective-permute-start.3 = (f32[2,4,128,128]{3,2,1,0:T(8,128)S(1)}, f32[2,4,128,128]{3,2,1,0:T(8,128)}, u32[]{:S(2)}, u32[]{:S(2)}) collective-permute-start(f32[2,4,128,128]{3,2,1,0:T(8,128)S(1)} %get-tuple-element.75), channel_id=1, source_target_pairs={{1,3},{3,5},{5,7},{7,9},{9,11},{11,13},{13,15},{15,17},{17,19},{19... | collective-permute-start | bytes 1572872 | tf_op jit(solution)/shard_map/ppermute | solution.py:428
  3.4 26.5 %collective-permute-start.2 = (f32[2,4,128,128]{3,2,1,0:T(8,128)S(1)}, f32[2,4,128,128]{3,2,1,0:T(8,128)S(1)}, u32[]{:S(2)}, u32[]{:S(2)}) collective-permute-start(f32[2,4,128,128]{3,2,1,0:T(8,128)S(1)} %get-tuple-element.76), channel_id=1, source_target_pairs={{0,2},{2,4},{4,6},{6,8},{8,10},{10,12},{12,14},{14,16},{16,18},{18... | collective-permute-start | bytes 1572872 | tf_op jit(solution)/shard_map/ppermute | solution.py:427
  18.5 8.8 %collective-permute-start.1 = (f32[4,16,128]{2,1,0:T(8,128)S(1)}, f32[4,16,128]{2,1,0:T(8,128)S(1)}, u32[]{:S(2)}, u32[]{:S(2)}) collective-permute-start(f32[4,16,128]{2,1,0:T(8,128)S(1)} %get-tuple-element.57.own), channel_id=1, source_target_pairs={{0,1},{1,2},{2,3},{3,4},{4,5},{5,6},{6,7},{7,8},{8,9},{9,10},{10,1... | collective-permute-start | bytes 98312 | tf_op jit(solution)/shard_map/ppermute | solution.py:395
  18.6 68.3 %collective-permute-start.4 = (f32[2,2,128,128]{3,2,1,0:T(8,128)}, f32[2,2,128,128]{3,2,1,0:T(8,128)S(1)}, u32[]{:S(2)}, u32[]{:S(2)}) collective-permute-start(f32[2,2,128,128]{3,2,1,0:T(8,128)} %get-tuple-element.62), channel_id=1, source_target_pairs={{0,2},{1,3},{2,4},{3,5},{4,6},{5,7},{6,8},{7,9},{8,10},{9,11},{10,... | collective-permute-start | bytes 786440 | tf_op jit(solution)/shard_map/ppermute | solution.py:395
  20.1 66.7 %collective-permute-start.5 = (f32[2,2,128,128]{3,2,1,0:T(8,128)}, f32[2,2,128,128]{3,2,1,0:T(8,128)S(1)}, u32[]{:S(2)}, u32[]{:S(2)}) collective-permute-start(f32[2,2,128,128]{3,2,1,0:T(8,128)} %get-tuple-element.63), channel_id=1, source_target_pairs={{0,2},{1,3},{2,4},{3,5},{4,6},{5,7},{6,8},{7,9},{8,10},{9,11},{10,... | collective-permute-start | bytes 786440 | tf_op jit(solution)/shard_map/ppermute | solution.py:395
  27.3 59.5 %collective-permute-start.6 = (f32[2,2,128,128]{3,2,1,0:T(8,128)}, f32[2,2,128,128]{3,2,1,0:T(8,128)S(1)}, u32[]{:S(2)}, u32[]{:S(2)}) collective-permute-start(f32[2,2,128,128]{3,2,1,0:T(8,128)} %get-tuple-element.64), channel_id=1, source_target_pairs={{0,2},{1,3},{2,4},{3,5},{4,6},{5,7},{6,8},{7,9},{8,10},{9,11},{10,... | collective-permute-start | bytes 786440 | tf_op jit(solution)/shard_map/ppermute | solution.py:395
  27.3 59.5 %collective-permute-start.7 = (f32[2,2,128,128]{3,2,1,0:T(8,128)}, f32[2,2,128,128]{3,2,1,0:T(8,128)}, u32[]{:S(2)}, u32[]{:S(2)}) collective-permute-start(f32[2,2,128,128]{3,2,1,0:T(8,128)} %get-tuple-element.65), channel_id=1, source_target_pairs={{0,2},{1,3},{2,4},{3,5},{4,6},{5,7},{6,8},{7,9},{8,10},{9,11},{10,... | collective-permute-start | bytes 786440 | tf_op jit(solution)/shard_map/ppermute | solution.py:395
  27.4 2.6 %copy-start.2 = (s32[8,1024]{1,0:T(8,128)S(1)}, s32[8,1024]{1,0:T(8,128)}, u32[]{:S(2)}) copy-start(s32[8,1024]{1,0:T(8,128)} %get-tuple-element.60) | copy-start | bytes 98308
  29.9 0.8 copy-start
  30.7 50.4 %all-to-all-start = ((f32[5248,1,128]{2,1,0:T(1,128)}), f32[5248,1,128]{2,1,0:T(1,128)S(1)}, u32[]{:S(2)}, u32[]{:S(2)}) async-start(f32[5248,1,128]{2,1,0:T(1,128)} %bitcast.16), calls=%async_computation | async-start | bytes 5373952 | tf_op jit(solution)/shard_map/cond/branch_1_fun/all_to_all | solution.py:491
  42.6 3.1 %copy-start.1 = (bf16[4,128,128]{2,1,0:T(8,128)(2,1)S(1)}, bf16[4,128,128]{2,1,0:T(8,128)(2,1)}, u32[]{:S(2)}) copy-start(bf16[4,128,128]{2,1,0:T(8,128)(2,1)} %get-tuple-element.27.parts) | copy-start | bytes 393220 | tf_op jit(solution)/shard_map/cond
  44.8 42.1 %collective-permute-start = (f32[2,4,128,128]{3,2,1,0:T(8,128)}, f32[2,4,128,128]{3,2,1,0:T(8,128)}, u32[]{:S(2)}, u32[]{:S(2)}) collective-permute-start(f32[2,4,128,128]{3,2,1,0:T(8,128)} %slice_select_fusion), channel_id=1, source_target_pairs={{0,2},{1,3},{2,4},{3,5},{4,6},{5,7},{6,0},{7,1},{8,10},{9,11},{10,... | collective-permute-start | bytes 1572872 | tf_op jit(solution)/shard_map/cond/branch_1_fun/ppermute | solution.py:490

commit v16 on v14

--- a/solution.py
+++ b/solution.py
@@ -363,11 +363,13 @@
 
     finish(0, EARLY)
     lay_out(parts, left, right)
-    planes = [(piece[0, k], piece[1, k]) for piece in (piece_b0, piece_b1, piece_b2, piece_b3) for k in range(piece.shape[1])]
-    for k, (re, im) in enumerate(twice_diffracted(planes, left, right)):
-        rest[0, k] = re
-        rest[1, k] = im
-    finish(EARLY, LATE)
+    halfway = (EARLY + LATE) // 2
+    for low, high, pieces in ((EARLY, halfway, (piece_b0, piece_b1)), (halfway, LATE, (piece_b2, piece_b3))):
+        planes = [(piece[0, k], piece[1, k]) for piece in pieces for k in range(piece.shape[1])]
+        for k, (re, im) in enumerate(twice_diffracted(planes, left, right)):
+            rest[0, low - EARLY + k] = re
+            rest[1, low - EARLY + k] = im
+        finish(low, high)
     planes = [(piece_c[0, k], piece_c[1, k]) for k in range(piece_c.shape[1])]
     for k, (re, im) in enumerate(twice_diffracted(planes, left, right)):
         rest[0, LATE - EARLY + k] = re
@@ -524,7 +526,7 @@
             vmem(2, GROUPS - EARLY, GRID, GRID),
             vmem(2, GROUPS, GRID, GRID),
             *tables,
-            pltpu.SemaphoreType.DMA((6,)),
+            pltpu.SemaphoreType.DMA((8,)),
         ],
         compiler_params=params,
         name="last_field",

time: 91.1 us -> 90.9 us (level)
  no operation moved by 1% of the time
where the time goes in v16:
time: 90.9 us; the launch traced here: 89.3 us
  waiting for transfers between devices  36.7 us (40%)
  Pallas kernels  25 us (28%)
  starting transfers between devices  22.6 us (25%)
  other arithmetic  2.11 us (2%)
  local copies, waits for them, and re-layouts  2.1 us (2%)
    all_to_all x1, waiting for transfers between devices, exchange(): lax.all_to_all(send.reshape(ROWS, 1, BLOCK), 'cuts', split_axis=0, concat...  32 us
    all_to_all x1, starting transfers between devices, exchange(): lax.all_to_all(send.reshape(ROWS, 1, BLOCK), 'cuts', split_axis=0, concat...  11.9 us
    pallas_call x1, Pallas kernels, per_device(): pl.pallas_call(first_kernel, out_shape=(pltpu.HBM((ROWS, 1, BLOCK), jnp.f...  9.53 us
    pallas_call x1, Pallas kernels, exchange(): pl.pallas_call(pick_kernel, out_shape=(shape(COUNT, BLOCK), shape(COUNT,...  5.05 us
    ppermute x5, starting transfers between devices, shifted(): return lax.ppermute(value, axis, pairs)  4.87 us
    pallas_call x1, Pallas kernels, per_device(): pl.pallas_call(last_kernel, out_shape=shape(2, GROUPS, GRID, GRID), in_sp...  4.52 us
    ppermute x5, waiting for transfers between devices, shifted(): return lax.ppermute(value, axis, pairs)  3.98 us
    ppermute x1, starting transfers between devices, per_device(): lax.ppermute(lax.dynamic_slice_in_dim(field, core * (GROUPS - EARLY), EAR...  3.47 us
  transfers between devices with their start and end apart: 9, of which 3 were waited for; matrix products, arithmetic and copies ran while one was open for 2% of the time, Pallas kernels for 23%

profile of v16, /device:TPU:0, one launch (start us, length us, event | category | flops | bytes accessed | tf_op | source)
XLA Modules:
  0.0 89.3 jit_solution(16714344108731697957)
XLA Ops:
  0.7 1.3 %dynamic-slice_bitcast_fusion = (f32[2,4,128,128]{3,2,1,0:T(8,128)S(1)}, f32[2,4,128,128]{3,2,1,0:T(8,128)S(1)}) fusion(f32[2,16,1,128,128]{4,3,2,1,0:T(8,128)} %param.11, s32[]{:T(128)S(6)} %select_n.33, s32[]{:T(128)S(6)} %select_n.32), kind=kLoop, calls=%fused_computation.1 | loop fusion | bytes 2097160 | tf_op jit(solution)/shard_map/dynamic_slice | solution.py:428
  2.0 1.5 %collective-permute-start.3 = (f32[2,4,128,128]{3,2,1,0:T(8,128)S(1)}, f32[2,4,128,128]{3,2,1,0:T(8,128)}, u32[]{:S(2)}, u32[]{:S(2)}) collective-permute-start(f32[2,4,128,128]{3,2,1,0:T(8,128)S(1)} %get-tuple-element.75), channel_id=1, source_target_pairs={{1,3},{3,5},{5,7},{7,9},{9,11},{11,13},{13,15},{15,17},{17,19},{19... | collective-permute-start | bytes 1572872 | tf_op jit(solution)/shard_map/ppermute | solution.py:428
  3.4 3.5 %collective-permute-start.2 = (f32[2,4,128,128]{3,2,1,0:T(8,128)S(1)}, f32[2,4,128,128]{3,2,1,0:T(8,128)S(1)}, u32[]{:S(2)}, u32[]{:S(2)}) collective-permute-start(f32[2,4,128,128]{3,2,1,0:T(8,128)S(1)} %get-tuple-element.76), channel_id=1, source_target_pairs={{0,2},{2,4},{4,6},{6,8},{8,10},{10,12},{12,14},{14,16},{16,18},{18... | collective-permute-start | bytes 1572872 | tf_op jit(solution)/shard_map/ppermute | solution.py:427
  6.9 9.5 %push_place.1 = (f32[5248,1,128]{2,1,0:T(1,128)}, f32[1024,128]{1,0:T(8,128)S(1)}, f32[1024,128]{1,0:T(8,128)S(1)}, s32[8,1024]{1,0:T(8,128)}, f32[3,128,128]{2,...) custom-call(s32[1]{0:T(128)} %bitcast.3.mine, ...), custom_call_target="tpu_custom_call" | custom-call | tf_op jit(solution)/shard_map/push_place/pallas_call | solution.py:430
  16.4 0.1 collective-permute-start.1
  16.5 1.6 %collective-permute-start.4 = (f32[2,2,128,128]{3,2,1,0:T(8,128)}, f32[2,2,128,128]{3,2,1,0:T(8,128)S(1)}, u32[]{:S(2)}, u32[]{:S(2)}) collective-permute-start(f32[2,2,128,128]{3,2,1,0:T(8,128)} %get-tuple-element.62), channel_id=1, source_target_pairs={{0,2},{1,3},{2,4},{3,5},{4,6},{5,7},{6,8},{7,9},{8,10},{9,11},{10,... | collective-permute-start | bytes 786440 | tf_op jit(solution)/shard_map/ppermute | solution.py:395
  18.1 3.2 %collective-permute-start.5 = (f32[2,2,128,128]{3,2,1,0:T(8,128)}, f32[2,2,128,128]{3,2,1,0:T(8,128)S(1)}, u32[]{:S(2)}, u32[]{:S(2)}) collective-permute-start(f32[2,2,128,128]{3,2,1,0:T(8,128)} %get-tuple-element.63), channel_id=1, source_target_pairs={{0,2},{1,3},{2,4},{3,5},{4,6},{5,7},{6,8},{7,9},{8,10},{9,11},{10,... | collective-permute-start | bytes 786440 | tf_op jit(solution)/shard_map/ppermute | solution.py:395
  21.3 4.0 %collective-permute-done.1.arrived = f32[4,16,128]{2,1,0:T(8,128)S(1)} collective-permute-done((f32[4,16,128]{2,1,0:T(8,128)S(1)}, f32[4,16,128]{2,1,0:T(8,128)S(1)}, u32[]{:S(2)}, u32[]{:S(2)}) %collective-permute-start.1) | collective-permute-done | bytes 32800 | tf_op jit(solution)/shard_map/ppermute | solution.py:395
  25.3 0.0 collective-permute-start.6
  25.3 0.0 collective-permute-done.3
  25.3 0.0 collective-permute-start.7
  25.3 0.0 copy-start.2
  25.3 2.5 %second_push.1 = f32[128,41,1,128]{3,2,1,0:T(1,128)} custom-call(s32[1]{0:T(128)} %bitcast.3.mine, f32[1024,128]{1,0:T(8,128)S(1)} %get-tuple-element.55.phases1, f32[1024,128]{1,0:T(8,128)S(1)} %get-tuple-element.56.energies1, f32[4,16,128]{2,1,0:T(8,128)S(1)} %collective-permute-done.1.arrived, ...), custom_call_target="tpu_custom_call", output_to_operand_aliasing={{}: (5, {})} | custom-call | tf_op jit(solution)/shard_map/second_push/pallas_call | solution.py:463
  27.9 0.0 collective-permute-done.2
  27.9 0.0 copy-done.2
  27.9 56.9 %conditional.1 = (f32[2,5,128,128]{3,2,1,0:T(8,128)}, f32[2,4,128,128]{3,2,1,0:T(8,128)}, f32[4,16,128]{2,1,0:T(8,128)S(1)}, f32[16,1,8192]{2,1,0:T(1,128)}, f32[16,1,8192]{2,1,0:T(1,128)}) conditional(s32[]{:T(128)} %convert_element_type.3, () %tuple.21, (f32[128,41,1,128]{3,2,1,0:T(1,128)}, s32[1]{0:T(128)}, f32[2,4,128,128]{3,2,1,0:T(8,128)S(1)}, ...), branch_computations={%region_0.1_spmd, %region_1.2_spmd} | conditional | flops 262157 | bytes 14876969 | solution.py:516
  27.9 0.0 copy-start
  27.9 0.8 copy-done
  28.7 11.9 %all-to-all-start = ((f32[5248,1,128]{2,1,0:T(1,128)}), f32[5248,1,128]{2,1,0:T(1,128)S(1)}, u32[]{:S(2)}, u32[]{:S(2)}) async-start(f32[5248,1,128]{2,1,0:T(1,128)} %bitcast.18), calls=%async_computation | async-start | bytes 5373952 | tf_op jit(solution)/shard_map/cond/branch_1_fun/all_to_all | solution.py:491
  40.6 0.0 copy-start.1
  40.6 2.1 %slice_select_fusion = f32[2,4,128,128]{3,2,1,0:T(8,128)} fusion(f32[2,16,128,128]{3,2,1,0:T(8,128)} %get-tuple-element.31, f32[2,4,128,128]{3,2,1,0:T(8,128)} %get-tuple-element.25.piece_1, f32[2,4,128,128]{3,2,1,0:T(8,128)} %copy-done, pred[]{:T(512)S(6)} %eq.5, pred[]{:T(512)S(6)} %ge.2), kind=kLoop, calls=%fused_computation | loop fusion | flops 262144 | bytes 2097154 | tf_op jit(solution)/shard_map/cond/branch_1_fun/jit(_where)/select_n | solution.py:489
  42.7 1.0 %collective-permute-start = (f32[2,4,128,128]{3,2,1,0:T(8,128)}, f32[2,4,128,128]{3,2,1,0:T(8,128)}, u32[]{:S(2)}, u32[]{:S(2)}) collective-permute-start(f32[2,4,128,128]{3,2,1,0:T(8,128)} %slice_select_fusion), channel_id=1, source_target_pairs={{0,2},{1,3},{2,4},{3,5},{4,6},{5,7},{6,0},{7,1},{8,10},{9,11},{10,... | collective-permute-start | bytes 1572872 | tf_op jit(solution)/shard_map/cond/branch_1_fun/ppermute | solution.py:490
  43.7 0.0 copy-done.1
  43.7 3.4 %early_field.1 = f32[2,5,128,128]{3,2,1,0:T(8,128)} custom-call(s32[1]{0:T(128)} %get-tuple-element.23.mine, f32[2,4,128,128]{3,2,1,0:T(8,128)} %copy-done, f32[2,4,128,128]{3,2,1,0:T(8,128)} %get-tuple-element.25.piece_1, f32[3,128,128]{2,1,0:T(8,128)} %get-tuple-element.26.beam, bf16[4,128,128]{2,1,0:T(8,128)(2,1)S(1)} %copy-done.1), custom_call_target="tpu_custom_call" | custom-call | tf_op jit(solution)/shard_map/cond/branch_1_fun/early_field/pallas_call | solution.py:479
  47.1 32.0 %all-to-all-done.recv = f32[5248,1,128]{2,1,0:T(1,128)S(1)} async-done(((f32[5248,1,128]{2,1,0:T(1,128)}), f32[5248,1,128]{2,1,0:T(1,128)S(1)}, u32[]{:S(2)}, u32[]{:S(2)}) %all-to-all-start) | async-done | bytes 2687008 | tf_op jit(solution)/shard_map/cond/branch_1_fun/all_to_all | solution.py:491
  79.1 5.0 %pick.1 = (f32[1024,128]{1,0:T(8,128)}, f32[1024,128]{1,0:T(8,128)}, f32[4,16,128]{2,1,0:T(8,128)S(1)}) custom-call(s32[1]{0:T(128)} %get-tuple-element.23.mine, f32[5248,1,128]{2,1,0:T(1,128)S(1)} %all-to-all-done.recv, s32[8,1024]{1,0:T(8,128)S(1)} %get-tuple-element.33.places), custom_call_target="tpu_custom_call" | custom-call | tf_op jit(solution)/shard_map/cond/branch_1_fun/pick/pallas_call | solution.py:493
  84.2 0.6 collective-permute-done
  84.8 0.0 collective-permute-done.4.piece_b0
  84.8 0.0 collective-permute-done.5.piece_b1
  84.8 0.0 collective-permute-done.6.piece_b2
  84.8 0.0 collective-permute-done.7.piece_b3
  84.8 4.5 %last_field.1 = f32[2,16,128,128]{3,2,1,0:T(8,128)} custom-call(s32[1]{0:T(128)} %bitcast.3.mine, f32[2,5,128,128]{3,2,1,0:T(8,128)} %get-tuple-element.61.early, f32[2,2,128,128]{3,2,1,0:T(8,128)S(1)} %collective-permute-done.4.piece_b0, f32[2,2,128,128]{3,2,1,0:T(8,128)S(1)} %collective-permute-done.5.piece_b1, ...), custom_call_target="tpu_custom_call" | custom-call | tf_op jit(solution)/shard_map/last_field/pallas_call | solution.py:519
Async XLA Ops:
  2.0 23.3 %collective-permute-start.3 = (f32[2,4,128,128]{3,2,1,0:T(8,128)S(1)}, f32[2,4,128,128]{3,2,1,0:T(8,128)}, u32[]{:S(2)}, u32[]{:S(2)}) collective-permute-start(f32[2,4,128,128]{3,2,1,0:T(8,128)S(1)} %get-tuple-element.75), channel_id=1, source_target_pairs={{1,3},{3,5},{5,7},{7,9},{9,11},{11,13},{13,15},{15,17},{17,19},{19... | collective-permute-start | bytes 1572872 | tf_op jit(solution)/shard_map/ppermute | solution.py:428
  3.4 24.4 %collective-permute-start.2 = (f32[2,4,128,128]{3,2,1,0:T(8,128)S(1)}, f32[2,4,128,128]{3,2,1,0:T(8,128)S(1)}, u32[]{:S(2)}, u32[]{:S(2)}) collective-permute-start(f32[2,4,128,128]{3,2,1,0:T(8,128)S(1)} %get-tuple-element.76), channel_id=1, source_target_pairs={{0,2},{2,4},{4,6},{6,8},{8,10},{10,12},{12,14},{14,16},{16,18},{18... | collective-permute-start | bytes 1572872 | tf_op jit(solution)/shard_map/ppermute | solution.py:427
  16.4 8.8 %collective-permute-start.1 = (f32[4,16,128]{2,1,0:T(8,128)S(1)}, f32[4,16,128]{2,1,0:T(8,128)S(1)}, u32[]{:S(2)}, u32[]{:S(2)}) collective-permute-start(f32[4,16,128]{2,1,0:T(8,128)S(1)} %get-tuple-element.57.own), channel_id=1, source_target_pairs={{0,1},{1,2},{2,3},{3,4},{4,5},{5,6},{6,7},{7,8},{8,9},{9,10},{10,1... | collective-permute-start | bytes 98312 | tf_op jit(solution)/shard_map/ppermute | solution.py:395
  16.5 68.3 %collective-permute-start.4 = (f32[2,2,128,128]{3,2,1,0:T(8,128)}, f32[2,2,128,128]{3,2,1,0:T(8,128)S(1)}, u32[]{:S(2)}, u32[]{:S(2)}) collective-permute-start(f32[2,2,128,128]{3,2,1,0:T(8,128)} %get-tuple-element.62), channel_id=1, source_target_pairs={{0,2},{1,3},{2,4},{3,5},{4,6},{5,7},{6,8},{7,9},{8,10},{9,11},{10,... | collective-permute-start | bytes 786440 | tf_op jit(solution)/shard_map/ppermute | solution.py:395
  18.1 66.7 %collective-permute-start.5 = (f32[2,2,128,128]{3,2,1,0:T(8,128)}, f32[2,2,128,128]{3,2,1,0:T(8,128)S(1)}, u32[]{:S(2)}, u32[]{:S(2)}) collective-permute-start(f32[2,2,128,128]{3,2,1,0:T(8,128)} %get-tuple-element.63), channel_id=1, source_target_pairs={{0,2},{1,3},{2,4},{3,5},{4,6},{5,7},{6,8},{7,9},{8,10},{9,11},{10,... | collective-permute-start | bytes 786440 | tf_op jit(solution)/shard_map/ppermute | solution.py:395
  25.3 59.5 %collective-permute-start.6 = (f32[2,2,128,128]{3,2,1,0:T(8,128)}, f32[2,2,128,128]{3,2,1,0:T(8,128)S(1)}, u32[]{:S(2)}, u32[]{:S(2)}) collective-permute-start(f32[2,2,128,128]{3,2,1,0:T(8,128)} %get-tuple-element.64), channel_id=1, source_target_pairs={{0,2},{1,3},{2,4},{3,5},{4,6},{5,7},{6,8},{7,9},{8,10},{9,11},{10,... | collective-permute-start | bytes 786440 | tf_op jit(solution)/shard_map/ppermute | solution.py:395
  25.3 59.5 %collective-permute-start.7 = (f32[2,2,128,128]{3,2,1,0:T(8,128)}, f32[2,2,128,128]{3,2,1,0:T(8,128)}, u32[]{:S(2)}, u32[]{:S(2)}) collective-permute-start(f32[2,2,128,128]{3,2,1,0:T(8,128)} %get-tuple-element.65), channel_id=1, source_target_pairs={{0,2},{1,3},{2,4},{3,5},{4,6},{5,7},{6,8},{7,9},{8,10},{9,11},{10,... | collective-permute-start | bytes 786440 | tf_op jit(solution)/shard_map/ppermute | solution.py:395
  25.3 2.6 %copy-start.2 = (s32[8,1024]{1,0:T(8,128)S(1)}, s32[8,1024]{1,0:T(8,128)}, u32[]{:S(2)}) copy-start(s32[8,1024]{1,0:T(8,128)} %get-tuple-element.60) | copy-start | bytes 98308
  27.9 0.8 copy-start
  28.7 50.4 %all-to-all-start = ((f32[5248,1,128]{2,1,0:T(1,128)}), f32[5248,1,128]{2,1,0:T(1,128)S(1)}, u32[]{:S(2)}, u32[]{:S(2)}) async-start(f32[5248,1,128]{2,1,0:T(1,128)} %bitcast.18), calls=%async_computation | async-start | bytes 5373952 | tf_op jit(solution)/shard_map/cond/branch_1_fun/all_to_all | solution.py:491
  40.6 3.1 %copy-start.1 = (bf16[4,128,128]{2,1,0:T(8,128)(2,1)S(1)}, bf16[4,128,128]{2,1,0:T(8,128)(2,1)}, u32[]{:S(2)}) copy-start(bf16[4,128,128]{2,1,0:T(8,128)(2,1)} %get-tuple-element.27.parts) | copy-start | bytes 393220 | tf_op jit(solution)/shard_map/cond
  42.7 42.1 %collective-permute-start = (f32[2,4,128,128]{3,2,1,0:T(8,128)}, f32[2,4,128,128]{3,2,1,0:T(8,128)}, u32[]{:S(2)}, u32[]{:S(2)}) collective-permute-start(f32[2,4,128,128]{3,2,1,0:T(8,128)} %slice_select_fusion), channel_id=1, source_target_pairs={{0,2},{1,3},{2,4},{3,5},{4,6},{5,7},{6,0},{7,1},{8,10},{9,11},{10,... | collective-permute-start | bytes 1572872 | tf_op jit(solution)/shard_map/cond/branch_1_fun/ppermute | solution.py:490
